TPU v7x, 32 devices: a whole 2x2x4 slice. The times are simulated.
32 devices in a mesh: dp: 8 (over y, x, core), tensor: 4 (over z).
Axes of the slice: x: 2, y: 2, z: 4, core: 2. Of those that a mesh axis runs over, the one named last changes fastest.
Arguments:
- tokens: bfloat16 [4096, 2048], P('dp'), may hold values from -6 to 6
- cotangent: bfloat16 [4096, 2048], P('dp'), may hold values from -6 to 6
- parents: int32 [8, 4], P('dp'), may hold values from 0 to 2, as said below
- attention_routes: int32 [4096, 2], P('dp'), may hold values from 0 to 7, all different within a row; in each aligned block of 512 rows (0 to 511, 512 to 1023, ...) at most 160 rows name the same one
- expert_routes: int32 [4096, 2], P('dp'), may hold values from 0 to 7, all different within a row
- slot_order: int32 [8, 512], P('dp'), may hold values from 0 to 511, each once within a row
- gain_attention: bfloat16 [2048], P('dp'), may hold values from 0.5 to 1.5
- keyval_weight: bfloat16 [2, 2048, 2048], P(None, 'dp', 'tensor'), may hold values from -0.125 to 0.125
- query_weight: bfloat16 [8, 2048, 2048], P(None, 'dp', 'tensor'), may hold values from -0.125 to 0.125
- output_weight: bfloat16 [8, 2048, 2048], P(None, 'tensor', 'dp'), may hold values from -1.5 to 1.5
- attention_router: bfloat16 [2048, 8], P('dp'), may hold values from -0.0625 to 0.0625
- gain_feedforward: bfloat16 [2048], P('dp'), may hold values from 0.5 to 1.5
- expert_router: bfloat16 [2048, 8], P('dp'), may hold values from -0.0625 to 0.0625
- gate_up_weight: bfloat16 [8, 2, 2048, 5632], P(None, None, 'dp', 'tensor'), may hold values from -0.125 to 0.125
- down_weight: bfloat16 [8, 5632, 2048], P(None, 'tensor', 'dp'), may hold values from -0.15625 to 0.15625
Outputs:
- mixed: bfloat16 [4096, 2048], P('dp')
- grad_tokens: float32 [4096, 2048], P('dp')
- grad_gain_attention: float32 [2048], P('dp')
- grad_keyval: float32 [2, 2048, 2048], P(None, 'dp', 'tensor')
- grad_query: float32 [8, 2048, 2048], P(None, 'dp', 'tensor')
- grad_output: float32 [8, 2048, 2048], P(None, 'tensor', 'dp')
- grad_attention_router: float32 [2048, 8], P('dp')
- grad_gain_feedforward: float32 [2048], P('dp')
- grad_expert_router: float32 [2048, 8], P('dp')
- grad_gate_up: float32 [8, 2, 2048, 5632], P(None, None, 'dp', 'tensor')
- grad_down: float32 [8, 5632, 2048], P(None, 'tensor', 'dp')
Inputs may be any that keep to these rules, and one draw needn't show every extreme that they name: `parents`: segment 0 of each tree is its root with parent 0; every other segment's parent is an earlier segment, and the last segment's parent is the one before it. `attention_routes`: each token names two different attention experts; among the pairs of one tree no attention expert is named more than 160 times, and in every draw some tree names some expert exactly 160 times. `expert_routes`: each token names two different feed-forward experts. `slot_order`: each tree's row holds every number of 0 to 511 once.
All inputs are finite; a program needn't handle non-finite values.
Results may differ from a plain program's by a relative error of at most 0.019.
Values may be sent and summed in bfloat16 or wider, within the bound.
A program may use at most 512 MiB of HBM per device.

v0:
```python
import jax
import jax.numpy as jnp
from jax import lax
from jax.sharding import PartitionSpec as P

HD = 128
TOPK = 2
SEG = 128


EPSILON = 1e-06
NEGATIVE = -1e30
ROPE_BASE = 10000.0


def pad_rows(matrix):
    return jnp.concatenate([matrix, jnp.zeros((1,) + matrix.shape[1:], matrix.dtype)], axis=0)


def slot_maps(routes, priority, capacity, experts):
    pair_total = routes.shape[0] * routes.shape[1]
    flat_routes = routes.reshape(pair_total)
    flat_order = priority.reshape(pair_total)
    numbers = jnp.arange(pair_total, dtype=jnp.int32)
    same_expert = flat_routes[:, None] == flat_routes[None, :]
    earlier = flat_order[None, :] < flat_order[:, None]
    slot_rank = jnp.sum((same_expert & earlier).astype(jnp.int32), axis=1)
    slot_place = jnp.where(
        slot_rank < capacity, flat_routes * capacity + slot_rank, experts * capacity
    )
    slot_index = jnp.arange(experts * capacity, dtype=jnp.int32)
    matches = slot_place[None, :] == slot_index[:, None]
    found = jnp.any(matches, axis=1)
    picked = jnp.sum(jnp.where(matches, numbers[None, :], 0), axis=1)
    slot_source = jnp.where(found, picked, pair_total)
    return (slot_place, slot_source)


def ancestry(parent_row):
    segment_count = parent_row.shape[0]
    indices = jnp.arange(segment_count, dtype=jnp.int32)
    walker = indices
    inside = indices[:, None] == indices[None, :]
    for travel in range(segment_count):
        walker = parent_row[walker]
        inside = inside | (walker[:, None] == indices[None, :])
    depth = jnp.sum(inside.astype(jnp.int32), axis=1) - 1
    return (inside, depth)


def rope_tables(position):
    half_width = HD // 2
    frequency = ROPE_BASE ** (-jnp.arange(half_width, dtype=jnp.float32) / half_width)
    angles = position.astype(jnp.float32)[:, None] * frequency[None, :]
    return (jnp.cos(angles)[:, None, :], jnp.sin(angles)[:, None, :])


def rotate(vector, cosine_table, sine_table):
    half_width = vector.shape[-1] // 2
    former, latter = (vector[..., :half_width], vector[..., half_width:])
    return jnp.concatenate(
        [former * cosine_table - latter * sine_table, latter * cosine_table + former * sine_table],
        axis=-1,
    )


def rotate_back(vector, cosine_table, sine_table):
    half_width = vector.shape[-1] // 2
    former, latter = (vector[..., :half_width], vector[..., half_width:])
    return jnp.concatenate(
        [former * cosine_table + latter * sine_table, latter * cosine_table - former * sine_table],
        axis=-1,
    )


def norm_forward(values_in):
    scale = lax.rsqrt(jnp.mean(values_in * values_in, axis=-1, keepdims=True) + EPSILON)
    return (values_in * scale, scale)


def norm_backward(grad_normed, normal, scale, gain):
    weighted = grad_normed * gain
    grad_in = scale * (weighted - normal * jnp.mean(weighted * normal, axis=-1, keepdims=True))
    return (grad_in, jnp.sum(grad_normed * normal, axis=0))


def router_backward(gates, grad_gates, picks, experts):
    grad_select = gates * (grad_gates - jnp.sum(gates * grad_gates, axis=1, keepdims=True))
    picked_hot = (picks[:, :, None] == jnp.arange(experts, dtype=jnp.int32)[None, None, :]).astype(
        jnp.float32
    )
    return jnp.sum(picked_hot * grad_select[:, :, None], axis=1).astype(jnp.bfloat16)


def visible(inside, seg_rows, seg_cols, tok_rows, tok_cols):
    segment_count = inside.shape[0]
    row_hot = (seg_rows[:, None] == jnp.arange(segment_count)[None, :]).astype(jnp.float32)
    col_hot = (seg_cols[None, :] == jnp.arange(segment_count)[:, None]).astype(jnp.float32)
    reach = jnp.dot(jnp.dot(row_hot, inside.astype(jnp.float32)), col_hot)
    return (reach > 0.5) & (tok_cols[None, :] <= tok_rows[:, None])


def block_scores(query_block, key_rows, allowed):
    scores = jnp.einsum(
        "phd,jhd->hpj", query_block, key_rows, preferred_element_type=jnp.float32
    ) * HD ** (-0.5)
    return jnp.where(allowed[None], scores, NEGATIVE)


def on_device(
    tokens,
    cotangent,
    parents,
    attention_routes,
    expert_routes,
    slot_order,
    gain_attention,
    keyval_weight,
    query_weight,
    output_weight,
    attention_router,
    gain_feedforward,
    expert_router,
    gate_up_weight,
    down_weight,
):
    gathered = (
        lax.all_gather(gain_attention, "dp", axis=0, tiled=True),
        lax.all_gather(keyval_weight, "dp", axis=1, tiled=True),
        lax.all_gather(query_weight, "dp", axis=1, tiled=True),
        lax.all_gather(output_weight, "dp", axis=2, tiled=True),
        lax.all_gather(attention_router, "dp", axis=0, tiled=True),
        lax.all_gather(gain_feedforward, "dp", axis=0, tiled=True),
        lax.all_gather(expert_router, "dp", axis=0, tiled=True),
    )
    gain_attn_full = gathered[0].astype(jnp.float32)
    keyval_full, query_full, output_full, router_att = (
        gathered[1],
        gathered[2],
        gathered[3],
        gathered[4],
    )
    gain_mlp_full = gathered[5].astype(jnp.float32)
    router_mlp = gathered[6]
    tok_count = tokens.shape[0]
    model_width = tokens.shape[1]
    pair_count = TOPK * tok_count
    width_here = keyval_full.shape[2]
    heads_here = width_here // HD
    att_experts = query_full.shape[0]
    mlp_experts = gate_up_weight.shape[0]
    att_cap = tok_count * 5 // 16
    mlp_cap = pair_count // mlp_experts
    inside, depth = ancestry(parents[0])
    token_index = jnp.arange(tok_count, dtype=jnp.int32)
    segment = token_index // SEG
    position = depth[segment] * SEG + token_index % SEG
    cosine_table, sine_table = rope_tables(position)
    pair_cosine = jnp.repeat(cosine_table, TOPK, axis=0)
    pair_sine = jnp.repeat(sine_table, TOPK, axis=0)
    inputs = tokens.astype(jnp.float32)
    normal_attn, scale_attn = norm_forward(inputs)
    normed = (normal_attn * gain_attn_full).astype(jnp.bfloat16)
    keyval = jnp.einsum("td,cdf->ctf", normed, keyval_full, preferred_element_type=jnp.float32)
    key_rows = rotate(
        keyval[0].reshape(tok_count, heads_here, HD), cosine_table, sine_table
    ).astype(jnp.bfloat16)
    values = keyval[1].reshape(tok_count, heads_here, HD).astype(jnp.bfloat16)
    att_logits = jnp.dot(normed, router_att, preferred_element_type=jnp.float32)
    att_gates = jax.nn.softmax(jnp.take_along_axis(att_logits, attention_routes, axis=1), axis=-1)
    pair_order = jnp.arange(pair_count, dtype=jnp.int32).reshape(tok_count, TOPK)
    att_place, att_source = slot_maps(attention_routes, pair_order, att_cap, att_experts)
    slot_token = jnp.where(att_source < pair_count, att_source // TOPK, tok_count)
    routed = pad_rows(normed)[slot_token].reshape(att_experts, att_cap, model_width)
    query_slots = jnp.einsum("ecd,edf->ecf", routed, query_full, preferred_element_type=jnp.float32)
    query_raw = query_slots.reshape(att_experts * att_cap, width_here)[att_place]
    queries = rotate(query_raw.reshape(pair_count, heads_here, HD), pair_cosine, pair_sine).astype(
        jnp.bfloat16
    )
    block_rows = min(512, pair_count)
    blocks = pair_count // block_rows
    query_blocks = queries.reshape(blocks, block_rows, heads_here, HD)
    starts = jnp.arange(blocks, dtype=jnp.int32) * block_rows

    def mask_for(row_start):
        rows_token = (row_start + jnp.arange(block_rows, dtype=jnp.int32)) // TOPK
        return visible(inside, segment[rows_token], segment, rows_token, token_index)

    def attend(packed):
        query_block, row_start = packed
        scores = block_scores(query_block, key_rows, mask_for(row_start))
        highest = jnp.max(scores, axis=-1, keepdims=True)
        exp_scores = jnp.exp(scores - highest)
        row_total = jnp.sum(exp_scores, axis=-1, keepdims=True)
        probs = (exp_scores / row_total).astype(jnp.bfloat16)
        attended = jnp.einsum("hpj,jhd->phd", probs, values, preferred_element_type=jnp.float32)
        return (attended, (highest + jnp.log(row_total))[..., 0])

    attended_blocks, logsum = lax.map(attend, (query_blocks, starts))
    attended_pairs = attended_blocks.reshape(pair_count, width_here)
    pair_gate = att_gates.reshape(pair_count, 1)
    gated = (attended_pairs * pair_gate).astype(jnp.bfloat16)
    gated_slots = pad_rows(gated)[att_source].reshape(att_experts, att_cap, width_here)
    att_slots = jnp.einsum(
        "ecf,efd->ecd", gated_slots, output_full, preferred_element_type=jnp.float32
    )
    att_part = (
        att_slots.reshape(att_experts * att_cap, model_width)[att_place]
        .reshape(tok_count, TOPK, model_width)
        .sum(axis=1)
    )
    hidden_state = inputs + lax.psum(att_part, "tensor")
    normal_mlp, scale_mlp = norm_forward(hidden_state)
    mlp_in = (normal_mlp * gain_mlp_full).astype(jnp.bfloat16)
    mlp_logits = jnp.dot(mlp_in, router_mlp, preferred_element_type=jnp.float32)
    mlp_gates = jax.nn.softmax(jnp.take_along_axis(mlp_logits, expert_routes, axis=1), axis=-1)
    priority = slot_order[0][:, None] * TOPK + jnp.arange(TOPK, dtype=jnp.int32)[None, :]
    mlp_place, mlp_source = slot_maps(expert_routes, priority, mlp_cap, mlp_experts)
    mlp_token = jnp.where(mlp_source < pair_count, mlp_source // TOPK, tok_count)
    expert_in = pad_rows(mlp_in)[mlp_token].reshape(mlp_experts, mlp_cap, model_width)
    kept_weights = []
    gate_ups = []
    expert_outs = []
    for expert in range(mlp_experts):
        up_full, down_full = (
            lax.all_gather(gate_up_weight[expert], "dp", axis=1, tiled=True),
            lax.all_gather(down_weight[expert], "dp", axis=1, tiled=True),
        )
        gate_up = jnp.einsum(
            "cd,gdf->gcf", expert_in[expert], up_full, preferred_element_type=jnp.float32
        )
        activated = (jax.nn.silu(gate_up[0]) * gate_up[1]).astype(jnp.bfloat16)
        expert_outs.append(jnp.dot(activated, down_full, preferred_element_type=jnp.float32))
        gate_ups.append(gate_up)
        kept_weights.append((up_full, down_full))
    routed_out = pad_rows(jnp.concatenate(expert_outs, axis=0))[mlp_place]
    mlp_part = (
        (routed_out * mlp_gates.reshape(pair_count, 1))
        .reshape(tok_count, TOPK, model_width)
        .sum(axis=1)
    )
    block_out = hidden_state + lax.psum(mlp_part.astype(jnp.bfloat16), "tensor").astype(jnp.float32)
    grad_out = cotangent.astype(jnp.float32)
    grad_pairs = jnp.repeat(grad_out, TOPK, axis=0)
    grad_gates_part = jnp.sum(grad_pairs * routed_out, axis=-1).reshape(tok_count, TOPK)
    grad_slots_in = (
        pad_rows(grad_pairs * mlp_gates.reshape(pair_count, 1))[mlp_source]
        .astype(jnp.bfloat16)
        .reshape(mlp_experts, mlp_cap, model_width)
    )
    grad_expert_in = []
    up_shards = []
    down_shards = []
    for expert in range(mlp_experts):
        up_full, down_full = kept_weights[expert]
        gate_up = gate_ups[expert]
        sigmoid_gate = jax.nn.sigmoid(gate_up[0])
        silu_gate = gate_up[0] * sigmoid_gate
        activated = (silu_gate * gate_up[1]).astype(jnp.bfloat16)
        grad_slot = grad_slots_in[expert]
        grad_act = jnp.einsum("cd,fd->cf", grad_slot, down_full, preferred_element_type=jnp.float32)
        grad_gate = (
            grad_act * gate_up[1] * sigmoid_gate * (1.0 + gate_up[0] * (1.0 - sigmoid_gate))
        ).astype(jnp.bfloat16)
        grad_up = (grad_act * silu_gate).astype(jnp.bfloat16)
        grad_both = jnp.stack([grad_gate, grad_up])
        grad_expert_in.append(
            jnp.einsum("gcf,gdf->cd", grad_both, up_full, preferred_element_type=jnp.float32)
        )
        grad_down_w = jnp.einsum(
            "cf,cd->fd", activated, grad_slot, preferred_element_type=jnp.float32
        )
        grad_up_w = jnp.einsum(
            "cd,gcf->gdf", expert_in[expert], grad_both, preferred_element_type=jnp.float32
        )
        shard_up, shard_down = (
            lax.psum_scatter(
                grad_up_w.astype(jnp.bfloat16), "dp", scatter_dimension=1, tiled=True
            ).astype(jnp.float32),
            lax.psum_scatter(
                grad_down_w.astype(jnp.bfloat16), "dp", scatter_dimension=1, tiled=True
            ).astype(jnp.float32),
        )
        up_shards.append(shard_up)
        down_shards.append(shard_down)
    grad_mlp_part = (
        pad_rows(jnp.concatenate(grad_expert_in, axis=0))[mlp_place]
        .reshape(tok_count, TOPK, model_width)
        .sum(axis=1)
    )
    grad_mlp_in, grad_mlp_gates = lax.psum((grad_mlp_part, grad_gates_part), "tensor")
    grad_mlp_logits = router_backward(mlp_gates, grad_mlp_gates, expert_routes, mlp_experts)
    grad_router_mlp = jnp.einsum(
        "td,te->de", mlp_in, grad_mlp_logits, preferred_element_type=jnp.float32
    )
    grad_mlp_in = grad_mlp_in + jnp.einsum(
        "te,de->td", grad_mlp_logits, router_mlp, preferred_element_type=jnp.float32
    )
    grad_hidden_norm, grad_gain_mlp = norm_backward(
        grad_mlp_in, normal_mlp, scale_mlp, gain_mlp_full
    )
    grad_hidden = grad_out + grad_hidden_norm
    grad_att_slots = (
        pad_rows(jnp.repeat(grad_hidden, TOPK, axis=0))[att_source]
        .astype(jnp.bfloat16)
        .reshape(att_experts, att_cap, model_width)
    )
    grad_output_w = jnp.einsum(
        "ecf,ecd->efd", gated_slots, grad_att_slots, preferred_element_type=jnp.float32
    )
    grad_gated_slots = jnp.einsum(
        "ecd,efd->ecf", grad_att_slots, output_full, preferred_element_type=jnp.float32
    )
    grad_gated = grad_gated_slots.reshape(att_experts * att_cap, width_here)[att_place]
    grad_att_part = jnp.sum(grad_gated * attended_pairs, axis=-1).reshape(tok_count, TOPK)
    grad_attended = (grad_gated * pair_gate).astype(jnp.bfloat16)

    def attend_back(carried, packed):
        query_block, grad_block, logsum_block, row_start = packed
        scores = block_scores(query_block, key_rows, mask_for(row_start))
        probs = jnp.exp(scores - logsum_block[..., None])
        grad_probs = jnp.einsum(
            "phd,jhd->hpj", grad_block, values, preferred_element_type=jnp.float32
        )
        centre = jnp.sum(probs * grad_probs, axis=-1, keepdims=True)
        grad_scores = (probs * (grad_probs - centre)).astype(jnp.bfloat16)
        grad_query = jnp.einsum(
            "hpj,jhd->phd", grad_scores, key_rows, preferred_element_type=jnp.float32
        ) * HD ** (-0.5)
        grad_keys = carried[0] + jnp.einsum(
            "hpj,phd->jhd", grad_scores, query_block, preferred_element_type=jnp.float32
        ) * HD ** (-0.5)
        grad_values = carried[1] + jnp.einsum(
            "hpj,phd->jhd",
            probs.astype(jnp.bfloat16),
            grad_block,
            preferred_element_type=jnp.float32,
        )
        return ((grad_keys, grad_values), grad_query)

    zero_rows = jnp.zeros((tok_count, heads_here, HD), jnp.float32)
    key_value_grads, grad_queries = lax.scan(
        attend_back,
        (zero_rows, zero_rows),
        (query_blocks, grad_attended.reshape(blocks, block_rows, heads_here, HD), logsum, starts),
    )
    grad_query_raw = rotate_back(
        grad_queries.reshape(pair_count, heads_here, HD), pair_cosine, pair_sine
    ).reshape(pair_count, width_here)
    grad_query_slots = (
        pad_rows(grad_query_raw)[att_source]
        .astype(jnp.bfloat16)
        .reshape(att_experts, att_cap, width_here)
    )
    grad_query_w = jnp.einsum(
        "ecd,ecf->edf", routed, grad_query_slots, preferred_element_type=jnp.float32
    )
    grad_routed = jnp.einsum(
        "ecf,edf->ecd", grad_query_slots, query_full, preferred_element_type=jnp.float32
    )
    grad_normed = (
        pad_rows(grad_routed.reshape(att_experts * att_cap, model_width))[att_place]
        .reshape(tok_count, TOPK, model_width)
        .sum(axis=1)
    )
    grad_key_raw = rotate_back(key_value_grads[0], cosine_table, sine_table).reshape(
        tok_count, width_here
    )
    grad_kv_raw = jnp.stack(
        [grad_key_raw, key_value_grads[1].reshape(tok_count, width_here)]
    ).astype(jnp.bfloat16)
    grad_keyval_w = jnp.einsum(
        "td,ctf->cdf", normed, grad_kv_raw, preferred_element_type=jnp.float32
    )
    grad_normed = grad_normed + jnp.einsum(
        "ctf,cdf->td", grad_kv_raw, keyval_full, preferred_element_type=jnp.float32
    )
    grad_normed, grad_att_gates = lax.psum((grad_normed, grad_att_part), "tensor")
    grad_att_logits = router_backward(att_gates, grad_att_gates, attention_routes, att_experts)
    grad_router_att = jnp.einsum(
        "td,te->de", normed, grad_att_logits, preferred_element_type=jnp.float32
    )
    grad_normed = grad_normed + jnp.einsum(
        "te,de->td", grad_att_logits, router_att, preferred_element_type=jnp.float32
    )
    grad_input_norm, grad_gain_attn = norm_backward(
        grad_normed, normal_attn, scale_attn, gain_attn_full
    )
    grad_tokens = grad_hidden + grad_input_norm
    shards = (
        lax.psum_scatter(
            grad_gain_attn.astype(jnp.bfloat16), "dp", scatter_dimension=0, tiled=True
        ).astype(jnp.float32),
        lax.psum_scatter(
            grad_keyval_w.astype(jnp.bfloat16), "dp", scatter_dimension=1, tiled=True
        ).astype(jnp.float32),
        lax.psum_scatter(
            grad_query_w.astype(jnp.bfloat16), "dp", scatter_dimension=1, tiled=True
        ).astype(jnp.float32),
        lax.psum_scatter(
            grad_output_w.astype(jnp.bfloat16), "dp", scatter_dimension=2, tiled=True
        ).astype(jnp.float32),
        lax.psum_scatter(
            grad_router_att.astype(jnp.bfloat16), "dp", scatter_dimension=0, tiled=True
        ).astype(jnp.float32),
        lax.psum_scatter(
            grad_gain_mlp.astype(jnp.bfloat16), "dp", scatter_dimension=0, tiled=True
        ).astype(jnp.float32),
        lax.psum_scatter(
            grad_router_mlp.astype(jnp.bfloat16), "dp", scatter_dimension=0, tiled=True
        ).astype(jnp.float32),
    )
    return (
        block_out.astype(jnp.bfloat16),
        grad_tokens,
        shards[0],
        shards[1],
        shards[2],
        shards[3],
        shards[4],
        shards[5],
        shards[6],
        jnp.stack(up_shards),
        jnp.stack(down_shards),
    )


def solution(mesh):
    placed = (
        P("dp", None),
        P("dp", None),
        P("dp", None),
        P("dp", None),
        P("dp", None),
        P("dp", None),
        P("dp"),
        P(None, "dp", "tensor"),
        P(None, "dp", "tensor"),
        P(None, "tensor", "dp"),
        P("dp", None),
        P("dp"),
        P("dp", None),
        P(None, None, "dp", "tensor"),
        P(None, "tensor", "dp"),
    )
    return jax.shard_map(
        on_device,
        mesh=mesh,
        in_specs=placed,
        out_specs=(
            P("dp", None),
            P("dp", None),
            P("dp"),
            P(None, "dp", "tensor"),
            P(None, "dp", "tensor"),
            P(None, "tensor", "dp"),
            P("dp", None),
            P("dp"),
            P("dp", None),
            P(None, None, "dp", "tensor"),
            P(None, "tensor", "dp"),
        ),
        check_vma=False,
    )
```

profile of v0, /device:TPU:0, one launch (start us, length us, event | category | flops | bytes accessed | tf_op | source)
XLA Modules:
  0.0 3715.9 jit_solution(13325160600376180085)
XLA Ops:
  65.7 76.9 %all-gather.38.cloned.1.call-done = bf16[8,2048,512]{2,1,0:T(8,128)(2,1)} async-done(((bf16[8,256,512]{2,1,0:T(8,128)(2,1)}), bf16[8,2048,512]{2,1,0:T(8,128)(2,1)}) %all-gather.38.cloned.1.call-update) | async-done | bytes 16777232 | tf_op jit(solution)/shard_map/all_gather | solution.py:130
  169.3 25.0 while.34
  202.0 35.7 all-gather.42.cloned.1.call-done
  349.5 93.4 %all-reduce.15.cloned.1.call-done = f32[512,2048]{1,0:T(8,128)} async-done(((f32[512,2048]{1,0:T(8,128)}), f32[512,2048]{1,0:T(8,128)}) %all-reduce.15.cloned.1.call-update) | async-done | bytes 4194320 | tf_op jit(solution)/shard_map/psum | solution.py:212
  454.7 56.8 %all-gather.44.cloned.1.call-done = bf16[1,2,2048,1408]{3,2,1,0:T(8,128)(2,1)} async-done(((bf16[1,2,256,1408]{3,2,1,0:T(8,128)(2,1)}), bf16[1,2,2048,1408]{3,2,1,0:T(8,128)(2,1)}) %all-gather.44.cloned.1.call-update) | async-done | bytes 11534352 | tf_op jit(solution)/shard_map/all_gather | solution.py:226
  519.0 62.2 %all-gather.48.cloned.1.call-done = bf16[1,2,2048,1408]{3,2,1,0:T(8,128)(2,1)} async-done(((bf16[1,2,256,1408]{3,2,1,0:T(8,128)(2,1)}), bf16[1,2,2048,1408]{3,2,1,0:T(8,128)(2,1)}) %all-gather.48.cloned.1.call-update) | async-done | bytes 11534352 | tf_op jit(solution)/shard_map/all_gather | solution.py:226
  588.6 39.0 %all-gather.46.cloned.1.call-done = bf16[1,1408,2048]{2,1,0:T(8,128)(2,1)} async-done(((bf16[1,1408,256]{2,1,0:T(8,128)(2,1)}), bf16[1,1408,2048]{2,1,0:T(8,128)(2,1)}) %all-gather.46.cloned.1.call-update) | async-done | bytes 5767184 | tf_op jit(solution)/shard_map/all_gather | solution.py:227
  632.2 41.7 %all-gather.50.cloned.1.call-done = bf16[1,1408,2048]{2,1,0:T(8,128)(2,1)} async-done(((bf16[1,1408,256]{2,1,0:T(8,128)(2,1)}), bf16[1,1408,2048]{2,1,0:T(8,128)(2,1)}) %all-gather.50.cloned.1.call-update) | async-done | bytes 5767184 | tf_op jit(solution)/shard_map/all_gather | solution.py:227
  678.7 65.1 %all-gather.52.cloned.1.call-done = bf16[1,2,2048,1408]{3,2,1,0:T(8,128)(2,1)} async-done(((bf16[1,2,256,1408]{3,2,1,0:T(8,128)(2,1)}), bf16[1,2,2048,1408]{3,2,1,0:T(8,128)(2,1)}) %all-gather.52.cloned.1.call-update) | async-done | bytes 11534352 | tf_op jit(solution)/shard_map/all_gather | solution.py:226
  751.2 38.8 %all-gather.54.cloned.1.call-done = bf16[1,1408,2048]{2,1,0:T(8,128)(2,1)} async-done(((bf16[1,1408,256]{2,1,0:T(8,128)(2,1)}), bf16[1,1408,2048]{2,1,0:T(8,128)(2,1)}) %all-gather.54.cloned.1.call-update) | async-done | bytes 5767184 | tf_op jit(solution)/shard_map/all_gather | solution.py:227
  794.7 65.1 %all-gather.56.cloned.1.call-done = bf16[1,2,2048,1408]{3,2,1,0:T(8,128)(2,1)} async-done(((bf16[1,2,256,1408]{3,2,1,0:T(8,128)(2,1)}), bf16[1,2,2048,1408]{3,2,1,0:T(8,128)(2,1)}) %all-gather.56.cloned.1.call-update) | async-done | bytes 11534352 | tf_op jit(solution)/shard_map/all_gather | solution.py:226
  867.3 38.8 %all-gather.58.cloned.1.call-done = bf16[1,1408,2048]{2,1,0:T(8,128)(2,1)} async-done(((bf16[1,1408,256]{2,1,0:T(8,128)(2,1)}), bf16[1,1408,2048]{2,1,0:T(8,128)(2,1)}) %all-gather.58.cloned.1.call-update) | async-done | bytes 5767184 | tf_op jit(solution)/shard_map/all_gather | solution.py:227
  910.8 65.1 %all-gather.60.cloned.1.call-done = bf16[1,2,2048,1408]{3,2,1,0:T(8,128)(2,1)} async-done(((bf16[1,2,256,1408]{3,2,1,0:T(8,128)(2,1)}), bf16[1,2,2048,1408]{3,2,1,0:T(8,128)(2,1)}) %all-gather.60.cloned.1.call-update) | async-done | bytes 11534352 | tf_op jit(solution)/shard_map/all_gather | solution.py:226
  983.6 38.6 %all-gather.62.cloned.1.call-done = bf16[1,1408,2048]{2,1,0:T(8,128)(2,1)} async-done(((bf16[1,1408,256]{2,1,0:T(8,128)(2,1)}), bf16[1,1408,2048]{2,1,0:T(8,128)(2,1)}) %all-gather.62.cloned.1.call-update) | async-done | bytes 5767184 | tf_op jit(solution)/shard_map/all_gather | solution.py:227
  1026.9 65.0 %all-gather.64.cloned.1.call-done = bf16[1,2,2048,1408]{3,2,1,0:T(8,128)(2,1)} async-done(((bf16[1,2,256,1408]{3,2,1,0:T(8,128)(2,1)}), bf16[1,2,2048,1408]{3,2,1,0:T(8,128)(2,1)}) %all-gather.64.cloned.1.call-update) | async-done | bytes 11534352 | tf_op jit(solution)/shard_map/all_gather | solution.py:226
  1099.3 38.8 %all-gather.66.cloned.1.call-done = bf16[1,1408,2048]{2,1,0:T(8,128)(2,1)} async-done(((bf16[1,1408,256]{2,1,0:T(8,128)(2,1)}), bf16[1,1408,2048]{2,1,0:T(8,128)(2,1)}) %all-gather.66.cloned.1.call-update) | async-done | bytes 5767184 | tf_op jit(solution)/shard_map/all_gather | solution.py:227
  1142.8 65.0 %all-gather.68.cloned.1.call-done = bf16[1,2,2048,1408]{3,2,1,0:T(8,128)(2,1)} async-done(((bf16[1,2,256,1408]{3,2,1,0:T(8,128)(2,1)}), bf16[1,2,2048,1408]{3,2,1,0:T(8,128)(2,1)}) %all-gather.68.cloned.1.call-update) | async-done | bytes 11534352 | tf_op jit(solution)/shard_map/all_gather | solution.py:226
  1215.2 38.8 %all-gather.70.cloned.1.call-done = bf16[1,1408,2048]{2,1,0:T(8,128)(2,1)} async-done(((bf16[1,1408,256]{2,1,0:T(8,128)(2,1)}), bf16[1,1408,2048]{2,1,0:T(8,128)(2,1)}) %all-gather.70.cloned.1.call-update) | async-done | bytes 5767184 | tf_op jit(solution)/shard_map/all_gather | solution.py:227
  1258.7 65.7 %all-gather.72.cloned.1.call-done = bf16[1,2,2048,1408]{3,2,1,0:T(8,128)(2,1)} async-done(((bf16[1,2,256,1408]{3,2,1,0:T(8,128)(2,1)}), bf16[1,2,2048,1408]{3,2,1,0:T(8,128)(2,1)}) %all-gather.72.cloned.1.call-update) | async-done | bytes 11534352 | tf_op jit(solution)/shard_map/all_gather | solution.py:226
  1331.9 38.8 %all-gather.74.cloned.1.call-done = bf16[1,1408,2048]{2,1,0:T(8,128)(2,1)} async-done(((bf16[1,1408,256]{2,1,0:T(8,128)(2,1)}), bf16[1,1408,2048]{2,1,0:T(8,128)(2,1)}) %all-gather.74.cloned.1.call-update) | async-done | bytes 5767184 | tf_op jit(solution)/shard_map/all_gather | solution.py:227
  1574.4 15.7 multiply_reduce_fusion.2
  1591.5 124.4 %all-reduce.19.cloned.1.call-done = f32[512,2048]{1,0:T(8,128)} async-done(((f32[512,2048]{1,0:T(8,128)}), f32[512,2048]{1,0:T(8,128)}) %all-reduce.19.cloned.1.call-update) | async-done | bytes 4194320 | tf_op jit(solution)/shard_map/psum | solution.py:291
  1723.2 80.6 %all-reduce.17.cloned.1.call-done = bf16[512,2048]{1,0:T(8,128)(2,1)} async-done(((bf16[512,2048]{1,0:T(8,128)(2,1)}), bf16[512,2048]{1,0:T(8,128)(2,1)}) %all-reduce.17.cloned.1.call-update) | async-done | bytes 2097168 | tf_op jit(solution)/shard_map/psum | solution.py:242
  1828.1 13.6 gather_fusion.14
  1864.2 49.8 %while.35 = (s32[]{:T(128)}, f32[512,4,128]{0,2,1:T(8,128)}, f32[512,4,128]{0,2,1:T(8,128)}, f32[2,512,4,128]{3,1,0,2:T(8,128)}, bf16[2,512,4,128]{3,1,2,0:T(8,1...) while((s32[]{:T(128)}, f32[512,4,128]{0,2,1:T(8,128)}, ...), condition=%wide.region_30.32_spmd.clone.clone, body=%wide.region_28.31_spmd.clone.clone.sunk | while | flops 1362403968 | bytes 92356992 | solution.py:342
  1983.1 13.5 reduce_sum.256
  2155.8 28.6 all-reduce.21.cloned.1.call-done
  2190.0 14.1 all-reduce.9
  2212.2 34.2 reduce-scatter.48.cloned.1.call-done
  2248.4 60.7 %reduce-scatter.50.cloned.1.call-done = bf16[1408,256]{1,0:T(8,128)(2,1)} async-done(((bf16[1408,2048]{1,0:T(8,128)(2,1)}), bf16[1408,256]{1,0:T(8,128)(2,1)}) %reduce-scatter.50.cloned.1.call-update) | async-done | bytes 720912 | tf_op jit(solution)/shard_map/reduce_scatter | solution.py:280
  2311.1 60.5 %reduce-scatter.52.cloned.1.call-done = bf16[1408,256]{1,0:T(8,128)(2,1)} async-done(((bf16[1408,2048]{1,0:T(8,128)(2,1)}), bf16[1408,256]{1,0:T(8,128)(2,1)}) %reduce-scatter.52.cloned.1.call-update) | async-done | bytes 720912 | tf_op jit(solution)/shard_map/reduce_scatter | solution.py:280
  2373.7 60.8 %reduce-scatter.54.cloned.1.call-done = bf16[1408,256]{1,0:T(8,128)(2,1)} async-done(((bf16[1408,2048]{1,0:T(8,128)(2,1)}), bf16[1408,256]{1,0:T(8,128)(2,1)}) %reduce-scatter.54.cloned.1.call-update) | async-done | bytes 720912 | tf_op jit(solution)/shard_map/reduce_scatter | solution.py:280
  2436.6 60.3 %reduce-scatter.56.cloned.1.call-done = bf16[1408,256]{1,0:T(8,128)(2,1)} async-done(((bf16[1408,2048]{1,0:T(8,128)(2,1)}), bf16[1408,256]{1,0:T(8,128)(2,1)}) %reduce-scatter.56.cloned.1.call-update) | async-done | bytes 720912 | tf_op jit(solution)/shard_map/reduce_scatter | solution.py:280
  2498.9 60.9 %reduce-scatter.58.cloned.1.call-done = bf16[1408,256]{1,0:T(8,128)(2,1)} async-done(((bf16[1408,2048]{1,0:T(8,128)(2,1)}), bf16[1408,256]{1,0:T(8,128)(2,1)}) %reduce-scatter.58.cloned.1.call-update) | async-done | bytes 720912 | tf_op jit(solution)/shard_map/reduce_scatter | solution.py:280
  2561.8 60.5 %reduce-scatter.60.cloned.1.call-done = bf16[1408,256]{1,0:T(8,128)(2,1)} async-done(((bf16[1408,2048]{1,0:T(8,128)(2,1)}), bf16[1408,256]{1,0:T(8,128)(2,1)}) %reduce-scatter.60.cloned.1.call-update) | async-done | bytes 720912 | tf_op jit(solution)/shard_map/reduce_scatter | solution.py:280
  2624.3 60.7 %reduce-scatter.62.cloned.1.call-done = bf16[1408,256]{1,0:T(8,128)(2,1)} async-done(((bf16[1408,2048]{1,0:T(8,128)(2,1)}), bf16[1408,256]{1,0:T(8,128)(2,1)}) %reduce-scatter.62.cloned.1.call-update) | async-done | bytes 720912 | tf_op jit(solution)/shard_map/reduce_scatter | solution.py:280
  2695.2 44.6 %reduce-scatter.22.cloned.1.call-done = bf16[2,256,512]{1,2,0:T(8,128)(2,1)} async-done(((bf16[2,2048,512]{1,2,0:T(8,128)(2,1)}), bf16[2,256,512]{1,2,0:T(8,128)(2,1)}) %reduce-scatter.22.cloned.1.call-update) | async-done | bytes 524304 | tf_op jit(solution)/shard_map/reduce_scatter | solution.py:394
  2742.0 89.0 %reduce-scatter.32.cloned.1.call-done = bf16[2,256,1408]{1,2,0:T(8,128)(2,1)} async-done(((bf16[2,2048,1408]{1,2,0:T(8,128)(2,1)}), bf16[2,256,1408]{1,2,0:T(8,128)(2,1)}) %reduce-scatter.32.cloned.1.call-update) | async-done | bytes 1441808 | tf_op jit(solution)/shard_map/reduce_scatter | solution.py:277
  2833.6 88.0 %reduce-scatter.34.cloned.1.call-done = bf16[2,256,1408]{1,2,0:T(8,128)(2,1)} async-done(((bf16[2,2048,1408]{1,2,0:T(8,128)(2,1)}), bf16[2,256,1408]{1,2,0:T(8,128)(2,1)}) %reduce-scatter.34.cloned.1.call-update) | async-done | bytes 1441808 | tf_op jit(solution)/shard_map/reduce_scatter | solution.py:277
  2924.2 87.9 %reduce-scatter.36.cloned.1.call-done = bf16[2,256,1408]{1,2,0:T(8,128)(2,1)} async-done(((bf16[2,2048,1408]{1,2,0:T(8,128)(2,1)}), bf16[2,256,1408]{1,2,0:T(8,128)(2,1)}) %reduce-scatter.36.cloned.1.call-update) | async-done | bytes 1441808 | tf_op jit(solution)/shard_map/reduce_scatter | solution.py:277
  3014.6 88.1 %reduce-scatter.38.cloned.1.call-done = bf16[2,256,1408]{1,2,0:T(8,128)(2,1)} async-done(((bf16[2,2048,1408]{1,2,0:T(8,128)(2,1)}), bf16[2,256,1408]{1,2,0:T(8,128)(2,1)}) %reduce-scatter.38.cloned.1.call-update) | async-done | bytes 1441808 | tf_op jit(solution)/shard_map/reduce_scatter | solution.py:277
  3105.4 88.0 %reduce-scatter.40.cloned.1.call-done = bf16[2,256,1408]{1,2,0:T(8,128)(2,1)} async-done(((bf16[2,2048,1408]{1,2,0:T(8,128)(2,1)}), bf16[2,256,1408]{1,2,0:T(8,128)(2,1)}) %reduce-scatter.40.cloned.1.call-update) | async-done | bytes 1441808 | tf_op jit(solution)/shard_map/reduce_scatter | solution.py:277
  3195.9 88.1 %reduce-scatter.42.cloned.1.call-done = bf16[2,256,1408]{1,2,0:T(8,128)(2,1)} async-done(((bf16[2,2048,1408]{1,2,0:T(8,128)(2,1)}), bf16[2,256,1408]{1,2,0:T(8,128)(2,1)}) %reduce-scatter.42.cloned.1.call-update) | async-done | bytes 1441808 | tf_op jit(solution)/shard_map/reduce_scatter | solution.py:277
  3286.6 88.1 %reduce-scatter.44.cloned.1.call-done = bf16[2,256,1408]{1,2,0:T(8,128)(2,1)} async-done(((bf16[2,2048,1408]{1,2,0:T(8,128)(2,1)}), bf16[2,256,1408]{1,2,0:T(8,128)(2,1)}) %reduce-scatter.44.cloned.1.call-update) | async-done | bytes 1441808 | tf_op jit(solution)/shard_map/reduce_scatter | solution.py:277
  3377.3 88.1 %reduce-scatter.46.cloned.1.call-done = bf16[2,256,1408]{1,2,0:T(8,128)(2,1)} async-done(((bf16[2,2048,1408]{1,2,0:T(8,128)(2,1)}), bf16[2,256,1408]{1,2,0:T(8,128)(2,1)}) %reduce-scatter.46.cloned.1.call-update) | async-done | bytes 1441808 | tf_op jit(solution)/shard_map/reduce_scatter | solution.py:277
  3467.9 17.7 copy.284
  3485.6 99.6 %reduce-scatter.24.cloned.1.call-done = bf16[8,256,512]{2,1,0:T(8,128)(2,1)} async-done(((bf16[8,2048,512]{2,1,0:T(8,128)(2,1)}), bf16[8,256,512]{2,1,0:T(8,128)(2,1)}) %reduce-scatter.24.cloned.1.call-update) | async-done | bytes 2097168 | tf_op jit(solution)/shard_map/reduce_scatter | solution.py:397
  3589.4 115.8 %reduce-scatter.26.cloned.1.call-done = bf16[8,512,256]{2,1,0:T(8,128)(2,1)} async-done(((bf16[8,512,2048]{2,1,0:T(8,128)(2,1)}), bf16[8,512,256]{2,1,0:T(8,128)(2,1)}) %reduce-scatter.26.cloned.1.call-update) | async-done | bytes 2097168 | tf_op jit(solution)/shard_map/reduce_scatter | solution.py:400
  (770 shorter events, 936.6 us)
Async XLA Ops:
  7.2 50.6 %all-gather.40.cloned.1.call-start = ((), (), s32[]{:S(2)}) async-start(), calls=%async_computation.22 | async-start | bytes 4718592 | tf_op jit(solution)/shard_map/all_gather | solution.py:129
  9.3 133.3 %all-gather.38.cloned.1.call-start = ((), (), s32[]{:S(2)}) async-start(), calls=%async_computation.21 | async-start | bytes 18874368 | tf_op jit(solution)/shard_map/all_gather | solution.py:130
  10.1 227.6 %all-gather.42.cloned.1.call-start = ((), (), s32[]{:S(2)}) async-start(), calls=%async_computation.23 | async-start | bytes 18874368 | tf_op jit(solution)/shard_map/all_gather | solution.py:131
  10.8 432.0 %all-reduce.15.cloned.1.call-start = ((), (), s32[]{:S(2)}) async-start(), calls=%async_computation.24 | async-start | bytes 8388608 | tf_op jit(solution)/shard_map/psum | solution.py:212
  57.8 192.8 %copy-start.116 = (s32[1024]{0:T(1024)}, s32[1024]{0:T(1024)S(1)}, u32[]{:S(2)}) copy-start(s32[1024]{0:T(1024)S(1)} %broadcast_clamp_fusion.4) | copy-start | bytes 12292
  287.7 223.8 %all-gather.44.cloned.1.call-start = ((), (), s32[]{:S(2)}) async-start(), calls=%async_computation.49 | async-start | bytes 12976128 | tf_op jit(solution)/shard_map/all_gather | solution.py:226
  296.4 284.8 %all-gather.48.cloned.1.call-start = ((), (), s32[]{:S(2)}) async-start(), calls=%async_computation.51 | async-start | bytes 12976128 | tf_op jit(solution)/shard_map/all_gather | solution.py:226
  297.0 330.6 %all-gather.46.cloned.1.call-start = ((), (), s32[]{:S(2)}) async-start(), calls=%async_computation.50 | async-start | bytes 6488064 | tf_op jit(solution)/shard_map/all_gather | solution.py:227
  302.3 371.7 %all-gather.50.cloned.1.call-start = ((), (), s32[]{:S(2)}) async-start(), calls=%async_computation.52 | async-start | bytes 6488064 | tf_op jit(solution)/shard_map/all_gather | solution.py:227
  303.0 440.8 %all-gather.52.cloned.1.call-start = ((), (), s32[]{:S(2)}) async-start(), calls=%async_computation.53 | async-start | bytes 12976128 | tf_op jit(solution)/shard_map/all_gather | solution.py:226
  303.8 486.3 %all-gather.54.cloned.1.call-start = ((), (), s32[]{:S(2)}) async-start(), calls=%async_computation.54 | async-start | bytes 6488064 | tf_op jit(solution)/shard_map/all_gather | solution.py:227
  304.4 555.5 %all-gather.56.cloned.1.call-start = ((), (), s32[]{:S(2)}) async-start(), calls=%async_computation.55 | async-start | bytes 12976128 | tf_op jit(solution)/shard_map/all_gather | solution.py:226
  305.1 601.0 %all-gather.58.cloned.1.call-start = ((), (), s32[]{:S(2)}) async-start(), calls=%async_computation.56 | async-start | bytes 6488064 | tf_op jit(solution)/shard_map/all_gather | solution.py:227
  305.7 670.2 %all-gather.60.cloned.1.call-start = ((), (), s32[]{:S(2)}) async-start(), calls=%async_computation.57 | async-start | bytes 12976128 | tf_op jit(solution)/shard_map/all_gather | solution.py:226
  306.4 715.8 %all-gather.62.cloned.1.call-start = ((), (), s32[]{:S(2)}) async-start(), calls=%async_computation.58 | async-start | bytes 6488064 | tf_op jit(solution)/shard_map/all_gather | solution.py:227
  307.0 784.8 %all-gather.64.cloned.1.call-start = ((), (), s32[]{:S(2)}) async-start(), calls=%async_computation.59 | async-start | bytes 12976128 | tf_op jit(solution)/shard_map/all_gather | solution.py:226
  307.6 830.5 %all-gather.66.cloned.1.call-start = ((), (), s32[]{:S(2)}) async-start(), calls=%async_computation.60 | async-start | bytes 6488064 | tf_op jit(solution)/shard_map/all_gather | solution.py:227
  308.2 899.6 %all-gather.68.cloned.1.call-start = ((), (), s32[]{:S(2)}) async-start(), calls=%async_computation.61 | async-start | bytes 12976128 | tf_op jit(solution)/shard_map/all_gather | solution.py:226
  308.8 945.3 %all-gather.70.cloned.1.call-start = ((), (), s32[]{:S(2)}) async-start(), calls=%async_computation.62 | async-start | bytes 6488064 | tf_op jit(solution)/shard_map/all_gather | solution.py:227
  309.3 1015.0 %all-gather.72.cloned.1.call-start = ((), (), s32[]{:S(2)}) async-start(), calls=%async_computation.63 | async-start | bytes 12976128 | tf_op jit(solution)/shard_map/all_gather | solution.py:226
  310.1 1060.6 %all-gather.74.cloned.1.call-start = ((), (), s32[]{:S(2)}) async-start(), calls=%async_computation.64 | async-start | bytes 6488064 | tf_op jit(solution)/shard_map/all_gather | solution.py:227
  310.7 1405.2 %all-reduce.19.cloned.1.call-start = ((), (), s32[]{:S(2)}) async-start(), calls=%async_computation.26 | async-start | bytes 8388608 | tf_op jit(solution)/shard_map/psum | solution.py:291
  340.3 1036.6 %copy-start.119 = (s32[1024]{0:T(1024)}, s32[1024]{0:T(1024)S(1)}, u32[]{:S(2)}) copy-start(s32[1024]{0:T(1024)S(1)} %broadcast_clamp_fusion.2) | copy-start | bytes 12292
  348.6 1059.4 %copy-start.96 = (bf16[2048,8]{0,1:T(8,128)(2,1)}, bf16[2048,8]{0,1:T(8,128)(2,1)S(1)}, u32[]{:S(2)}) copy-start(bf16[2048,8]{0,1:T(8,128)(2,1)S(1)} %all_gather.91) | copy-start | bytes 98308
  1563.5 240.3 %all-reduce.17.cloned.1.call-start = ((), (), s32[]{:S(2)}) async-start(), calls=%async_computation.25 | async-start | bytes 4194304 | tf_op jit(solution)/shard_map/psum | solution.py:242
  1590.1 563.1 %reduce-scatter.30.cloned.1.call-start = ((), (), s32[]{:S(2)}) async-start(), calls=%async_computation.32 | async-start | bytes 36864 | tf_op jit(solution)/shard_map/reduce_scatter | solution.py:409
  1591.4 212.4 %copy-start.39 = (bf16[512,2048]{1,0:T(8,128)(2,1)S(1)}, bf16[512,2048]{1,0:T(8,128)(2,1)}, u32[]{:S(2)}) copy-start(bf16[512,2048]{1,0:T(8,128)(2,1)} %param.22) | copy-start | bytes 6291460
  1591.4 563.1 %reduce-scatter.28.cloned.1.call-start = ((), (), s32[]{:S(2)}) async-start(), calls=%async_computation.31 | async-start | bytes 36864 | tf_op jit(solution)/shard_map/reduce_scatter | solution.py:403
  1997.2 187.2 %all-reduce.21.cloned.1.call-start = ((), (), s32[]{:S(2)}) async-start(), calls=%async_computation.27 | async-start | bytes 8388608 | tf_op jit(solution)/shard_map/psum | solution.py:378
  2005.7 240.6 %reduce-scatter.48.cloned.1.call-start = ((), (), s32[]{:S(2)}) async-start(), calls=%async_computation.41 | async-start | bytes 6488064 | tf_op jit(solution)/shard_map/reduce_scatter | solution.py:280
  2012.0 297.1 %reduce-scatter.50.cloned.1.call-start = ((), (), s32[]{:S(2)}) async-start(), calls=%async_computation.42 | async-start | bytes 6488064 | tf_op jit(solution)/shard_map/reduce_scatter | solution.py:280
  2018.2 353.4 %reduce-scatter.52.cloned.1.call-start = ((), (), s32[]{:S(2)}) async-start(), calls=%async_computation.43 | async-start | bytes 6488064 | tf_op jit(solution)/shard_map/reduce_scatter | solution.py:280
  2024.4 410.1 %reduce-scatter.54.cloned.1.call-start = ((), (), s32[]{:S(2)}) async-start(), calls=%async_computation.44 | async-start | bytes 6488064 | tf_op jit(solution)/shard_map/reduce_scatter | solution.py:280
  2030.6 466.3 %reduce-scatter.56.cloned.1.call-start = ((), (), s32[]{:S(2)}) async-start(), calls=%async_computation.45 | async-start | bytes 6488064 | tf_op jit(solution)/shard_map/reduce_scatter | solution.py:280
  2036.8 523.0 %reduce-scatter.58.cloned.1.call-start = ((), (), s32[]{:S(2)}) async-start(), calls=%async_computation.46 | async-start | bytes 6488064 | tf_op jit(solution)/shard_map/reduce_scatter | solution.py:280
  2042.9 579.4 %reduce-scatter.60.cloned.1.call-start = ((), (), s32[]{:S(2)}) async-start(), calls=%async_computation.47 | async-start | bytes 6488064 | tf_op jit(solution)/shard_map/reduce_scatter | solution.py:280
  2049.1 635.9 %reduce-scatter.62.cloned.1.call-start = ((), (), s32[]{:S(2)}) async-start(), calls=%async_computation.48 | async-start | bytes 6488064 | tf_op jit(solution)/shard_map/reduce_scatter | solution.py:280
  2055.3 684.4 %reduce-scatter.22.cloned.1.call-start = ((), (), s32[]{:S(2)}) async-start(), calls=%async_computation.28 | async-start | bytes 4718592 | tf_op jit(solution)/shard_map/reduce_scatter | solution.py:394
  2062.5 768.5 %reduce-scatter.32.cloned.1.call-start = ((), (), s32[]{:S(2)}) async-start(), calls=%async_computation.33 | async-start | bytes 12976128 | tf_op jit(solution)/shard_map/reduce_scatter | solution.py:277
  2070.8 850.8 %reduce-scatter.34.cloned.1.call-start = ((), (), s32[]{:S(2)}) async-start(), calls=%async_computation.34 | async-start | bytes 12976128 | tf_op jit(solution)/shard_map/reduce_scatter | solution.py:277
  2078.9 933.2 %reduce-scatter.36.cloned.1.call-start = ((), (), s32[]{:S(2)}) async-start(), calls=%async_computation.35 | async-start | bytes 12976128 | tf_op jit(solution)/shard_map/reduce_scatter | solution.py:277
  2087.0 1015.8 %reduce-scatter.38.cloned.1.call-start = ((), (), s32[]{:S(2)}) async-start(), calls=%async_computation.36 | async-start | bytes 12976128 | tf_op jit(solution)/shard_map/reduce_scatter | solution.py:277
  2095.1 1098.3 %reduce-scatter.40.cloned.1.call-start = ((), (), s32[]{:S(2)}) async-start(), calls=%async_computation.37 | async-start | bytes 12976128 | tf_op jit(solution)/shard_map/reduce_scatter | solution.py:277
  2103.4 1180.7 %reduce-scatter.42.cloned.1.call-start = ((), (), s32[]{:S(2)}) async-start(), calls=%async_computation.38 | async-start | bytes 12976128 | tf_op jit(solution)/shard_map/reduce_scatter | solution.py:277
  2111.5 1263.2 %reduce-scatter.44.cloned.1.call-start = ((), (), s32[]{:S(2)}) async-start(), calls=%async_computation.39 | async-start | bytes 12976128 | tf_op jit(solution)/shard_map/reduce_scatter | solution.py:277
  2119.7 1345.7 %reduce-scatter.46.cloned.1.call-start = ((), (), s32[]{:S(2)}) async-start(), calls=%async_computation.40 | async-start | bytes 12976128 | tf_op jit(solution)/shard_map/reduce_scatter | solution.py:277
  2127.8 1457.4 %reduce-scatter.24.cloned.1.call-start = ((), (), s32[]{:S(2)}) async-start(), calls=%async_computation.29 | async-start | bytes 18874368 | tf_op jit(solution)/shard_map/reduce_scatter | solution.py:397
  2139.3 1565.9 %reduce-scatter.26.cloned.1.call-start = ((), (), s32[]{:S(2)}) async-start(), calls=%async_computation.30 | async-start | bytes 18874368 | tf_op jit(solution)/shard_map/reduce_scatter | solution.py:400
  (171 other events, 2480.6 us)
Sparse Core Ops, SparseCore 0:
  10.5 40.2 all-gather.39
  52.7 89.8 all-gather.37
  144.5 93.1 all-gather.41
  287.8 154.9 all-reduce.14
  444.8 66.6 all-gather.43
  513.4 67.6 all-gather.47
  583.2 44.3 all-gather.45
  629.6 44.3 all-gather.49
  676.1 67.6 all-gather.51
  745.7 44.3 all-gather.53
  792.1 67.6 all-gather.55
  861.7 44.3 all-gather.57
  908.2 67.6 all-gather.59
  977.8 44.3 all-gather.61
  1024.1 67.6 all-gather.63
  1093.7 44.3 all-gather.65
  1140.0 67.6 all-gather.67
  1209.6 44.3 all-gather.69
  1256.7 67.6 all-gather.71
  1326.3 44.3 all-gather.73
  1563.6 152.2 all-reduce.18
  1718.2 85.5 all-reduce.16
  1807.1 30.2 reduce-scatter.29
  1997.3 29.4 reduce-scatter.27
  2029.3 154.9 all-reduce.20
  2188.3 58.0 reduce-scatter.47
  2250.1 58.9 reduce-scatter.49
  2312.5 59.0 reduce-scatter.51
  2375.4 59.0 reduce-scatter.53
  2437.8 59.0 reduce-scatter.55
  2500.7 59.0 reduce-scatter.57
  2563.2 59.0 reduce-scatter.59
  2626.0 59.0 reduce-scatter.61
  2688.4 51.3 reduce-scatter.21
  2744.2 86.7 reduce-scatter.31
  2834.8 86.7 reduce-scatter.33
  2925.3 86.7 reduce-scatter.35
  3016.0 86.7 reduce-scatter.37
  3106.5 86.7 reduce-scatter.39
  3197.2 86.7 reduce-scatter.41
  3287.9 86.7 reduce-scatter.43
  3378.6 86.7 reduce-scatter.45
  3469.2 115.9 reduce-scatter.23
  3589.2 115.9 reduce-scatter.25
where the time goes:
time: 3730 us; the launch traced here: 3720 us
  waiting for transfers between devices  2700 us (72%)
  matrix products  421 us (11%)
  local copies, waits for them, and re-layouts  367 us (10%)
  other arithmetic  139 us (4%)
  blocking collectives  72.3 us (2%)
    reduce_scatter x8, waiting for transfers between devices, on_device(): lax.psum_scatter(grad_up_w.astype(jnp.bfloat16), 'dp', scatter_dimension=...  705 us
    all_gather x8, waiting for transfers between devices, on_device(): lax.all_gather(gate_up_weight[expert], 'dp', axis=1, tiled=True)  510 us
    reduce_scatter x8, waiting for transfers between devices, on_device(): lax.psum_scatter(grad_down_w.astype(jnp.bfloat16), 'dp', scatter_dimensio...  459 us
    all_gather x8, waiting for transfers between devices, on_device(): lax.all_gather(down_weight[expert], 'dp', axis=1, tiled=True)  313 us
    psum x1, waiting for transfers between devices, on_device(): lax.psum((grad_mlp_part, grad_gates_part), 'tensor')  124 us
    reduce_scatter x1, waiting for transfers between devices, on_device(): lax.psum_scatter(grad_output_w.astype(jnp.bfloat16), 'dp', scatter_dimens...  116 us
    reduce_scatter x1, waiting for transfers between devices, on_device(): lax.psum_scatter(grad_query_w.astype(jnp.bfloat16), 'dp', scatter_dimensi...  99.6 us
    psum x1, waiting for transfers between devices, on_device(): hidden_state = inputs + lax.psum(att_part, 'tensor')  93.4 us
  transfers between devices with their start and end apart: 44, of which 41 were waited for; matrix products, arithmetic and copies ran while one was open for 18% of the time, Pallas kernels for 0%

commit v1 on v0

v1 whole, which is shorter than its diff:
```python
import functools

import jax
import jax.numpy as jnp
from jax import lax
from jax.experimental import pallas as pl
from jax.experimental.pallas import tpu as pltpu
from jax.sharding import PartitionSpec as P

HD = 128
TOPK = 2
SEG = 128

EPSILON = 1e-06
NEGATIVE = -1e30
ROPE_BASE = 10000.0
F32 = jnp.float32
BF16 = jnp.bfloat16


def dot(a, b, out=F32):
    return jnp.dot(a, b, preferred_element_type=out)


def dot_tn(a, b, out=F32):
    return lax.dot_general(a, b, (((0,), (0,)), ((), ())), preferred_element_type=out)


def dot_nt(a, b, out=F32):
    return lax.dot_general(a, b, (((1,), (1,)), ((), ())), preferred_element_type=out)


def slot_places(routes, priority, capacity, experts):
    pair_total = routes.shape[0] * routes.shape[1]
    flat_routes = routes.reshape(pair_total)
    flat_order = priority.reshape(pair_total)
    same_expert = flat_routes[:, None] == flat_routes[None, :]
    earlier = flat_order[None, :] < flat_order[:, None]
    slot_rank = jnp.sum((same_expert & earlier).astype(jnp.int32), axis=1)
    slot_place = jnp.where(
        slot_rank < capacity, flat_routes * capacity + slot_rank, experts * capacity
    )
    return slot_place.reshape(routes.shape)


def slot_hits(place, slots):
    index = jnp.arange(slots, dtype=jnp.int32)[:, None]
    return [place[:, k][None, :] == index for k in range(place.shape[1])]


def ancestry(parent_row):
    segment_count = parent_row.shape[0]
    indices = jnp.arange(segment_count, dtype=jnp.int32)
    walker = indices
    inside = indices[:, None] == indices[None, :]
    for travel in range(segment_count):
        walker = parent_row[walker]
        inside = inside | (walker[:, None] == indices[None, :])
    depth = jnp.sum(inside.astype(jnp.int32), axis=1) - 1
    return (inside, depth)


def rope_tables(position):
    half_width = HD // 2
    frequency = ROPE_BASE ** (-jnp.arange(half_width, dtype=F32) / half_width)
    angles = position.astype(F32)[:, None] * frequency[None, :]
    cosine, sine = jnp.cos(angles), jnp.sin(angles)
    return (
        jnp.concatenate([cosine, cosine], axis=1),
        jnp.concatenate([-sine, sine], axis=1),
    )


def norm_forward(values_in):
    scale = lax.rsqrt(jnp.mean(values_in * values_in, axis=-1, keepdims=True) + EPSILON)
    return (values_in * scale, scale)


def norm_backward(grad_normed, normal, scale, gain):
    weighted = grad_normed * gain
    grad_in = scale * (weighted - normal * jnp.mean(weighted * normal, axis=-1, keepdims=True))
    return (grad_in, jnp.sum(grad_normed * normal, axis=0))


def router_backward(gates, grad_gates, picks, experts):
    grad_select = gates * (grad_gates - jnp.sum(gates * grad_gates, axis=1, keepdims=True))
    picked_hot = (picks[:, :, None] == jnp.arange(experts, dtype=jnp.int32)[None, None, :]).astype(
        F32
    )
    return jnp.sum(picked_hot * grad_select[:, :, None], axis=1).astype(BF16)


def picked_softmax(logits, picks):
    experts = logits.shape[1]
    hot = picks[:, :, None] == jnp.arange(experts, dtype=jnp.int32)[None, None, :]
    return jax.nn.softmax(jnp.sum(jnp.where(hot, logits[:, None, :], 0.0), axis=2), axis=-1)


def rope(v, cosine, sine):
    return v * cosine + pltpu.roll(v, HD // 2, axis=1) * sine


def rope_back(v, cosine, sine):
    return v * cosine - pltpu.roll(v, HD // 2, axis=1) * sine


def softmax_block(q, k, bias):
    scores = dot_nt(q, k) * HD ** (-0.5) + bias
    exp_scores = jnp.exp(scores - jnp.max(scores, axis=-1, keepdims=True))
    return exp_scores / jnp.sum(exp_scores, axis=-1, keepdims=True)


def attend_kernel(
    rows, q_raw, k_raw, v_raw, bias, gate, slot_cos, slot_sin, tok_cos, tok_sin,
    q_out, k_out, v_out, att_out, gated_out,
):
    k_out[...] = rope(k_raw[...], tok_cos[...], tok_sin[...]).astype(BF16)
    v_out[...] = v_raw[...].astype(BF16)

    @pl.loop(0, q_raw.shape[0] // rows)
    def _(i):
        at = pl.ds(pl.multiple_of(i * rows, rows), rows)
        q = rope(q_raw[at, :], slot_cos[at, :], slot_sin[at, :]).astype(BF16)
        q_out[at, :] = q
        probs = softmax_block(q, k_out[...], bias[at, :].astype(F32)).astype(BF16)
        attended = dot(probs, v_out[...])
        att_out[at, :] = attended
        gated_out[at, :] = (attended * gate[at, :]).astype(BF16)


def attend(q_raw, keyval, bias, gate, slot_tables, tok_tables):
    slots, width = q_raw.shape
    tok = keyval.shape[0]
    heads = width // HD
    head = lambda h: (0, h)
    whole = lambda h: (0, 0)
    rows = 256
    return pl.pallas_call(
        functools.partial(attend_kernel, rows),
        grid=(heads,),
        in_specs=[
            pl.BlockSpec((slots, HD), head),
            pl.BlockSpec((tok, HD), head),
            pl.BlockSpec((tok, HD), lambda h: (0, heads + h)),
            pl.BlockSpec((slots, tok), whole),
            pl.BlockSpec((slots, 1), whole),
            pl.BlockSpec((slots, HD), whole),
            pl.BlockSpec((slots, HD), whole),
            pl.BlockSpec((tok, HD), whole),
            pl.BlockSpec((tok, HD), whole),
        ],
        out_specs=[
            pl.BlockSpec((slots, HD), head),
            pl.BlockSpec((tok, HD), head),
            pl.BlockSpec((tok, HD), head),
            pl.BlockSpec((slots, HD), head),
            pl.BlockSpec((slots, HD), head),
        ],
        out_shape=[
            jax.ShapeDtypeStruct((slots, width), BF16),
            jax.ShapeDtypeStruct((tok, width), BF16),
            jax.ShapeDtypeStruct((tok, width), BF16),
            jax.ShapeDtypeStruct((slots, width), F32),
            jax.ShapeDtypeStruct((slots, width), BF16),
        ],
        compiler_params=pltpu.CompilerParams(vmem_limit_bytes=40 << 20),
        cost_estimate=pl.CostEstimate(
            flops=4 * slots * tok * width,
            bytes_accessed=slots * width * 12 + slots * tok * 2,
            transcendentals=slots * tok * heads,
        ),
    )(q_raw, keyval, keyval, bias, gate, *slot_tables, *tok_tables)


def attend_back_kernel(
    rows, q_ref, k_ref, v_ref, bias, gate, slot_cos, slot_sin, tok_cos, tok_sin, grad_gated,
    gq_out, gk_out, gv_out, gk_sum, gv_sum,
):
    gk_sum[...] = jnp.zeros_like(gk_sum)
    gv_sum[...] = jnp.zeros_like(gv_sum)

    @pl.loop(0, q_ref.shape[0] // rows)
    def _(i):
        at = pl.ds(pl.multiple_of(i * rows, rows), rows)
        q = q_ref[at, :]
        probs = softmax_block(q, k_ref[...], bias[at, :].astype(F32))
        grad_att = (grad_gated[at, :] * gate[at, :]).astype(BF16)
        grad_probs = dot_nt(grad_att, v_ref[...])
        centre = jnp.sum(probs * grad_probs, axis=-1, keepdims=True)
        grad_scores = (probs * (grad_probs - centre)).astype(BF16)
        grad_q = dot(grad_scores, k_ref[...]) * HD ** (-0.5)
        gq_out[at, :] = rope_back(grad_q, slot_cos[at, :], slot_sin[at, :]).astype(BF16)
        gk_sum[...] += dot_tn(grad_scores, q)
        gv_sum[...] += dot_tn(probs.astype(BF16), grad_att)

    grad_k = gk_sum[...] * HD ** (-0.5)
    gk_out[...] = rope_back(grad_k, tok_cos[...], tok_sin[...]).astype(BF16)
    gv_out[...] = gv_sum[...].astype(BF16)


def attend_back(q, k, v, bias, gate, slot_tables, tok_tables, grad_gated):
    slots, width = q.shape
    tok = k.shape[0]
    heads = width // HD
    head = lambda h: (0, h)
    whole = lambda h: (0, 0)
    rows = 256
    return pl.pallas_call(
        functools.partial(attend_back_kernel, rows),
        grid=(heads,),
        in_specs=[
            pl.BlockSpec((slots, HD), head),
            pl.BlockSpec((tok, HD), head),
            pl.BlockSpec((tok, HD), head),
            pl.BlockSpec((slots, tok), whole),
            pl.BlockSpec((slots, 1), whole),
            pl.BlockSpec((slots, HD), whole),
            pl.BlockSpec((slots, HD), whole),
            pl.BlockSpec((tok, HD), whole),
            pl.BlockSpec((tok, HD), whole),
            pl.BlockSpec((slots, HD), head),
        ],
        out_specs=[
            pl.BlockSpec((slots, HD), head),
            pl.BlockSpec((tok, HD), head),
            pl.BlockSpec((tok, HD), head),
        ],
        out_shape=[
            jax.ShapeDtypeStruct((slots, width), BF16),
            jax.ShapeDtypeStruct((tok, width), BF16),
            jax.ShapeDtypeStruct((tok, width), BF16),
        ],
        scratch_shapes=[pltpu.VMEM((tok, HD), F32), pltpu.VMEM((tok, HD), F32)],
        compiler_params=pltpu.CompilerParams(vmem_limit_bytes=40 << 20),
        cost_estimate=pl.CostEstimate(
            flops=10 * slots * tok * width,
            bytes_accessed=slots * width * 8 + slots * tok * 2,
            transcendentals=slots * tok * heads,
        ),
    )(q, k, v, bias, gate, *slot_tables, *tok_tables, grad_gated)


class Movers:
    def __init__(self, dp, experts):
        self.dp, self.experts, self.ratio = dp, experts, dp // experts
        self.groups = self.pairs = None
        if self.ratio > 1:
            self.groups = [[g * experts + e for e in range(experts)] for g in range(self.ratio)]
            self.pairs = [[g * experts + e for g in range(self.ratio)] for e in range(experts)]

    def swap(self, blocks):
        return lax.all_to_all(blocks, "dp", 0, 0, axis_index_groups=self.groups, tiled=True)

    def fetch(self, shards):
        mine = self.swap(shards)
        if self.ratio > 1:
            mine = lax.all_gather(mine, "dp", axis=0, axis_index_groups=self.pairs, tiled=True)
        return mine

    def give_back(self, slices):
        if self.ratio > 1:
            slices = lax.psum_scatter(
                slices, "dp", scatter_dimension=0, axis_index_groups=self.pairs, tiled=True
            )
        return self.swap(slices)


def reduce_rows(part):
    return lax.psum_scatter(part.astype(BF16), "tensor", scatter_dimension=0, tiled=True).astype(
        F32
    )


def gather_rows(rows):
    return lax.all_gather(rows.astype(BF16), "tensor", axis=0, tiled=True)


def on_device(
    dp_size,
    tensor_size,
    tokens,
    cotangent,
    parents,
    attention_routes,
    expert_routes,
    slot_order,
    gain_attention,
    keyval_weight,
    query_weight,
    output_weight,
    attention_router,
    gain_feedforward,
    expert_router,
    gate_up_weight,
    down_weight,
):
    tok_count, model_width = tokens.shape
    pair_count = TOPK * tok_count
    att_experts = query_weight.shape[0]
    mlp_experts = gate_up_weight.shape[0]
    att_cap = tok_count * 5 // 16
    mlp_cap = pair_count // mlp_experts
    att_slots = att_experts * att_cap
    mlp_slots = mlp_experts * mlp_cap
    width_here = query_weight.shape[2]
    rows_here = tok_count // tensor_size
    movers = Movers(dp_size, mlp_experts)

    small = jnp.concatenate(
        [gain_attention[:, None], gain_feedforward[:, None], attention_router, expert_router], axis=1
    )
    small_full = lax.all_gather(small, "dp", axis=0, tiled=True)
    keyval_full = lax.all_gather(keyval_weight, "dp", axis=1, tiled=True)
    query_full = lax.all_gather(query_weight, "dp", axis=1, tiled=True)
    output_full = lax.all_gather(output_weight, "dp", axis=2, tiled=True)
    gain_attn_full = small_full[:, 0].astype(F32)
    gain_mlp_full = small_full[:, 1].astype(F32)
    router_att = small_full[:, 2 : 2 + att_experts]
    router_mlp = small_full[:, 2 + att_experts :]

    gate_full = movers.fetch(gate_up_weight[:, 0]).reshape(model_width, -1)
    up_full = movers.fetch(gate_up_weight[:, 1]).reshape(model_width, -1)
    down_full = movers.fetch(down_weight)
    down_full = down_full.transpose(1, 0, 2).reshape(down_full.shape[1], model_width)

    inside, depth = ancestry(parents[0])
    token_index = jnp.arange(tok_count, dtype=jnp.int32)
    pair_order = jnp.arange(pair_count, dtype=jnp.int32).reshape(tok_count, TOPK)
    att_hits = slot_hits(
        slot_places(attention_routes, pair_order, att_cap, att_experts), att_slots
    )
    priority = slot_order[0][:, None] * TOPK + jnp.arange(TOPK, dtype=jnp.int32)[None, :]
    mlp_hits = slot_hits(slot_places(expert_routes, priority, mlp_cap, mlp_experts), mlp_slots)
    att_pick = (att_hits[0] | att_hits[1]).astype(BF16)
    mlp_pick = (mlp_hits[0] | mlp_hits[1]).astype(BF16)

    def to_slots(hits, pair_values):
        return jnp.sum(
            sum(jnp.where(hits[k], pair_values[:, k][None, :], 0) for k in range(TOPK)), axis=1
        )

    def to_pairs(hits, slot_values):
        return jnp.stack(
            [jnp.sum(jnp.where(hits[k], slot_values[:, None], 0.0), axis=0) for k in range(TOPK)],
            axis=1,
        )

    def position_of(token):
        segment = token // SEG
        level = jnp.sum(
            jnp.where(segment[:, None] == jnp.arange(depth.shape[0])[None, :], depth[None, :], 0),
            axis=1,
        )
        return level * SEG + token % SEG

    pair_token = jnp.broadcast_to(token_index[:, None], (tok_count, TOPK))
    slot_token = to_slots(att_hits, pair_token)
    slot_filled = jnp.any(att_hits[0] | att_hits[1], axis=1)
    slot_tables = rope_tables(position_of(slot_token))
    tok_tables = rope_tables(position_of(token_index))
    segment_hot = (
        (slot_token // SEG)[:, None] == jnp.arange(inside.shape[0], dtype=jnp.int32)[None, :]
    ).astype(F32)
    reach = dot(segment_hot, jnp.repeat(inside.astype(F32), SEG, axis=1)) > 0.5
    allowed = reach & (token_index[None, :] <= slot_token[:, None]) & slot_filled[:, None]
    bias = jnp.where(allowed, 0.0, NEGATIVE).astype(BF16)

    inputs = tokens.astype(F32)
    normal_attn, scale_attn = norm_forward(inputs)
    normed = (normal_attn * gain_attn_full).astype(BF16)
    att_gates = picked_softmax(dot(normed, router_att), attention_routes)
    att_gate_slots = to_slots(att_hits, att_gates)[:, None]
    keyval = jnp.concatenate([dot(normed, keyval_full[0]), dot(normed, keyval_full[1])], axis=1)
    routed = dot(att_pick, normed, BF16).reshape(att_experts, att_cap, model_width)
    query_raw = jnp.einsum(
        "ecd,edf->ecf", routed, query_full, preferred_element_type=F32
    ).reshape(att_slots, width_here)
    queries, key_rows, values, attended, gated = attend(
        query_raw, keyval, bias, att_gate_slots, slot_tables, tok_tables
    )
    gated_slots = gated.reshape(att_experts, att_cap, width_here)
    att_rows = jnp.einsum(
        "ecf,efd->ecd", gated_slots, output_full, preferred_element_type=F32
    ).reshape(att_slots, model_width)
    att_part = dot_tn(att_pick, att_rows.astype(BF16))

    z = lax.axis_index("tensor")

    def share(rows):
        return lax.dynamic_slice_in_dim(rows, z * rows_here, rows_here, axis=0)

    hidden = share(inputs) + reduce_rows(att_part)
    normal_mlp, scale_mlp = norm_forward(hidden)
    mlp_in_here = (normal_mlp * gain_mlp_full).astype(BF16)
    mlp_in = gather_rows(mlp_in_here)
    mlp_gates = picked_softmax(dot(mlp_in, router_mlp), expert_routes)
    mlp_gate_slots = to_slots(mlp_hits, mlp_gates)[:, None]
    expert_in = dot(mlp_pick, mlp_in, BF16)
    grad_rows = (dot(mlp_pick, cotangent) * mlp_gate_slots).astype(BF16)

    def send(rows):
        return movers.swap(rows.reshape(mlp_experts, mlp_cap, model_width)).reshape(
            mlp_slots, model_width
        )

    x_rows = send(expert_in)
    g_rows = send(grad_rows)
    gate = dot(x_rows, gate_full)
    up = dot(x_rows, up_full)
    sigmoid_gate = jax.nn.sigmoid(gate)
    silu_gate = gate * sigmoid_gate
    activated = (silu_gate * up).astype(BF16)
    expert_out = dot(activated, down_full, BF16)
    grad_act = dot_nt(g_rows, down_full)
    grad_gate = (grad_act * up * sigmoid_gate * (1.0 + gate * (1.0 - sigmoid_gate))).astype(BF16)
    grad_up = (grad_act * silu_gate).astype(BF16)
    grad_expert_in = (dot_nt(grad_gate, gate_full) + dot_nt(grad_up, up_full)).astype(BF16)
    out_slots = send(expert_out)
    grad_in_slots = send(grad_expert_in)
    per_dp = model_width // dp_size
    grad_gate_w = dot_tn(x_rows, grad_gate, BF16).reshape(dp_size, per_dp, -1)
    grad_up_w = dot_tn(x_rows, grad_up, BF16).reshape(dp_size, per_dp, -1)
    grad_down_w = (
        dot_tn(activated, g_rows, BF16).reshape(-1, dp_size, per_dp).transpose(1, 0, 2)
    )
    grad_gate_up_out = jnp.stack(
        [movers.give_back(grad_gate_w).astype(F32), movers.give_back(grad_up_w).astype(F32)], axis=1
    )
    grad_down_out = movers.give_back(grad_down_w).astype(F32)

    gate_matrix = sum(
        jnp.where(mlp_hits[k], mlp_gates[:, k][None, :], 0.0) for k in range(TOPK)
    )
    gate_high = gate_matrix.astype(BF16)
    gate_low = (gate_matrix - gate_high.astype(F32)).astype(BF16)
    mlp_part = dot_tn(gate_high, out_slots) + dot_tn(gate_low, out_slots)
    mixed = gather_rows(hidden + reduce_rows(mlp_part))
    alignment = dot_nt(out_slots, cotangent)
    grad_gates_part = jnp.stack(
        [jnp.sum(jnp.where(mlp_hits[k], alignment, 0.0), axis=0) for k in range(TOPK)], axis=1
    )
    grad_mlp_gates = lax.psum_scatter(grad_gates_part, "tensor", scatter_dimension=0, tiled=True)
    grad_mlp_in = reduce_rows(dot_tn(mlp_pick, grad_in_slots))
    grad_mlp_logits = router_backward(
        share(mlp_gates), grad_mlp_gates, share(expert_routes), mlp_experts
    )
    grad_router_mlp = dot_tn(mlp_in_here, grad_mlp_logits)
    grad_mlp_in = grad_mlp_in + dot_nt(grad_mlp_logits, router_mlp)
    grad_hidden_norm, grad_gain_mlp = norm_backward(
        grad_mlp_in, normal_mlp, scale_mlp, gain_mlp_full
    )
    grad_hidden = share(cotangent).astype(F32) + grad_hidden_norm
    grad_att_pair = gather_rows(grad_hidden)

    grad_att_rows = dot(att_pick, grad_att_pair, BF16).reshape(att_experts, att_cap, model_width)
    grad_gated = jnp.einsum(
        "ecd,efd->ecf", grad_att_rows, output_full, preferred_element_type=F32
    ).reshape(att_slots, width_here)
    grad_output_w = jnp.einsum(
        "ecf,ecd->efd", gated_slots, grad_att_rows, preferred_element_type=BF16
    )
    grad_output_out = lax.psum_scatter(grad_output_w, "dp", scatter_dimension=2, tiled=True)
    grad_att_gates = lax.psum_scatter(
        to_pairs(att_hits, jnp.sum(grad_gated * attended, axis=1)),
        "tensor",
        scatter_dimension=0,
        tiled=True,
    )
    grad_q, grad_k, grad_v = attend_back(
        queries, key_rows, values, bias, att_gate_slots, slot_tables, tok_tables, grad_gated
    )
    grad_query_slots = grad_q.reshape(att_experts, att_cap, width_here)
    grad_query_w = jnp.einsum(
        "ecd,ecf->edf", routed, grad_query_slots, preferred_element_type=BF16
    )
    grad_query_out = lax.psum_scatter(grad_query_w, "dp", scatter_dimension=1, tiled=True)
    grad_keyval_w = jnp.stack([dot_tn(normed, grad_k, BF16), dot_tn(normed, grad_v, BF16)])
    grad_keyval_out = lax.psum_scatter(grad_keyval_w, "dp", scatter_dimension=1, tiled=True)
    grad_routed = jnp.einsum(
        "ecf,edf->ecd", grad_query_slots, query_full, preferred_element_type=F32
    ).reshape(att_slots, model_width)
    grad_normed = reduce_rows(
        dot_tn(att_pick, grad_routed.astype(BF16))
        + dot_nt(grad_k, keyval_full[0])
        + dot_nt(grad_v, keyval_full[1])
    )
    grad_att_logits = router_backward(
        share(att_gates), grad_att_gates, share(attention_routes), att_experts
    )
    grad_router_att = dot_tn(share(normed), grad_att_logits)
    grad_normed = grad_normed + dot_nt(grad_att_logits, router_att)
    grad_input_norm, grad_gain_attn = norm_backward(
        grad_normed, share(normal_attn), share(scale_attn), gain_attn_full
    )
    grad_tokens = gather_rows(grad_hidden + grad_input_norm).astype(F32)
    small_grads = jnp.concatenate(
        [grad_gain_attn[:, None], grad_gain_mlp[:, None], grad_router_att, grad_router_mlp], axis=1
    )
    small_grads = lax.psum(
        lax.psum_scatter(small_grads, "dp", scatter_dimension=0, tiled=True), "tensor"
    )
    return (
        mixed,
        grad_tokens,
        small_grads[:, 0],
        grad_keyval_out.astype(F32),
        grad_query_out.astype(F32),
        grad_output_out.astype(F32),
        small_grads[:, 2 : 2 + att_experts],
        small_grads[:, 1],
        small_grads[:, 2 + att_experts :],
        grad_gate_up_out,
        grad_down_out,
    )


def solution(mesh):
    placed = (
        P("dp", None),
        P("dp", None),
        P("dp", None),
        P("dp", None),
        P("dp", None),
        P("dp", None),
        P("dp"),
        P(None, "dp", "tensor"),
        P(None, "dp", "tensor"),
        P(None, "tensor", "dp"),
        P("dp", None),
        P("dp"),
        P("dp", None),
        P(None, None, "dp", "tensor"),
        P(None, "tensor", "dp"),
    )
    return jax.shard_map(
        functools.partial(on_device, mesh.shape["dp"], mesh.shape["tensor"]),
        mesh=mesh,
        in_specs=placed,
        out_specs=(
            P("dp", None),
            P("dp", None),
            P("dp"),
            P(None, "dp", "tensor"),
            P(None, "dp", "tensor"),
            P(None, "tensor", "dp"),
            P("dp", None),
            P("dp"),
            P("dp", None),
            P(None, None, "dp", "tensor"),
            P(None, "tensor", "dp"),
        ),
        check_vma=False,
    )
```

time: 3730 us -> 1490 us (0.40)
  waiting for transfers between devices: 2700 us -> 845 us
  local copies, waits for them, and re-layouts: 367 us -> 89.5 us
  matrix products: 421 us -> 245 us
  other arithmetic: 139 us -> 58.4 us
  blocking collectives: 72.3 us -> 152 us
  starting transfers between devices: 2.56 us -> 45.2 us
    reduce_scatter x21 -> x8, waiting for transfers between devices: 1420 us -> 280 us  [the longest x4 137 us: reduce_rows(): lax.psum_scatter(part.astype(BF16), 'tensor', scatter_dimension=0, tiled=...]
    all_gather x19 -> x7, waiting for transfers between devices: 936 us -> 208 us  [the longest x4 88.4 us: gather_rows(): return lax.all_gather(rows.astype(BF16), 'tensor', axis=0, tiled=True)]
    all_to_all x0 -> x9, waiting for transfers between devices: none -> 355 us  [swap(): lax.all_to_all(blocks, 'dp', 0, 0, axis_index_groups=self.groups, tiled=T...]
    psum x4 -> x0, waiting for transfers between devices: 327 us -> none  [the longest x1 124 us: on_device(): lax.psum((grad_mlp_part, grad_gates_part), 'tensor')]
    dot_general x78 -> x35, matrix products: 385 us -> 215 us  [the longest x12 67.4 us: dot_tn(): lax.dot_general(a, b, (((0,), (0,)), ((), ())), preferred_element_type=out)]
    gather x29 -> x0, local copies, waits for them, and re-layouts: 150 us -> none  [the longest x2 23.2 us: on_device(): routed_out = pad_rows(jnp.concatenate(expert_outs, axis=0))[mlp_place]]
    reduce_sum x16 -> x14, other arithmetic: 71.1 us -> 4.03 us  [the longest x2 1.57 us: slot_places(): slot_rank = jnp.sum((same_expert & earlier).astype(jnp.int32), axis=1)]
    unnamed x351 -> x127, local copies, waits for them, and re-layouts: 91.2 us -> 25.6 us
  transfers between devices with their start and end apart: 44 -> 26, of which waited for: 41 -> 17; matrix products, arithmetic and copies ran while one was open for 18% -> 18% of each run, Pallas kernels for 0% -> 1%
where the time goes in v1:
time: 1490 us
  waiting for transfers between devices  845 us (57%)
  matrix products  245 us (16%)
  blocking collectives  152 us (10%)
  local copies, waits for them, and re-layouts  89.5 us (6%)
  other arithmetic  58.4 us (4%)
  starting transfers between devices  45.2 us (3%)
  Pallas kernels  35.1 us (2%)
  between operations  15.1 us (1%)
    all_to_all x9, waiting for transfers between devices, swap(): lax.all_to_all(blocks, 'dp', 0, 0, axis_index_groups=self.groups, tiled=T...  355 us
    reduce_scatter x4, waiting for transfers between devices, reduce_rows(): lax.psum_scatter(part.astype(BF16), 'tensor', scatter_dimension=0, tiled=...  137 us
    reduce_scatter x1, waiting for transfers between devices, on_device(): lax.psum_scatter(grad_output_w, 'dp', scatter_dimension=2, tiled=True)  115 us
    all_gather x4, waiting for transfers between devices, gather_rows(): return lax.all_gather(rows.astype(BF16), 'tensor', axis=0, tiled=True)  88.4 us
    all_gather x1, blocking collectives, on_device(): small_full = lax.all_gather(small, 'dp', axis=0, tiled=True)  82.1 us
    dot_general x12, matrix products, dot_tn(): lax.dot_general(a, b, (((0,), (0,)), ((), ())), preferred_element_type=out)  67.4 us
    all_gather x1, waiting for transfers between devices, on_device(): output_full = lax.all_gather(output_weight, 'dp', axis=2, tiled=True)  62.5 us
    dot_general x12, matrix products, dot(): return jnp.dot(a, b, preferred_element_type=out)  62.4 us
  transfers between devices with their start and end apart: 26, of which 17 were waited for; matrix products, arithmetic and copies ran while one was open for 18% of the time, Pallas kernels for 1%

profile of v1, /device:TPU:0, one launch (start us, length us, event | category | flops | bytes accessed | tf_op | source)
XLA Modules:
  0.0 1485.3 jit_solution(17348696148194659582)
XLA Ops:
  19.0 82.1 %all_gather.24 = bf16[2048,18]{0,1:T(8,128)(2,1)S(1)} all-gather(bf16[256,18]{0,1:T(8,128)(2,1)S(1)} %pad_maximum_fusion.7), channel_id=1, replica_groups=mesh['dp'=8,'tensor'=4] {'dp'}, dimensions={0}, use_global_device_ids=true | all-gather | bytes 82944 | tf_op jit(solution)/shard_map/all_gather | solution.py:312
  128.3 56.9 %all-gather.8.cloned.1.call-done = bf16[8,2048,512]{2,1,0:T(8,128)(2,1)} async-done(((bf16[8,256,512]{2,1,0:T(8,128)(2,1)}), bf16[8,2048,512]{2,1,0:T(8,128)(2,1)}) %all-gather.8.cloned.1.call-update) | async-done | bytes 16777232 | tf_op jit(solution)/shard_map/all_gather | solution.py:314
  185.2 11.8 fusion.93
  197.1 16.5 %shard_map.230 = (bf16[1280,512]{1,0:T(8,128)(2,1)S(1)}, bf16[512,512]{1,0:T(8,128)(2,1)S(1)}, bf16[512,512]{1,0:T(8,128)(2,1)S(1)}, f32[1280,512]{1,0:T(8,128)S(1)}, bf16[1280,512]{1,0:T(8,128)(2,1)S(1)}) custom-call(f32[1280,512]{1,0:T(8,128)} %bitcast.161, f32[512,1024]{1,0:T(8,128)S(1)} %pad_maximum_fusion.1.k_raw.v_raw, ...), custom_call_target="tpu_custom_call" | custom-call | flops 1342177280 | bytes 9175040 | tf_op jit(solution)/shard_map/pallas_call | solution.py:138
  217.7 62.5 %all-gather.12.cloned.1.call-done = bf16[8,512,2048]{2,1,0:T(8,128)(2,1)} async-done(((bf16[8,512,256]{2,1,0:T(8,128)(2,1)}), bf16[8,512,2048]{2,1,0:T(8,128)(2,1)}) %all-gather.12.cloned.1.call-update) | async-done | bytes 16777232 | tf_op jit(solution)/shard_map/all_gather | solution.py:315
  280.2 8.8 convolution_convert_fusion.1
  293.2 10.1 slice_bitcast_fusion.1
  310.8 26.4 %reduce-scatter.15.cloned.1.call-done = bf16[128,2048]{1,0:T(8,128)(2,1)} async-done(((bf16[512,2048]{1,0:T(8,128)(2,1)}), bf16[128,2048]{1,0:T(8,128)(2,1)}) %reduce-scatter.15.cloned.1.call-update) | async-done | bytes 524304 | tf_op jit(solution)/shard_map/reduce_scatter | solution.py:269
  342.2 43.0 %all-gather.14.cloned.1.call-done = bf16[512,2048]{1,0:T(8,128)(2,1)} async-done(((bf16[128,2048]{1,0:T(8,128)(2,1)}), bf16[512,2048]{1,0:T(8,128)(2,1)}) %all-gather.14.cloned.1.call-update) | async-done | bytes 2097168 | tf_op jit(solution)/shard_map/all_gather | solution.py:275
  391.2 53.6 %all_to_all.50 = bf16[8,128,2048]{2,1,0:T(8,128)(2,1)} all-to-all(bf16[8,128,2048]{2,1,0:T(8,128)(2,1)} %bitcast.171), channel_id=1, replica_groups=mesh['dp'=8,'tensor'=4] {'dp'}, dimensions={0} | all-to-all | bytes 8388608 | tf_op jit(solution)/shard_map/all_to_all | solution.py:252
  449.6 16.8 %copy.117 = bf16[1408,8,256]{2,1,0:T(8,128)(2,1)} copy(bf16[1408,8,256]{2,0,1:T(8,128)(2,1)} %bitcast.27) | data formatting | bytes 11534336 | tf_op jit(solution)/shard_map/transpose | solution.py:324
  466.4 9.8 reshape.379
  476.2 11.8 fusion.94
  488.0 27.6 %all-to-all-done.2 = bf16[8,256,1408]{2,1,0:T(8,128)(2,1)} async-done(((bf16[8,256,1408]{2,1,0:T(8,128)(2,1)}), bf16[8,256,1408]{2,1,0:T(8,128)(2,1)}, u32[]{:S(2)}, u32[]{:S(2)}) %all-to-all-start.2) | async-done | bytes 5767200 | tf_op jit(solution)/shard_map/all_to_all | solution.py:252
  515.6 12.8 multiply_convert_fusion.3
  530.1 8.4 fusion.95
  544.0 48.3 %all-to-all-done.4 = bf16[8,128,2048]{2,1,0:T(8,128)(2,1)} async-done(((bf16[8,128,2048]{2,1,0:T(8,128)(2,1)}), bf16[8,128,2048]{2,1,0:T(8,128)(2,1)}, u32[]{:S(2)}, u32[]{:S(2)}) %all-to-all-start.4) | async-done | bytes 4194336 | tf_op jit(solution)/shard_map/all_to_all | solution.py:252
  592.3 6.1 select_reduce_fusion.3
  613.8 43.2 %all-to-all-done.5 = bf16[8,128,2048]{2,1,0:T(8,128)(2,1)} async-done(((bf16[8,128,2048]{2,1,0:T(8,128)(2,1)}), bf16[8,128,2048]{2,1,0:T(8,128)(2,1)}, u32[]{:S(2)}, u32[]{:S(2)}) %all-to-all-start.5) | async-done | bytes 4194336 | tf_op jit(solution)/shard_map/all_to_all | solution.py:252
  657.0 14.1 multiply_convert_fusion.1
  671.2 10.8 fusion.96
  682.0 11.0 add_convert_fusion
  698.5 48.1 %all-to-all-done.6 = bf16[8,128,2048]{2,1,0:T(8,128)(2,1)} async-done(((bf16[8,128,2048]{2,1,0:T(8,128)(2,1)}), bf16[8,128,2048]{2,1,0:T(8,128)(2,1)}, u32[]{:S(2)}, u32[]{:S(2)}) %all-to-all-start.6) | async-done | bytes 4194336 | tf_op jit(solution)/shard_map/all_to_all | solution.py:252
  753.7 39.9 %reduce-scatter.19.cloned.1.call-done = bf16[128,2048]{1,0:T(8,128)(2,1)} async-done(((bf16[512,2048]{1,0:T(8,128)(2,1)}), bf16[128,2048]{1,0:T(8,128)(2,1)}) %reduce-scatter.19.cloned.1.call-update) | async-done | bytes 524304 | tf_op jit(solution)/shard_map/reduce_scatter | solution.py:269
  797.3 45.4 %all-gather.18.cloned.1.call-done = bf16[512,2048]{1,0:T(8,128)(2,1)} async-done(((bf16[128,2048]{1,0:T(8,128)(2,1)}), bf16[512,2048]{1,0:T(8,128)(2,1)}) %all-gather.18.cloned.1.call-update) | async-done | bytes 2097168 | tf_op jit(solution)/shard_map/all_gather | solution.py:275
  842.7 6.3 fusion.38
  849.0 11.0 fusion.97
  862.5 18.6 %shard_map.231 = (bf16[1280,512]{1,0:T(8,128)(2,1)S(1)}, bf16[512,512]{1,0:T(8,128)(2,1)S(1)}, bf16[512,512]{1,0:T(8,128)(2,1)S(1)}) custom-call(bf16[1280,512]{1,0:T(8,128)(2,1)S(1)} %copy-done.19, bf16[512,512]{1,0:T(8,128)(2,1)S(1)} %copy-done.21, bf16[512,512]{1,0:T(8,128)(2,1)S(1)} %copy-done.23, bf16[1280,512]{1,0:T(8,128)(2,1)S(1)} %copy-done.13, ...), custom_call_target="tpu_custom_call" | custom-call | flops 3355443200 | bytes 6553600 | tf_op jit(solution)/shard_map/pallas_call | solution.py:208
  881.1 9.2 convolution_convert_fusion
  907.5 6.3 add_convert_fusion.2
  925.0 34.0 %reduce-scatter.21.cloned.1.call-done = bf16[128,2048]{1,0:T(8,128)(2,1)} async-done(((bf16[512,2048]{1,0:T(8,128)(2,1)}), bf16[128,2048]{1,0:T(8,128)(2,1)}) %reduce-scatter.21.cloned.1.call-update) | async-done | bytes 524304 | tf_op jit(solution)/shard_map/reduce_scatter | solution.py:269
  968.2 36.5 %reduce-scatter.17.cloned.1.call-done = bf16[128,2048]{1,0:T(8,128)(2,1)} async-done(((bf16[512,2048]{1,0:T(8,128)(2,1)}), bf16[128,2048]{1,0:T(8,128)(2,1)}) %reduce-scatter.17.cloned.1.call-update) | async-done | bytes 524304 | tf_op jit(solution)/shard_map/reduce_scatter | solution.py:269
  1008.7 11.5 fusion.98
  1021.4 10.7 fusion.99
  1032.1 6.6 copy.119
  1038.7 10.6 fusion.5
  1054.3 11.0 fusion.3
  1065.4 71.7 %all-to-all-done.7 = bf16[8,256,1408]{2,1,0:T(8,128)(2,1)} async-done(((bf16[8,256,1408]{2,1,0:T(8,128)(2,1)}), bf16[8,256,1408]{2,1,0:T(8,128)(2,1)}, u32[]{:S(2)}, u32[]{:S(2)}) %all-to-all-start.7) | async-done | bytes 5767200 | tf_op jit(solution)/shard_map/all_to_all | solution.py:252
  1142.0 6.6 copy.120
  1148.6 10.7 convolution_bitcast_fusion
  1159.3 48.7 %all-to-all-done.8 = bf16[8,256,1408]{2,1,0:T(8,128)(2,1)} async-done(((bf16[8,256,1408]{2,1,0:T(8,128)(2,1)}), bf16[8,256,1408]{2,1,0:T(8,128)(2,1)}, u32[]{:S(2)}, u32[]{:S(2)}) %all-to-all-start.8) | async-done | bytes 5767200 | tf_op jit(solution)/shard_map/all_to_all | solution.py:252
  1212.7 6.2 maximum_convert_fusion
  1218.9 8.2 copy.122
  1227.1 66.9 %all-to-all-done.9 = bf16[8,1408,256]{2,1,0:T(8,128)(2,1)} async-done(((bf16[8,1408,256]{2,1,0:T(8,128)(2,1)}), bf16[8,1408,256]{2,1,0:T(8,128)(2,1)}, u32[]{:S(2)}, u32[]{:S(2)}) %all-to-all-start.9) | async-done | bytes 5767200 | tf_op jit(solution)/shard_map/all_to_all | solution.py:252
  1294.0 8.2 convert_element_type.208
  1302.1 16.4 %psum.7 = f32[256,18]{0,1:T(8,128)S(1)} all-reduce(f32[256,18]{0,1:T(8,128)} %reduce-scatter.23.cloned.1.call-done), channel_id=1, replica_groups=mesh['dp'=8,'tensor'=4] {'tensor'}, use_global_device_ids=true, to_apply=%region_37.38 | all-reduce | flops 4608 | bytes 36864 | tf_op jit(solution)/shard_map/psum | solution.py:499
  1325.9 27.9 %reduce-scatter.27.cloned.1.call-done = bf16[8,256,512]{2,1,0:T(8,128)(2,1)} async-done(((bf16[8,2048,512]{2,1,0:T(8,128)(2,1)}), bf16[8,256,512]{2,1,0:T(8,128)(2,1)}) %reduce-scatter.27.cloned.1.call-update) | async-done | bytes 2097168 | tf_op jit(solution)/shard_map/reduce_scatter | solution.py:476
  1358.1 115.2 %reduce-scatter.29.cloned.1.call-done = bf16[8,512,256]{2,1,0:T(8,128)(2,1)} async-done(((bf16[8,512,2048]{2,1,0:T(8,128)(2,1)}), bf16[8,512,256]{2,1,0:T(8,128)(2,1)}) %reduce-scatter.29.cloned.1.call-update) | async-done | bytes 2097168 | tf_op jit(solution)/shard_map/reduce_scatter | solution.py:462
  (294 shorter events, 185.5 us)
Async XLA Ops:
  7.2 116.6 %all-gather.10.cloned.1.call-start = ((), (), s32[]{:S(2)}) async-start(), calls=%async_computation.21 | async-start | bytes 4718592 | tf_op jit(solution)/shard_map/all_gather | solution.py:313
  7.9 177.2 %all-gather.8.cloned.1.call-start = ((), (), s32[]{:S(2)}) async-start(), calls=%async_computation.20 | async-start | bytes 18874368 | tf_op jit(solution)/shard_map/all_gather | solution.py:314
  8.7 271.5 %all-gather.12.cloned.1.call-start = ((), (), s32[]{:S(2)}) async-start(), calls=%async_computation.22 | async-start | bytes 18874368 | tf_op jit(solution)/shard_map/all_gather | solution.py:315
  9.4 9.5 copy-start.46
  9.5 293.9 %all-to-all-start.3 = ((bf16[8,1408,256]{2,1,0:T(8,128)(2,1)}), bf16[8,1408,256]{2,1,0:T(8,128)(2,1)}, u32[]{:S(2)}, u32[]{:S(2)}) async-start(bf16[8,1408,256]{2,1,0:T(8,128)(2,1)} %param.29), calls=%async_computation.4 | async-start | bytes 11534336 | tf_op jit(solution)/shard_map/all_to_all | solution.py:252
  14.8 86.3 %copy-start.24 = (bf16[512,2048]{1,0:T(8,128)(2,1)S(1)}, bf16[512,2048]{1,0:T(8,128)(2,1)}, u32[]{:S(2)}) copy-start(bf16[512,2048]{1,0:T(8,128)(2,1)} %param.15) | copy-start | bytes 6291460
  14.8 322.4 %reduce-scatter.15.cloned.1.call-start = ((), (), s32[]{:S(2)}) async-start(), calls=%async_computation.23 | async-start | bytes 2621440 | tf_op jit(solution)/shard_map/reduce_scatter | solution.py:269
  185.2 11.9 copy-start.6
  185.2 11.9 copy-start.8
  185.2 11.9 copy-start.10
  185.2 11.9 copy-start.12
  185.2 11.9 copy-start.14
  185.2 11.9 copy-start.16
  217.7 71.3 %copy-start.2 = (bf16[1280,512]{1,0:T(8,128)(2,1)}, bf16[1280,512]{1,0:T(8,128)(2,1)S(1)}, u32[]{:S(2)}) copy-start(bf16[1280,512]{1,0:T(8,128)(2,1)S(1)} %get-tuple-element.19) | copy-start | bytes 3932164
  303.3 87.9 %all-to-all-start.1 = ((bf16[8,256,1408]{2,1,0:T(8,128)(2,1)}), bf16[8,256,1408]{2,1,0:T(8,128)(2,1)}, u32[]{:S(2)}, u32[]{:S(2)}) async-start(bf16[8,256,1408]{2,1,0:T(8,128)(2,1)} %get-tuple-element.101), calls=%async_computation.2 | async-start | bytes 11534336 | tf_op jit(solution)/shard_map/all_to_all | solution.py:252
  308.2 77.1 %all-gather.14.cloned.1.call-start = ((), (), s32[]{:S(2)}) async-start(), calls=%async_computation.24 | async-start | bytes 2621440 | tf_op jit(solution)/shard_map/all_gather | solution.py:275
  308.3 31.6 %copy-start.41 = (s32[512,2]{0,1:T(2,128)S(1)}, s32[512,2]{0,1:T(2,128)}, u32[]{:S(2)}) copy-start(s32[512,2]{0,1:T(2,128)} %param.19) | copy-start | bytes 12292
  310.8 29.3 %copy-start.48 = (s32[1,512]{1,0:T(1,128)S(1)}, s32[1,512]{1,0:T(1,128)}, u32[]{:S(2)}) copy-start(s32[1,512]{1,0:T(1,128)} %param.20) | copy-start | bytes 6148
  444.8 70.9 %all-to-all-start.2 = ((bf16[8,256,1408]{2,1,0:T(8,128)(2,1)}), bf16[8,256,1408]{2,1,0:T(8,128)(2,1)}, u32[]{:S(2)}, u32[]{:S(2)}) async-start(bf16[8,256,1408]{2,1,0:T(8,128)(2,1)} %get-tuple-element.102), calls=%async_computation.3 | async-start | bytes 11534336 | tf_op jit(solution)/shard_map/all_to_all | solution.py:252
  476.2 53.8 %slice-start = ((s8[5767168]{0:T(1024)(128)(4,1)}), s8[1572864]{0:T(1024)(128)(4,1)S(1)}, s32[]{:S(2)}) async-start(s8[5767168]{0:T(1024)(128)(4,1)} %bitcast.164), calls=%async_computation.37 | async-start | bytes 3145728
  515.6 14.5 slice-start.1
  538.5 53.8 %all-to-all-start.4 = ((bf16[8,128,2048]{2,1,0:T(8,128)(2,1)}), bf16[8,128,2048]{2,1,0:T(8,128)(2,1)}, u32[]{:S(2)}, u32[]{:S(2)}) async-start(bf16[8,128,2048]{2,1,0:T(8,128)(2,1)} %fusion.95), calls=%async_computation.5 | async-start | bytes 8388608 | tf_op jit(solution)/shard_map/all_to_all | solution.py:252
  602.9 54.2 %all-to-all-start.5 = ((bf16[8,128,2048]{2,1,0:T(8,128)(2,1)}), bf16[8,128,2048]{2,1,0:T(8,128)(2,1)}, u32[]{:S(2)}, u32[]{:S(2)}) async-start(bf16[8,128,2048]{2,1,0:T(8,128)(2,1)} %bitcast.170), calls=%async_computation.7 | async-start | bytes 8388608 | tf_op jit(solution)/shard_map/all_to_all | solution.py:252
  671.2 10.8 copy-start.53
  671.2 10.8 copy-start.55
  693.0 53.7 %all-to-all-start.6 = ((bf16[8,128,2048]{2,1,0:T(8,128)(2,1)}), bf16[8,128,2048]{2,1,0:T(8,128)(2,1)}, u32[]{:S(2)}, u32[]{:S(2)}) async-start(bf16[8,128,2048]{2,1,0:T(8,128)(2,1)} %bitcast.167), calls=%async_computation.8 | async-start | bytes 8388608 | tf_op jit(solution)/shard_map/all_to_all | solution.py:252
  697.5 55.1 %reduce-scatter.31.cloned.1.call-start = ((), (), s32[]{:S(2)}) async-start(), calls=%async_computation.35 | async-start | bytes 327680
  698.5 95.0 %reduce-scatter.19.cloned.1.call-start = ((), (), s32[]{:S(2)}) async-start(), calls=%async_computation.27 | async-start | bytes 2621440 | tf_op jit(solution)/shard_map/reduce_scatter | solution.py:269
  752.6 90.1 %all-gather.18.cloned.1.call-start = ((), (), s32[]{:S(2)}) async-start(), calls=%async_computation.28 | async-start | bytes 2621440 | tf_op jit(solution)/shard_map/all_gather | solution.py:275
  797.3 125.5 %reduce-scatter.33.cloned.1.call-start = ((), (), s32[]{:S(2)}) async-start(), calls=%async_computation.36 | async-start | bytes 327680
  849.0 11.1 copy-start.5
  849.0 12.0 copy-start.21
  849.0 12.1 copy-start.23
  895.7 63.3 %reduce-scatter.21.cloned.1.call-start = ((), (), s32[]{:S(2)}) async-start(), calls=%async_computation.29 | async-start | bytes 2621440 | tf_op jit(solution)/shard_map/reduce_scatter | solution.py:269
  902.6 102.1 %reduce-scatter.17.cloned.1.call-start = ((), (), s32[]{:S(2)}) async-start(), calls=%async_computation.25 | async-start | bytes 2621440 | tf_op jit(solution)/shard_map/reduce_scatter | solution.py:269
  913.8 388.3 %reduce-scatter.23.cloned.1.call-start = ((), (), s32[]{:S(2)}) async-start(), calls=%async_computation.31 | async-start | bytes 221184 | tf_op jit(solution)/shard_map/reduce_scatter | solution.py:500
  920.2 38.8 %copy-start.40 = (f32[2048,1]{0,1:T(1,128)S(1)}, f32[2048,1]{0,1:T(1,128)}, u32[]{:S(2)}) copy-start(f32[2048,1]{0,1:T(1,128)} %copy-done.39) | copy-start | bytes 24580
  962.6 357.1 %reduce-scatter.25.cloned.1.call-start = ((), (), s32[]{:S(2)}) async-start(), calls=%async_computation.32 | async-start | bytes 4718592 | tf_op jit(solution)/shard_map/reduce_scatter | solution.py:478
  967.3 37.4 %copy-start.30 = (f32[128,2048]{1,0:T(8,128)S(1)}, f32[128,2048]{1,0:T(8,128)}, u32[]{:S(2)}) copy-start(f32[128,2048]{1,0:T(8,128)} %copy-done.29) | copy-start | bytes 3145732
  967.3 354.5 %all-gather.16.cloned.1.call-start = ((), (), s32[]{:S(2)}) async-start(), calls=%async_computation.26 | async-start | bytes 2621440 | tf_op jit(solution)/shard_map/all_gather | solution.py:275
  1008.0 313.8 %all-gather.20.cloned.1.call-start = ((), (), s32[]{:S(2)}) async-start(), calls=%async_computation.30 | async-start | bytes 2621440 | tf_op jit(solution)/shard_map/all_gather | solution.py:275
  1008.6 345.2 %reduce-scatter.27.cloned.1.call-start = ((), (), s32[]{:S(2)}) async-start(), calls=%async_computation.33 | async-start | bytes 18874368 | tf_op jit(solution)/shard_map/reduce_scatter | solution.py:476
  1020.1 453.1 %reduce-scatter.29.cloned.1.call-start = ((), (), s32[]{:S(2)}) async-start(), calls=%async_computation.34 | async-start | bytes 18874368 | tf_op jit(solution)/shard_map/reduce_scatter | solution.py:462
  1049.3 87.8 %all-to-all-start.7 = ((bf16[8,256,1408]{2,1,0:T(8,128)(2,1)}), bf16[8,256,1408]{2,1,0:T(8,128)(2,1)}, u32[]{:S(2)}, u32[]{:S(2)}) async-start(bf16[8,256,1408]{2,1,0:T(8,128)(2,1)} %fusion.5), calls=%async_computation.15 | async-start | bytes 11534336 | tf_op jit(solution)/shard_map/all_to_all | solution.py:252
  1137.1 70.9 %all-to-all-start.8 = ((bf16[8,256,1408]{2,1,0:T(8,128)(2,1)}), bf16[8,256,1408]{2,1,0:T(8,128)(2,1)}, u32[]{:S(2)}, u32[]{:S(2)}) async-start(bf16[8,256,1408]{2,1,0:T(8,128)(2,1)} %fusion.3), calls=%async_computation.16 | async-start | bytes 11534336 | tf_op jit(solution)/shard_map/all_to_all | solution.py:252
  1208.0 86.0 %all-to-all-start.9 = ((bf16[8,1408,256]{2,1,0:T(8,128)(2,1)}), bf16[8,1408,256]{2,1,0:T(8,128)(2,1)}, u32[]{:S(2)}, u32[]{:S(2)}) async-start(bf16[8,1408,256]{2,1,0:T(8,128)(2,1)} %convolution_bitcast_fusion), calls=%async_computation.17 | async-start | bytes 11534336 | tf_op jit(solution)/shard_map/all_to_all | solution.py:252
  1353.9 124.7 %copy-start.1 = (s32[1,4]{1,0:T(1,128)S(1)}, s32[1,4]{1,0:T(1,128)}, u32[]{:S(2)}) copy-start(s32[1,4]{1,0:T(1,128)} %param.17) | copy-start | bytes 52
  1358.0 119.2 %copy-start.34 = (bf16[512,2048]{1,0:T(8,128)(2,1)S(1)}, bf16[512,2048]{1,0:T(8,128)(2,1)}, u32[]{:S(2)}) copy-start(bf16[512,2048]{1,0:T(8,128)(2,1)} %all-gather.16.cloned.1.call-done) | copy-start | bytes 6291460
  (37 other events, 130.5 us)
Sparse Core Ops, SparseCore 0:
  9.9 69.9 all-gather.9
  81.8 103.2 all-gather.7
  187.0 93.1 all-gather.11
  293.3 43.8 reduce-scatter.14
  339.9 45.2 all-gather.13
  701.0 18.7 reduce-scatter.30
  752.7 40.7 reduce-scatter.18
  797.4 45.2 all-gather.17
  895.8 18.2 reduce-scatter.32
  916.9 42.1 reduce-scatter.20
  961.4 43.1 reduce-scatter.16
  1007.6 32.8 reduce-scatter.22
  1044.7 83.7 reduce-scatter.24
  1130.0 45.7 all-gather.15
  1177.7 44.6 all-gather.19
  1225.8 127.9 reduce-scatter.26
  1357.3 115.9 reduce-scatter.28

commit v2 on v1

--- a/solution.py
+++ b/solution.py
@@ -240,9 +240,176 @@
     )(q, k, v, bias, gate, *slot_tables, *tok_tables, grad_gated)
 
 
+class Square:
+    def __init__(self):
+        me = lax.axis_index("dp")
+        self.core = lax.rem(me, 2)
+        self.chip = me // 2
+        x, y = lax.rem(self.chip, 2), self.chip // 2
+        self.chip_x = self.chip + 1 - 2 * x
+        self.chip_y = self.chip + 2 - 4 * y
+        self.chip_far = 3 - self.chip
+        self.twin = me + 1 - 2 * self.core
+        self.near_x = 2 * self.chip_x + self.core
+        self.near_y = 2 * self.chip_y + self.core
+
+
+def send_to(source, target, send_sem, recv_sem, device):
+    return pltpu.make_async_remote_copy(
+        src_ref=source,
+        dst_ref=target,
+        send_sem=send_sem,
+        recv_sem=recv_sem,
+        device_id={"dp": device},
+        device_id_type=pl.DeviceIdType.MESH,
+    )
+
+
+def map_grads_kernel(
+    routed, grad_q, normed, grad_kv, out,
+    give, keep, twin_in, far_in, near_in,
+    twin_send, twin_recv, far_send, far_recv, near_send, near_recv,
+):
+    at = Square()
+    experts = routed.shape[0]
+    units, _, size, _ = keep.shape
+    half = size // 2
+    barrier = pltpu.get_barrier_semaphore()
+    for device in (at.twin, at.near_x, at.near_y):
+        pl.semaphore_signal(
+            barrier, inc=1, device_id={"dp": device}, device_id_type=pl.DeviceIdType.MESH
+        )
+    pl.semaphore_wait(barrier, 3)
+
+    def to_twin(u):
+        return send_to(give.at[u], twin_in.at[u], twin_send.at[u], twin_recv.at[u], at.twin)
+
+    def to_far(u):
+        first = send_to(
+            keep.at[u, at.chip_far, pl.ds(0, half)],
+            far_in.at[u, 0], far_send.at[u, 0], far_recv.at[u, 0], at.near_x,
+        )
+        second = send_to(
+            keep.at[u, at.chip_far, pl.ds(half, half)],
+            far_in.at[u, 1], far_send.at[u, 1], far_recv.at[u, 1], at.near_y,
+        )
+        return first, second
+
+    def to_near(u):
+        first = send_to(
+            keep.at[u, at.chip_x], near_in.at[u, 0], near_send.at[u, 0], near_recv.at[u, 0],
+            at.near_x,
+        )
+        second = send_to(
+            keep.at[u, at.chip_y], near_in.at[u, 1], near_send.at[u, 1], near_recv.at[u, 1],
+            at.near_y,
+        )
+        return first, second
+
+    def multiply(u, rows, grads):
+        for target, core in ((give, 1 - at.core), (keep, at.core)):
+            for chip in range(4):
+                columns = pl.ds(pl.multiple_of((2 * chip + core) * size, size), size)
+                target[u, chip] = dot_tn(rows[:, columns], grads[...]).astype(BF16)
+            if target is give:
+                to_twin(u).start()
+
+    def join_twin(u):
+        to_twin(u).wait_recv()
+
+        def add(chip):
+            keep[u, chip] = (keep[u, chip].astype(F32) + twin_in[u, chip].astype(F32)).astype(BF16)
+
+        add(at.chip_far)
+        for copy in to_far(u):
+            copy.start()
+        add(at.chip_x)
+        add(at.chip_y)
+        add(at.chip)
+
+    @pl.loop(0, experts)
+    def _(u):
+        multiply(u, routed.at[u], grad_q.at[u])
+
+        @pl.when(u > 0)
+        def _():
+            join_twin(u - 1)
+
+    @pl.loop(experts, units)
+    def _(u):
+        multiply(u, normed, grad_kv.at[u - experts])
+        join_twin(u - 1)
+
+    join_twin(units - 1)
+
+    @pl.loop(0, units)
+    def _(u):
+        for copy in to_far(u):
+            copy.wait_recv()
+        top, bottom = pl.ds(0, half), pl.ds(half, half)
+        keep[u, at.chip_y, top, :] = (
+            keep[u, at.chip_y, top, :].astype(F32) + far_in[u, 0].astype(F32)
+        ).astype(BF16)
+        keep[u, at.chip_x, bottom, :] = (
+            keep[u, at.chip_x, bottom, :].astype(F32) + far_in[u, 1].astype(F32)
+        ).astype(BF16)
+        for copy in to_near(u):
+            copy.start()
+
+    @pl.loop(0, units)
+    def _(u):
+        for copy in to_near(u):
+            copy.wait_recv()
+        out[u] = (
+            keep[u, at.chip].astype(F32) + near_in[u, 0].astype(F32) + near_in[u, 1].astype(F32)
+        ).astype(BF16)
+
+    @pl.loop(0, units)
+    def _(u):
+        to_twin(u).wait_send()
+        for copy in (*to_far(u), *to_near(u)):
+            copy.wait_send()
+
+
+def map_grads(routed, grad_q, normed, grad_kv):
+    experts, _, model_width = routed.shape
+    width = grad_q.shape[2]
+    units = experts + grad_kv.shape[0]
+    size = model_width // 8
+    vmem = pl.BlockSpec(memory_space=pltpu.VMEM)
+    return pl.pallas_call(
+        map_grads_kernel,
+        in_specs=[vmem] * 4,
+        out_specs=vmem,
+        out_shape=jax.ShapeDtypeStruct((units, size, width), BF16),
+        scratch_shapes=[
+            pltpu.VMEM((units, 4, size, width), BF16),
+            pltpu.VMEM((units, 4, size, width), BF16),
+            pltpu.VMEM((units, 4, size, width), BF16),
+            pltpu.VMEM((units, 2, size // 2, width), BF16),
+            pltpu.VMEM((units, 2, size, width), BF16),
+            pltpu.SemaphoreType.DMA((units,)),
+            pltpu.SemaphoreType.DMA((units,)),
+            pltpu.SemaphoreType.DMA((units, 2)),
+            pltpu.SemaphoreType.DMA((units, 2)),
+            pltpu.SemaphoreType.DMA((units, 2)),
+            pltpu.SemaphoreType.DMA((units, 2)),
+        ],
+        compiler_params=pltpu.CompilerParams(
+            collective_id=1, has_side_effects=True, vmem_limit_bytes=60 << 20
+        ),
+        cost_estimate=pl.CostEstimate(
+            flops=2 * units * 160 * model_width * width,
+            bytes_accessed=250 << 20,
+            transcendentals=0,
+        ),
+    )(routed, grad_q, normed, grad_kv)
+
+
 class Movers:
-    def __init__(self, dp, experts):
-        self.dp, self.experts, self.ratio = dp, experts, dp // experts
+    def __init__(self, dp, experts, tensor):
+        self.dp, self.experts, self.tensor = dp, experts, tensor
+        self.ratio = dp // experts
         self.groups = self.pairs = None
         if self.ratio > 1:
             self.groups = [[g * experts + e for e in range(experts)] for g in range(self.ratio)]
@@ -264,15 +431,48 @@
             )
         return self.swap(slices)
 
-
-def reduce_rows(part):
-    return lax.psum_scatter(part.astype(BF16), "tensor", scatter_dimension=0, tiled=True).astype(
-        F32
-    )
-
-
-def gather_rows(rows):
-    return lax.all_gather(rows.astype(BF16), "tensor", axis=0, tiled=True)
+    def exchange(self, rows):
+        size = rows.shape[0] // self.experts
+        blocks = [rows[:size]]
+        for k in range(1, self.experts):
+            pairs = [(i, i ^ k) for i in range(self.dp)]
+            blocks.append(lax.ppermute(rows[k * size : (k + 1) * size], "dp", pairs))
+        return jnp.concatenate(blocks, axis=0)
+
+    def across(self, block, k):
+        return lax.ppermute(block, "tensor", [(i, i ^ k) for i in range(self.tensor)])
+
+    def reduce_rows(self, part, dtype=BF16):
+        z = lax.axis_index("tensor")
+        size = part.shape[0] // self.tensor
+        total = lax.dynamic_slice_in_dim(part, z * size, size, axis=0)
+        sent = part.astype(dtype)
+        for k in range(1, self.tensor):
+            block = lax.dynamic_slice_in_dim(sent, (z ^ k) * size, size, axis=0)
+            total = total + self.across(block, k).astype(F32)
+        return total
+
+    def gather_rows(self, rows):
+        z = lax.axis_index("tensor")
+        size = rows.shape[0]
+        rows = rows.astype(BF16)
+        full = jnp.zeros((size * self.tensor,) + rows.shape[1:], BF16)
+        for k in range(self.tensor):
+            block = rows if k == 0 else self.across(rows, k)
+            full = lax.dynamic_update_slice_in_dim(full, block, (z ^ k) * size, axis=0)
+        return full
+
+
+def map_sums(dp_size, routed, grad_q, normed, grad_k, grad_v):
+    if dp_size == 8:
+        both = map_grads(routed, grad_q, normed, jnp.stack([grad_k, grad_v]))
+        return both[:-2], both[-2:]
+    grad_query_w = jnp.einsum("ecd,ecf->edf", routed, grad_q, preferred_element_type=BF16)
+    grad_keyval_w = jnp.stack([dot_tn(normed, grad_k, BF16), dot_tn(normed, grad_v, BF16)])
+    return (
+        lax.psum_scatter(grad_query_w, "dp", scatter_dimension=1, tiled=True),
+        lax.psum_scatter(grad_keyval_w, "dp", scatter_dimension=1, tiled=True),
+    )
 
 
 def on_device(
@@ -304,12 +504,16 @@
     mlp_slots = mlp_experts * mlp_cap
     width_here = query_weight.shape[2]
     rows_here = tok_count // tensor_size
-    movers = Movers(dp_size, mlp_experts)
+    movers = Movers(dp_size, mlp_experts, tensor_size)
+    tie = lax.optimization_barrier
 
     small = jnp.concatenate(
         [gain_attention[:, None], gain_feedforward[:, None], attention_router, expert_router], axis=1
     )
     small_full = lax.all_gather(small, "dp", axis=0, tiled=True)
+    small_full, keyval_weight, query_weight, output_weight, gate_up_weight, down_weight = tie(
+        (small_full, keyval_weight, query_weight, output_weight, gate_up_weight, down_weight)
+    )
     keyval_full = lax.all_gather(keyval_weight, "dp", axis=1, tiled=True)
     query_full = lax.all_gather(query_weight, "dp", axis=1, tiled=True)
     output_full = lax.all_gather(output_weight, "dp", axis=2, tiled=True)
@@ -330,7 +534,10 @@
         slot_places(attention_routes, pair_order, att_cap, att_experts), att_slots
     )
     priority = slot_order[0][:, None] * TOPK + jnp.arange(TOPK, dtype=jnp.int32)[None, :]
-    mlp_hits = slot_hits(slot_places(expert_routes, priority, mlp_cap, mlp_experts), mlp_slots)
+    home = lax.rem(lax.axis_index("dp"), mlp_experts)
+    mlp_hits = slot_hits(
+        slot_places(expert_routes ^ home, priority, mlp_cap, mlp_experts), mlp_slots
+    )
     att_pick = (att_hits[0] | att_hits[1]).astype(BF16)
     mlp_pick = (mlp_hits[0] | mlp_hits[1]).astype(BF16)
 
@@ -364,6 +571,8 @@
     reach = dot(segment_hot, jnp.repeat(inside.astype(F32), SEG, axis=1)) > 0.5
     allowed = reach & (token_index[None, :] <= slot_token[:, None]) & slot_filled[:, None]
     bias = jnp.where(allowed, 0.0, NEGATIVE).astype(BF16)
+
+    cot_rows = movers.exchange(dot(mlp_pick, cotangent, BF16))
 
     inputs = tokens.astype(F32)
     normal_attn, scale_attn = norm_forward(inputs)
@@ -389,58 +598,60 @@
     def share(rows):
         return lax.dynamic_slice_in_dim(rows, z * rows_here, rows_here, axis=0)
 
-    hidden = share(inputs) + reduce_rows(att_part)
+    hidden = share(inputs) + movers.reduce_rows(att_part)
     normal_mlp, scale_mlp = norm_forward(hidden)
     mlp_in_here = (normal_mlp * gain_mlp_full).astype(BF16)
-    mlp_in = gather_rows(mlp_in_here)
+    mlp_in = movers.gather_rows(mlp_in_here)
     mlp_gates = picked_softmax(dot(mlp_in, router_mlp), expert_routes)
     mlp_gate_slots = to_slots(mlp_hits, mlp_gates)[:, None]
-    expert_in = dot(mlp_pick, mlp_in, BF16)
-    grad_rows = (dot(mlp_pick, cotangent) * mlp_gate_slots).astype(BF16)
-
-    def send(rows):
-        return movers.swap(rows.reshape(mlp_experts, mlp_cap, model_width)).reshape(
-            mlp_slots, model_width
-        )
-
-    x_rows = send(expert_in)
-    g_rows = send(grad_rows)
+    gate_high = mlp_gate_slots.astype(BF16)
+    gate_rest = mlp_gate_slots - gate_high.astype(F32)
+    gate_mid = gate_rest.astype(BF16)
+    gate_low = (gate_rest - gate_mid.astype(F32)).astype(BF16)
+    expert_in = jnp.concatenate(
+        [dot(mlp_pick, mlp_in, BF16), gate_high, gate_mid, gate_low]
+        + [jnp.zeros((mlp_slots, HD - 3), BF16)],
+        axis=1,
+    )
+
+    received = movers.exchange(expert_in)
+    x_rows = received[:, :model_width]
+    gate_columns = received[:, model_width : model_width + 3].astype(F32)
+    gate_of_row = gate_columns[:, :1] + gate_columns[:, 1:2] + gate_columns[:, 2:]
+    g_rows = (cot_rows.astype(F32) * gate_of_row).astype(BF16)
     gate = dot(x_rows, gate_full)
     up = dot(x_rows, up_full)
     sigmoid_gate = jax.nn.sigmoid(gate)
     silu_gate = gate * sigmoid_gate
     activated = (silu_gate * up).astype(BF16)
     expert_out = dot(activated, down_full, BF16)
+    out_slots = movers.exchange(expert_out)
     grad_act = dot_nt(g_rows, down_full)
     grad_gate = (grad_act * up * sigmoid_gate * (1.0 + gate * (1.0 - sigmoid_gate))).astype(BF16)
     grad_up = (grad_act * silu_gate).astype(BF16)
     grad_expert_in = (dot_nt(grad_gate, gate_full) + dot_nt(grad_up, up_full)).astype(BF16)
-    out_slots = send(expert_out)
-    grad_in_slots = send(grad_expert_in)
+    grad_in_slots = movers.exchange(grad_expert_in)
+    grad_gate, grad_up, activated, _ = tie((grad_gate, grad_up, activated, grad_expert_in))
     per_dp = model_width // dp_size
     grad_gate_w = dot_tn(x_rows, grad_gate, BF16).reshape(dp_size, per_dp, -1)
+    grad_up, activated, grad_gate_w, out_slots = tie((grad_up, activated, grad_gate_w, out_slots))
     grad_up_w = dot_tn(x_rows, grad_up, BF16).reshape(dp_size, per_dp, -1)
     grad_down_w = (
         dot_tn(activated, g_rows, BF16).reshape(-1, dp_size, per_dp).transpose(1, 0, 2)
     )
-    grad_gate_up_out = jnp.stack(
-        [movers.give_back(grad_gate_w).astype(F32), movers.give_back(grad_up_w).astype(F32)], axis=1
-    )
-    grad_down_out = movers.give_back(grad_down_w).astype(F32)
-
-    gate_matrix = sum(
-        jnp.where(mlp_hits[k], mlp_gates[:, k][None, :], 0.0) for k in range(TOPK)
-    )
-    gate_high = gate_matrix.astype(BF16)
-    gate_low = (gate_matrix - gate_high.astype(F32)).astype(BF16)
-    mlp_part = dot_tn(gate_high, out_slots) + dot_tn(gate_low, out_slots)
-    mixed = gather_rows(hidden + reduce_rows(mlp_part))
+    grad_in_slots, out_slots, grad_gate_w, grad_up_w, grad_down_w = tie(
+        (grad_in_slots, out_slots, grad_gate_w, grad_up_w, grad_down_w)
+    )
+    grad_gate_w = movers.give_back(grad_gate_w)
+    grad_up_w = movers.give_back(grad_up_w)
+    grad_down_w = movers.give_back(grad_down_w)
+
     alignment = dot_nt(out_slots, cotangent)
     grad_gates_part = jnp.stack(
         [jnp.sum(jnp.where(mlp_hits[k], alignment, 0.0), axis=0) for k in range(TOPK)], axis=1
     )
-    grad_mlp_gates = lax.psum_scatter(grad_gates_part, "tensor", scatter_dimension=0, tiled=True)
-    grad_mlp_in = reduce_rows(dot_tn(mlp_pick, grad_in_slots))
+    grad_mlp_gates = movers.reduce_rows(grad_gates_part, F32)
+    grad_mlp_in = movers.reduce_rows(dot_tn(mlp_pick, grad_in_slots))
     grad_mlp_logits = router_backward(
         share(mlp_gates), grad_mlp_gates, share(expert_routes), mlp_experts
     )
@@ -450,39 +661,52 @@
         grad_mlp_in, normal_mlp, scale_mlp, gain_mlp_full
     )
     grad_hidden = share(cotangent).astype(F32) + grad_hidden_norm
-    grad_att_pair = gather_rows(grad_hidden)
+    grad_hidden, grad_gate_w = tie((grad_hidden, grad_gate_w))
+    grad_att_pair = movers.gather_rows(grad_hidden)
+
+    gate_matrix = sum(
+        jnp.where(mlp_hits[k], mlp_gates[:, k][None, :], 0.0) for k in range(TOPK)
+    )
+    matrix_high = gate_matrix.astype(BF16)
+    matrix_low = (gate_matrix - matrix_high.astype(F32)).astype(BF16)
+    mlp_part = dot_tn(matrix_high, out_slots) + dot_tn(matrix_low, out_slots)
+    mlp_part, grad_att_pair = tie((mlp_part, grad_att_pair))
+    mlp_sum = movers.reduce_rows(mlp_part)
 
     grad_att_rows = dot(att_pick, grad_att_pair, BF16).reshape(att_experts, att_cap, model_width)
+    grad_output_w = jnp.einsum(
+        "ecf,ecd->efd", gated_slots, grad_att_rows, preferred_element_type=BF16
+    )
+    grad_att_rows, grad_output_w = tie((grad_att_rows, grad_output_w))
     grad_gated = jnp.einsum(
         "ecd,efd->ecf", grad_att_rows, output_full, preferred_element_type=F32
     ).reshape(att_slots, width_here)
-    grad_output_w = jnp.einsum(
-        "ecf,ecd->efd", gated_slots, grad_att_rows, preferred_element_type=BF16
-    )
     grad_output_out = lax.psum_scatter(grad_output_w, "dp", scatter_dimension=2, tiled=True)
-    grad_att_gates = lax.psum_scatter(
-        to_pairs(att_hits, jnp.sum(grad_gated * attended, axis=1)),
-        "tensor",
-        scatter_dimension=0,
-        tiled=True,
+    grad_att_gates = movers.reduce_rows(
+        to_pairs(att_hits, jnp.sum(grad_gated * attended, axis=1)), F32
     )
     grad_q, grad_k, grad_v = attend_back(
         queries, key_rows, values, bias, att_gate_slots, slot_tables, tok_tables, grad_gated
     )
     grad_query_slots = grad_q.reshape(att_experts, att_cap, width_here)
-    grad_query_w = jnp.einsum(
-        "ecd,ecf->edf", routed, grad_query_slots, preferred_element_type=BF16
-    )
-    grad_query_out = lax.psum_scatter(grad_query_w, "dp", scatter_dimension=1, tiled=True)
-    grad_keyval_w = jnp.stack([dot_tn(normed, grad_k, BF16), dot_tn(normed, grad_v, BF16)])
-    grad_keyval_out = lax.psum_scatter(grad_keyval_w, "dp", scatter_dimension=1, tiled=True)
     grad_routed = jnp.einsum(
         "ecf,edf->ecd", grad_query_slots, query_full, preferred_element_type=F32
     ).reshape(att_slots, model_width)
-    grad_normed = reduce_rows(
+    normed_part = (
         dot_tn(att_pick, grad_routed.astype(BF16))
         + dot_nt(grad_k, keyval_full[0])
         + dot_nt(grad_v, keyval_full[1])
+    )
+    grad_normed = movers.reduce_rows(normed_part)
+    grad_query_slots, grad_k, grad_v, _, grad_up_w, mlp_sum = tie(
+        (grad_query_slots, grad_k, grad_v, normed_part, grad_up_w, mlp_sum)
+    )
+    mixed = movers.gather_rows(hidden + mlp_sum)
+    grad_query_out, grad_keyval_out = map_sums(
+        dp_size, routed, grad_query_slots, normed, grad_k, grad_v
+    )
+    grad_normed, grad_down_w, grad_query_out, grad_output_out, mixed = tie(
+        (grad_normed, grad_down_w, grad_query_out, grad_output_out, mixed)
     )
     grad_att_logits = router_backward(
         share(att_gates), grad_att_gates, share(attention_routes), att_experts
@@ -492,7 +716,7 @@
     grad_input_norm, grad_gain_attn = norm_backward(
         grad_normed, share(normal_attn), share(scale_attn), gain_attn_full
     )
-    grad_tokens = gather_rows(grad_hidden + grad_input_norm).astype(F32)
+    grad_tokens = movers.gather_rows(grad_hidden + grad_input_norm).astype(F32)
     small_grads = jnp.concatenate(
         [grad_gain_attn[:, None], grad_gain_mlp[:, None], grad_router_att, grad_router_mlp], axis=1
     )
@@ -509,8 +733,8 @@
         small_grads[:, 2 : 2 + att_experts],
         small_grads[:, 1],
         small_grads[:, 2 + att_experts :],
-        grad_gate_up_out,
-        grad_down_out,
+        jnp.stack([grad_gate_w.astype(F32), grad_up_w.astype(F32)], axis=1),
+        grad_down_w.astype(F32),
     )
 
 

time: 1490 us -> 1250 us (0.84)
  waiting for transfers between devices: 845 us -> 509 us
  Pallas kernels: 35.1 us -> 153 us
  starting transfers between devices: 45.2 us -> 162 us
  blocking collectives: 152 us -> 40.9 us
  matrix products: 245 us -> 215 us
    all_to_all x9 -> x6, waiting for transfers between devices: 355 us -> 53.7 us  [swap(): lax.all_to_all(blocks, 'dp', 0, 0, axis_index_groups=self.groups, tiled=T...]
    ppermute x0 -> x58, waiting for transfers between devices: none -> 255 us  [the longest x30 131 us: across(): lax.ppermute(block, 'tensor', [(i, i ^ k) for i in range(self.tensor)])]
    reduce_scatter x6 -> x0, waiting for transfers between devices: 165 us -> none  [the longest x4 137 us: reduce_rows(): lax.psum_scatter(part.astype(BF16), 'tensor', scatter_dimension=0, tiled=...]
    ppermute x0 -> x58, starting transfers between devices: none -> 132 us  [the longest x30 108 us: across(): lax.ppermute(block, 'tensor', [(i, i ^ k) for i in range(self.tensor)])]
    pallas_call x0 -> x1, Pallas kernels: none -> 118 us  [map_grads(): pl.pallas_call(map_grads_kernel, in_specs=[vmem] * 4, out_specs=vmem, out...]
    reduce_scatter x1, waiting for transfers between devices: 115 us -> 0.01 us  [on_device(): lax.psum_scatter(grad_output_w, 'dp', scatter_dimension=2, tiled=True)]
    all_gather x4 -> x0, waiting for transfers between devices: 88.4 us -> none  [gather_rows(): return lax.all_gather(rows.astype(BF16), 'tensor', axis=0, tiled=True)]
    all_gather x1, blocking collectives: 82.1 us -> 10.7 us  [on_device(): small_full = lax.all_gather(small, 'dp', axis=0, tiled=True)]
  transfers between devices with their start and end apart: 26 -> 69, of which waited for: 17 -> 23; matrix products, arithmetic and copies ran while one was open for 18% -> 23% of each run, Pallas kernels for 1% -> 12%
where the time goes in v2:
time: 1250 us; the launch traced here: 1240 us
  waiting for transfers between devices  509 us (41%)
  matrix products  215 us (17%)
  starting transfers between devices  162 us (13%)
  Pallas kernels  153 us (12%)
  local copies, waits for them, and re-layouts  82.6 us (7%)
  other arithmetic  65.2 us (5%)
  blocking collectives  40.9 us (3%)
  between operations  16 us (1%)
    ppermute x30, waiting for transfers between devices, across(): lax.ppermute(block, 'tensor', [(i, i ^ k) for i in range(self.tensor)])  131 us
    ppermute x28, waiting for transfers between devices, exchange(): blocks.append(lax.ppermute(rows[k * size:(k + 1) * size], 'dp', pairs))  124 us
    all_gather x1, waiting for transfers between devices, on_device(): query_full = lax.all_gather(query_weight, 'dp', axis=1, tiled=True)  121 us
    pallas_call x1, Pallas kernels, map_grads(): pl.pallas_call(map_grads_kernel, in_specs=[vmem] * 4, out_specs=vmem, out...  118 us
    ppermute x30, starting transfers between devices, across(): lax.ppermute(block, 'tensor', [(i, i ^ k) for i in range(self.tensor)])  108 us
    all_gather x1, waiting for transfers between devices, on_device(): output_full = lax.all_gather(output_weight, 'dp', axis=2, tiled=True)  63 us
    dot_general x12, matrix products, dot(): return jnp.dot(a, b, preferred_element_type=out)  60.1 us
    dot_general x10, matrix products, dot_tn(): lax.dot_general(a, b, (((0,), (0,)), ((), ())), preferred_element_type=out)  56.8 us
  transfers between devices with their start and end apart: 69, of which 23 were waited for; matrix products, arithmetic and copies ran while one was open for 23% of the time, Pallas kernels for 12%

profile of v2, /device:TPU:0, one launch (start us, length us, event | category | flops | bytes accessed | tf_op | source)
XLA Modules:
  0.0 1243.4 jit_solution(15747400906094106196)
XLA Ops:
  9.4 10.7 all_gather.12
  30.2 8.3 copy.97
  77.5 120.9 %all-gather.4.cloned.1.call-done = bf16[8,2048,512]{2,1,0:T(8,128)(2,1)} async-done(((bf16[8,256,512]{2,1,0:T(8,128)(2,1)}), bf16[8,2048,512]{2,1,0:T(8,128)(2,1)}) %all-gather.4.cloned.1.call-update) | async-done | bytes 16777232 | tf_op jit(solution)/shard_map/all_gather | solution.py:518
  198.4 11.8 fusion.123
  210.3 16.0 %shard_map.230 = (bf16[1280,512]{1,0:T(8,128)(2,1)S(1)}, bf16[512,512]{1,0:T(8,128)(2,1)S(1)}, bf16[512,512]{1,0:T(8,128)(2,1)S(1)}, f32[1280,512]{1,0:T(8,128)S(1)}, bf16[1280,512]{1,0:T(8,128)(2,1)S(1)}) custom-call(f32[1280,512]{1,0:T(8,128)} %bitcast.133, f32[512,1024]{1,0:T(8,128)S(1)} %pad_maximum_fusion.k_raw.v_raw, ...), custom_call_target="tpu_custom_call" | custom-call | flops 1342177280 | bytes 9175040 | tf_op jit(solution)/shard_map/pallas_call | solution.py:138
  230.5 63.0 %all-gather.8.cloned.1.call-done = bf16[8,512,2048]{2,1,0:T(8,128)(2,1)} async-done(((bf16[8,512,256]{2,1,0:T(8,128)(2,1)}), bf16[8,512,2048]{2,1,0:T(8,128)(2,1)}) %all-gather.8.cloned.1.call-update) | async-done | bytes 16777232 | tf_op jit(solution)/shard_map/all_gather | solution.py:519
  293.4 8.8 convolution_convert_fusion.1
  312.9 10.2 slice_bitcast_fusion.1
  333.7 14.7 %collective-permute-done.1 = bf16[128,2048]{1,0:T(8,128)(2,1)} collective-permute-done((bf16[128,2048]{1,0:T(8,128)(2,1)}, bf16[128,2048]{1,0:T(8,128)(2,1)}, u32[]{:S(2)}, u32[]{:S(2)}) %collective-permute-start.1) | collective-permute-done | bytes 524320 | tf_op jit(solution)/shard_map/ppermute | solution.py:443
  352.7 10.9 collective-permute-start.3
  369.8 13.7 %collective-permute-done.3 = bf16[128,2048]{1,0:T(8,128)(2,1)S(1)} collective-permute-done((bf16[128,2048]{1,0:T(8,128)(2,1)S(1)}, bf16[128,2048]{1,0:T(8,128)(2,1)S(1)}, u32[]{:S(2)}, u32[]{:S(2)}) %collective-permute-start.3) | collective-permute-done | bytes 524320 | tf_op jit(solution)/shard_map/ppermute | solution.py:443
  383.6 20.1 %collective-permute-done.4 = bf16[128,2048]{1,0:T(8,128)(2,1)S(1)} collective-permute-done((bf16[128,2048]{1,0:T(8,128)(2,1)S(1)}, bf16[128,2048]{1,0:T(8,128)(2,1)S(1)}, u32[]{:S(2)}, u32[]{:S(2)}) %collective-permute-start.4) | collective-permute-done | bytes 524320 | tf_op jit(solution)/shard_map/ppermute | solution.py:443
  439.9 46.9 %collective-permute-done.14 = bf16[128,2176]{1,0:T(8,128)(2,1)S(1)} collective-permute-done((bf16[128,2176]{1,0:T(8,128)(2,1)S(1)}, bf16[128,2176]{1,0:T(8,128)(2,1)S(1)}, u32[]{:S(2)}, u32[]{:S(2)}) %collective-permute-start.14) | collective-permute-done | bytes 557088 | tf_op jit(solution)/shard_map/ppermute | solution.py:439
  487.9 9.9 collective-permute-done.15
  500.4 11.2 collective-permute-done.18
  525.1 11.8 fusion.6
  536.9 10.4 fusion.20
  547.3 37.8 %all-to-all-done.1 = bf16[8,256,1408]{2,1,0:T(8,128)(2,1)} async-done(((bf16[8,256,1408]{2,1,0:T(8,128)(2,1)}), bf16[8,256,1408]{2,1,0:T(8,128)(2,1)}, u32[]{:S(2)}, u32[]{:S(2)}) %all-to-all-start.1) | async-done | bytes 5767200 | tf_op jit(solution)/shard_map/all_to_all | solution.py:419
  585.1 14.4 %multiply_convert_fusion.1 = (bf16[1024,1408]{1,0:T(8,128)(2,1)S(1)}, bf16[1024,1408]{1,0:T(8,128)(2,1)S(1)}, bf16[1024,1408]{1,0:T(8,128)(2,1)S(1)}) fusion(f32[1024,1408]{1,0:T(8,128)} %fusion.6, f32[1024,1408]{1,0:T(8,128)} %fusion.20, bf16[2048,1408]{1,0:T(8,128)(2,1)} %bitcast.24, bf16[1024,2176]{1,0:T(8,128)(2,1)} %constant_dynamic-update-slice_fusion.7), kind=kOutput, calls=%fused_computation.8 | convolution fusion | flops 5927206912 | bytes 30146560 | tf_op jit(solution)/shard_map/dot_general | solution.py:22
  599.5 9.8 fusion.125
  609.3 8.9 fusion.124
  618.2 8.7 add_convert_fusion
  631.8 10.8 fusion.4
  655.0 22.4 %collective-permute-done.31 = bf16[128,2048]{1,0:T(8,128)(2,1)S(1)} collective-permute-done((bf16[128,2048]{1,0:T(8,128)(2,1)S(1)}, bf16[128,2048]{1,0:T(8,128)(2,1)S(1)}, u32[]{:S(2)}, u32[]{:S(2)}) %collective-permute-start.31) | collective-permute-done | bytes 524320 | tf_op jit(solution)/shard_map/ppermute | solution.py:439
  679.7 12.9 %fusion.2 = bf16[2048,1408]{1,0:T(8,128)(2,1)} fusion(bf16[1024,1408]{1,0:T(8,128)(2,1)S(1)} %get-tuple-element.68, bf16[1024,2176]{1,0:T(8,128)(2,1)} %constant_dynamic-update-slice_fusion.7), kind=kOutput, calls=%fused_computation.26 | convolution fusion | flops 5905580032 | bytes 12845056 | tf_op jit(solution)/shard_map/dot_general | solution.py:26
  705.8 9.4 collective-permute-done.25
  715.2 11.0 collective-permute-done.26
  738.5 9.3 collective-permute-start.37
  762.1 19.3 %collective-permute-done.34 = bf16[128,2048]{1,0:T(8,128)(2,1)S(1)} collective-permute-done((bf16[128,2048]{1,0:T(8,128)(2,1)S(1)}, bf16[128,2048]{1,0:T(8,128)(2,1)S(1)}, u32[]{:S(2)}, u32[]{:S(2)}) %collective-permute-start.34) | collective-permute-done | bytes 524320 | tf_op jit(solution)/shard_map/ppermute | solution.py:443
  781.4 15.4 %collective-permute-done.35 = bf16[128,2048]{1,0:T(8,128)(2,1)S(1)} collective-permute-done((bf16[128,2048]{1,0:T(8,128)(2,1)S(1)}, bf16[128,2048]{1,0:T(8,128)(2,1)S(1)}, u32[]{:S(2)}, u32[]{:S(2)}) %collective-permute-start.35) | collective-permute-done | bytes 524320 | tf_op jit(solution)/shard_map/ppermute | solution.py:443
  800.2 10.1 collective-permute-start.40
  819.5 11.1 collective-permute-done.40
  830.6 17.9 %collective-permute-done.41 = bf16[128,2048]{1,0:T(8,128)(2,1)S(1)} collective-permute-done((bf16[128,2048]{1,0:T(8,128)(2,1)S(1)}, bf16[128,2048]{1,0:T(8,128)(2,1)S(1)}, u32[]{:S(2)}, u32[]{:S(2)}) %collective-permute-start.41) | collective-permute-done | bytes 524320 | tf_op jit(solution)/shard_map/ppermute | solution.py:443
  853.3 10.7 fusion.126
  875.2 9.8 collective-permute-start.46
  885.9 14.5 %fusion.127 = f32[8,160,512]{2,1,0:T(8,128)S(1)} fusion(bf16[8,160,2048]{2,1,0:T(8,128)(2,1)} %bitcast.131, bf16[8,512,2048]{2,1,0:T(8,128)(2,1)} %all-gather.8.cloned.1.call-done), kind=kOutput, calls=%fused_computation.330 | convolution fusion | flops 2684354560 | bytes 24641536 | tf_op jit(solution)/shard_map/ecd,efd->ecf/dot_general | solution.py:681
  906.1 18.7 %shard_map.231 = (bf16[1280,512]{1,0:T(8,128)(2,1)S(1)}, bf16[512,512]{1,0:T(8,128)(2,1)S(1)}, bf16[512,512]{1,0:T(8,128)(2,1)S(1)}) custom-call(bf16[1280,512]{1,0:T(8,128)(2,1)S(1)} %copy-done.20, bf16[512,512]{1,0:T(8,128)(2,1)S(1)} %copy-done.22, bf16[512,512]{1,0:T(8,128)(2,1)S(1)} %copy-done.24, bf16[1280,512]{1,0:T(8,128)(2,1)S(1)} %copy-done.14, ...), custom_call_target="tpu_custom_call" | custom-call | flops 3355443200 | bytes 6553600 | tf_op jit(solution)/shard_map/pallas_call | solution.py:208
  926.1 10.9 convolution_convert_fusion
  946.7 15.9 %all-to-all-done.5 = bf16[8,256,1408]{2,1,0:T(8,128)(2,1)} async-done(((bf16[8,256,1408]{2,1,0:T(8,128)(2,1)}), bf16[8,256,1408]{2,1,0:T(8,128)(2,1)}, u32[]{:S(2)}, u32[]{:S(2)}) %all-to-all-start.5) | async-done | bytes 5767200 | tf_op jit(solution)/shard_map/all_to_all | solution.py:419
  968.9 15.4 %collective-permute-start.43 = (bf16[128,2048]{1,0:T(8,128)(2,1)}, bf16[128,2048]{1,0:T(8,128)(2,1)S(1)}, u32[]{:S(2)}, u32[]{:S(2)}) collective-permute-start(bf16[128,2048]{1,0:T(8,128)(2,1)} %get-tuple-element.165), channel_id=1, source_target_pairs={{0,1},{1,0},{2,3},{3,2},{4,5},{5,4},{6,7},{7,6},{8,9},{9,8},{10,11... | collective-permute-start | bytes 1572872 | tf_op jit(solution)/shard_map/ppermute | solution.py:443
  993.3 8.9 collective-permute-start.49
  1003.1 13.1 %maximum_convert_fusion = f32[8,2,256,1408]{3,2,1,0:T(8,128)} fusion(bf16[8,1,256,1408]{3,2,1,0:T(8,128)(2,1)} %bitcast.46, bf16[8,1,256,1408]{3,2,1,0:T(8,128)(2,1)} %bitcast.45), kind=kLoop, calls=%fused_computation.4 | loop fusion | flops 11534336 | bytes 34603008 | tf_op jit(solution)/shard_map/stack | solution.py:736
  1017.6 13.2 %collective-permute-done.44 = bf16[128,2048]{1,0:T(8,128)(2,1)S(1)} collective-permute-done((bf16[128,2048]{1,0:T(8,128)(2,1)}, bf16[128,2048]{1,0:T(8,128)(2,1)S(1)}, u32[]{:S(2)}, u32[]{:S(2)}) %collective-permute-start.44) | collective-permute-done | bytes 524320 | tf_op jit(solution)/shard_map/ppermute | solution.py:443
  1033.4 118.2 %shard_map.232 = bf16[10,256,512]{2,1,0:T(8,128)(2,1)} custom-call(bf16[8,160,2048]{2,1,0:T(8,128)(2,1)} %bitcast.139, bf16[8,160,512]{2,1,0:T(8,128)(2,1)} %bitcast.129, bf16[512,2048]{1,0:T(8,128)(2,1)} %copy-done.29, bf16[2,512,512]{2,1,0:T(8,128)(2,1)} %pad_maximum_fusion.1.grad_kv), custom_call_target="tpu_custom_call" | custom-call | flops 3355443200 | bytes 262144000 | tf_op jit(solution)/shard_map/pallas_call | solution.py:380
  1159.6 13.2 %collective-permute-start.55 = (bf16[128,2048]{1,0:T(8,128)(2,1)}, bf16[128,2048]{1,0:T(8,128)(2,1)S(1)}, u32[]{:S(2)}, u32[]{:S(2)}) collective-permute-start(bf16[128,2048]{1,0:T(8,128)(2,1)} %get-tuple-element.108), channel_id=1, source_target_pairs={{0,1},{1,0},{2,3},{3,2},{4,5},{5,4},{6,7},{7,6},{8,9},{9,8},{10,11... | collective-permute-start | bytes 1572872 | tf_op jit(solution)/shard_map/ppermute | solution.py:443
  1176.4 8.2 convert_element_type.324
  1189.6 11.7 reduce-scatter.5.cloned.1.call-done
  1201.3 30.2 %psum.7 = f32[256,18]{0,1:T(8,128)S(1)} all-reduce(f32[256,18]{0,1:T(8,128)} %reduce-scatter.5.cloned.1.call-done), channel_id=1, replica_groups=mesh['dp'=8,'tensor'=4] {'tensor'}, use_global_device_ids=true, to_apply=%region_32.33 | all-reduce | flops 4608 | bytes 36864 | tf_op jit(solution)/shard_map/psum | solution.py:723
  (467 shorter events, 286.3 us)
Async XLA Ops:
  7.2 65.8 %all-gather.6.cloned.1.call-start = ((), (), s32[]{:S(2)}) async-start(), calls=%async_computation.9 | async-start | bytes 4718592 | tf_op jit(solution)/shard_map/all_gather | solution.py:517
  20.1 178.3 %all-gather.4.cloned.1.call-start = ((), (), s32[]{:S(2)}) async-start(), calls=%async_computation.8 | async-start | bytes 18874368 | tf_op jit(solution)/shard_map/all_gather | solution.py:518
  20.9 272.6 %all-gather.8.cloned.1.call-start = ((), (), s32[]{:S(2)}) async-start(), calls=%async_computation.10 | async-start | bytes 18874368 | tf_op jit(solution)/shard_map/all_gather | solution.py:519
  28.4 297.2 %collective-permute-start.6 = (bf16[128,2048]{1,0:T(8,128)(2,1)}, bf16[128,2048]{1,0:T(8,128)(2,1)}, u32[]{:S(2)}, u32[]{:S(2)}) collective-permute-start(bf16[128,2048]{1,0:T(8,128)(2,1)} %get-tuple-element.158), channel_id=1, source_target_pairs={{0,4},{4,0},{8,12},{12,8},{16,20},{20,16},{24,28},{28,24},{1,5},{5... | collective-permute-start | bytes 1572872 | tf_op jit(solution)/shard_map/ppermute | solution.py:439
  28.8 324.0 %collective-permute-start.7 = (bf16[128,2048]{1,0:T(8,128)(2,1)}, bf16[128,2048]{1,0:T(8,128)(2,1)}, u32[]{:S(2)}, u32[]{:S(2)}) collective-permute-start(bf16[128,2048]{1,0:T(8,128)(2,1)} %get-tuple-element.157), channel_id=1, source_target_pairs={{0,8},{4,12},{8,0},{12,4},{16,24},{20,28},{24,16},{28,20},{1,9},{5... | collective-permute-start | bytes 1572872 | tf_op jit(solution)/shard_map/ppermute | solution.py:439
  38.5 366.2 %all-to-all-start = ((bf16[8,1408,256]{1,2,0:T(8,128)(2,1)}), bf16[8,1408,256]{1,2,0:T(8,128)(2,1)}, u32[]{:S(2)}, u32[]{:S(2)}) async-start(bf16[8,1408,256]{1,2,0:T(8,128)(2,1)} %copy.97), calls=%async_computation | async-start | bytes 11534336 | tf_op jit(solution)/shard_map/all_to_all | solution.py:419
  310.0 38.5 %collective-permute-start.1 = (bf16[128,2048]{1,0:T(8,128)(2,1)}, bf16[128,2048]{1,0:T(8,128)(2,1)}, u32[]{:S(2)}, u32[]{:S(2)}) collective-permute-start(bf16[128,2048]{1,0:T(8,128)(2,1)} %get-tuple-element.173), channel_id=1, source_target_pairs={{0,2},{1,3},{2,0},{3,1},{4,6},{5,7},{6,4},{7,5},{8,10},{9,11},{10,... | collective-permute-start | bytes 1572872 | tf_op jit(solution)/shard_map/ppermute | solution.py:443
  312.4 36.1 %collective-permute-start.2 = (bf16[128,2048]{1,0:T(8,128)(2,1)}, bf16[128,2048]{1,0:T(8,128)(2,1)}, u32[]{:S(2)}, u32[]{:S(2)}) collective-permute-start(bf16[128,2048]{1,0:T(8,128)(2,1)} %get-tuple-element.172), channel_id=1, source_target_pairs={{0,3},{1,2},{2,1},{3,0},{4,7},{5,6},{6,5},{7,4},{8,11},{9,10},{10,... | collective-permute-start | bytes 1572872 | tf_op jit(solution)/shard_map/ppermute | solution.py:443
  325.7 39.9 %collective-permute-start.8 = (bf16[128,2048]{1,0:T(8,128)(2,1)}, bf16[128,2048]{1,0:T(8,128)(2,1)S(1)}, u32[]{:S(2)}, u32[]{:S(2)}) collective-permute-start(bf16[128,2048]{1,0:T(8,128)(2,1)} %get-tuple-element.156), channel_id=1, source_target_pairs={{0,12},{4,8},{8,4},{12,0},{16,28},{20,24},{24,20},{28,16},{1,13},{... | collective-permute-start | bytes 1572872 | tf_op jit(solution)/shard_map/ppermute | solution.py:439
  348.5 78.8 %collective-permute-start.10 = (bf16[128,2048]{1,0:T(8,128)(2,1)}, bf16[128,2048]{1,0:T(8,128)(2,1)}, u32[]{:S(2)}, u32[]{:S(2)}) collective-permute-start(bf16[128,2048]{1,0:T(8,128)(2,1)} %get-tuple-element.154), channel_id=1, source_target_pairs={{0,20},{4,16},{8,28},{12,24},{16,4},{20,0},{24,12},{28,8},{1,21},{... | collective-permute-start | bytes 1572872 | tf_op jit(solution)/shard_map/ppermute | solution.py:439
  348.5 80.7 %collective-permute-start.11 = (bf16[128,2048]{1,0:T(8,128)(2,1)}, bf16[128,2048]{1,0:T(8,128)(2,1)}, u32[]{:S(2)}, u32[]{:S(2)}) collective-permute-start(bf16[128,2048]{1,0:T(8,128)(2,1)} %get-tuple-element.153), channel_id=1, source_target_pairs={{0,24},{4,28},{8,16},{12,20},{16,8},{20,12},{24,0},{28,4},{1,25},{... | collective-permute-start | bytes 1572872 | tf_op jit(solution)/shard_map/ppermute | solution.py:439
  365.6 38.2 %collective-permute-start.4 = (bf16[128,2048]{1,0:T(8,128)(2,1)S(1)}, bf16[128,2048]{1,0:T(8,128)(2,1)S(1)}, u32[]{:S(2)}, u32[]{:S(2)}) collective-permute-start(bf16[128,2048]{1,0:T(8,128)(2,1)S(1)} %get-tuple-element.118), channel_id=1, source_target_pairs={{0,2},{1,3},{2,0},{3,1},{4,6},{5,7},{6,4},{7,5},{8,10},{9,11},{10,... | collective-permute-start | bytes 1572872 | tf_op jit(solution)/shard_map/ppermute | solution.py:443
  367.5 36.3 %collective-permute-start.5 = (bf16[128,2048]{1,0:T(8,128)(2,1)S(1)}, bf16[128,2048]{1,0:T(8,128)(2,1)S(1)}, u32[]{:S(2)}, u32[]{:S(2)}) collective-permute-start(bf16[128,2048]{1,0:T(8,128)(2,1)S(1)} %get-tuple-element.118), channel_id=1, source_target_pairs={{0,3},{1,2},{2,1},{3,0},{4,7},{5,6},{6,5},{7,4},{8,11},{9,10},{10,... | collective-permute-start | bytes 1572872 | tf_op jit(solution)/shard_map/ppermute | solution.py:443
  383.6 49.2 %collective-permute-start.12 = (bf16[128,2048]{1,0:T(8,128)(2,1)S(1)}, bf16[128,2048]{1,0:T(8,128)(2,1)}, u32[]{:S(2)}, u32[]{:S(2)}) collective-permute-start(bf16[128,2048]{1,0:T(8,128)(2,1)S(1)} %copy-done.46), channel_id=1, source_target_pairs={{0,28},{4,24},{8,20},{12,16},{16,12},{20,8},{24,4},{28,0},{1,29},{... | collective-permute-start | bytes 1572872 | tf_op jit(solution)/shard_map/ppermute | solution.py:439
  404.7 107.8 %all-to-all-start.2 = ((bf16[8,256,1408]{2,1,0:T(8,128)(2,1)}), bf16[8,256,1408]{2,1,0:T(8,128)(2,1)}, u32[]{:S(2)}, u32[]{:S(2)}) async-start(bf16[8,256,1408]{2,1,0:T(8,128)(2,1)} %get-tuple-element.127), calls=%async_computation.2 | async-start | bytes 11534336 | tf_op jit(solution)/shard_map/all_to_all | solution.py:419
  431.0 55.8 %collective-permute-start.14 = (bf16[128,2176]{1,0:T(8,128)(2,1)S(1)}, bf16[128,2176]{1,0:T(8,128)(2,1)S(1)}, u32[]{:S(2)}, u32[]{:S(2)}) collective-permute-start(bf16[128,2176]{1,0:T(8,128)(2,1)S(1)} %get-tuple-element.133), channel_id=1, source_target_pairs={{0,8},{4,12},{8,0},{12,4},{16,24},{20,28},{24,16},{28,20},{1,9},{5... | collective-permute-start | bytes 1671176 | tf_op jit(solution)/shard_map/ppermute | solution.py:439
  434.6 63.2 %collective-permute-start.15 = (bf16[128,2176]{1,0:T(8,128)(2,1)S(1)}, bf16[128,2176]{1,0:T(8,128)(2,1)S(1)}, u32[]{:S(2)}, u32[]{:S(2)}) collective-permute-start(bf16[128,2176]{1,0:T(8,128)(2,1)S(1)} %get-tuple-element.132), channel_id=1, source_target_pairs={{0,12},{4,8},{8,4},{12,0},{16,28},{20,24},{24,20},{28,16},{1,13},{... | collective-permute-start | bytes 1671176 | tf_op jit(solution)/shard_map/ppermute | solution.py:439
  434.6 64.0 %collective-permute-start.16 = (bf16[128,2176]{1,0:T(8,128)(2,1)S(1)}, bf16[128,2176]{1,0:T(8,128)(2,1)S(1)}, u32[]{:S(2)}, u32[]{:S(2)}) collective-permute-start(bf16[128,2176]{1,0:T(8,128)(2,1)S(1)} %get-tuple-element.131), channel_id=1, source_target_pairs={{0,16},{4,20},{8,24},{12,28},{16,0},{20,4},{24,8},{28,12},{1,17},{... | collective-permute-start | bytes 1671176 | tf_op jit(solution)/shard_map/ppermute | solution.py:439
  436.3 63.2 %collective-permute-start.17 = (bf16[128,2176]{1,0:T(8,128)(2,1)S(1)}, bf16[128,2176]{1,0:T(8,128)(2,1)S(1)}, u32[]{:S(2)}, u32[]{:S(2)}) collective-permute-start(bf16[128,2176]{1,0:T(8,128)(2,1)S(1)} %get-tuple-element.130), channel_id=1, source_target_pairs={{0,20},{4,16},{8,28},{12,24},{16,4},{20,0},{24,12},{28,8},{1,21},{... | collective-permute-start | bytes 1671176 | tf_op jit(solution)/shard_map/ppermute | solution.py:439
  436.4 75.2 %collective-permute-start.18 = (bf16[128,2176]{1,0:T(8,128)(2,1)S(1)}, bf16[128,2176]{1,0:T(8,128)(2,1)S(1)}, u32[]{:S(2)}, u32[]{:S(2)}) collective-permute-start(bf16[128,2176]{1,0:T(8,128)(2,1)S(1)} %get-tuple-element.129), channel_id=1, source_target_pairs={{0,24},{4,28},{8,16},{12,20},{16,8},{20,12},{24,0},{28,4},{1,25},{... | collective-permute-start | bytes 1671176 | tf_op jit(solution)/shard_map/ppermute | solution.py:439
  486.8 35.9 %collective-permute-start.19 = (bf16[128,2176]{1,0:T(8,128)(2,1)S(1)}, bf16[128,2176]{1,0:T(8,128)(2,1)S(1)}, u32[]{:S(2)}, u32[]{:S(2)}) collective-permute-start(bf16[128,2176]{1,0:T(8,128)(2,1)S(1)} %get-tuple-element.128), channel_id=1, source_target_pairs={{0,28},{4,24},{8,20},{12,16},{16,12},{20,8},{24,4},{28,0},{1,29},{... | collective-permute-start | bytes 1671176 | tf_op jit(solution)/shard_map/ppermute | solution.py:439
  512.5 72.6 %all-to-all-start.1 = ((bf16[8,256,1408]{2,1,0:T(8,128)(2,1)}), bf16[8,256,1408]{2,1,0:T(8,128)(2,1)}, u32[]{:S(2)}, u32[]{:S(2)}) async-start(bf16[8,256,1408]{2,1,0:T(8,128)(2,1)} %get-tuple-element.126), calls=%async_computation.1 | async-start | bytes 11534336 | tf_op jit(solution)/shard_map/all_to_all | solution.py:419
  630.6 46.8 %collective-permute-start.31 = (bf16[128,2048]{1,0:T(8,128)(2,1)S(1)}, bf16[128,2048]{1,0:T(8,128)(2,1)S(1)}, u32[]{:S(2)}, u32[]{:S(2)}) collective-permute-start(bf16[128,2048]{1,0:T(8,128)(2,1)S(1)} %get-tuple-element.138), channel_id=1, source_target_pairs={{0,20},{4,16},{8,28},{12,24},{16,4},{20,0},{24,12},{28,8},{1,21},{... | collective-permute-start | bytes 1572872 | tf_op jit(solution)/shard_map/ppermute | solution.py:439
  653.3 46.1 %collective-permute-start.20 = (bf16[128,2048]{1,0:T(8,128)(2,1)S(1)}, bf16[128,2048]{1,0:T(8,128)(2,1)S(1)}, u32[]{:S(2)}, u32[]{:S(2)}) collective-permute-start(bf16[128,2048]{1,0:T(8,128)(2,1)S(1)} %get-tuple-element.150), channel_id=1, source_target_pairs={{0,4},{4,0},{8,12},{12,8},{16,20},{20,16},{24,28},{28,24},{1,5},{5... | collective-permute-start | bytes 1572872 | tf_op jit(solution)/shard_map/ppermute | solution.py:439
  654.4 46.9 %collective-permute-start.21 = (bf16[128,2048]{1,0:T(8,128)(2,1)S(1)}, bf16[128,2048]{1,0:T(8,128)(2,1)S(1)}, u32[]{:S(2)}, u32[]{:S(2)}) collective-permute-start(bf16[128,2048]{1,0:T(8,128)(2,1)S(1)} %get-tuple-element.149), channel_id=1, source_target_pairs={{0,8},{4,12},{8,0},{12,4},{16,24},{20,28},{24,16},{28,20},{1,9},{5... | collective-permute-start | bytes 1572872 | tf_op jit(solution)/shard_map/ppermute | solution.py:439
  728.3 71.6 %all-to-all-start.3 = ((bf16[8,256,1408]{2,1,0:T(8,128)(2,1)}), bf16[8,256,1408]{2,1,0:T(8,128)(2,1)}, u32[]{:S(2)}, u32[]{:S(2)}) async-start(bf16[8,256,1408]{2,1,0:T(8,128)(2,1)} %bitcast.136), calls=%async_computation.3 | async-start | bytes 11534336 | tf_op jit(solution)/shard_map/all_to_all | solution.py:419
  733.1 421.1 %reduce-scatter.3.cloned.1.call-start = ((), (), s32[]{:S(2)}) async-start(), calls=%async_computation.11 | async-start | bytes 18874368 | tf_op jit(solution)/shard_map/reduce_scatter | solution.py:684
  758.6 38.2 %collective-permute-start.35 = (bf16[128,2048]{1,0:T(8,128)(2,1)S(1)}, bf16[128,2048]{1,0:T(8,128)(2,1)S(1)}, u32[]{:S(2)}, u32[]{:S(2)}) collective-permute-start(bf16[128,2048]{1,0:T(8,128)(2,1)S(1)} %get-tuple-element.170), channel_id=1, source_target_pairs={{0,2},{1,3},{2,0},{3,1},{4,6},{5,7},{6,4},{7,5},{8,10},{9,11},{10,... | collective-permute-start | bytes 1572872 | tf_op jit(solution)/shard_map/ppermute | solution.py:443
  760.5 36.3 %collective-permute-start.36 = (bf16[128,2048]{1,0:T(8,128)(2,1)S(1)}, bf16[128,2048]{1,0:T(8,128)(2,1)S(1)}, u32[]{:S(2)}, u32[]{:S(2)}) collective-permute-start(bf16[128,2048]{1,0:T(8,128)(2,1)S(1)} %get-tuple-element.169), channel_id=1, source_target_pairs={{0,3},{1,2},{2,1},{3,0},{4,7},{5,6},{6,5},{7,4},{8,11},{9,10},{10,... | collective-permute-start | bytes 1572872 | tf_op jit(solution)/shard_map/ppermute | solution.py:443
  810.3 38.2 %collective-permute-start.41 = (bf16[128,2048]{1,0:T(8,128)(2,1)S(1)}, bf16[128,2048]{1,0:T(8,128)(2,1)S(1)}, u32[]{:S(2)}, u32[]{:S(2)}) collective-permute-start(bf16[128,2048]{1,0:T(8,128)(2,1)S(1)} %get-tuple-element.114), channel_id=1, source_target_pairs={{0,2},{1,3},{2,0},{3,1},{4,6},{5,7},{6,4},{7,5},{8,10},{9,11},{10,... | collective-permute-start | bytes 1572872 | tf_op jit(solution)/shard_map/ppermute | solution.py:443
  811.4 37.3 %collective-permute-start.42 = (bf16[128,2048]{1,0:T(8,128)(2,1)S(1)}, bf16[128,2048]{1,0:T(8,128)(2,1)S(1)}, u32[]{:S(2)}, u32[]{:S(2)}) collective-permute-start(bf16[128,2048]{1,0:T(8,128)(2,1)S(1)} %get-tuple-element.114), channel_id=1, source_target_pairs={{0,3},{1,2},{2,1},{3,0},{4,7},{5,6},{6,5},{7,4},{8,11},{9,10},{10,... | collective-permute-start | bytes 1572872 | tf_op jit(solution)/shard_map/ppermute | solution.py:443
  865.5 97.1 %all-to-all-start.5 = ((bf16[8,256,1408]{2,1,0:T(8,128)(2,1)}), bf16[8,256,1408]{2,1,0:T(8,128)(2,1)}, u32[]{:S(2)}, u32[]{:S(2)}) async-start(bf16[8,256,1408]{2,1,0:T(8,128)(2,1)} %bitcast.135), calls=%async_computation.5 | async-start | bytes 11534336 | tf_op jit(solution)/shard_map/all_to_all | solution.py:419
  875.2 111.2 %collective-permute-start.46 = (bf16[128,2048]{1,0:T(8,128)(2,1)}, bf16[128,2048]{1,0:T(8,128)(2,1)}, u32[]{:S(2)}, u32[]{:S(2)}) collective-permute-start(bf16[128,2048]{1,0:T(8,128)(2,1)} %get-tuple-element.162), channel_id=1, source_target_pairs={{0,1},{1,0},{2,3},{3,2},{4,5},{5,4},{6,7},{7,6},{8,9},{9,8},{10,11... | collective-permute-start | bytes 1572872 | tf_op jit(solution)/shard_map/ppermute | solution.py:443
  885.0 103.8 %collective-permute-start.47 = (bf16[128,2048]{1,0:T(8,128)(2,1)}, bf16[128,2048]{1,0:T(8,128)(2,1)}, u32[]{:S(2)}, u32[]{:S(2)}) collective-permute-start(bf16[128,2048]{1,0:T(8,128)(2,1)} %get-tuple-element.164), channel_id=1, source_target_pairs={{0,2},{1,3},{2,0},{3,1},{4,6},{5,7},{6,4},{7,5},{8,10},{9,11},{10,... | collective-permute-start | bytes 1572872 | tf_op jit(solution)/shard_map/ppermute | solution.py:443
  901.6 65.9 %collective-permute-start.52 = (f32[128,2]{0,1:T(2,128)S(1)}, f32[128,2]{0,1:T(2,128)S(1)}, u32[]{:S(2)}, u32[]{:S(2)}) collective-permute-start(f32[128,2]{0,1:T(2,128)S(1)} %get-tuple-element.183), channel_id=1, source_target_pairs={{0,1},{1,0},{2,3},{3,2},{4,5},{5,4},{6,7},{7,6},{8,9},{9,8},{10,11... | collective-permute-start | bytes 3080 | tf_op jit(solution)/shard_map/ppermute | solution.py:443
  903.4 65.5 %collective-permute-start.53 = (f32[128,2]{0,1:T(2,128)S(1)}, f32[128,2]{0,1:T(2,128)S(1)}, u32[]{:S(2)}, u32[]{:S(2)}) collective-permute-start(f32[128,2]{0,1:T(2,128)S(1)} %get-tuple-element.184), channel_id=1, source_target_pairs={{0,2},{1,3},{2,0},{3,1},{4,6},{5,7},{6,4},{7,5},{8,10},{9,11},{10,... | collective-permute-start | bytes 3080 | tf_op jit(solution)/shard_map/ppermute | solution.py:443
  903.5 80.9 %collective-permute-start.54 = (f32[128,2]{0,1:T(2,128)S(1)}, f32[128,2]{0,1:T(2,128)S(1)}, u32[]{:S(2)}, u32[]{:S(2)}) collective-permute-start(f32[128,2]{0,1:T(2,128)S(1)} %get-tuple-element.185), channel_id=1, source_target_pairs={{0,3},{1,2},{2,1},{3,0},{4,7},{5,6},{6,5},{7,4},{8,11},{9,10},{10,... | collective-permute-start | bytes 3080 | tf_op jit(solution)/shard_map/ppermute | solution.py:443
  962.6 191.6 %all-to-all-start.4 = ((bf16[8,1408,256]{2,1,0:T(8,128)(2,1)}), bf16[8,1408,256]{2,1,0:T(8,128)(2,1)}, u32[]{:S(2)}, u32[]{:S(2)}) async-start(bf16[8,1408,256]{2,1,0:T(8,128)(2,1)} %bitcast.132), calls=%async_computation.4 | async-start | bytes 11534336 | tf_op jit(solution)/shard_map/all_to_all | solution.py:419
  967.4 233.8 %reduce-scatter.5.cloned.1.call-start = ((), (), s32[]{:S(2)}) async-start(), calls=%async_computation.12 | async-start | bytes 221184 | tf_op jit(solution)/shard_map/reduce_scatter | solution.py:724
  968.9 47.3 %collective-permute-start.43 = (bf16[128,2048]{1,0:T(8,128)(2,1)}, bf16[128,2048]{1,0:T(8,128)(2,1)S(1)}, u32[]{:S(2)}, u32[]{:S(2)}) collective-permute-start(bf16[128,2048]{1,0:T(8,128)(2,1)} %get-tuple-element.165), channel_id=1, source_target_pairs={{0,1},{1,0},{2,3},{3,2},{4,5},{5,4},{6,7},{7,6},{8,9},{9,8},{10,11... | collective-permute-start | bytes 1572872 | tf_op jit(solution)/shard_map/ppermute | solution.py:443
  984.4 46.4 %collective-permute-start.44 = (bf16[128,2048]{1,0:T(8,128)(2,1)}, bf16[128,2048]{1,0:T(8,128)(2,1)S(1)}, u32[]{:S(2)}, u32[]{:S(2)}) collective-permute-start(bf16[128,2048]{1,0:T(8,128)(2,1)} %get-tuple-element.167), channel_id=1, source_target_pairs={{0,2},{1,3},{2,0},{3,1},{4,6},{5,7},{6,4},{7,5},{8,10},{9,11},{10,... | collective-permute-start | bytes 1572872 | tf_op jit(solution)/shard_map/ppermute | solution.py:443
  986.4 44.5 %collective-permute-start.45 = (bf16[128,2048]{1,0:T(8,128)(2,1)}, bf16[128,2048]{1,0:T(8,128)(2,1)S(1)}, u32[]{:S(2)}, u32[]{:S(2)}) collective-permute-start(bf16[128,2048]{1,0:T(8,128)(2,1)} %get-tuple-element.166), channel_id=1, source_target_pairs={{0,3},{1,2},{2,1},{3,0},{4,7},{5,6},{6,5},{7,4},{8,11},{9,10},{10,... | collective-permute-start | bytes 1572872 | tf_op jit(solution)/shard_map/ppermute | solution.py:443
  993.3 158.4 %collective-permute-start.49 = (bf16[128,2048]{1,0:T(8,128)(2,1)}, bf16[128,2048]{1,0:T(8,128)(2,1)S(1)}, u32[]{:S(2)}, u32[]{:S(2)}) collective-permute-start(bf16[128,2048]{1,0:T(8,128)(2,1)} %get-tuple-element.112), channel_id=1, source_target_pairs={{0,1},{1,0},{2,3},{3,2},{4,5},{5,4},{6,7},{7,6},{8,9},{9,8},{10,11... | collective-permute-start | bytes 1572872 | tf_op jit(solution)/shard_map/ppermute | solution.py:443
  1002.1 150.4 %collective-permute-start.50 = (bf16[128,2048]{1,0:T(8,128)(2,1)}, bf16[128,2048]{1,0:T(8,128)(2,1)S(1)}, u32[]{:S(2)}, u32[]{:S(2)}) collective-permute-start(bf16[128,2048]{1,0:T(8,128)(2,1)} %get-tuple-element.112), channel_id=1, source_target_pairs={{0,2},{1,3},{2,0},{3,1},{4,6},{5,7},{6,4},{7,5},{8,10},{9,11},{10,... | collective-permute-start | bytes 1572872 | tf_op jit(solution)/shard_map/ppermute | solution.py:443
  1016.3 137.1 %collective-permute-start.51 = (bf16[128,2048]{1,0:T(8,128)(2,1)}, bf16[128,2048]{1,0:T(8,128)(2,1)S(1)}, u32[]{:S(2)}, u32[]{:S(2)}) collective-permute-start(bf16[128,2048]{1,0:T(8,128)(2,1)} %get-tuple-element.112), channel_id=1, source_target_pairs={{0,3},{1,2},{2,1},{3,0},{4,7},{5,6},{6,5},{7,4},{8,11},{9,10},{10,... | collective-permute-start | bytes 1572872 | tf_op jit(solution)/shard_map/ppermute | solution.py:443
  1159.6 73.1 %collective-permute-start.55 = (bf16[128,2048]{1,0:T(8,128)(2,1)}, bf16[128,2048]{1,0:T(8,128)(2,1)S(1)}, u32[]{:S(2)}, u32[]{:S(2)}) collective-permute-start(bf16[128,2048]{1,0:T(8,128)(2,1)} %get-tuple-element.108), channel_id=1, source_target_pairs={{0,1},{1,0},{2,3},{3,2},{4,5},{5,4},{6,7},{7,6},{8,9},{9,8},{10,11... | collective-permute-start | bytes 1572872 | tf_op jit(solution)/shard_map/ppermute | solution.py:443
  1173.9 58.9 %collective-permute-start.56 = (bf16[128,2048]{1,0:T(8,128)(2,1)}, bf16[128,2048]{1,0:T(8,128)(2,1)}, u32[]{:S(2)}, u32[]{:S(2)}) collective-permute-start(bf16[128,2048]{1,0:T(8,128)(2,1)} %get-tuple-element.108), channel_id=1, source_target_pairs={{0,2},{1,3},{2,0},{3,1},{4,6},{5,7},{6,4},{7,5},{8,10},{9,11},{10,... | collective-permute-start | bytes 1572872 | tf_op jit(solution)/shard_map/ppermute | solution.py:443
  1175.0 58.8 %collective-permute-start.57 = (bf16[128,2048]{1,0:T(8,128)(2,1)}, bf16[128,2048]{1,0:T(8,128)(2,1)S(1)}, u32[]{:S(2)}, u32[]{:S(2)}) collective-permute-start(bf16[128,2048]{1,0:T(8,128)(2,1)} %get-tuple-element.108), channel_id=1, source_target_pairs={{0,3},{1,2},{2,1},{3,0},{4,7},{5,6},{6,5},{7,4},{8,11},{9,10},{10,... | collective-permute-start | bytes 1572872 | tf_op jit(solution)/shard_map/ppermute | solution.py:443
  (103 other events, 2816.0 us)
Sparse Core Ops, SparseCore 0:
  20.2 52.7 all-gather.5
  74.9 123.4 all-gather.3
  200.3 93.1 all-gather.7
  864.1 208.7 reduce-scatter.2
  1156.9 44.3 reduce-scatter.4

commit v3 on v2

--- a/solution.py
+++ b/solution.py
@@ -82,12 +82,28 @@
     return (grad_in, jnp.sum(grad_normed * normal, axis=0))
 
 
-def router_backward(gates, grad_gates, picks, experts):
-    grad_select = gates * (grad_gates - jnp.sum(gates * grad_gates, axis=1, keepdims=True))
+def router_backward(gates, products, picks, experts):
+    grad_select = products - gates * jnp.sum(products, axis=1, keepdims=True)
     picked_hot = (picks[:, :, None] == jnp.arange(experts, dtype=jnp.int32)[None, None, :]).astype(
         F32
     )
     return jnp.sum(picked_hot * grad_select[:, :, None], axis=1).astype(BF16)
+
+
+def with_column(rows, column):
+    high = column.astype(BF16)
+    rest = column - high.astype(F32)
+    mid = rest.astype(BF16)
+    low = (rest - mid.astype(F32)).astype(BF16)
+    return jnp.concatenate(
+        [rows, high, mid, low, jnp.zeros((rows.shape[0], HD - 3), BF16)], axis=1
+    )
+
+
+def without_column(both):
+    width = both.shape[1] - HD
+    parts = both[:, width : width + 3].astype(F32)
+    return both[:, :width], parts[:, :1] + parts[:, 1:2] + parts[:, 2:]
 
 
 def picked_softmax(logits, picks):
@@ -265,24 +281,434 @@
     )
 
 
-def map_grads_kernel(
-    routed, grad_q, normed, grad_kv, out,
-    give, keep, twin_in, far_in, near_in,
-    twin_send, twin_recv, far_send, far_recv, near_send, near_recv,
+def greet(places):
+    barrier = pltpu.get_barrier_semaphore()
+    for place in places:
+        pl.semaphore_signal(
+            barrier, inc=1, device_id=place, device_id_type=pl.DeviceIdType.MESH
+        )
+    pl.semaphore_wait(barrier, len(places))
+
+
+def send_across(source, target, send_sem, recv_sem, device):
+    return pltpu.make_async_remote_copy(
+        src_ref=source,
+        dst_ref=target,
+        send_sem=send_sem,
+        recv_sem=recv_sem,
+        device_id={"tensor": device},
+        device_id_type=pl.DeviceIdType.MESH,
+    )
+
+
+def tensor_peers(count):
+    z = lax.axis_index("tensor")
+    return [lax.rem(z + k, count) for k in range(1, count)]
+
+
+def share_rows(size):
+    return pl.ds(pl.multiple_of(lax.axis_index("tensor") * size, size), size)
+
+
+def rows_of(place, size):
+    return pl.ds(pl.multiple_of(place * size, size), size)
+
+
+def spread(count, source, target, sems):
+    size = source.shape[0] // count
+    copies = [
+        send_to(
+            source.at[pl.ds(k * size, size)], target.at[pl.ds(k * size, size)],
+            sems[0].at[k], sems[1].at[k], partner(k),
+        )
+        for k in range(1, count)
+    ]
+    here = pltpu.make_async_copy(
+        source.at[pl.ds(0, size)], target.at[pl.ds(0, size)], sems[0].at[0]
+    )
+    for copy in (*copies, here):
+        copy.start()
+    return (*copies, here)
+
+
+def gather_kernel(axes, chunks, *refs):
+    amount = len(axes)
+    sources, targets = refs[:amount], refs[amount : 2 * amount]
+    send_sem, recv_sem, own_sem = refs[2 * amount :]
+    at = Square()
+    me = 2 * at.chip + at.core
+    far = 2 * at.chip_far + at.core
+    greet([{"dp": p} for p in (at.twin, at.near_x, at.near_y)])
+
+    def region(ref, axis, source, place, experts):
+        size = source.shape[axis]
+        at_place = pl.ds(pl.multiple_of(place * size, size), size)
+        return ref.at[experts, at_place] if axis == 1 else ref.at[experts, :, at_place]
+
+    first = 0
+    plans = []
+    for i in range(amount):
+        count = sources[i].shape[0] // chunks[i]
+        plans.append((i, first, count))
+        first += count
+
+    def copies(i, first, n):
+        source, target, axis, size = sources[i], targets[i], axes[i], chunks[i]
+        half = size // 2
+        whole = pl.ds(n * size, size)
+        top, bottom = pl.ds(n * size, half), pl.ds(n * size + half, half)
+        unit = first + n
+
+        def move(slot, place, experts, device, own=False):
+            there = region(target, axis, source, place, experts)
+            return send_to(
+                source.at[experts] if own else there, there,
+                send_sem.at[unit, slot], recv_sem.at[unit, slot], device,
+            )
+
+        return [
+            functools.partial(move, 0, me, whole, at.near_x, True),
+            functools.partial(move, 1, me, whole, at.near_y, True),
+            functools.partial(move, 2, at.near_y, top, at.near_x),
+            functools.partial(move, 3, at.near_x, bottom, at.near_y),
+            functools.partial(move, 4, me, whole, at.twin, True),
+            functools.partial(move, 5, at.near_x, whole, at.twin),
+            functools.partial(move, 6, at.near_y, whole, at.twin),
+            functools.partial(move, 7, far, top, at.twin),
+            functools.partial(move, 8, far, bottom, at.twin),
+        ]
+
+    here = [
+        pltpu.make_async_copy(
+            sources[i], region(targets[i], axes[i], sources[i], me, pl.ds(0, sources[i].shape[0])),
+            own_sem.at[i],
+        )
+        for i in range(amount)
+    ]
+    for i, first, count in plans:
+
+        @pl.loop(0, count)
+        def _(n):
+            moves = copies(i, first, n)
+            for slot in (0, 1, 4):
+                moves[slot]().start()
+
+    for copy in here:
+        copy.start()
+    for i, first, count in plans:
+
+        @pl.loop(0, count)
+        def _(n):
+            moves = copies(i, first, n)
+            moves[0]().wait_recv()
+            moves[3]().start()
+            moves[5]().start()
+            moves[1]().wait_recv()
+            moves[2]().start()
+            moves[6]().start()
+
+    for i, first, count in plans:
+
+        @pl.loop(0, count)
+        def _(n):
+            moves = copies(i, first, n)
+            moves[2]().wait_recv()
+            moves[7]().start()
+            moves[3]().wait_recv()
+            moves[8]().start()
+
+    for i, first, count in plans:
+
+        @pl.loop(0, count)
+        def _(n):
+            moves = copies(i, first, n)
+            for slot in (4, 5, 6, 7, 8):
+                moves[slot]().wait_recv()
+            for move in moves:
+                move().wait_send()
+
+    for copy in here:
+        copy.wait()
+
+
+def gather_maps(arrays, axes, chunks):
+    units = sum(a.shape[0] // c for a, c in zip(arrays, chunks))
+    shapes = [
+        tuple(n * 8 if d == axis else n for d, n in enumerate(a.shape))
+        for a, axis in zip(arrays, axes)
+    ]
+    return pl.pallas_call(
+        functools.partial(gather_kernel, axes, chunks),
+        in_specs=[HBM] * len(arrays),
+        out_specs=[HBM] * len(arrays),
+        out_shape=[jax.ShapeDtypeStruct(shape, BF16) for shape in shapes],
+        scratch_shapes=[sems(units, 9), sems(units, 9), sems(len(arrays))],
+        compiler_params=pltpu.CompilerParams(collective_id=5, has_side_effects=True),
+        cost_estimate=pl.CostEstimate(flops=0, bytes_accessed=600 << 20, transcendentals=0),
+    )(*arrays)
+
+
+def deal(source, target, sems):
+    me = lax.axis_index("dp")
+    copies = [
+        send_to(
+            source.at[partner(k)], target.at[me], sems[0].at[k], sems[1].at[k], partner(k)
+        )
+        for k in range(1, source.shape[0])
+    ]
+    copies.append(pltpu.make_async_copy(source.at[me], target.at[me], sems[0].at[0]))
+    for copy in copies:
+        copy.start()
+    return copies
+
+
+def norm_back(total, products, hots, router, base, gain, hot_out, gain_out):
+    first, second = products
+    weights = hots[0] * first + hots[1] * second - hots[2] * (first + second)
+    hot_out[...] = weights.astype(BF16)
+    total = total + dot_nt(hot_out[...], router[...])
+    scale = lax.rsqrt(jnp.mean(base * base, axis=-1, keepdims=True) + EPSILON)
+    normal = base * scale
+    gain_out[...] = jnp.sum(total * normal, axis=0, keepdims=True)
+    weighted = total * gain
+    return scale * (weighted - normal * jnp.mean(weighted * normal, axis=-1, keepdims=True))
+
+
+def three_columns(block):
+    return block[:, 0:1] + block[:, 1:2] + block[:, 2:3]
+
+
+def hidden_kernel(
+    pick, rows, x_here, gain, cot_hbm,
+    hidden_out, mlp_in_out, cot_out,
+    parts, sent, got, z_send, z_recv, g_send, g_recv, e_send, e_recv,
+):
+    count = z_send.shape[0] + 1
+    width = rows.shape[1]
+    tokens = pick.shape[1]
+    size = tokens // count
+    peers = tensor_peers(count)
+    exchange_count = e_send.shape[0]
+    greet(
+        [{"dp": partner(k)} for k in range(1, exchange_count)] + [{"tensor": p} for p in peers]
+    )
+    moves = spread(exchange_count, cot_hbm, cot_out, (e_send, e_recv))
+
+    @pl.loop(0, width // 512)
+    def _(i):
+        at = pl.ds(pl.multiple_of(i * 512, 512), 512)
+        piece = dot_tn(pick[...], rows[:, at])
+        parts[:, at] = piece
+        sent[:, at] = piece.astype(BF16)
+
+    copies = [
+        send_across(sent.at[rows_of(p, size)], got.at[k], z_send.at[k], z_recv.at[k], p)
+        for k, p in enumerate(peers)
+    ]
+    for copy in copies:
+        copy.start()
+    here = share_rows(size)
+    hidden_out[...] = x_here[...].astype(F32) + parts[here, :]
+    for k, copy in enumerate(copies):
+        copy.wait_recv()
+        hidden_out[...] += got[k].astype(F32)
+    hidden = hidden_out[...]
+    scale = lax.rsqrt(jnp.mean(hidden * hidden, axis=-1, keepdims=True) + EPSILON)
+    mlp_in_out[here, :] = (hidden * scale * gain[...]).astype(BF16)
+    more = [
+        send_across(
+            mlp_in_out.at[here], mlp_in_out.at[here], g_send.at[k], g_recv.at[k], p
+        )
+        for k, p in enumerate(peers)
+    ]
+    for copy in more:
+        copy.start()
+    for copy in copies:
+        copy.wait_send()
+    for copy in more:
+        copy.wait()
+    for copy in moves:
+        copy.wait()
+
+
+VMEM = pl.BlockSpec(memory_space=pltpu.VMEM)
+HBM = pl.BlockSpec(memory_space=pl.ANY)
+
+
+def sems(*shape):
+    return pltpu.SemaphoreType.DMA(shape)
+
+
+def hidden_step(tensor_size, peers, pick, rows, x_here, gain, cot_send):
+    tokens, width = pick.shape[1], rows.shape[1]
+    size = tokens // tensor_size
+    around = tensor_size - 1
+    return pl.pallas_call(
+        hidden_kernel,
+        in_specs=[VMEM, VMEM, VMEM, VMEM, HBM],
+        out_specs=[VMEM, VMEM, HBM],
+        out_shape=[
+            jax.ShapeDtypeStruct((size, width), F32),
+            jax.ShapeDtypeStruct((tokens, width), BF16),
+            jax.ShapeDtypeStruct(cot_send.shape, BF16),
+        ],
+        scratch_shapes=[
+            pltpu.VMEM((tokens, width), F32),
+            pltpu.VMEM((tokens, width), BF16),
+            pltpu.VMEM((around, size, width), BF16),
+            sems(around), sems(around), sems(around), sems(around), sems(peers), sems(peers),
+        ],
+        compiler_params=pltpu.CompilerParams(
+            collective_id=3, has_side_effects=True, vmem_limit_bytes=40 << 20
+        ),
+        cost_estimate=pl.CostEstimate(
+            flops=2 * pick.shape[0] * tokens * width, bytes_accessed=300 << 20, transcendentals=0
+        ),
+    )(pick, rows, x_here, gain, cot_send)
+
+
+def back_kernel(
+    back, pick, hit_0, hit_1, hidden, cot_here, gain, router, hots, rows_hbm, maps_hbm,
+    grad_out, pair_out, gain_out, hot_out, rows_out, maps_out,
+    parts, sent, got, z_send, z_recv, g_send, g_recv, e_send, e_recv, w_send, w_recv,
+):
+    count = z_send.shape[0] + 1
+    width = back.shape[1] - HD
+    tokens = pick.shape[1]
+    size = tokens // count
+    peers = tensor_peers(count)
+    exchange_count = e_send.shape[0]
+    greet(
+        [{"dp": partner(k)} for k in range(1, exchange_count)] + [{"tensor": p} for p in peers]
+    )
+
+    @pl.loop(0, width // 512)
+    def _(i):
+        at = pl.ds(pl.multiple_of(i * 512, 512), 512)
+        piece = dot_tn(pick[...], back[:, at])
+        parts[:, at] = piece
+        sent[:, at] = piece.astype(BF16)
+
+    for k, hit in enumerate((hit_0, hit_1)):
+        at = pl.ds(width + k * HD, HD)
+        piece = dot_tn(hit[...], back[:, width:])
+        parts[:, at] = piece
+        sent[:, at] = piece.astype(BF16)
+
+    copies = [
+        send_across(sent.at[rows_of(p, size)], got.at[k], z_send.at[k], z_recv.at[k], p)
+        for k, p in enumerate(peers)
+    ]
+    for copy in copies:
+        copy.start()
+    moves = spread(exchange_count, rows_hbm, rows_out, (e_send, e_recv))
+    dealt = deal(maps_hbm, maps_out, (w_send, w_recv))
+    here = share_rows(size)
+    total = parts[here, :]
+    for k, copy in enumerate(copies):
+        copy.wait_recv()
+        total = total + got[k].astype(F32)
+    products = (
+        three_columns(total[:, width : width + HD]), three_columns(total[:, width + HD :])
+    )
+    grad_out[...] = cot_here[...].astype(F32) + norm_back(
+        total[:, :width], products, hots, router, hidden[...], gain[...], hot_out, gain_out
+    )
+    pair_out[here, :] = grad_out[...].astype(BF16)
+    more = [
+        send_across(pair_out.at[here], pair_out.at[here], g_send.at[k], g_recv.at[k], p)
+        for k, p in enumerate(peers)
+    ]
+    for copy in more:
+        copy.start()
+    for copy in copies:
+        copy.wait_send()
+    for copy in more:
+        copy.wait()
+    for copy in (*moves, *dealt):
+        copy.wait()
+
+
+def back_step(
+    tensor_size, peers, back, pick, hits, hidden, cot_here, gain, router, hots, rows_send,
+    maps,
+):
+    tokens, width = pick.shape[1], back.shape[1] - HD
+    size = tokens // tensor_size
+    around = tensor_size - 1
+    wide = width + 2 * HD
+    return pl.pallas_call(
+        back_kernel,
+        in_specs=[VMEM] * 9 + [HBM] * 2,
+        out_specs=[VMEM] * 4 + [HBM] * 2,
+        out_shape=[
+            jax.ShapeDtypeStruct((size, width), F32),
+            jax.ShapeDtypeStruct((tokens, width), BF16),
+            jax.ShapeDtypeStruct((1, width), F32),
+            jax.ShapeDtypeStruct((size, HD), BF16),
+            jax.ShapeDtypeStruct(rows_send.shape, BF16),
+            jax.ShapeDtypeStruct(maps.shape, BF16),
+        ],
+        scratch_shapes=[
+            pltpu.VMEM((tokens, wide), F32),
+            pltpu.VMEM((tokens, wide), BF16),
+            pltpu.VMEM((around, size, wide), BF16),
+            sems(around), sems(around), sems(around), sems(around), sems(peers), sems(peers),
+            sems(peers), sems(peers),
+        ],
+        compiler_params=pltpu.CompilerParams(
+            collective_id=4, has_side_effects=True, vmem_limit_bytes=40 << 20
+        ),
+        cost_estimate=pl.CostEstimate(
+            flops=2 * pick.shape[0] * tokens * width, bytes_accessed=300 << 20, transcendentals=0
+        ),
+    )(back, pick, hits[0], hits[1], hidden, cot_here, gain, router, hots, rows_send, maps)
+
+
+GIVE = 4
+HALF_SMALL = 8
+
+
+def final_kernel(
+    routed_hbm, grad_q, normed, grad_kv, part_hbm, maps_hbm,
+    grad_hidden, x_here, gain, router, hots, small,
+    out, maps_out, tokens_out, small_out,
+    give, keep, twin_in, far_in, near_in, routed, got_part, tokens_here,
+    twin_send, twin_recv, far_send, far_recv, near_send, near_recv, load, own,
+    p_send, p_recv, t_send, t_recv,
+    hot_here, small_all, small_in, small_sum, small_got,
+    s_send, s_recv, w_send, w_recv, d_send, d_recv,
 ):
     at = Square()
-    experts = routed.shape[0]
+    experts = grad_q.shape[0]
     units, _, size, _ = keep.shape
     half = size // 2
-    barrier = pltpu.get_barrier_semaphore()
-    for device in (at.twin, at.near_x, at.near_y):
-        pl.semaphore_signal(
-            barrier, inc=1, device_id={"dp": device}, device_id_type=pl.DeviceIdType.MESH
-        )
-    pl.semaphore_wait(barrier, 3)
+    count = p_send.shape[0] + 1
+    peers = tensor_peers(count)
+    width = normed.shape[1]
+    share = part_hbm.shape[0] // count
+
+    def fetch(u):
+        return pltpu.make_async_copy(
+            routed_hbm.at[u], routed.at[lax.rem(u, 2)], load.at[lax.rem(u, 2)]
+        )
+
+    fetch(0).start()
+    here = share_rows(share)
+    mine = pltpu.make_async_copy(part_hbm.at[here], got_part.at[count - 1], own.at[0])
+    mine.start()
+    greet([{"dp": partner(k)} for k in range(1, 8)] + [{"tensor": p} for p in peers])
+    part_copies = [
+        send_across(part_hbm.at[rows_of(p, share)], got_part.at[k], p_send.at[k], p_recv.at[k], p)
+        for k, p in enumerate(peers)
+    ]
+    for copy in part_copies:
+        copy.start()
+    dealt = deal(maps_hbm, maps_out, (d_send, d_recv))
 
     def to_twin(u):
-        return send_to(give.at[u], twin_in.at[u], twin_send.at[u], twin_recv.at[u], at.twin)
+        slot = lax.rem(u, GIVE)
+        return send_to(give.at[slot], twin_in.at[u], twin_send.at[slot], twin_recv.at[u], at.twin)
 
     def to_far(u):
         first = send_to(
@@ -307,12 +733,19 @@
         return first, second
 
     def multiply(u, rows, grads):
-        for target, core in ((give, 1 - at.core), (keep, at.core)):
-            for chip in range(4):
-                columns = pl.ds(pl.multiple_of((2 * chip + core) * size, size), size)
-                target[u, chip] = dot_tn(rows[:, columns], grads[...]).astype(BF16)
-            if target is give:
-                to_twin(u).start()
+        slot = lax.rem(u, GIVE)
+
+        @pl.when(u >= GIVE)
+        def _():
+            to_twin(u - GIVE).wait_send()
+
+        for chip in range(4):
+            columns = rows_of(2 * chip + 1 - at.core, size)
+            give[slot, chip] = dot_tn(rows[:, columns], grads[...]).astype(BF16)
+        to_twin(u).start()
+        for chip in range(4):
+            columns = rows_of(2 * chip + at.core, size)
+            keep[u, chip] = dot_tn(rows[:, columns], grads[...]).astype(BF16)
 
     def join_twin(u):
         to_twin(u).wait_recv()
@@ -329,7 +762,13 @@
 
     @pl.loop(0, experts)
     def _(u):
-        multiply(u, routed.at[u], grad_q.at[u])
+        fetch(u).wait()
+
+        @pl.when(u < experts - 1)
+        def _():
+            fetch(u + 1).start()
+
+        multiply(u, routed.at[lax.rem(u, 2)], grad_q.at[u])
 
         @pl.when(u > 0)
         def _():
@@ -341,6 +780,46 @@
         join_twin(u - 1)
 
     join_twin(units - 1)
+
+    mine.wait()
+    total = got_part[count - 1].astype(F32)
+    for k, copy in enumerate(part_copies):
+        copy.wait_recv()
+        total = total + got_part[k].astype(F32)
+    products = (
+        three_columns(total[:, width : width + HD]), three_columns(total[:, width + HD :])
+    )
+    tokens_here[...] = (
+        grad_hidden[...]
+        + norm_back(
+            total[:, :width], products, hots, router, x_here[...].astype(F32), gain[...],
+            hot_here, small_all.at[pl.ds(0, 1)],
+        )
+    ).astype(BF16)
+    token_copies = [
+        send_across(tokens_here, tokens_out.at[here], t_send.at[k], t_recv.at[k], p)
+        for k, p in enumerate(peers)
+    ]
+    for copy in token_copies:
+        copy.start()
+    kept = pltpu.make_async_copy(tokens_here, tokens_out.at[here], own.at[1])
+    kept.start()
+
+    small_all[1:HALF_SMALL, :] = small[1:HALF_SMALL, :]
+    small_all[HALF_SMALL : 2 * HALF_SMALL, :] = dot_tn(hot_here[...], normed[here, :])[:HALF_SMALL]
+    small_all[2 * HALF_SMALL :, :] = small[HALF_SMALL:, :]
+
+    def small_block(place):
+        return small_all.at[:, rows_of(place, size)]
+
+    small_copies = [
+        send_to(
+            small_block(partner(k)), small_in.at[k], s_send.at[k], s_recv.at[k], partner(k)
+        )
+        for k in range(1, 8)
+    ]
+    for copy in small_copies:
+        copy.start()
 
     @pl.loop(0, units)
     def _(u):
@@ -364,46 +843,332 @@
             keep[u, at.chip].astype(F32) + near_in[u, 0].astype(F32) + near_in[u, 1].astype(F32)
         ).astype(BF16)
 
+    block = small_all[:, rows_of(2 * at.chip + at.core, size)]
+    for k, copy in enumerate(small_copies):
+        copy.wait_recv()
+        block = block + small_in[k + 1]
+    small_sum[...] = block
+    last_copies = [
+        send_across(small_sum, small_got.at[k], w_send.at[k], w_recv.at[k], p)
+        for k, p in enumerate(peers)
+    ]
+    for copy in last_copies:
+        copy.start()
+
+    @pl.loop(units - GIVE, units)
+    def _(u):
+        to_twin(u).wait_send()
+
     @pl.loop(0, units)
     def _(u):
-        to_twin(u).wait_send()
         for copy in (*to_far(u), *to_near(u)):
             copy.wait_send()
 
-
-def map_grads(routed, grad_q, normed, grad_kv):
-    experts, _, model_width = routed.shape
-    width = grad_q.shape[2]
+    for k, copy in enumerate(last_copies):
+        copy.wait_recv()
+        block = block + small_got[k]
+    small_out[...] = block
+    for copy in (*part_copies, *small_copies, *last_copies):
+        copy.wait_send()
+    for copy in (*token_copies, *dealt, kept):
+        copy.wait()
+
+
+def final_step(
+    tensor_size, routed, grad_q, normed, grad_kv, part, maps,
+    grad_hidden, x_here, gain, router, hots, small,
+):
+    experts, rows, width = routed.shape
+    columns = grad_q.shape[2]
     units = experts + grad_kv.shape[0]
-    size = model_width // 8
-    vmem = pl.BlockSpec(memory_space=pltpu.VMEM)
+    size = width // 8
+    tokens, wide = part.shape
+    share = tokens // tensor_size
+    around = tensor_size - 1
     return pl.pallas_call(
-        map_grads_kernel,
-        in_specs=[vmem] * 4,
-        out_specs=vmem,
-        out_shape=jax.ShapeDtypeStruct((units, size, width), BF16),
+        final_kernel,
+        in_specs=[HBM, VMEM, VMEM, VMEM, HBM, HBM] + [VMEM] * 6,
+        out_specs=[VMEM, HBM, HBM, VMEM],
+        out_shape=[
+            jax.ShapeDtypeStruct((units, size, columns), BF16),
+            jax.ShapeDtypeStruct(maps.shape, BF16),
+            jax.ShapeDtypeStruct((tokens, width), BF16),
+            jax.ShapeDtypeStruct((3 * HALF_SMALL, size), F32),
+        ],
         scratch_shapes=[
-            pltpu.VMEM((units, 4, size, width), BF16),
-            pltpu.VMEM((units, 4, size, width), BF16),
-            pltpu.VMEM((units, 4, size, width), BF16),
-            pltpu.VMEM((units, 2, size // 2, width), BF16),
-            pltpu.VMEM((units, 2, size, width), BF16),
-            pltpu.SemaphoreType.DMA((units,)),
-            pltpu.SemaphoreType.DMA((units,)),
-            pltpu.SemaphoreType.DMA((units, 2)),
-            pltpu.SemaphoreType.DMA((units, 2)),
-            pltpu.SemaphoreType.DMA((units, 2)),
-            pltpu.SemaphoreType.DMA((units, 2)),
+            pltpu.VMEM((GIVE, 4, size, columns), BF16),
+            pltpu.VMEM((units, 4, size, columns), BF16),
+            pltpu.VMEM((units, 4, size, columns), BF16),
+            pltpu.VMEM((units, 2, size // 2, columns), BF16),
+            pltpu.VMEM((units, 2, size, columns), BF16),
+            pltpu.VMEM((2, rows, width), BF16),
+            pltpu.VMEM((tensor_size, share, wide), BF16),
+            pltpu.VMEM((share, width), BF16),
+            sems(GIVE), sems(units), sems(units, 2), sems(units, 2), sems(units, 2),
+            sems(units, 2), sems(2), sems(2),
+            sems(around), sems(around), sems(around), sems(around),
+            pltpu.VMEM((share, HD), BF16),
+            pltpu.VMEM((3 * HALF_SMALL, width), F32),
+            pltpu.VMEM((8, 3 * HALF_SMALL, size), F32),
+            pltpu.VMEM((3 * HALF_SMALL, size), F32),
+            pltpu.VMEM((around, 3 * HALF_SMALL, size), F32),
+            sems(8), sems(8), sems(around), sems(around), sems(8), sems(8),
         ],
         compiler_params=pltpu.CompilerParams(
             collective_id=1, has_side_effects=True, vmem_limit_bytes=60 << 20
         ),
         cost_estimate=pl.CostEstimate(
-            flops=2 * units * 160 * model_width * width,
-            bytes_accessed=250 << 20,
+            flops=2 * units * rows * width * columns,
+            bytes_accessed=350 << 20,
             transcendentals=0,
         ),
-    )(routed, grad_q, normed, grad_kv)
+    )(
+        routed, grad_q, normed, grad_kv, part, maps,
+        grad_hidden, x_here, gain, router, hots, small,
+    )
+
+
+def partner(k):
+    me = lax.axis_index("dp")
+    place = me
+    for bit in (1, 2, 4):
+        place = place + bit * lax.rem(k // bit, 2) * (1 - 2 * lax.rem(me // bit, 2))
+    return place
+
+
+def expert_kernel(
+    x_ref, cot_hbm, gate_up_hbm, down_hbm,
+    back_out, rows_out, grad_gate_hbm, grad_up_hbm, grad_down_hbm,
+    x_all, g_all, w_gate, w_up, w_down, act, grads, back, product, stage_up, stage_down,
+    x_send, x_recv, b_send, b_recv, load, up_sem, down_sem,
+):
+    peers = x_send.shape[0]
+    slots, wide = x_all.shape
+    width = wide - HD
+    hidden = w_gate.shape[1]
+    size = slots // peers
+    pair = 2 * size
+    step = 256
+    whole_steps = hidden // step
+    tail = hidden - whole_steps * step
+
+    per = width // peers
+    loads = [
+        pltpu.make_async_copy(cot_hbm, g_all, load.at[0]),
+        pltpu.make_async_copy(down_hbm, w_down, load.at[1]),
+    ]
+    for j in range(peers):
+        for g, target in enumerate((w_gate, w_up)):
+            loads.append(
+                pltpu.make_async_copy(
+                    gate_up_hbm.at[j, g], target.at[pl.ds(j * per, per)], load.at[2 + 2 * j + g]
+                )
+            )
+    for copy in loads:
+        copy.start()
+
+    barrier = pltpu.get_barrier_semaphore()
+    for k in range(1, peers):
+        pl.semaphore_signal(
+            barrier, inc=1, device_id={"dp": partner(k)}, device_id_type=pl.DeviceIdType.MESH
+        )
+    pl.semaphore_wait(barrier, peers - 1)
+
+    def block(k):
+        return pl.ds(pl.multiple_of(k * size, size), size)
+
+    def send_x(k):
+        return send_to(
+            x_ref.at[block(k)], x_all.at[block(k)], x_send.at[k], x_recv.at[k], partner(k)
+        )
+
+    def send_back(k):
+        return send_to(
+            back.at[block(k)], back_out.at[block(k)], b_send.at[k], b_recv.at[k], partner(k)
+        )
+
+    for k in (1, 2, 4, 3, 5):
+        send_x(k).start()
+    x_all[0:size, :] = x_ref[0:size, :]
+    for copy in loads:
+        copy.wait()
+
+    @pl.loop(0, peers // 2)
+    def _(group):
+        rows = pl.ds(pl.multiple_of(group * pair, pair), pair)
+
+        @pl.when(group > 0)
+        def _():
+            send_x(2 * group).wait_recv()
+
+        send_x(2 * group + 1).wait_recv()
+        columns = x_all[rows, width:].astype(F32)
+        gate_of_row = columns[:, 0:1] + columns[:, 1:2] + columns[:, 2:3]
+        g_all[rows, :] = (g_all[rows, :].astype(F32) * gate_of_row).astype(BF16)
+        product[...] = jnp.zeros_like(product)
+
+        def chunk(start, amount):
+            cols = pl.ds(start, amount)
+            x = x_all[rows, 0:width]
+            gate = dot(x, w_gate[:, cols])
+            up = dot(x, w_up[:, cols])
+            grad_act = jnp.zeros((pair, amount), F32)
+            for j in range(peers):
+                grad_act += dot_nt(g_all[rows, j * per : (j + 1) * per], w_down[j, cols, :])
+            sigmoid = 1.0 / (1.0 + jnp.exp(-gate))
+            silu = gate * sigmoid
+            activated = (silu * up).astype(BF16)
+            act[rows, cols] = activated
+            both = activated.astype(F32) * grad_act
+            for part in range(amount // HD):
+                product[...] += both[:, part * HD : (part + 1) * HD]
+            grads[rows, cols] = (
+                grad_act * up * sigmoid * (1.0 + gate * (1.0 - sigmoid))
+            ).astype(BF16)
+            grads[rows, pl.ds(hidden + start, amount)] = (grad_act * silu).astype(BF16)
+
+        @pl.loop(0, whole_steps)
+        def _(i):
+            chunk(pl.multiple_of(i * step, step), step)
+
+        if tail:
+            chunk(whole_steps * step, tail)
+
+        @pl.loop(0, width // step)
+        def _(i):
+            at = pl.ds(pl.multiple_of(i * step, step), step)
+            back[rows, at] = (
+                dot_nt(grads[rows, 0:hidden], w_gate[at, :])
+                + dot_nt(grads[rows, hidden:], w_up[at, :])
+            ).astype(BF16)
+
+        total = jnp.sum(product[...], axis=1, keepdims=True)
+        high = total.astype(BF16).astype(F32)
+        mid = (total - high).astype(BF16).astype(F32)
+        lane = lax.broadcasted_iota(jnp.int32, (pair, HD), 1)
+        back[rows, width:] = jnp.where(
+            lane == 0, high, jnp.where(lane == 1, mid, jnp.where(lane == 2, total - high - mid, 0.0))
+        ).astype(BF16)
+
+        @pl.when(group == 0)
+        def _():
+            send_x(6).start()
+            send_x(7).start()
+            back_out[0:size, :] = back[0:size, :]
+
+        @pl.when(group > 0)
+        def _():
+            send_back(2 * group).start()
+
+        send_back(2 * group + 1).start()
+
+    def store_up(j, slot):
+        return (
+            pltpu.make_async_copy(
+                stage_up.at[slot, :, pl.ds(0, hidden)], grad_gate_hbm.at[j], up_sem.at[slot, 0]
+            ),
+            pltpu.make_async_copy(
+                stage_up.at[slot, :, pl.ds(hidden, hidden)], grad_up_hbm.at[j], up_sem.at[slot, 1]
+            ),
+        )
+
+    @pl.loop(0, peers)
+    def _(j):
+        slot = lax.rem(j, 2)
+
+        @pl.when(j > 1)
+        def _():
+            for copy in store_up(j - 2, slot):
+                copy.wait()
+
+        at = pl.ds(pl.multiple_of(j * per, per), per)
+        stage_up[slot] = dot_tn(x_all[:, at], grads[...]).astype(BF16)
+        for copy in store_up(j, slot):
+            copy.start()
+        rows_out[:, at] = dot(act[...], w_down[j]).astype(BF16)
+
+    def store_down(start, amount, slot):
+        return pltpu.make_async_copy(
+            stage_down.at[slot, :, pl.ds(0, amount)],
+            grad_down_hbm.at[:, pl.ds(start, amount)],
+            down_sem.at[slot],
+        )
+
+    def down_piece(start, amount, slot):
+        piece = dot_tn(act[:, pl.ds(start, amount)], g_all[...]).astype(BF16)
+        for j in range(peers):
+            stage_down[slot, j, 0:amount, :] = piece[:, j * per : (j + 1) * per]
+        store_down(start, amount, slot).start()
+
+    @pl.loop(0, whole_steps)
+    def _(i):
+        slot = lax.rem(i, 2)
+
+        @pl.when(i > 1)
+        def _():
+            store_down(pl.multiple_of((i - 2) * step, step), step, slot).wait()
+
+        down_piece(pl.multiple_of(i * step, step), step, slot)
+
+    last = whole_steps - 1
+    store_down((last - 1) * step, step, (last - 1) % 2).wait()
+    if tail:
+        down_piece(whole_steps * step, tail, (last - 1) % 2)
+        store_down(whole_steps * step, tail, (last - 1) % 2).wait()
+    store_down(last * step, step, last % 2).wait()
+    for j in (peers - 2, peers - 1):
+        for copy in store_up(j, j % 2):
+            copy.wait()
+    for k in range(1, peers):
+        send_x(k).wait_send()
+        send_back(k).wait()
+
+
+def expert_step(x_rows, cot_rows, up_slices, down_slices):
+    slots, wide = x_rows.shape
+    width = wide - HD
+    peers, hidden, per = down_slices.shape
+    vmem = pl.BlockSpec(memory_space=pltpu.VMEM)
+    hbm = pl.BlockSpec(memory_space=pl.ANY)
+    step = 256
+    return pl.pallas_call(
+        expert_kernel,
+        in_specs=[vmem, hbm, hbm, hbm],
+        out_specs=[vmem, vmem, hbm, hbm, hbm],
+        out_shape=[
+            jax.ShapeDtypeStruct((slots, wide), BF16),
+            jax.ShapeDtypeStruct((slots, width), BF16),
+            jax.ShapeDtypeStruct((peers, per, hidden), BF16),
+            jax.ShapeDtypeStruct((peers, per, hidden), BF16),
+            jax.ShapeDtypeStruct((peers, hidden, per), BF16),
+        ],
+        scratch_shapes=[
+            pltpu.VMEM((slots, wide), BF16),
+            pltpu.VMEM((slots, width), BF16),
+            pltpu.VMEM((width, hidden), BF16),
+            pltpu.VMEM((width, hidden), BF16),
+            pltpu.VMEM((peers, hidden, per), BF16),
+            pltpu.VMEM((slots, hidden), BF16),
+            pltpu.VMEM((slots, 2 * hidden), BF16),
+            pltpu.VMEM((slots, wide), BF16),
+            pltpu.VMEM((2 * slots // peers, HD), F32),
+            pltpu.VMEM((2, per, 2 * hidden), BF16),
+            pltpu.VMEM((2, peers, step, per), BF16),
+            pltpu.SemaphoreType.DMA((peers,)),
+            pltpu.SemaphoreType.DMA((peers,)),
+            pltpu.SemaphoreType.DMA((peers,)),
+            pltpu.SemaphoreType.DMA((peers,)),
+            pltpu.SemaphoreType.DMA((2 + 2 * peers,)),
+            pltpu.SemaphoreType.DMA((2, 2)),
+            pltpu.SemaphoreType.DMA((2,)),
+        ],
+        compiler_params=pltpu.CompilerParams(
+            collective_id=2, has_side_effects=True, vmem_limit_bytes=60 << 20
+        ),
+        cost_estimate=pl.CostEstimate(
+            flops=18 * slots * width * hidden, bytes_accessed=300 << 20, transcendentals=0
+        ),
+    )(x_rows, cot_rows, up_slices, down_slices)
 
 
 class Movers:
@@ -463,15 +1228,31 @@
         return full
 
 
-def map_sums(dp_size, routed, grad_q, normed, grad_k, grad_v):
-    if dp_size == 8:
-        both = map_grads(routed, grad_q, normed, jnp.stack([grad_k, grad_v]))
-        return both[:-2], both[-2:]
-    grad_query_w = jnp.einsum("ecd,ecf->edf", routed, grad_q, preferred_element_type=BF16)
-    grad_keyval_w = jnp.stack([dot_tn(normed, grad_k, BF16), dot_tn(normed, grad_v, BF16)])
+def expert_plain(movers, expert_in, cot_rows, up_slices, down_slices):
+    dp_size, hidden_here, per_dp = down_slices.shape
+    model_width = dp_size * per_dp
+    gate_full, up_full = (up_slices[:, g].reshape(model_width, hidden_here) for g in range(2))
+    down_full = down_slices.transpose(1, 0, 2).reshape(hidden_here, model_width)
+    x_rows, gate_of_row = without_column(movers.exchange(expert_in))
+    g_rows = (cot_rows.astype(F32) * gate_of_row).astype(BF16)
+    gate = dot(x_rows, gate_full)
+    up = dot(x_rows, up_full)
+    sigmoid_gate = jax.nn.sigmoid(gate)
+    silu_gate = gate * sigmoid_gate
+    activated = (silu_gate * up).astype(BF16)
+    grad_act = dot_nt(g_rows, down_full)
+    grad_gate = (grad_act * up * sigmoid_gate * (1.0 + gate * (1.0 - sigmoid_gate))).astype(BF16)
+    grad_up = (grad_act * silu_gate).astype(BF16)
+    gate_times_grad = jnp.sum(activated.astype(F32) * grad_act, axis=1, keepdims=True)
+    grad_expert_in = with_column(
+        (dot_nt(grad_gate, gate_full) + dot_nt(grad_up, up_full)).astype(BF16), gate_times_grad
+    )
     return (
-        lax.psum_scatter(grad_query_w, "dp", scatter_dimension=1, tiled=True),
-        lax.psum_scatter(grad_keyval_w, "dp", scatter_dimension=1, tiled=True),
+        movers.exchange(grad_expert_in),
+        dot(activated, down_full, BF16),
+        dot_tn(x_rows, grad_gate, BF16).reshape(dp_size, per_dp, -1),
+        dot_tn(x_rows, grad_up, BF16).reshape(dp_size, per_dp, -1),
+        dot_tn(activated, g_rows, BF16).reshape(-1, dp_size, per_dp).transpose(1, 0, 2),
     )
 
 
@@ -505,27 +1286,18 @@
     width_here = query_weight.shape[2]
     rows_here = tok_count // tensor_size
     movers = Movers(dp_size, mlp_experts, tensor_size)
+    fast = dp_size == 8 and mlp_experts == 8
     tie = lax.optimization_barrier
 
     small = jnp.concatenate(
         [gain_attention[:, None], gain_feedforward[:, None], attention_router, expert_router], axis=1
     )
     small_full = lax.all_gather(small, "dp", axis=0, tiled=True)
-    small_full, keyval_weight, query_weight, output_weight, gate_up_weight, down_weight = tie(
-        (small_full, keyval_weight, query_weight, output_weight, gate_up_weight, down_weight)
-    )
-    keyval_full = lax.all_gather(keyval_weight, "dp", axis=1, tiled=True)
-    query_full = lax.all_gather(query_weight, "dp", axis=1, tiled=True)
-    output_full = lax.all_gather(output_weight, "dp", axis=2, tiled=True)
+    small_full, down_weight = tie((small_full, down_weight))
     gain_attn_full = small_full[:, 0].astype(F32)
     gain_mlp_full = small_full[:, 1].astype(F32)
     router_att = small_full[:, 2 : 2 + att_experts]
     router_mlp = small_full[:, 2 + att_experts :]
-
-    gate_full = movers.fetch(gate_up_weight[:, 0]).reshape(model_width, -1)
-    up_full = movers.fetch(gate_up_weight[:, 1]).reshape(model_width, -1)
-    down_full = movers.fetch(down_weight)
-    down_full = down_full.transpose(1, 0, 2).reshape(down_full.shape[1], model_width)
 
     inside, depth = ancestry(parents[0])
     token_index = jnp.arange(tok_count, dtype=jnp.int32)
@@ -572,15 +1344,34 @@
     allowed = reach & (token_index[None, :] <= slot_token[:, None]) & slot_filled[:, None]
     bias = jnp.where(allowed, 0.0, NEGATIVE).astype(BF16)
 
-    cot_rows = movers.exchange(dot(mlp_pick, cotangent, BF16))
+    down_slices = movers.fetch(down_weight)
+    cot_send = dot(mlp_pick, cotangent, BF16)
 
     inputs = tokens.astype(F32)
     normal_attn, scale_attn = norm_forward(inputs)
     normed = (normal_attn * gain_attn_full).astype(BF16)
     att_gates = picked_softmax(dot(normed, router_att), attention_routes)
     att_gate_slots = to_slots(att_hits, att_gates)[:, None]
+    routed = dot(att_pick, normed, BF16).reshape(att_experts, att_cap, model_width)
+    if fast:
+        keyval_weight, query_weight, output_weight, *before = tie(
+            (keyval_weight, query_weight, output_weight, routed, cot_send, bias, att_gate_slots)
+            + slot_tables + tok_tables
+        )
+        routed, cot_send, bias, att_gate_slots = before[:4]
+        slot_tables, tok_tables = before[4:6], before[6:8]
+        keyval_full, query_full, output_full = gather_maps(
+            (keyval_weight, query_weight, output_weight), (1, 1, 2), (2, 2, 2)
+        )
+    else:
+        keyval_full = lax.all_gather(keyval_weight, "dp", axis=1, tiled=True)
+        query_full = lax.all_gather(query_weight, "dp", axis=1, tiled=True)
+        output_full = lax.all_gather(output_weight, "dp", axis=2, tiled=True)
+    query_full, keyval_full, down_slices, gate_up_weight = tie(
+        (query_full, keyval_full, down_slices, gate_up_weight)
+    )
+    up_slices = movers.fetch(gate_up_weight)
     keyval = jnp.concatenate([dot(normed, keyval_full[0]), dot(normed, keyval_full[1])], axis=1)
-    routed = dot(att_pick, normed, BF16).reshape(att_experts, att_cap, model_width)
     query_raw = jnp.einsum(
         "ecd,edf->ecf", routed, query_full, preferred_element_type=F32
     ).reshape(att_slots, width_here)
@@ -591,86 +1382,76 @@
     att_rows = jnp.einsum(
         "ecf,efd->ecd", gated_slots, output_full, preferred_element_type=F32
     ).reshape(att_slots, model_width)
-    att_part = dot_tn(att_pick, att_rows.astype(BF16))
+    att_rows = att_rows.astype(BF16)
 
     z = lax.axis_index("tensor")
 
     def share(rows):
         return lax.dynamic_slice_in_dim(rows, z * rows_here, rows_here, axis=0)
 
-    hidden = share(inputs) + movers.reduce_rows(att_part)
-    normal_mlp, scale_mlp = norm_forward(hidden)
-    mlp_in_here = (normal_mlp * gain_mlp_full).astype(BF16)
-    mlp_in = movers.gather_rows(mlp_in_here)
+    def hots(gates, picks, experts):
+        lanes = jnp.arange(HD, dtype=jnp.int32)[None, :]
+        hot = [(share(picks)[:, k : k + 1] == lanes).astype(F32) for k in range(TOPK)]
+        return jnp.stack(hot + [sum(hot[k] * share(gates)[:, k : k + 1] for k in range(TOPK))])
+
+    def padded(router):
+        return jnp.pad(router, ((0, 0), (0, HD - router.shape[1])))
+
+    if fast:
+        hidden, mlp_in, cot_rows = hidden_step(
+            tensor_size, mlp_experts, att_pick, att_rows, share(tokens), gain_mlp_full[None],
+            cot_send,
+        )
+    else:
+        hidden = share(inputs) + movers.reduce_rows(dot_tn(att_pick, att_rows))
+        mlp_in = movers.gather_rows((norm_forward(hidden)[0] * gain_mlp_full).astype(BF16))
+        cot_rows = movers.exchange(cot_send)
+    mlp_in, up_slices, cot_rows = tie((mlp_in, up_slices, cot_rows))
     mlp_gates = picked_softmax(dot(mlp_in, router_mlp), expert_routes)
     mlp_gate_slots = to_slots(mlp_hits, mlp_gates)[:, None]
-    gate_high = mlp_gate_slots.astype(BF16)
-    gate_rest = mlp_gate_slots - gate_high.astype(F32)
-    gate_mid = gate_rest.astype(BF16)
-    gate_low = (gate_rest - gate_mid.astype(F32)).astype(BF16)
-    expert_in = jnp.concatenate(
-        [dot(mlp_pick, mlp_in, BF16), gate_high, gate_mid, gate_low]
-        + [jnp.zeros((mlp_slots, HD - 3), BF16)],
-        axis=1,
-    )
-
-    received = movers.exchange(expert_in)
-    x_rows = received[:, :model_width]
-    gate_columns = received[:, model_width : model_width + 3].astype(F32)
-    gate_of_row = gate_columns[:, :1] + gate_columns[:, 1:2] + gate_columns[:, 2:]
-    g_rows = (cot_rows.astype(F32) * gate_of_row).astype(BF16)
-    gate = dot(x_rows, gate_full)
-    up = dot(x_rows, up_full)
-    sigmoid_gate = jax.nn.sigmoid(gate)
-    silu_gate = gate * sigmoid_gate
-    activated = (silu_gate * up).astype(BF16)
-    expert_out = dot(activated, down_full, BF16)
-    out_slots = movers.exchange(expert_out)
-    grad_act = dot_nt(g_rows, down_full)
-    grad_gate = (grad_act * up * sigmoid_gate * (1.0 + gate * (1.0 - sigmoid_gate))).astype(BF16)
-    grad_up = (grad_act * silu_gate).astype(BF16)
-    grad_expert_in = (dot_nt(grad_gate, gate_full) + dot_nt(grad_up, up_full)).astype(BF16)
-    grad_in_slots = movers.exchange(grad_expert_in)
-    grad_gate, grad_up, activated, _ = tie((grad_gate, grad_up, activated, grad_expert_in))
-    per_dp = model_width // dp_size
-    grad_gate_w = dot_tn(x_rows, grad_gate, BF16).reshape(dp_size, per_dp, -1)
-    grad_up, activated, grad_gate_w, out_slots = tie((grad_up, activated, grad_gate_w, out_slots))
-    grad_up_w = dot_tn(x_rows, grad_up, BF16).reshape(dp_size, per_dp, -1)
-    grad_down_w = (
-        dot_tn(activated, g_rows, BF16).reshape(-1, dp_size, per_dp).transpose(1, 0, 2)
-    )
-    grad_in_slots, out_slots, grad_gate_w, grad_up_w, grad_down_w = tie(
-        (grad_in_slots, out_slots, grad_gate_w, grad_up_w, grad_down_w)
-    )
-    grad_gate_w = movers.give_back(grad_gate_w)
+    expert_in = with_column(dot(mlp_pick, mlp_in, BF16), mlp_gate_slots)
+
+    if fast:
+        back = expert_step(expert_in, cot_rows, up_slices, down_slices)
+    else:
+        back = expert_plain(movers, expert_in, cot_rows, up_slices, down_slices)
+    grad_in_slots, expert_out, grad_gate_w, grad_up_w, grad_down_w = back
+
+    if fast:
+        grad_hidden, grad_att_pair, grad_gain_mlp, grad_mlp_logits, out_slots, grad_gate_w = back_step(
+            tensor_size, mlp_experts, grad_in_slots, mlp_pick,
+            [hit.astype(BF16) for hit in mlp_hits], hidden, share(cotangent),
+            gain_mlp_full[None], padded(router_mlp),
+            hots(mlp_gates, expert_routes, mlp_experts), expert_out, grad_gate_w,
+        )
+        grad_gain_mlp = grad_gain_mlp[0]
+        grad_mlp_logits = grad_mlp_logits[:, :mlp_experts]
+    else:
+        out_slots = movers.exchange(expert_out)
+        grad_gate_w = movers.give_back(grad_gate_w)
+        grad_in_slots, gate_times_grad = without_column(grad_in_slots)
+        mlp_products = movers.reduce_rows(to_pairs(mlp_hits, gate_times_grad[:, 0]), F32)
+        grad_mlp_in = movers.reduce_rows(dot_tn(mlp_pick, grad_in_slots))
+        grad_mlp_logits = router_backward(
+            share(mlp_gates), mlp_products, share(expert_routes), mlp_experts
+        )
+        grad_mlp_in = grad_mlp_in + dot_nt(grad_mlp_logits, router_mlp)
+        normal_mlp, scale_mlp = norm_forward(hidden)
+        grad_hidden_norm, grad_gain_mlp = norm_backward(
+            grad_mlp_in, normal_mlp, scale_mlp, gain_mlp_full
+        )
+        grad_hidden = share(cotangent).astype(F32) + grad_hidden_norm
+        grad_att_pair = movers.gather_rows(grad_hidden)
+    grad_att_pair, grad_up_w = tie((grad_att_pair, grad_up_w))
     grad_up_w = movers.give_back(grad_up_w)
-    grad_down_w = movers.give_back(grad_down_w)
-
-    alignment = dot_nt(out_slots, cotangent)
-    grad_gates_part = jnp.stack(
-        [jnp.sum(jnp.where(mlp_hits[k], alignment, 0.0), axis=0) for k in range(TOPK)], axis=1
-    )
-    grad_mlp_gates = movers.reduce_rows(grad_gates_part, F32)
-    grad_mlp_in = movers.reduce_rows(dot_tn(mlp_pick, grad_in_slots))
-    grad_mlp_logits = router_backward(
-        share(mlp_gates), grad_mlp_gates, share(expert_routes), mlp_experts
-    )
-    grad_router_mlp = dot_tn(mlp_in_here, grad_mlp_logits)
-    grad_mlp_in = grad_mlp_in + dot_nt(grad_mlp_logits, router_mlp)
-    grad_hidden_norm, grad_gain_mlp = norm_backward(
-        grad_mlp_in, normal_mlp, scale_mlp, gain_mlp_full
-    )
-    grad_hidden = share(cotangent).astype(F32) + grad_hidden_norm
-    grad_hidden, grad_gate_w = tie((grad_hidden, grad_gate_w))
-    grad_att_pair = movers.gather_rows(grad_hidden)
+    grad_router_mlp = dot_tn(share(mlp_in), grad_mlp_logits)
 
     gate_matrix = sum(
         jnp.where(mlp_hits[k], mlp_gates[:, k][None, :], 0.0) for k in range(TOPK)
     )
     matrix_high = gate_matrix.astype(BF16)
     matrix_low = (gate_matrix - matrix_high.astype(F32)).astype(BF16)
-    mlp_part = dot_tn(matrix_high, out_slots) + dot_tn(matrix_low, out_slots)
-    mlp_part, grad_att_pair = tie((mlp_part, grad_att_pair))
+    mlp_part = (dot_tn(matrix_high, out_slots) + dot_tn(matrix_low, out_slots)).astype(BF16)
     mlp_sum = movers.reduce_rows(mlp_part)
 
     grad_att_rows = dot(att_pick, grad_att_pair, BF16).reshape(att_experts, att_cap, model_width)
@@ -682,8 +1463,8 @@
         "ecd,efd->ecf", grad_att_rows, output_full, preferred_element_type=F32
     ).reshape(att_slots, width_here)
     grad_output_out = lax.psum_scatter(grad_output_w, "dp", scatter_dimension=2, tiled=True)
-    grad_att_gates = movers.reduce_rows(
-        to_pairs(att_hits, jnp.sum(grad_gated * attended, axis=1)), F32
+    att_products = to_pairs(
+        att_hits, jnp.sum(grad_gated * attended, axis=1) * att_gate_slots[:, 0]
     )
     grad_q, grad_k, grad_v = attend_back(
         queries, key_rows, values, bias, att_gate_slots, slot_tables, tok_tables, grad_gated
@@ -697,32 +1478,56 @@
         + dot_nt(grad_k, keyval_full[0])
         + dot_nt(grad_v, keyval_full[1])
     )
-    grad_normed = movers.reduce_rows(normed_part)
-    grad_query_slots, grad_k, grad_v, _, grad_up_w, mlp_sum = tie(
-        (grad_query_slots, grad_k, grad_v, normed_part, grad_up_w, mlp_sum)
-    )
+    normed_part = with_column(normed_part.astype(BF16), att_products[:, :1])
+    normed_part = with_column(normed_part, att_products[:, 1:])
+    grad_kv = jnp.stack([grad_k, grad_v])
+    normed_part, grad_up_w, mlp_sum = tie((normed_part, grad_up_w, mlp_sum))
     mixed = movers.gather_rows(hidden + mlp_sum)
-    grad_query_out, grad_keyval_out = map_sums(
-        dp_size, routed, grad_query_slots, normed, grad_k, grad_v
-    )
-    grad_normed, grad_down_w, grad_query_out, grad_output_out, mixed = tie(
-        (grad_normed, grad_down_w, grad_query_out, grad_output_out, mixed)
-    )
-    grad_att_logits = router_backward(
-        share(att_gates), grad_att_gates, share(attention_routes), att_experts
-    )
-    grad_router_att = dot_tn(share(normed), grad_att_logits)
-    grad_normed = grad_normed + dot_nt(grad_att_logits, router_att)
-    grad_input_norm, grad_gain_attn = norm_backward(
-        grad_normed, share(normal_attn), share(scale_attn), gain_attn_full
-    )
-    grad_tokens = movers.gather_rows(grad_hidden + grad_input_norm).astype(F32)
-    small_grads = jnp.concatenate(
-        [grad_gain_attn[:, None], grad_gain_mlp[:, None], grad_router_att, grad_router_mlp], axis=1
-    )
-    small_grads = lax.psum(
-        lax.psum_scatter(small_grads, "dp", scatter_dimension=0, tiled=True), "tensor"
-    )
+    if fast:
+        small = jnp.concatenate(
+            [
+                jnp.zeros((1, model_width), F32),
+                grad_gain_mlp[None],
+                jnp.zeros((HALF_SMALL - 2, model_width), F32),
+                grad_router_mlp.T,
+            ],
+            axis=0,
+        )
+        map_sums, grad_down_w, grad_tokens, small_grads = final_step(
+            tensor_size, routed, grad_query_slots, normed, grad_kv, normed_part, grad_down_w,
+            grad_hidden, share(tokens), gain_attn_full[None], padded(router_att),
+            hots(att_gates, attention_routes, att_experts), small,
+        )
+        small_grads = jnp.concatenate([small_grads[:2], small_grads[HALF_SMALL:]], axis=0).T
+        grad_query_out, grad_keyval_out = map_sums[:att_experts], map_sums[att_experts:]
+    else:
+        grad_query_w = jnp.einsum(
+            "ecd,ecf->edf", routed, grad_query_slots, preferred_element_type=BF16
+        )
+        grad_keyval_w = jnp.stack([dot_tn(normed, grad, BF16) for grad in (grad_k, grad_v)])
+        grad_query_out = lax.psum_scatter(grad_query_w, "dp", scatter_dimension=1, tiled=True)
+        grad_keyval_out = lax.psum_scatter(grad_keyval_w, "dp", scatter_dimension=1, tiled=True)
+        grad_down_w = movers.give_back(grad_down_w)
+        grad_normed = movers.reduce_rows(normed_part[:, :model_width])
+        grad_att_logits = router_backward(
+            share(att_gates), movers.reduce_rows(att_products, F32), share(attention_routes),
+            att_experts,
+        )
+        grad_normed = grad_normed + dot_nt(grad_att_logits, router_att)
+        grad_input_norm, grad_gain_attn = norm_backward(
+            grad_normed, share(normal_attn), share(scale_attn), gain_attn_full
+        )
+        grad_tokens = movers.gather_rows(grad_hidden + grad_input_norm)
+        grad_router_att = dot_tn(share(normed), grad_att_logits)
+        small_grads = jnp.concatenate(
+            [grad_gain_attn[:, None], grad_gain_mlp[:, None], grad_router_att, grad_router_mlp],
+            axis=1,
+        )
+        small_grads = lax.psum(
+            lax.psum_scatter(small_grads, "dp", scatter_dimension=0, tiled=True), "tensor"
+        )
+    grad_tokens, grad_output_out = tie((grad_tokens, grad_output_out))
+    grad_tokens = grad_tokens.astype(F32)
     return (
         mixed,
         grad_tokens,

time: 1250 us -> 1090 us (0.87)
  Pallas kernels: 153 us -> 752 us
  waiting for transfers between devices: 509 us -> 53.3 us
  starting transfers between devices: 162 us -> 24.2 us
  matrix products: 215 us -> 102 us
  blocking collectives: 40.9 us -> 11.3 us
  other arithmetic: 65.2 us -> 50.1 us
    pallas_call x1 -> x5, Pallas kernels: 118 us -> 717 us  [the longest x1 190 us: gather_maps(): pl.pallas_call(functools.partial(gather_kernel, axes, chunks), in_specs=[...]
    all_gather x3 -> x0, waiting for transfers between devices: 187 us -> none  [the longest x1 121 us: on_device(): query_full = lax.all_gather(query_weight, 'dp', axis=1, tiled=True)]
    ppermute x28 -> x0, waiting for transfers between devices: 124 us -> none  [exchange(): blocks.append(lax.ppermute(rows[k * size:(k + 1) * size], 'dp', pairs))]
    ppermute x30 -> x6, waiting for transfers between devices: 131 us -> 8.92 us  [across(): lax.ppermute(block, 'tensor', [(i, i ^ k) for i in range(self.tensor)])]
    ppermute x30 -> x6, starting transfers between devices: 108 us -> 8.77 us  [across(): lax.ppermute(block, 'tensor', [(i, i ^ k) for i in range(self.tensor)])]
    dot_general x10 -> x4, matrix products: 56.8 us -> 14.7 us  [dot_tn(): lax.dot_general(a, b, (((0,), (0,)), ((), ())), preferred_element_type=out)]
    dot_general x8 -> x2, matrix products: 41.1 us -> 2.57 us  [dot_nt(): lax.dot_general(a, b, (((1,), (1,)), ((), ())), preferred_element_type=out)]
    dot_general x12 -> x9, matrix products: 60.1 us -> 26.7 us  [dot(): return jnp.dot(a, b, preferred_element_type=out)]
  transfers between devices with their start and end apart: 69 -> 10, of which waited for: 23 -> 2; matrix products, arithmetic and copies ran while one was open for 23% -> 14% of each run, Pallas kernels for 12% -> 49%
where the time goes in v3:
time: 1090 us; the launch traced here: 1080 us
  Pallas kernels  752 us (69%)
  matrix products  102 us (9%)
  local copies, waits for them, and re-layouts  70.5 us (6%)
  waiting for transfers between devices  53.3 us (5%)
  other arithmetic  50.1 us (5%)
  starting transfers between devices  24.2 us (2%)
  between operations  15.7 us (1%)
  blocking collectives  11.3 us (1%)
    pallas_call x1, Pallas kernels, gather_maps(): pl.pallas_call(functools.partial(gather_kernel, axes, chunks), in_specs=[...  190 us
    pallas_call x1, Pallas kernels, final_step(): pl.pallas_call(final_kernel, in_specs=[HBM, VMEM, VMEM, VMEM, HBM, HBM] +...  185 us
    pallas_call x1, Pallas kernels, hidden_step(): pl.pallas_call(hidden_kernel, in_specs=[VMEM, VMEM, VMEM, VMEM, HBM], out...  119 us
    pallas_call x1, Pallas kernels, back_step(): pl.pallas_call(back_kernel, in_specs=[VMEM] * 9 + [HBM] * 2, out_specs=[V...  117 us
    pallas_call x1, Pallas kernels, expert_step(): pl.pallas_call(expert_kernel, in_specs=[vmem, hbm, hbm, hbm], out_specs=[...  106 us
    all_to_all x3, waiting for transfers between devices, swap(): lax.all_to_all(blocks, 'dp', 0, 0, axis_index_groups=self.groups, tiled=T...  44.3 us
    unnamed x162, local copies, waits for them, and re-layouts  32.8 us
    dot_general x9, matrix products, dot(): return jnp.dot(a, b, preferred_element_type=out)  26.7 us
  transfers between devices with their start and end apart: 10, of which 2 were waited for; matrix products, arithmetic and copies ran while one was open for 14% of the time, Pallas kernels for 49%

profile of v3, /device:TPU:0, one launch (start us, length us, event | category | flops | bytes accessed | tf_op | source)
XLA Modules:
  0.0 1078.4 jit_solution(12593146405413054622)
XLA Ops:
  9.4 11.3 %all_gather.3 = bf16[2048,18]{1,0:T(8,128)(2,1)S(1)} all-gather(bf16[256,18]{1,0:T(8,128)(2,1)S(1)} %copy.120), channel_id=1, replica_groups=mesh['dp'=8,'tensor'=4] {'dp'}, dimensions={0}, use_global_device_ids=true | all-gather | bytes 82944 | tf_op jit(solution)/shard_map/all_gather | solution.py:1295
  20.7 4.9 all-to-all-start
  40.3 2.8 select_convert_fusion.bias
  43.2 2.4 fusion.50
  45.6 1.5 pad_maximum_fusion.2
  47.0 4.4 fusion.26.cot_hbm
  51.4 4.6 fusion.47
  56.0 189.7 %shard_map.230 = (bf16[2,2048,512]{2,1,0:T(8,128)(2,1)}, bf16[8,2048,512]{2,1,0:T(8,128)(2,1)}, bf16[8,512,2048]{2,1,0:T(8,128)(2,1)}) custom-call(bf16[2,256,512]{2,1,0:T(8,128)(2,1)} %refs_0_, bf16[8,256,512]{2,1,0:T(8,128)(2,1)} %refs_1_, bf16[8,512,256]{2,1,0:T(8,128)(2,1)} %refs_2_), custom_call_target="tpu_custom_call" | custom-call | bytes 629145600 | tf_op jit(solution)/shard_map/pallas_call | solution.py:440
  245.7 5.3 all-to-all-start.1
  255.1 2.2 constant_dynamic-slice_fusion.7
  257.4 2.9 fusion.16
  263.1 10.3 fusion.97
  273.4 16.1 %shard_map.231 = (bf16[1280,512]{1,0:T(8,128)(2,1)S(1)}, bf16[512,512]{1,0:T(8,128)(2,1)S(1)}, bf16[512,512]{1,0:T(8,128)(2,1)S(1)}, f32[1280,512]{1,0:T(8,128)S(1)}, bf16[1280,512]{1,0:T(8,128)(2,1)S(1)}) custom-call(f32[1280,512]{1,0:T(8,128)} %bitcast.115, f32[512,1024]{1,0:T(8,128)S(1)} %pad_maximum_fusion.k_raw.v_raw, ...), custom_call_target="tpu_custom_call" | custom-call | flops 1342177280 | bytes 9175040 | tf_op jit(solution)/shard_map/pallas_call | solution.py:154
  292.2 12.2 %convolution_convert_fusion.1 = bf16[8,160,2048]{2,1,0:T(8,128)(2,1)} fusion(bf16[8,160,512]{2,1,0:T(8,128)(2,1)S(1)} %bitcast.100, bf16[8,512,2048]{2,1,0:T(8,128)(2,1)} %get-tuple-element.86), kind=kOutput, calls=%fused_computation.17 | convolution fusion | flops 2686976000 | bytes 23330816 | tf_op jit(solution)/shard_map/ecf,efd->ecd/dot_general | solution.py:1382
  304.4 119.0 %shard_map.232 = (f32[128,2048]{1,0:T(8,128)S(1)}, bf16[512,2048]{1,0:T(8,128)(2,1)S(1)}, bf16[1024,2048]{1,0:T(8,128)(2,1)S(1)}) custom-call(bf16[1280,512]{1,0:T(8,128)(2,1)S(1)} %get-tuple-element.228.pick, bf16[1280,2048]{1,0:T(8,128)(2,1)} %bitcast.110, bf16[128,2048]{1,0:T(8,128)(2,1)S(1)} %get-tuple-element.244.x_here, f32[1,2048]{1,0:T(1,128)S(1)} %bitcast.106, ...), custom_call_target="tpu_custom_call" | custom-call | flops 2684354560 | bytes 314572800 | tf_op jit(solution)/shard_map/pallas_call | solution.py:546
  425.7 2.0 copy-done.35
  427.7 2.6 fusion.87
  432.2 4.4 fusion.24
  438.3 1.5 pad_maximum_fusion.6.hots
  439.9 7.8 concatenate.36.x_ref
  447.7 106.4 %shard_map.233 = (bf16[1024,2176]{1,0:T(8,128)(2,1)}, bf16[1024,2048]{1,0:T(8,128)(2,1)}, bf16[8,256,1408]{2,1,0:T(8,128)(2,1)}, bf16[8,256,1408]{2,1,0:T(8,128)(2,1)}, bf16[8,1408,256]{2,1,0:T(8,128)(2,1)}) custom-call(bf16[1024,2176]{1,0:T(8,128)(2,1)} %concatenate.36.x_ref, bf16[1024,2048]{1,0:T(8,128)(2,1)} %copy-done.35, ...), custom_call_target="tpu_custom_call" | custom-call | flops 53150220288 | bytes 314572800 | tf_op jit(solution)/shard_map/pallas_call | solution.py:1134
  558.5 117.0 %shard_map.234 = (f32[128,2048]{1,0:T(8,128)S(1)}, bf16[512,2048]{1,0:T(8,128)(2,1)S(1)}, f32[1,2048]{1,0:T(1,128)S(1)}, bf16[128,128]{1,0:T(8,128)(2,1)S(1)}, b...) custom-call(bf16[1024,2176]{1,0:T(8,128)(2,1)} %get-tuple-element.99.back, bf16[1024,512]{1,0:T(8,128)(2,1)S(1)} %copy-done.8, ...), custom_call_target="tpu_custom_call" | custom-call | flops 2147483648 | bytes 314572800 | tf_op jit(solution)/shard_map/pallas_call | solution.py:640
  675.6 4.6 fusion.44
  680.2 10.8 %fusion.98 = bf16[8,512,2048]{2,1,0:T(8,128)(2,1)} fusion(bf16[8,160,512]{2,1,0:T(8,128)(2,1)S(1)} %bitcast.101, bf16[8,160,2048]{2,1,0:T(8,128)(2,1)} %bitcast.108), kind=kOutput, calls=%fused_computation.223 | convolution fusion | flops 2684354560 | bytes 23330816 | tf_op jit(solution)/shard_map/ecf,ecd->efd/dot_general | solution.py:1458
  693.9 13.6 %fusion.99 = f32[8,160,512]{2,1,0:T(8,128)S(1)} fusion(bf16[8,160,2048]{2,1,0:T(8,128)(2,1)} %bitcast.109, bf16[8,512,2048]{2,1,0:T(8,128)(2,1)} %get-tuple-element.86), kind=kOutput, calls=%fused_computation.224 | convolution fusion | flops 2684354560 | bytes 24641536 | tf_op jit(solution)/shard_map/ecd,efd->ecf/dot_general | solution.py:1462
  709.1 5.6 fusion.38
  714.7 2.8 add_convert_fusion
  721.0 3.1 collective-permute-start.1
  727.7 5.0 all-to-all-start.2
  732.8 1.7 subtract_convert_fusion.3
  734.5 1.7 subtract_convert_fusion.4
  739.5 1.5 copy-done.26
  745.3 18.5 %shard_map.235 = (bf16[1280,512]{1,0:T(8,128)(2,1)S(1)}, bf16[512,512]{1,0:T(8,128)(2,1)S(1)}, bf16[512,512]{1,0:T(8,128)(2,1)S(1)}) custom-call(bf16[1280,512]{1,0:T(8,128)(2,1)S(1)} %copy-done.37, bf16[512,512]{1,0:T(8,128)(2,1)S(1)} %copy-done.39, bf16[512,512]{1,0:T(8,128)(2,1)S(1)} %copy-done.41, bf16[1280,512]{1,0:T(8,128)(2,1)S(1)} %copy-done.26, ...), custom_call_target="tpu_custom_call" | custom-call | flops 3355443200 | bytes 6553600 | tf_op jit(solution)/shard_map/pallas_call | solution.py:224
  765.2 10.9 %convolution_convert_fusion = bf16[8,160,2048]{2,1,0:T(8,128)(2,1)} fusion(bf16[8,160,512]{2,1,0:T(8,128)(2,1)S(1)} %bitcast.102, bf16[8,2048,512]{2,1,0:T(8,128)(2,1)} %get-tuple-element.77), kind=kOutput, calls=%fused_computation.16 | convolution fusion | flops 2686976000 | bytes 23330816 | tf_op jit(solution)/shard_map/ecf,edf->ecd/dot_general | solution.py:1473
  776.0 5.1 fusion.42
  782.5 4.6 concatenate.37.part_hbm
  790.2 1.8 convert_add_fusion
  792.1 44.3 %all-to-all-done.2 = bf16[8,256,1408]{2,1,0:T(8,128)(2,1)} async-done(((bf16[8,256,1408]{2,1,0:T(8,128)(2,1)}), bf16[8,256,1408]{2,1,0:T(8,128)(2,1)}, u32[]{:S(2)}, u32[]{:S(2)}) %all-to-all-start.2) | async-done | bytes 5767200 | tf_op jit(solution)/shard_map/all_to_all | solution.py:1184
  836.4 185.0 %shard_map.236 = (bf16[10,256,512]{2,1,0:T(8,128)(2,1)}, bf16[8,1408,256]{2,1,0:T(8,128)(2,1)}, bf16[512,2048]{1,0:T(8,128)(2,1)}, f32[24,256]{1,0:T(8,128)}) custom-call(bf16[8,160,2048]{2,1,0:T(8,128)(2,1)} %bitcast.111, bf16[8,160,512]{2,1,0:T(8,128)(2,1)} %bitcast.103, bf16[512,2048]{1,0:T(8,128)(2,1)} %copy-done.43, ...), custom_call_target="tpu_custom_call" | custom-call | flops 3355443200 | bytes 367001600 | tf_op jit(solution)/shard_map/pallas_call | solution.py:888
  1022.9 1.6 broadcast_in_dim.225
  1027.3 2.5 collective-permute-start.5
  1030.9 2.6 slice_convert_fusion
  1033.5 6.4 maximum_convert_fusion
  1041.1 8.2 copy.135
  1049.2 5.5 convert_element_type.456
  1055.6 8.9 collective-permute-done.4
  1066.2 2.5 convert_element_type.452
  1068.7 2.4 convert_element_type.455
  (299 shorter events, 70.3 us)
Async XLA Ops:
  7.2 18.6 %copy-start = (s32[1,4]{1,0:T(1,128)S(1)}, s32[1,4]{1,0:T(1,128)}, u32[]{:S(2)}) copy-start(s32[1,4]{1,0:T(1,128)} %param.17) | copy-start | bytes 52
  20.7 231.7 %copy-start.42 = (bf16[2048,18]{1,0:T(8,128)(2,1)}, bf16[2048,18]{1,0:T(8,128)(2,1)S(1)}, u32[]{:S(2)}) copy-start(bf16[2048,18]{1,0:T(8,128)(2,1)S(1)} %all_gather.3) | copy-start | bytes 221188
  20.7 4.9 copy-start.58
  20.7 225.0 %all-to-all-start = ((bf16[8,1408,256]{2,1,0:T(8,128)(2,1)}), bf16[8,1408,256]{2,1,0:T(8,128)(2,1)}, u32[]{:S(2)}, u32[]{:S(2)}) async-start(bf16[8,1408,256]{2,1,0:T(8,128)(2,1)} %param.29), calls=%async_computation | async-start | bytes 11534336 | tf_op jit(solution)/shard_map/all_to_all | solution.py:1184
  37.6 219.7 %copy-start.60 = (s32[512]{0:T(512)}, s32[512]{0:T(512)S(1)}, u32[]{:S(2)}) copy-start(s32[512]{0:T(512)S(1)} %get-tuple-element.195) | copy-start | bytes 6148
  37.6 219.7 %copy-start.63 = (s32[512]{0:T(512)}, s32[512]{0:T(512)S(1)}, u32[]{:S(2)}) copy-start(s32[512]{0:T(512)S(1)} %get-tuple-element.196) | copy-start | bytes 6148
  39.6 233.8 %copy-start.28 = (f32[512,128]{1,0:T(8,128)}, f32[512,128]{1,0:T(8,128)S(1)}, u32[]{:S(2)}) copy-start(f32[512,128]{1,0:T(8,128)S(1)} %get-tuple-element.83.tok_cos) | copy-start | bytes 786436
  245.7 182.0 %all-to-all-start.1 = ((bf16[8,2,256,1408]{3,2,1,0:T(8,128)(2,1)}), bf16[8,2,256,1408]{3,2,1,0:T(8,128)(2,1)}, u32[]{:S(2)}, u32[]{:S(2)}) async-start(bf16[8,2,256,1408]{3,2,1,0:T(8,128)(2,1)} %param.28), calls=%async_computation.1 | async-start | bytes 23068672 | tf_op jit(solution)/shard_map/all_to_all | solution.py:1184
  251.0 815.2 %reduce-scatter.2.cloned.1.call-start = ((), (), s32[]{:S(2)}) async-start(), calls=%async_computation.4 | async-start | bytes 18874368 | tf_op jit(solution)/shard_map/reduce_scatter | solution.py:1465
  253.5 6.8 copy-start.47
  254.4 5.8 copy-start.70
  254.4 5.8 copy-start.72
  255.1 5.1 copy-start.45
  257.4 47.1 %copy-start.3 = (bf16[128,2048]{1,0:T(8,128)(2,1)}, bf16[128,2048]{1,0:T(8,128)(2,1)S(1)}, u32[]{:S(2)}) copy-start(bf16[128,2048]{1,0:T(8,128)(2,1)S(1)} %get-tuple-element.244.x_here) | copy-start | bytes 1572868
  263.0 10.3 copy-start.15
  263.0 10.3 copy-start.17
  263.0 10.3 copy-start.19
  263.0 10.3 copy-start.25
  263.0 10.3 copy-start.30
  292.2 12.2 %copy-start.13 = (f32[1280,512]{1,0:T(8,128)}, f32[1280,512]{1,0:T(8,128)S(1)}, u32[]{:S(2)}) copy-start(f32[1280,512]{1,0:T(8,128)S(1)} %get-tuple-element.109) | copy-start | bytes 7864324
  292.2 12.2 %copy-start.10 = (bf16[1024,2048]{1,0:T(8,128)(2,1)S(1)}, bf16[1024,2048]{1,0:T(8,128)(2,1)}, u32[]{:S(2)}) copy-start(bf16[1024,2048]{1,0:T(8,128)(2,1)} %fusion.26.cot_hbm) | copy-start | bytes 12582916
  430.5 6.0 copy-start.68
  432.2 4.8 copy-start.71
  432.2 4.8 copy-start.73
  447.7 106.4 %copy-start.5 = (f32[128,2048]{1,0:T(8,128)S(1)}, f32[128,2048]{1,0:T(8,128)}, u32[]{:S(2)}) copy-start(f32[128,2048]{1,0:T(8,128)} %copy-done.4) | copy-start | bytes 3145732
  447.7 106.4 %copy-start.7 = (bf16[1024,512]{1,0:T(8,128)(2,1)S(1)}, bf16[1024,512]{1,0:T(8,128)(2,1)}, u32[]{:S(2)}) copy-start(bf16[1024,512]{1,0:T(8,128)(2,1)} %get-tuple-element.232.hit_1) | copy-start | bytes 3145732
  447.7 106.4 %copy-start.21 = (bf16[128,2048]{1,0:T(8,128)(2,1)S(1)}, bf16[128,2048]{1,0:T(8,128)(2,1)}, u32[]{:S(2)}) copy-start(bf16[128,2048]{1,0:T(8,128)(2,1)} %get-tuple-element.243.cot_here) | copy-start | bytes 1572868
  675.6 4.6 copy-start.27
  675.6 4.6 copy-start.33
  693.9 13.7 %copy-start.14 = (f32[1280,512]{1,0:T(8,128)S(1)}, f32[1280,512]{1,0:T(8,128)}, u32[]{:S(2)}) copy-start(f32[1280,512]{1,0:T(8,128)} %copy-done.13) | copy-start | bytes 7864324
  709.1 5.6 copy-start.34
  720.0 70.2 %collective-permute-start = (bf16[128,2048]{1,0:T(8,128)(2,1)}, bf16[128,2048]{1,0:T(8,128)(2,1)}, u32[]{:S(2)}, u32[]{:S(2)}) collective-permute-start(bf16[128,2048]{1,0:T(8,128)(2,1)} %get-tuple-element.205), channel_id=1, source_target_pairs={{0,1},{1,0},{2,3},{3,2},{4,5},{5,4},{6,7},{7,6},{8,9},{9,8},{10,11... | collective-permute-start | bytes 1572872 | tf_op jit(solution)/shard_map/ppermute | solution.py:1208
  721.0 69.2 %collective-permute-start.1 = (bf16[128,2048]{1,0:T(8,128)(2,1)}, bf16[128,2048]{1,0:T(8,128)(2,1)}, u32[]{:S(2)}, u32[]{:S(2)}) collective-permute-start(bf16[128,2048]{1,0:T(8,128)(2,1)} %get-tuple-element.207), channel_id=1, source_target_pairs={{0,2},{1,3},{2,0},{3,1},{4,6},{5,7},{6,4},{7,5},{8,10},{9,11},{10,... | collective-permute-start | bytes 1572872 | tf_op jit(solution)/shard_map/ppermute | solution.py:1208
  724.0 66.1 %collective-permute-start.2 = (bf16[128,2048]{1,0:T(8,128)(2,1)}, bf16[128,2048]{1,0:T(8,128)(2,1)}, u32[]{:S(2)}, u32[]{:S(2)}) collective-permute-start(bf16[128,2048]{1,0:T(8,128)(2,1)} %get-tuple-element.206), channel_id=1, source_target_pairs={{0,3},{1,2},{2,1},{3,0},{4,7},{5,6},{6,5},{7,4},{8,11},{9,10},{10,... | collective-permute-start | bytes 1572872 | tf_op jit(solution)/shard_map/ppermute | solution.py:1208
  727.7 8.5 copy-start.29
  727.7 108.7 %all-to-all-start.2 = ((bf16[8,256,1408]{2,1,0:T(8,128)(2,1)}), bf16[8,256,1408]{2,1,0:T(8,128)(2,1)}, u32[]{:S(2)}, u32[]{:S(2)}) async-start(bf16[8,256,1408]{2,1,0:T(8,128)(2,1)} %get-tuple-element.110), calls=%async_computation.2 | async-start | bytes 11534336 | tf_op jit(solution)/shard_map/all_to_all | solution.py:1184
  745.3 18.6 %copy-start.48 = (bf16[2,2048,512]{2,1,0:T(8,128)(2,1)S(1)}, bf16[2,2048,512]{2,1,0:T(8,128)(2,1)}, u32[]{:S(2)}) copy-start(bf16[2,2048,512]{2,1,0:T(8,128)(2,1)} %get-tuple-element.78) | copy-start | bytes 12582916
  763.8 17.3 %copy-start.23 = (bf16[512,512]{1,0:T(8,128)(2,1)}, bf16[512,512]{1,0:T(8,128)(2,1)S(1)}, u32[]{:S(2)}) copy-start(bf16[512,512]{1,0:T(8,128)(2,1)S(1)} %get-tuple-element.108) | copy-start | bytes 1572868
  776.0 5.1 copy-start.49
  782.5 5.9 copy-start.24
  1022.9 6.9 copy-start.50
  1025.4 29.3 %collective-permute-start.3 = (bf16[128,2048]{1,0:T(8,128)(2,1)S(1)}, bf16[128,2048]{1,0:T(8,128)(2,1)S(1)}, u32[]{:S(2)}, u32[]{:S(2)}) collective-permute-start(bf16[128,2048]{1,0:T(8,128)(2,1)S(1)} %get-tuple-element.202), channel_id=1, source_target_pairs={{0,1},{1,0},{2,3},{3,2},{4,5},{5,4},{6,7},{7,6},{8,9},{9,8},{10,11... | collective-permute-start | bytes 1572872 | tf_op jit(solution)/shard_map/ppermute | solution.py:1208
  1026.2 38.2 %collective-permute-start.4 = (bf16[128,2048]{1,0:T(8,128)(2,1)S(1)}, bf16[128,2048]{1,0:T(8,128)(2,1)S(1)}, u32[]{:S(2)}, u32[]{:S(2)}) collective-permute-start(bf16[128,2048]{1,0:T(8,128)(2,1)S(1)} %get-tuple-element.202), channel_id=1, source_target_pairs={{0,2},{1,3},{2,0},{3,1},{4,6},{5,7},{6,4},{7,5},{8,10},{9,11},{10,... | collective-permute-start | bytes 1572872 | tf_op jit(solution)/shard_map/ppermute | solution.py:1208
  1027.3 38.0 %collective-permute-start.5 = (bf16[128,2048]{1,0:T(8,128)(2,1)S(1)}, bf16[128,2048]{1,0:T(8,128)(2,1)S(1)}, u32[]{:S(2)}, u32[]{:S(2)}) collective-permute-start(bf16[128,2048]{1,0:T(8,128)(2,1)S(1)} %get-tuple-element.202), channel_id=1, source_target_pairs={{0,3},{1,2},{2,1},{3,0},{4,7},{5,6},{6,5},{7,4},{8,11},{9,10},{10,... | collective-permute-start | bytes 1572872 | tf_op jit(solution)/shard_map/ppermute | solution.py:1208
  1033.5 15.7 %slice-start.2 = ((s8[5767168]{0:T(1024)(128)(4,1)}), s8[4194304]{0:T(1024)(128)(4,1)S(1)}, s32[]{:S(2)}) async-start(s8[5767168]{0:T(1024)(128)(4,1)} %bitcast.117), calls=%async_computation.7 | async-start | bytes 8388608
  1041.1 8.2 slice-start.3
  1054.7 11.4 %copy-start.52 = (bf16[512,2048]{1,0:T(8,128)(2,1)S(1)}, bf16[512,2048]{1,0:T(8,128)(2,1)}, u32[]{:S(2)}) copy-start(bf16[512,2048]{1,0:T(8,128)(2,1)} %get-tuple-element.120) | copy-start | bytes 6291460
  1066.2 4.9 copy-start.1
  (41 other events, 72.6 us)
Sparse Core Ops, SparseCore 0:
  691.2 199.3 reduce-scatter.1

commit v4 on v3

--- a/solution.py
+++ b/solution.py
@@ -249,9 +249,7 @@
         scratch_shapes=[pltpu.VMEM((tok, HD), F32), pltpu.VMEM((tok, HD), F32)],
         compiler_params=pltpu.CompilerParams(vmem_limit_bytes=40 << 20),
         cost_estimate=pl.CostEstimate(
-            flops=10 * slots * tok * width,
-            bytes_accessed=slots * width * 8 + slots * tok * 2,
-            transcendentals=slots * tok * heads,
+            flops=0, bytes_accessed=slots * width, transcendentals=0
         ),
     )(q, k, v, bias, gate, *slot_tables, *tok_tables, grad_gated)
 
@@ -333,12 +331,32 @@
 
 def gather_kernel(axes, chunks, *refs):
     amount = len(axes)
-    sources, targets = refs[:amount], refs[amount : 2 * amount]
-    send_sem, recv_sem, own_sem = refs[2 * amount :]
+    sources, rows = refs[:amount], refs[amount]
+    targets, rows_out = refs[amount + 1 : 2 * amount + 1], refs[2 * amount + 1]
+    send_sem, recv_sem, own_sem, e_send, e_recv, z_send, z_recv = refs[2 * amount + 2 :]
+    count = z_send.shape[0] + 1
+    exchange_count = e_send.shape[0]
+    peers = tensor_peers(count)
     at = Square()
     me = 2 * at.chip + at.core
     far = 2 * at.chip_far + at.core
-    greet([{"dp": p} for p in (at.twin, at.near_x, at.near_y)])
+    greet(
+        [{"dp": partner(k)} for k in range(1, exchange_count)] + [{"tensor": p} for p in peers]
+    )
+    columns = share_rows(rows.shape[1] // count)
+    size = rows.shape[0] // exchange_count
+    moved = [
+        send_to(
+            rows.at[pl.ds(k * size, size), columns], rows_out.at[pl.ds(k * size, size), columns],
+            e_send.at[k], e_recv.at[k], partner(k),
+        )
+        for k in range(1, exchange_count)
+    ]
+    stay = pltpu.make_async_copy(
+        rows.at[pl.ds(0, size), columns], rows_out.at[pl.ds(0, size), columns], e_send.at[0]
+    )
+    for copy in (*moved, stay):
+        copy.start()
 
     def region(ref, axis, source, place, experts):
         size = source.shape[axis]
@@ -407,6 +425,19 @@
             moves[2]().start()
             moves[6]().start()
 
+        if i == 0:
+            stay.wait()
+            for copy in moved:
+                copy.wait_recv()
+            across = [
+                send_across(
+                    rows_out.at[:, columns], rows_out.at[:, columns], z_send.at[k], z_recv.at[k], p
+                )
+                for k, p in enumerate(peers)
+            ]
+            for copy in across:
+                copy.start()
+
     for i, first, count in plans:
 
         @pl.loop(0, count)
@@ -427,11 +458,13 @@
             for move in moves:
                 move().wait_send()
 
-    for copy in here:
+    for copy in (*here, *across):
         copy.wait()
-
-
-def gather_maps(arrays, axes, chunks):
+    for copy in moved:
+        copy.wait_send()
+
+
+def gather_maps(tensor_size, peers, arrays, axes, chunks, rows):
     units = sum(a.shape[0] // c for a, c in zip(arrays, chunks))
     shapes = [
         tuple(n * 8 if d == axis else n for d, n in enumerate(a.shape))
@@ -439,13 +472,16 @@
     ]
     return pl.pallas_call(
         functools.partial(gather_kernel, axes, chunks),
-        in_specs=[HBM] * len(arrays),
-        out_specs=[HBM] * len(arrays),
-        out_shape=[jax.ShapeDtypeStruct(shape, BF16) for shape in shapes],
-        scratch_shapes=[sems(units, 9), sems(units, 9), sems(len(arrays))],
+        in_specs=[HBM] * (len(arrays) + 1),
+        out_specs=[HBM] * (len(arrays) + 1),
+        out_shape=[jax.ShapeDtypeStruct(shape, BF16) for shape in (*shapes, rows.shape)],
+        scratch_shapes=[
+            sems(units, 9), sems(units, 9), sems(len(arrays)), sems(peers), sems(peers),
+            sems(tensor_size - 1), sems(tensor_size - 1),
+        ],
         compiler_params=pltpu.CompilerParams(collective_id=5, has_side_effects=True),
         cost_estimate=pl.CostEstimate(flops=0, bytes_accessed=600 << 20, transcendentals=0),
-    )(*arrays)
+    )(*arrays, rows)
 
 
 def deal(source, target, sems):
@@ -478,21 +514,28 @@
     return block[:, 0:1] + block[:, 1:2] + block[:, 2:3]
 
 
+def in_columns(column, lane):
+    high = column.astype(BF16).astype(F32)
+    mid = (column - high).astype(BF16).astype(F32)
+    return jnp.where(
+        lane == 0, high, jnp.where(lane == 1, mid, jnp.where(lane == 2, column - high - mid, 0.0))
+    ).astype(BF16)
+
+
 def hidden_kernel(
-    pick, rows, x_here, gain, cot_hbm,
-    hidden_out, mlp_in_out, cot_out,
-    parts, sent, got, z_send, z_recv, g_send, g_recv, e_send, e_recv,
+    pick, rows, x_here, gain, router, hot_0, hot_1, hit_0, hit_1, maps_hbm,
+    hidden_out, mlp_in_out, gates_out, x_out, maps_out,
+    parts, sent, got, z_send, z_recv, g_send, g_recv, d_send, d_recv,
 ):
     count = z_send.shape[0] + 1
     width = rows.shape[1]
     tokens = pick.shape[1]
     size = tokens // count
     peers = tensor_peers(count)
-    exchange_count = e_send.shape[0]
     greet(
-        [{"dp": partner(k)} for k in range(1, exchange_count)] + [{"tensor": p} for p in peers]
-    )
-    moves = spread(exchange_count, cot_hbm, cot_out, (e_send, e_recv))
+        [{"dp": partner(k)} for k in range(1, d_send.shape[0])] + [{"tensor": p} for p in peers]
+    )
+    dealt = deal(maps_hbm, maps_out, (d_send, d_recv))
 
     @pl.loop(0, width // 512)
     def _(i):
@@ -527,7 +570,22 @@
         copy.wait_send()
     for copy in more:
         copy.wait()
-    for copy in moves:
+
+    logits = dot(mlp_in_out[...], router[...])
+    picked = [jnp.sum(logits * hot[...], axis=1, keepdims=True) for hot in (hot_0, hot_1)]
+    highest = jnp.maximum(picked[0], picked[1])
+    raised = [jnp.exp(value - highest) for value in picked]
+    gates = [value / (raised[0] + raised[1]) for value in raised]
+    lane = lax.broadcasted_iota(jnp.int32, (tokens, HD), 1)
+    gates_out[...] = jnp.where(lane == 0, gates[0], jnp.where(lane == 1, gates[1], 0.0))
+    columns = [in_columns(gate, lane) for gate in gates]
+    x_out[:, width:] = (dot(hit_0[...], columns[0]) + dot(hit_1[...], columns[1])).astype(BF16)
+
+    @pl.loop(0, width // 512)
+    def _(i):
+        at = pl.ds(pl.multiple_of(i * 512, 512), 512)
+        x_out[:, at] = dot(hit_0[...] + hit_1[...], mlp_in_out[:, at]).astype(BF16)
+    for copy in dealt:
         copy.wait()
 
 
@@ -539,38 +597,43 @@
     return pltpu.SemaphoreType.DMA(shape)
 
 
-def hidden_step(tensor_size, peers, pick, rows, x_here, gain, cot_send):
+def hidden_step(tensor_size, pick, rows, x_here, gain, router, hots, hits, maps):
     tokens, width = pick.shape[1], rows.shape[1]
+    slots = hits[0].shape[0]
     size = tokens // tensor_size
     around = tensor_size - 1
     return pl.pallas_call(
         hidden_kernel,
-        in_specs=[VMEM, VMEM, VMEM, VMEM, HBM],
-        out_specs=[VMEM, VMEM, HBM],
+        in_specs=[VMEM] * 9 + [HBM],
+        out_specs=[VMEM] * 4 + [HBM],
         out_shape=[
             jax.ShapeDtypeStruct((size, width), F32),
             jax.ShapeDtypeStruct((tokens, width), BF16),
-            jax.ShapeDtypeStruct(cot_send.shape, BF16),
+            jax.ShapeDtypeStruct((tokens, HD), F32),
+            jax.ShapeDtypeStruct((slots, width + HD), BF16),
+            jax.ShapeDtypeStruct(maps.shape, BF16),
         ],
         scratch_shapes=[
             pltpu.VMEM((tokens, width), F32),
             pltpu.VMEM((tokens, width), BF16),
             pltpu.VMEM((around, size, width), BF16),
-            sems(around), sems(around), sems(around), sems(around), sems(peers), sems(peers),
+            sems(around), sems(around), sems(around), sems(around),
+            sems(maps.shape[0]), sems(maps.shape[0]),
         ],
         compiler_params=pltpu.CompilerParams(
-            collective_id=3, has_side_effects=True, vmem_limit_bytes=40 << 20
+            collective_id=3, has_side_effects=True, vmem_limit_bytes=48 << 20
         ),
         cost_estimate=pl.CostEstimate(
             flops=2 * pick.shape[0] * tokens * width, bytes_accessed=300 << 20, transcendentals=0
         ),
-    )(pick, rows, x_here, gain, cot_send)
+    )(pick, rows, x_here, gain, router, *hots, *hits, maps)
 
 
 def back_kernel(
-    back, pick, hit_0, hit_1, hidden, cot_here, gain, router, hots, rows_hbm, maps_hbm,
-    grad_out, pair_out, gain_out, hot_out, rows_out, maps_out,
-    parts, sent, got, z_send, z_recv, g_send, g_recv, e_send, e_recv, w_send, w_recv,
+    back, pick, hit_0, hit_1, hidden, cot_here, gain, router, hots, gates, rows_hbm, gate_hbm, up_hbm,
+    grad_out, pair_out, gain_out, hot_out, mixed_out, gate_maps, up_maps,
+    parts, sent, got, z_send, z_recv, g_send, g_recv, e_send, e_recv, w_send, w_recv, u_send, u_recv,
+    rows_in, columns_here, mlp_got, m_send, m_recv, own,
 ):
     count = z_send.shape[0] + 1
     width = back.shape[1] - HD
@@ -581,6 +644,9 @@
     greet(
         [{"dp": partner(k)} for k in range(1, exchange_count)] + [{"tensor": p} for p in peers]
     )
+    moves = spread(exchange_count, rows_hbm, rows_in, (e_send, e_recv))
+    dealt = deal(gate_hbm, gate_maps, (w_send, w_recv))
+    dealt += deal(up_hbm, up_maps, (u_send, u_recv))
 
     @pl.loop(0, width // 512)
     def _(i):
@@ -601,8 +667,6 @@
     ]
     for copy in copies:
         copy.start()
-    moves = spread(exchange_count, rows_hbm, rows_out, (e_send, e_recv))
-    dealt = deal(maps_hbm, maps_out, (w_send, w_recv))
     here = share_rows(size)
     total = parts[here, :]
     for k, copy in enumerate(copies):
@@ -621,17 +685,37 @@
     ]
     for copy in more:
         copy.start()
+    for copy in moves:
+        copy.wait()
+    matrix = hit_0[...].astype(F32) * gates[0:1, :] + hit_1[...].astype(F32) * gates[1:2, :]
+    high = matrix.astype(BF16)
+    low = (matrix - high.astype(F32)).astype(BF16)
+    columns_here[...] = (dot_tn(high, rows_in[...]) + dot_tn(low, rows_in[...])).astype(BF16)
+    columns = share_rows(width // count)
+    turned = [
+        send_across(
+            columns_here.at[rows_of(p, size)], mlp_got.at[:, columns], m_send.at[k], m_recv.at[k],
+            p,
+        )
+        for k, p in enumerate(peers)
+    ]
+    turned.append(
+        pltpu.make_async_copy(columns_here.at[here], mlp_got.at[:, columns], own.at[0])
+    )
+    for copy in turned:
+        copy.start()
+    for copy in turned:
+        copy.wait()
+    mixed_out[...] = (hidden[...] + mlp_got[...].astype(F32)).astype(BF16)
     for copy in copies:
         copy.wait_send()
-    for copy in more:
+    for copy in (*more, *dealt):
         copy.wait()
-    for copy in (*moves, *dealt):
-        copy.wait()
 
 
 def back_step(
-    tensor_size, peers, back, pick, hits, hidden, cot_here, gain, router, hots, rows_send,
-    maps,
+    tensor_size, peers, back, pick, hits, hidden, cot_here, gain, router, hots, gates,
+    rows_send, gate_maps, up_maps,
 ):
     tokens, width = pick.shape[1], back.shape[1] - HD
     size = tokens // tensor_size
@@ -639,22 +723,27 @@
     wide = width + 2 * HD
     return pl.pallas_call(
         back_kernel,
-        in_specs=[VMEM] * 9 + [HBM] * 2,
-        out_specs=[VMEM] * 4 + [HBM] * 2,
+        in_specs=[VMEM] * 10 + [HBM] * 3,
+        out_specs=[VMEM] * 5 + [HBM] * 2,
         out_shape=[
             jax.ShapeDtypeStruct((size, width), F32),
             jax.ShapeDtypeStruct((tokens, width), BF16),
             jax.ShapeDtypeStruct((1, width), F32),
             jax.ShapeDtypeStruct((size, HD), BF16),
-            jax.ShapeDtypeStruct(rows_send.shape, BF16),
-            jax.ShapeDtypeStruct(maps.shape, BF16),
+            jax.ShapeDtypeStruct((size, width), BF16),
+            jax.ShapeDtypeStruct(gate_maps.shape, BF16),
+            jax.ShapeDtypeStruct(up_maps.shape, BF16),
         ],
         scratch_shapes=[
             pltpu.VMEM((tokens, wide), F32),
             pltpu.VMEM((tokens, wide), BF16),
             pltpu.VMEM((around, size, wide), BF16),
             sems(around), sems(around), sems(around), sems(around), sems(peers), sems(peers),
-            sems(peers), sems(peers),
+            sems(peers), sems(peers), sems(peers), sems(peers),
+            pltpu.VMEM(rows_send.shape, BF16),
+            pltpu.VMEM((tokens, width // tensor_size), BF16),
+            pltpu.VMEM((size, width), BF16),
+            sems(around), sems(around), sems(1),
         ],
         compiler_params=pltpu.CompilerParams(
             collective_id=4, has_side_effects=True, vmem_limit_bytes=40 << 20
@@ -662,7 +751,7 @@
         cost_estimate=pl.CostEstimate(
             flops=2 * pick.shape[0] * tokens * width, bytes_accessed=300 << 20, transcendentals=0
         ),
-    )(back, pick, hits[0], hits[1], hidden, cot_here, gain, router, hots, rows_send, maps)
+    )(back, pick, hits[0], hits[1], hidden, cot_here, gain, router, hots, gates, rows_send, gate_maps, up_maps)
 
 
 GIVE = 4
@@ -670,14 +759,14 @@
 
 
 def final_kernel(
-    routed_hbm, grad_q, normed, grad_kv, part_hbm, maps_hbm,
-    grad_hidden, x_here, gain, router, hots, small,
-    out, maps_out, tokens_out, small_out,
+    routed_hbm, grad_q, normed, grad_kv, part_hbm,
+    grad_hidden, x_here, gain, router, hots, small, mixed_here,
+    out, tokens_out, small_out, mixed_out,
     give, keep, twin_in, far_in, near_in, routed, got_part, tokens_here,
     twin_send, twin_recv, far_send, far_recv, near_send, near_recv, load, own,
     p_send, p_recv, t_send, t_recv,
     hot_here, small_all, small_in, small_sum, small_got,
-    s_send, s_recv, w_send, w_recv, d_send, d_recv,
+    s_send, s_recv, w_send, w_recv, a_send, a_recv,
 ):
     at = Square()
     experts = grad_q.shape[0]
@@ -702,9 +791,13 @@
         send_across(part_hbm.at[rows_of(p, share)], got_part.at[k], p_send.at[k], p_recv.at[k], p)
         for k, p in enumerate(peers)
     ]
-    for copy in part_copies:
+    mixed_copies = [
+        send_across(mixed_here, mixed_out.at[here], a_send.at[k], a_recv.at[k], p)
+        for k, p in enumerate(peers)
+    ]
+    mixed_copies.append(pltpu.make_async_copy(mixed_here, mixed_out.at[here], own.at[2]))
+    for copy in (*part_copies, *mixed_copies):
         copy.start()
-    dealt = deal(maps_hbm, maps_out, (d_send, d_recv))
 
     def to_twin(u):
         slot = lax.rem(u, GIVE)
@@ -870,13 +963,13 @@
     small_out[...] = block
     for copy in (*part_copies, *small_copies, *last_copies):
         copy.wait_send()
-    for copy in (*token_copies, *dealt, kept):
+    for copy in (*token_copies, *mixed_copies, kept):
         copy.wait()
 
 
 def final_step(
-    tensor_size, routed, grad_q, normed, grad_kv, part, maps,
-    grad_hidden, x_here, gain, router, hots, small,
+    tensor_size, routed, grad_q, normed, grad_kv, part, grad_hidden, x_here, gain,
+    router, hots, small, mixed_here,
 ):
     experts, rows, width = routed.shape
     columns = grad_q.shape[2]
@@ -887,13 +980,13 @@
     around = tensor_size - 1
     return pl.pallas_call(
         final_kernel,
-        in_specs=[HBM, VMEM, VMEM, VMEM, HBM, HBM] + [VMEM] * 6,
-        out_specs=[VMEM, HBM, HBM, VMEM],
+        in_specs=[HBM, VMEM, VMEM, VMEM, HBM] + [VMEM] * 7,
+        out_specs=[VMEM, HBM, VMEM, HBM],
         out_shape=[
             jax.ShapeDtypeStruct((units, size, columns), BF16),
-            jax.ShapeDtypeStruct(maps.shape, BF16),
             jax.ShapeDtypeStruct((tokens, width), BF16),
             jax.ShapeDtypeStruct((3 * HALF_SMALL, size), F32),
+            jax.ShapeDtypeStruct((tokens, width), BF16),
         ],
         scratch_shapes=[
             pltpu.VMEM((GIVE, 4, size, columns), BF16),
@@ -905,27 +998,49 @@
             pltpu.VMEM((tensor_size, share, wide), BF16),
             pltpu.VMEM((share, width), BF16),
             sems(GIVE), sems(units), sems(units, 2), sems(units, 2), sems(units, 2),
-            sems(units, 2), sems(2), sems(2),
+            sems(units, 2), sems(2), sems(3),
             sems(around), sems(around), sems(around), sems(around),
             pltpu.VMEM((share, HD), BF16),
             pltpu.VMEM((3 * HALF_SMALL, width), F32),
             pltpu.VMEM((8, 3 * HALF_SMALL, size), F32),
             pltpu.VMEM((3 * HALF_SMALL, size), F32),
             pltpu.VMEM((around, 3 * HALF_SMALL, size), F32),
-            sems(8), sems(8), sems(around), sems(around), sems(8), sems(8),
+            sems(8), sems(8), sems(around), sems(around), sems(around), sems(around),
         ],
         compiler_params=pltpu.CompilerParams(
             collective_id=1, has_side_effects=True, vmem_limit_bytes=60 << 20
         ),
+        cost_estimate=pl.CostEstimate(flops=0, bytes_accessed=1 << 20, transcendentals=0),
+    )(
+        routed, grad_q, normed, grad_kv, part, grad_hidden, x_here, gain, router, hots, small,
+        mixed_here,
+    )
+
+
+def widen_kernel(first, second, third, both_out, third_out):
+    both_out[:, 0] = first[...].astype(F32)
+    both_out[:, 1] = second[...].astype(F32)
+    third_out[...] = third[...].astype(F32)
+
+
+def widen(first, second, third):
+    experts, rows, columns = first.shape
+    narrow = pl.BlockSpec((1, rows, columns), lambda e: (e, 0, 0))
+    turned = pl.BlockSpec((1,) + third.shape[1:], lambda e: (e, 0, 0))
+    return pl.pallas_call(
+        widen_kernel,
+        grid=(experts,),
+        in_specs=[narrow, narrow, turned],
+        out_specs=[pl.BlockSpec((1, 2, rows, columns), lambda e: (e, 0, 0, 0)), turned],
+        out_shape=[
+            jax.ShapeDtypeStruct((experts, 2, rows, columns), F32),
+            jax.ShapeDtypeStruct(third.shape, F32),
+        ],
+        compiler_params=pltpu.CompilerParams(vmem_limit_bytes=32 << 20),
         cost_estimate=pl.CostEstimate(
-            flops=2 * units * rows * width * columns,
-            bytes_accessed=350 << 20,
-            transcendentals=0,
+            flops=0, bytes_accessed=6 * (2 * first.size + third.size), transcendentals=0
         ),
-    )(
-        routed, grad_q, normed, grad_kv, part, maps,
-        grad_hidden, x_here, gain, router, hots, small,
-    )
+    )(first, second, third)
 
 
 def partner(k):
@@ -937,10 +1052,10 @@
 
 
 def expert_kernel(
-    x_ref, cot_hbm, gate_up_hbm, down_hbm,
+    x_hbm, cot_hbm, gate_up_hbm, down_hbm, rest_hbm,
     back_out, rows_out, grad_gate_hbm, grad_up_hbm, grad_down_hbm,
     x_all, g_all, w_gate, w_up, w_down, act, grads, back, product, stage_up, stage_down,
-    x_send, x_recv, b_send, b_recv, load, up_sem, down_sem,
+    rows_here, rows_got, x_send, x_recv, b_send, b_recv, load, up_sem, down_sem, r_send, r_recv,
 ):
     peers = x_send.shape[0]
     slots, wide = x_all.shape
@@ -953,9 +1068,16 @@
     tail = hidden - whole_steps * step
 
     per = width // peers
+    first = down_hbm.shape[1]
     loads = [
         pltpu.make_async_copy(cot_hbm, g_all, load.at[0]),
-        pltpu.make_async_copy(down_hbm, w_down, load.at[1]),
+        pltpu.make_async_copy(down_hbm, w_down.at[:, pl.ds(0, first)], load.at[1]),
+        pltpu.make_async_copy(
+            rest_hbm, w_down.at[:, pl.ds(first, hidden - first)], load.at[3 + 2 * peers]
+        ),
+        pltpu.make_async_copy(
+            x_hbm.at[pl.ds(0, size)], x_all.at[pl.ds(0, size)], load.at[2 + 2 * peers]
+        ),
     ]
     for j in range(peers):
         for g, target in enumerate((w_gate, w_up)):
@@ -967,19 +1089,16 @@
     for copy in loads:
         copy.start()
 
-    barrier = pltpu.get_barrier_semaphore()
-    for k in range(1, peers):
-        pl.semaphore_signal(
-            barrier, inc=1, device_id={"dp": partner(k)}, device_id_type=pl.DeviceIdType.MESH
-        )
-    pl.semaphore_wait(barrier, peers - 1)
+    around = tensor_peers(r_send.shape[0] + 1)
+    share = width // (len(around) + 1)
+    greet([{"dp": partner(k)} for k in range(1, peers)] + [{"tensor": p} for p in around])
 
     def block(k):
         return pl.ds(pl.multiple_of(k * size, size), size)
 
     def send_x(k):
         return send_to(
-            x_ref.at[block(k)], x_all.at[block(k)], x_send.at[k], x_recv.at[k], partner(k)
+            x_hbm.at[block(k)], x_all.at[block(k)], x_send.at[k], x_recv.at[k], partner(k)
         )
 
     def send_back(k):
@@ -989,9 +1108,15 @@
 
     for k in (1, 2, 4, 3, 5):
         send_x(k).start()
-    x_all[0:size, :] = x_ref[0:size, :]
     for copy in loads:
         copy.wait()
+
+    def send_rows(k, group):
+        rows = rows_of(group, pair)
+        return send_across(
+            rows_here.at[rows, rows_of(around[k], share)], rows_got.at[k, rows],
+            r_send.at[k, group], r_recv.at[k, group], around[k],
+        )
 
     @pl.loop(0, peers // 2)
     def _(group):
@@ -1043,12 +1168,9 @@
             ).astype(BF16)
 
         total = jnp.sum(product[...], axis=1, keepdims=True)
-        high = total.astype(BF16).astype(F32)
-        mid = (total - high).astype(BF16).astype(F32)
-        lane = lax.broadcasted_iota(jnp.int32, (pair, HD), 1)
-        back[rows, width:] = jnp.where(
-            lane == 0, high, jnp.where(lane == 1, mid, jnp.where(lane == 2, total - high - mid, 0.0))
-        ).astype(BF16)
+        back[rows, width:] = in_columns(
+            total, lax.broadcasted_iota(jnp.int32, (pair, HD), 1)
+        )
 
         @pl.when(group == 0)
         def _():
@@ -1061,6 +1183,10 @@
             send_back(2 * group).start()
 
         send_back(2 * group + 1).start()
+        for j in range(peers):
+            rows_here[rows, j * per : (j + 1) * per] = dot(act[rows, :], w_down[j]).astype(BF16)
+        for k in range(len(around)):
+            send_rows(k, group).start()
 
     def store_up(j, slot):
         return (
@@ -1085,7 +1211,6 @@
         stage_up[slot] = dot_tn(x_all[:, at], grads[...]).astype(BF16)
         for copy in store_up(j, slot):
             copy.start()
-        rows_out[:, at] = dot(act[...], w_down[j]).astype(BF16)
 
     def store_down(start, amount, slot):
         return pltpu.make_async_copy(
@@ -1119,25 +1244,36 @@
     for j in (peers - 2, peers - 1):
         for copy in store_up(j, j % 2):
             copy.wait()
+
+    @pl.loop(0, peers // 2)
+    def _(group):
+        rows = rows_of(group, pair)
+        total = rows_here[rows, share_rows(share)].astype(F32)
+        for k in range(len(around)):
+            send_rows(k, group).wait()
+            total = total + rows_got[k, rows, :].astype(F32)
+        rows_out[rows, :] = total.astype(BF16)
+
     for k in range(1, peers):
         send_x(k).wait_send()
         send_back(k).wait()
 
 
-def expert_step(x_rows, cot_rows, up_slices, down_slices):
+def expert_step(tensor_size, x_rows, cot_rows, up_slices, down_slices, down_rest):
     slots, wide = x_rows.shape
     width = wide - HD
     peers, hidden, per = down_slices.shape
+    hidden += down_rest.shape[1]
     vmem = pl.BlockSpec(memory_space=pltpu.VMEM)
     hbm = pl.BlockSpec(memory_space=pl.ANY)
     step = 256
     return pl.pallas_call(
         expert_kernel,
-        in_specs=[vmem, hbm, hbm, hbm],
+        in_specs=[hbm] * 5,
         out_specs=[vmem, vmem, hbm, hbm, hbm],
         out_shape=[
             jax.ShapeDtypeStruct((slots, wide), BF16),
-            jax.ShapeDtypeStruct((slots, width), BF16),
+            jax.ShapeDtypeStruct((slots, width // tensor_size), BF16),
             jax.ShapeDtypeStruct((peers, per, hidden), BF16),
             jax.ShapeDtypeStruct((peers, per, hidden), BF16),
             jax.ShapeDtypeStruct((peers, hidden, per), BF16),
@@ -1154,13 +1290,14 @@
             pltpu.VMEM((2 * slots // peers, HD), F32),
             pltpu.VMEM((2, per, 2 * hidden), BF16),
             pltpu.VMEM((2, peers, step, per), BF16),
+            pltpu.VMEM((slots, width), BF16),
+            pltpu.VMEM((tensor_size - 1, slots, width // tensor_size), BF16),
             pltpu.SemaphoreType.DMA((peers,)),
             pltpu.SemaphoreType.DMA((peers,)),
             pltpu.SemaphoreType.DMA((peers,)),
             pltpu.SemaphoreType.DMA((peers,)),
-            pltpu.SemaphoreType.DMA((2 + 2 * peers,)),
-            pltpu.SemaphoreType.DMA((2, 2)),
-            pltpu.SemaphoreType.DMA((2,)),
+            sems(4 + 2 * peers), sems(2, 2), sems(2),
+            sems(tensor_size - 1, peers // 2), sems(tensor_size - 1, peers // 2),
         ],
         compiler_params=pltpu.CompilerParams(
             collective_id=2, has_side_effects=True, vmem_limit_bytes=60 << 20
@@ -1168,7 +1305,7 @@
         cost_estimate=pl.CostEstimate(
             flops=18 * slots * width * hidden, bytes_accessed=300 << 20, transcendentals=0
         ),
-    )(x_rows, cot_rows, up_slices, down_slices)
+    )(x_rows, cot_rows, up_slices, down_slices, down_rest)
 
 
 class Movers:
@@ -1344,7 +1481,8 @@
     allowed = reach & (token_index[None, :] <= slot_token[:, None]) & slot_filled[:, None]
     bias = jnp.where(allowed, 0.0, NEGATIVE).astype(BF16)
 
-    down_slices = movers.fetch(down_weight)
+    early = down_weight.shape[1] // 2 if fast else down_weight.shape[1]
+    down_slices = movers.fetch(down_weight[:, :early])
     cot_send = dot(mlp_pick, cotangent, BF16)
 
     inputs = tokens.astype(F32)
@@ -1354,14 +1492,21 @@
     att_gate_slots = to_slots(att_hits, att_gates)[:, None]
     routed = dot(att_pick, normed, BF16).reshape(att_experts, att_cap, model_width)
     if fast:
+        mlp_bits = tuple(hit.astype(BF16) for hit in mlp_hits)
+        expert_lanes = [
+            (expert_routes[:, k : k + 1] == jnp.arange(HD, dtype=jnp.int32)[None, :]).astype(F32)
+            for k in range(TOPK)
+        ]
         keyval_weight, query_weight, output_weight, *before = tie(
             (keyval_weight, query_weight, output_weight, routed, cot_send, bias, att_gate_slots)
-            + slot_tables + tok_tables
+            + slot_tables + tok_tables + mlp_bits + tuple(expert_lanes)
         )
         routed, cot_send, bias, att_gate_slots = before[:4]
         slot_tables, tok_tables = before[4:6], before[6:8]
-        keyval_full, query_full, output_full = gather_maps(
-            (keyval_weight, query_weight, output_weight), (1, 1, 2), (2, 2, 2)
+        mlp_bits, expert_lanes = before[8:10], before[10:12]
+        keyval_full, query_full, output_full, cot_rows = gather_maps(
+            tensor_size, mlp_experts,
+            (keyval_weight, query_weight, output_weight), (1, 1, 2), (2, 2, 2), cot_send,
         )
     else:
         keyval_full = lax.all_gather(keyval_weight, "dp", axis=1, tiled=True)
@@ -1398,37 +1543,45 @@
         return jnp.pad(router, ((0, 0), (0, HD - router.shape[1])))
 
     if fast:
-        hidden, mlp_in, cot_rows = hidden_step(
-            tensor_size, mlp_experts, att_pick, att_rows, share(tokens), gain_mlp_full[None],
-            cot_send,
-        )
+        hidden, mlp_in, mlp_gates, expert_in, down_rest = hidden_step(
+            tensor_size, att_pick, att_rows, share(tokens), gain_mlp_full[None],
+            padded(router_mlp), expert_lanes, mlp_bits, down_weight[:, early:],
+        )
+        mlp_gates = mlp_gates[:, :TOPK]
     else:
         hidden = share(inputs) + movers.reduce_rows(dot_tn(att_pick, att_rows))
         mlp_in = movers.gather_rows((norm_forward(hidden)[0] * gain_mlp_full).astype(BF16))
         cot_rows = movers.exchange(cot_send)
-    mlp_in, up_slices, cot_rows = tie((mlp_in, up_slices, cot_rows))
-    mlp_gates = picked_softmax(dot(mlp_in, router_mlp), expert_routes)
-    mlp_gate_slots = to_slots(mlp_hits, mlp_gates)[:, None]
-    expert_in = with_column(dot(mlp_pick, mlp_in, BF16), mlp_gate_slots)
+        mlp_gates = picked_softmax(dot(mlp_in, router_mlp), expert_routes)
+        expert_in = with_column(
+            dot(mlp_pick, mlp_in, BF16), to_slots(mlp_hits, mlp_gates)[:, None]
+        )
+    expert_in, up_slices = tie((expert_in, up_slices))
 
     if fast:
-        back = expert_step(expert_in, cot_rows, up_slices, down_slices)
+        back = expert_step(
+            tensor_size, expert_in, cot_rows, up_slices, down_slices, down_rest
+        )
     else:
         back = expert_plain(movers, expert_in, cot_rows, up_slices, down_slices)
     grad_in_slots, expert_out, grad_gate_w, grad_up_w, grad_down_w = back
 
     if fast:
-        grad_hidden, grad_att_pair, grad_gain_mlp, grad_mlp_logits, out_slots, grad_gate_w = back_step(
+        (
+            grad_hidden, grad_att_pair, grad_gain_mlp, grad_mlp_logits, mixed, grad_gate_w,
+            grad_up_w,
+        ) = back_step(
             tensor_size, mlp_experts, grad_in_slots, mlp_pick,
-            [hit.astype(BF16) for hit in mlp_hits], hidden, share(cotangent),
+            mlp_bits, hidden, share(cotangent),
             gain_mlp_full[None], padded(router_mlp),
-            hots(mlp_gates, expert_routes, mlp_experts), expert_out, grad_gate_w,
+            hots(mlp_gates, expert_routes, mlp_experts), mlp_gates.T, expert_out, grad_gate_w, grad_up_w,
         )
         grad_gain_mlp = grad_gain_mlp[0]
         grad_mlp_logits = grad_mlp_logits[:, :mlp_experts]
     else:
         out_slots = movers.exchange(expert_out)
         grad_gate_w = movers.give_back(grad_gate_w)
+        grad_up_w = movers.give_back(grad_up_w)
         grad_in_slots, gate_times_grad = without_column(grad_in_slots)
         mlp_products = movers.reduce_rows(to_pairs(mlp_hits, gate_times_grad[:, 0]), F32)
         grad_mlp_in = movers.reduce_rows(dot_tn(mlp_pick, grad_in_slots))
@@ -1442,17 +1595,17 @@
         )
         grad_hidden = share(cotangent).astype(F32) + grad_hidden_norm
         grad_att_pair = movers.gather_rows(grad_hidden)
-    grad_att_pair, grad_up_w = tie((grad_att_pair, grad_up_w))
-    grad_up_w = movers.give_back(grad_up_w)
+        gate_matrix = sum(
+            jnp.where(mlp_hits[k], mlp_gates[:, k][None, :], 0.0) for k in range(TOPK)
+        )
+        matrix_high = gate_matrix.astype(BF16)
+        matrix_low = (gate_matrix - matrix_high.astype(F32)).astype(BF16)
+        mlp_part = (dot_tn(matrix_high, out_slots) + dot_tn(matrix_low, out_slots)).astype(BF16)
+        mixed = movers.gather_rows(hidden + movers.reduce_rows(mlp_part))
     grad_router_mlp = dot_tn(share(mlp_in), grad_mlp_logits)
 
-    gate_matrix = sum(
-        jnp.where(mlp_hits[k], mlp_gates[:, k][None, :], 0.0) for k in range(TOPK)
-    )
-    matrix_high = gate_matrix.astype(BF16)
-    matrix_low = (gate_matrix - matrix_high.astype(F32)).astype(BF16)
-    mlp_part = (dot_tn(matrix_high, out_slots) + dot_tn(matrix_low, out_slots)).astype(BF16)
-    mlp_sum = movers.reduce_rows(mlp_part)
+    grad_att_pair, grad_down_w = tie((grad_att_pair, grad_down_w))
+    grad_down_w = movers.give_back(grad_down_w)
 
     grad_att_rows = dot(att_pick, grad_att_pair, BF16).reshape(att_experts, att_cap, model_width)
     grad_output_w = jnp.einsum(
@@ -1481,8 +1634,6 @@
     normed_part = with_column(normed_part.astype(BF16), att_products[:, :1])
     normed_part = with_column(normed_part, att_products[:, 1:])
     grad_kv = jnp.stack([grad_k, grad_v])
-    normed_part, grad_up_w, mlp_sum = tie((normed_part, grad_up_w, mlp_sum))
-    mixed = movers.gather_rows(hidden + mlp_sum)
     if fast:
         small = jnp.concatenate(
             [
@@ -1493,10 +1644,10 @@
             ],
             axis=0,
         )
-        map_sums, grad_down_w, grad_tokens, small_grads = final_step(
-            tensor_size, routed, grad_query_slots, normed, grad_kv, normed_part, grad_down_w,
+        map_sums, grad_tokens, small_grads, mixed = final_step(
+            tensor_size, routed, grad_query_slots, normed, grad_kv, normed_part,
             grad_hidden, share(tokens), gain_attn_full[None], padded(router_att),
-            hots(att_gates, attention_routes, att_experts), small,
+            hots(att_gates, attention_routes, att_experts), small, mixed,
         )
         small_grads = jnp.concatenate([small_grads[:2], small_grads[HALF_SMALL:]], axis=0).T
         grad_query_out, grad_keyval_out = map_sums[:att_experts], map_sums[att_experts:]
@@ -1507,7 +1658,6 @@
         grad_keyval_w = jnp.stack([dot_tn(normed, grad, BF16) for grad in (grad_k, grad_v)])
         grad_query_out = lax.psum_scatter(grad_query_w, "dp", scatter_dimension=1, tiled=True)
         grad_keyval_out = lax.psum_scatter(grad_keyval_w, "dp", scatter_dimension=1, tiled=True)
-        grad_down_w = movers.give_back(grad_down_w)
         grad_normed = movers.reduce_rows(normed_part[:, :model_width])
         grad_att_logits = router_backward(
             share(att_gates), movers.reduce_rows(att_products, F32), share(attention_routes),
@@ -1526,8 +1676,9 @@
         small_grads = lax.psum(
             lax.psum_scatter(small_grads, "dp", scatter_dimension=0, tiled=True), "tensor"
         )
-    grad_tokens, grad_output_out = tie((grad_tokens, grad_output_out))
+    grad_tokens, grad_output_out, grad_down_w = tie((grad_tokens, grad_output_out, grad_down_w))
     grad_tokens = grad_tokens.astype(F32)
+    grad_up_w, grad_down_w = widen(grad_gate_w, grad_up_w, grad_down_w)
     return (
         mixed,
         grad_tokens,
@@ -1538,8 +1689,8 @@
         small_grads[:, 2 : 2 + att_experts],
         small_grads[:, 1],
         small_grads[:, 2 + att_experts :],
-        jnp.stack([grad_gate_w.astype(F32), grad_up_w.astype(F32)], axis=1),
-        grad_down_w.astype(F32),
+        grad_up_w,
+        grad_down_w,
     )
 
 

time: 1090 us -> 995 us (0.913)
  waiting for transfers between devices: 53.3 us -> 0.03 us
  other arithmetic: 50.1 us -> 35.2 us
  matrix products: 102 us -> 89.2 us
    all_to_all x3, waiting for transfers between devices: 44.3 us -> 0.01 us  [swap(): lax.all_to_all(blocks, 'dp', 0, 0, axis_index_groups=self.groups, tiled=T...]
    pallas_call x4 -> x5, Pallas kernels: 527 us -> 550 us  [the longest x1 171 us: final_step(): pl.pallas_call(final_kernel, in_specs=[HBM, VMEM, VMEM, VMEM, HBM] + [VME...]
    pallas_call x1, Pallas kernels: 190 us -> 173 us  [gather_maps(): pl.pallas_call(functools.partial(gather_kernel, axes, chunks), in_specs=[...]
    dot_general x9 -> x7, matrix products: 26.7 us -> 21.2 us  [dot(): return jnp.dot(a, b, preferred_element_type=out)]
  transfers between devices with their start and end apart: 10 -> 4, of which waited for: 2 -> 0; matrix products, arithmetic and copies ran while one was open for 14% -> 13% of each run, Pallas kernels for 49% -> 49%
where the time goes in v4:
time: 995 us; the launch traced here: 985 us
  Pallas kernels  758 us (76%)
  matrix products  89.2 us (9%)
  local copies, waits for them, and re-layouts  61.7 us (6%)
  other arithmetic  35.2 us (4%)
  between operations  15.5 us (2%)
  starting transfers between devices  14.8 us (1%)
  blocking collectives  11.3 us (1%)
    pallas_call x1, Pallas kernels, gather_maps(): pl.pallas_call(functools.partial(gather_kernel, axes, chunks), in_specs=[...  173 us
    pallas_call x1, Pallas kernels, final_step(): pl.pallas_call(final_kernel, in_specs=[HBM, VMEM, VMEM, VMEM, HBM] + [VME...  171 us
    pallas_call x1, Pallas kernels, back_step(): pl.pallas_call(back_kernel, in_specs=[VMEM] * 10 + [HBM] * 3, out_specs=[...  147 us
    pallas_call x1, Pallas kernels, expert_step(): pl.pallas_call(expert_kernel, in_specs=[hbm] * 5, out_specs=[vmem, vmem,...  110 us
    pallas_call x1, Pallas kernels, hidden_step(): pl.pallas_call(hidden_kernel, in_specs=[VMEM] * 9 + [HBM], out_specs=[VME...  109 us
    unnamed x162, local copies, waits for them, and re-layouts  27.4 us
    dot_general x7, matrix products, dot(): return jnp.dot(a, b, preferred_element_type=out)  21.2 us
  transfers between devices with their start and end apart: 4, of which 0 were waited for; matrix products, arithmetic and copies ran while one was open for 13% of the time, Pallas kernels for 49%

profile of v4, /device:TPU:0, one launch (start us, length us, event | category | flops | bytes accessed | tf_op | source)
XLA Modules:
  0.0 985.4 jit_solution(12730584111734204878)
XLA Ops:
  9.4 11.3 %all_gather.3 = bf16[2048,18]{1,0:T(8,128)(2,1)S(1)} all-gather(bf16[256,18]{1,0:T(8,128)(2,1)S(1)} %copy.104), channel_id=1, replica_groups=mesh['dp'=8,'tensor'=4] {'dp'}, dimensions={0}, use_global_device_ids=true | all-gather | bytes 82944 | tf_op jit(solution)/shard_map/all_gather | solution.py:1432
  20.7 5.7 fusion.74
  26.4 4.6 all-to-all-start
  33.2 1.7 fusion.32
  39.7 1.3 copy-done.45
  48.2 2.5 select_convert_fusion.bias
  50.7 2.4 fusion.38
  53.1 1.5 pad_maximum_fusion.2
  54.6 2.1 fusion.21
  56.6 4.4 fusion.22.refs_3_
  61.0 4.6 fusion.34
  65.6 173.1 %shard_map.230 = (bf16[2,2048,512]{2,1,0:T(8,128)(2,1)}, bf16[8,2048,512]{2,1,0:T(8,128)(2,1)}, bf16[8,512,2048]{2,1,0:T(8,128)(2,1)}, bf16[1024,2048]{1,0:T(8,128)(2,1)}) custom-call(bf16[2,256,512]{2,1,0:T(8,128)(2,1)} %refs_0_, bf16[8,256,512]{2,1,0:T(8,128)(2,1)} %refs_1_, bf16[8,512,256]{2,1,0:T(8,128)(2,1)} %refs_2_, bf16[1024,2048]{1,0:T(8,128)(2,1)} %fusion.22.refs_3_), custom_call_target="tpu_custom_call" | custom-call | bytes 629145600 | tf_op jit(solution)/shard_map/pallas_call | solution.py:473
  238.7 5.3 all-to-all-start.1
  247.7 2.3 constant_dynamic-slice_fusion.4
  249.9 3.1 fusion.12
  253.1 1.2 fusion.8
  254.6 10.4 %fusion.80 = f32[8,160,512]{2,1,0:T(8,128)} fusion(bf16[8,160,2048]{2,1,0:T(8,128)(2,1)S(1)} %bitcast.108, bf16[8,2048,512]{2,1,0:T(8,128)(2,1)} %get-tuple-element.85), kind=kOutput, calls=%fused_computation.192 | convolution fusion | flops 2684354560 | bytes 24641536 | tf_op jit(solution)/shard_map/ecd,edf->ecf/dot_general | solution.py:1520
  265.0 16.4 %shard_map.231 = (bf16[1280,512]{1,0:T(8,128)(2,1)S(1)}, bf16[512,512]{1,0:T(8,128)(2,1)S(1)}, bf16[512,512]{1,0:T(8,128)(2,1)S(1)}, f32[1280,512]{1,0:T(8,128)S(1)}, bf16[1280,512]{1,0:T(8,128)(2,1)S(1)}) custom-call(f32[1280,512]{1,0:T(8,128)} %bitcast.110, f32[512,1024]{1,0:T(8,128)S(1)} %pad_maximum_fusion.k_raw.v_raw, ...), custom_call_target="tpu_custom_call" | custom-call | flops 1342177280 | bytes 9175040 | tf_op jit(solution)/shard_map/pallas_call | solution.py:154
  284.1 12.1 %convolution_convert_fusion.1 = bf16[8,160,2048]{2,1,0:T(8,128)(2,1)} fusion(bf16[8,160,512]{2,1,0:T(8,128)(2,1)S(1)} %bitcast.95, bf16[8,512,2048]{2,1,0:T(8,128)(2,1)} %get-tuple-element.97), kind=kOutput, calls=%fused_computation.15 | convolution fusion | flops 2686976000 | bytes 23330816 | tf_op jit(solution)/shard_map/ecf,efd->ecd/dot_general | solution.py:1527
  296.3 108.9 %shard_map.232 = (f32[128,2048]{1,0:T(8,128)S(1)}, bf16[512,2048]{1,0:T(8,128)(2,1)}, f32[512,128]{1,0:T(8,128)S(1)}, bf16[1024,2176]{1,0:T(8,128)(2,1)}, bf16[8,704,256]{2,1,0:T(8,128)(2,1)}) custom-call(bf16[1280,512]{1,0:T(8,128)(2,1)} %get-tuple-element.168.pick, bf16[1280,2048]{1,0:T(8,128)(2,1)} %bitcast.109, ...), custom_call_target="tpu_custom_call" | custom-call | flops 2684354560 | bytes 314572800 | tf_op jit(solution)/shard_map/pallas_call | solution.py:605
  406.8 1.8 copy.109
  410.8 110.0 %shard_map.233 = (bf16[1024,2176]{1,0:T(8,128)(2,1)}, bf16[1024,512]{1,0:T(8,128)(2,1)}, bf16[8,256,1408]{2,1,0:T(8,128)(2,1)}, bf16[8,256,1408]{2,1,0:T(8,128)(2,1)}, bf16[8,1408,256]{2,1,0:T(8,128)(2,1)}) custom-call(bf16[1024,2176]{1,0:T(8,128)(2,1)} %get-tuple-element.104.x_hbm, bf16[1024,2048]{1,0:T(8,128)(2,1)} %get-tuple-element.105.cot_hbm, ...), custom_call_target="tpu_custom_call" | custom-call | flops 53150220288 | bytes 314572800 | tf_op jit(solution)/shard_map/pallas_call | solution.py:1270
  520.8 1.2 copy-done.16
  523.1 1.2 copy-done.32
  524.3 1.2 copy-done.33
  526.5 146.7 %shard_map.234 = (f32[128,2048]{1,0:T(8,128)S(1)}, bf16[512,2048]{1,0:T(8,128)(2,1)S(1)}, f32[1,2048]{1,0:T(1,128)S(1)}, bf16[128,128]{1,0:T(8,128)(2,1)S(1)}, b...) custom-call(bf16[1024,2176]{1,0:T(8,128)(2,1)} %get-tuple-element.109.back, ...), custom_call_target="tpu_custom_call" | custom-call | flops 2147483648 | bytes 314572800 | tf_op jit(solution)/shard_map/pallas_call | solution.py:724
  673.2 4.6 fusion.30
  677.8 11.1 %fusion.81 = bf16[8,512,2048]{2,1,0:T(8,128)(2,1)} fusion(bf16[8,160,512]{2,1,0:T(8,128)(2,1)S(1)} %bitcast.96, bf16[8,160,2048]{2,1,0:T(8,128)(2,1)} %bitcast.103), kind=kOutput, calls=%fused_computation.193 | convolution fusion | flops 2684354560 | bytes 23330816 | tf_op jit(solution)/shard_map/ecf,ecd->efd/dot_general | solution.py:1611
  692.7 14.5 %fusion.82 = f32[8,160,512]{2,1,0:T(8,128)S(1)} fusion(bf16[8,160,2048]{2,1,0:T(8,128)(2,1)} %bitcast.104, bf16[8,512,2048]{2,1,0:T(8,128)(2,1)} %get-tuple-element.97), kind=kOutput, calls=%fused_computation.194 | convolution fusion | flops 2684354560 | bytes 24641536 | tf_op jit(solution)/shard_map/ecd,efd->ecf/dot_general | solution.py:1615
  713.7 4.9 all-to-all-start.2
  720.7 1.3 copy-done.12
  723.0 1.4 copy-done.29
  726.5 18.5 %shard_map.235 = (bf16[1280,512]{1,0:T(8,128)(2,1)S(1)}, bf16[512,512]{1,0:T(8,128)(2,1)S(1)}, bf16[512,512]{1,0:T(8,128)(2,1)S(1)}) custom-call(bf16[1280,512]{1,0:T(8,128)(2,1)S(1)} %copy-done.29, bf16[512,512]{1,0:T(8,128)(2,1)S(1)} %copy-done.38, bf16[512,512]{1,0:T(8,128)(2,1)S(1)} %copy-done.40, bf16[1280,512]{1,0:T(8,128)(2,1)S(1)} %copy-done.12, ...), custom_call_target="tpu_custom_call" | custom-call | bytes 655360 | tf_op jit(solution)/shard_map/pallas_call | solution.py:224
  746.0 1.3 fusion.10
  748.1 10.9 %convolution_convert_fusion = bf16[8,160,2048]{2,1,0:T(8,128)(2,1)} fusion(bf16[8,160,512]{2,1,0:T(8,128)(2,1)S(1)} %bitcast.97, bf16[8,2048,512]{2,1,0:T(8,128)(2,1)} %get-tuple-element.85), kind=kOutput, calls=%fused_computation.14 | convolution fusion | flops 2686976000 | bytes 23330816 | tf_op jit(solution)/shard_map/ecf,edf->ecd/dot_general | solution.py:1626
  759.0 5.1 fusion.28
  764.1 1.3 add_convert_fusion
  765.4 4.7 concatenate.33.part_hbm
  771.2 1.3 fusion.26
  773.2 170.7 %shard_map.236 = (bf16[10,256,512]{2,1,0:T(8,128)(2,1)}, bf16[512,2048]{1,0:T(8,128)(2,1)}, f32[24,256]{1,0:T(8,128)}, bf16[512,2048]{1,0:T(8,128)(2,1)}) custom-call(bf16[8,160,2048]{2,1,0:T(8,128)(2,1)} %bitcast.105, bf16[8,160,512]{2,1,0:T(8,128)(2,1)} %bitcast.98, bf16[512,2048]{1,0:T(8,128)(2,1)} %copy-done.45, ...), custom_call_target="tpu_custom_call" | custom-call | bytes 1048576 | tf_op jit(solution)/shard_map/pallas_call | solution.py:981
  946.5 2.1 slice_convert_fusion.1
  948.7 4.3 slice_convert_fusion
  953.0 2.5 convert_element_type.341
  955.6 2.4 convert_element_type.344
  958.0 2.6 copy-done.9
  960.6 2.6 copy-done.10
  963.2 13.6 %shard_map.237 = (f32[8,2,256,1408]{3,2,1,0:T(8,128)}, f32[8,1408,256]{2,1,0:T(8,128)}) custom-call(bf16[8,256,1408]{2,1,0:T(8,128)(2,1)S(1)} %copy-done.9, bf16[8,256,1408]{2,1,0:T(8,128)(2,1)S(1)} %copy-done.10, bf16[8,1408,256]{2,1,0:T(8,128)(2,1)} %all-to-all-done.2.third), custom_call_target="tpu_custom_call" | custom-call | bytes 51904512 | tf_op jit(solution)/shard_map/pallas_call | solution.py:1030
  976.8 1.3 copy.125
  (266 shorter events, 50.1 us)
Async XLA Ops:
  7.2 28.0 %copy-start = (s32[1,4]{1,0:T(1,128)S(1)}, s32[1,4]{1,0:T(1,128)}, u32[]{:S(2)}) copy-start(s32[1,4]{1,0:T(1,128)} %param.17) | copy-start | bytes 52
  26.4 4.6 copy-start.65
  26.4 212.2 %all-to-all-start = ((bf16[8,704,256]{2,1,0:T(8,128)(2,1)}), bf16[8,704,256]{2,1,0:T(8,128)(2,1)}, u32[]{:S(2)}, u32[]{:S(2)}) async-start(bf16[8,704,256]{2,1,0:T(8,128)(2,1)} %get-tuple-element.152), calls=%async_computation | async-start | bytes 5767168 | tf_op jit(solution)/shard_map/all_to_all | solution.py:1321
  31.0 3.9 copy-start.69
  32.3 6.3 copy-start.48
  32.6 28.4 %copy-start.66 = (s32[512]{0:T(512)}, s32[512]{0:T(512)S(1)}, u32[]{:S(2)}) copy-start(s32[512]{0:T(512)S(1)} %get-tuple-element.146) | copy-start | bytes 6148
  47.2 196.8 %copy-start.63 = (f32[1280,1]{0,1:T(1,128)}, f32[1280,1]{0,1:T(1,128)S(1)}, u32[]{:S(2)}) copy-start(f32[1280,1]{0,1:T(1,128)S(1)} %broadcast_in_dim.191) | copy-start | bytes 15364
  53.1 3.5 copy-start.61
  56.6 4.4 copy-start.46
  238.7 172.2 %all-to-all-start.1 = ((bf16[8,2,256,1408]{3,2,1,0:T(8,128)(2,1)}), bf16[8,2,256,1408]{3,2,1,0:T(8,128)(2,1)}, u32[]{:S(2)}, u32[]{:S(2)}) async-start(bf16[8,2,256,1408]{3,2,1,0:T(8,128)(2,1)} %param.28), calls=%async_computation.1 | async-start | bytes 23068672 | tf_op jit(solution)/shard_map/all_to_all | solution.py:1321
  243.9 709.1 %reduce-scatter.2.cloned.1.call-start = ((), (), s32[]{:S(2)}) async-start(), calls=%async_computation.4 | async-start | bytes 18874368 | tf_op jit(solution)/shard_map/reduce_scatter | solution.py:1618
  245.2 4.8 copy-start.47
  246.4 49.8 %copy-start.14 = (bf16[2048,128]{1,0:T(8,128)(2,1)}, bf16[2048,128]{1,0:T(8,128)(2,1)S(1)}, u32[]{:S(2)}) copy-start(bf16[2048,128]{1,0:T(8,128)(2,1)S(1)} %pad.8.router) | copy-start | bytes 1572868
  247.1 6.0 copy-start.71
  247.7 5.4 copy-start.49
  249.9 46.3 %copy-start.13 = (bf16[128,2048]{1,0:T(8,128)(2,1)}, bf16[128,2048]{1,0:T(8,128)(2,1)S(1)}, u32[]{:S(2)}) copy-start(bf16[128,2048]{1,0:T(8,128)(2,1)S(1)} %get-tuple-element.197.x_here) | copy-start | bytes 1572868
  249.9 4.5 slice-start
  254.5 10.5 %copy-start.3 = (f32[1280,1]{1,0:T(8,128)S(1)}, f32[1280,1]{1,0:T(8,128)}, u32[]{:S(2)}) copy-start(f32[1280,1]{1,0:T(8,128)} %copy.108.gate) | copy-start | bytes 15364
  254.5 10.5 %copy-start.5 = (f32[1280,128]{1,0:T(8,128)S(1)}, f32[1280,128]{1,0:T(8,128)}, u32[]{:S(2)}) copy-start(f32[1280,128]{1,0:T(8,128)} %get-tuple-element.89.slot_cos) | copy-start | bytes 1966084
  254.5 10.5 %copy-start.7 = (f32[1280,128]{1,0:T(8,128)S(1)}, f32[1280,128]{1,0:T(8,128)}, u32[]{:S(2)}) copy-start(f32[1280,128]{1,0:T(8,128)} %get-tuple-element.90.slot_sin) | copy-start | bytes 1966084
  254.5 10.5 %copy-start.11 = (bf16[1280,512]{1,0:T(8,128)(2,1)S(1)}, bf16[1280,512]{1,0:T(8,128)(2,1)}, u32[]{:S(2)}) copy-start(bf16[1280,512]{1,0:T(8,128)(2,1)} %select_convert_fusion.bias) | copy-start | bytes 3932164
  254.6 10.5 %copy-start.21 = (f32[512,128]{1,0:T(8,128)S(1)}, f32[512,128]{1,0:T(8,128)}, u32[]{:S(2)}) copy-start(f32[512,128]{1,0:T(8,128)} %get-tuple-element.91.tok_cos) | copy-start | bytes 786436
  254.6 10.5 %copy-start.23 = (f32[512,128]{1,0:T(8,128)S(1)}, f32[512,128]{1,0:T(8,128)}, u32[]{:S(2)}) copy-start(f32[512,128]{1,0:T(8,128)} %get-tuple-element.92.tok_sin) | copy-start | bytes 786436
  284.1 12.2 %copy-start.19 = (f32[1280,512]{1,0:T(8,128)}, f32[1280,512]{1,0:T(8,128)S(1)}, u32[]{:S(2)}) copy-start(f32[1280,512]{1,0:T(8,128)S(1)} %get-tuple-element.122) | copy-start | bytes 7864324
  284.1 12.2 %copy-start.34 = (f32[512,128]{1,0:T(8,128)S(1)}, f32[512,128]{1,0:T(8,128)}, u32[]{:S(2)}) copy-start(f32[512,128]{1,0:T(8,128)} %get-tuple-element.98.hot_0) | copy-start | bytes 786436
  284.1 12.2 %copy-start.35 = (f32[512,128]{1,0:T(8,128)S(1)}, f32[512,128]{1,0:T(8,128)}, u32[]{:S(2)}) copy-start(f32[512,128]{1,0:T(8,128)} %get-tuple-element.99.hot_1) | copy-start | bytes 786436
  410.8 110.0 %copy-start.15 = (bf16[2048,128]{1,0:T(8,128)(2,1)S(1)}, bf16[2048,128]{1,0:T(8,128)(2,1)}, u32[]{:S(2)}) copy-start(bf16[2048,128]{1,0:T(8,128)(2,1)} %copy-done.14) | copy-start | bytes 1572868
  526.5 146.7 %copy-start.67 = (s32[512]{0:T(512)S(1)}, s32[512]{0:T(512)}, u32[]{:S(2)}) copy-start(s32[512]{0:T(512)} %copy-done.66) | copy-start | bytes 6148
  673.1 4.6 copy-start.30
  673.1 4.6 copy-start.41
  673.1 4.6 copy-start.43
  692.7 14.5 %copy-start.20 = (f32[1280,512]{1,0:T(8,128)S(1)}, f32[1280,512]{1,0:T(8,128)}, u32[]{:S(2)}) copy-start(f32[1280,512]{1,0:T(8,128)} %copy-done.19) | copy-start | bytes 7864324
  713.6 4.9 copy-start.4
  713.6 4.9 copy-start.22
  713.7 239.4 %all-to-all-start.2 = ((bf16[8,1408,256]{2,1,0:T(8,128)(2,1)}), bf16[8,1408,256]{2,1,0:T(8,128)(2,1)}, u32[]{:S(2)}, u32[]{:S(2)}) async-start(bf16[8,1408,256]{2,1,0:T(8,128)(2,1)} %get-tuple-element.131), calls=%async_computation.3 | async-start | bytes 11534336 | tf_op jit(solution)/shard_map/all_to_all | solution.py:1321
  726.5 18.6 %copy-start.57 = (f32[512,1]{1,0:T(8,128)S(1)}, f32[512,1]{1,0:T(8,128)}, u32[]{:S(2)}) copy-start(f32[512,1]{1,0:T(8,128)} %copy.113) | copy-start | bytes 6148
  726.5 18.6 %copy-start.59 = (f32[512,1]{1,0:T(8,128)S(1)}, f32[512,1]{1,0:T(8,128)}, u32[]{:S(2)}) copy-start(f32[512,1]{1,0:T(8,128)} %copy.114) | copy-start | bytes 6148
  726.5 19.5 %copy-start.50 = (bf16[2,2048,512]{2,1,0:T(8,128)(2,1)S(1)}, bf16[2,2048,512]{2,1,0:T(8,128)(2,1)}, u32[]{:S(2)}) copy-start(bf16[2,2048,512]{2,1,0:T(8,128)(2,1)} %get-tuple-element.86) | copy-start | bytes 12582916
  745.1 3.0 copy-start.2
  745.1 18.9 %copy-start.26 = (bf16[512,512]{1,0:T(8,128)(2,1)}, bf16[512,512]{1,0:T(8,128)(2,1)S(1)}, u32[]{:S(2)}) copy-start(bf16[512,512]{1,0:T(8,128)(2,1)S(1)} %get-tuple-element.121) | copy-start | bytes 1572868
  748.1 10.9 %copy-start.68 = (s32[512]{0:T(512)S(1)}, s32[512]{0:T(512)}, u32[]{:S(2)}) copy-start(s32[512]{0:T(512)} %copy-done.66) | copy-start | bytes 6148
  759.0 5.1 copy-start.51
  765.4 4.7 copy-start.18
  765.4 4.7 copy-start.27
  765.4 5.8 copy-start.44
  948.7 4.3 copy-start.53
  963.2 13.6 %copy-start.54 = (bf16[512,2048]{1,0:T(8,128)(2,1)S(1)}, bf16[512,2048]{1,0:T(8,128)(2,1)}, u32[]{:S(2)}) copy-start(bf16[512,2048]{1,0:T(8,128)(2,1)} %get-tuple-element.209) | copy-start | bytes 6291460
  963.2 14.9 %copy-start.1 = (s32[1,4]{1,0:T(1,128)S(1)}, s32[1,4]{1,0:T(1,128)}, u32[]{:S(2)}) copy-start(s32[1,4]{1,0:T(1,128)} %param.17) | copy-start | bytes 52
  (35 other events, 47.6 us)
Sparse Core Ops, SparseCore 0:
  689.0 213.6 reduce-scatter.1

commit v5 on v4

--- a/solution.py
+++ b/solution.py
@@ -484,15 +484,17 @@
     )(*arrays, rows)
 
 
-def deal(source, target, sems):
+def deal(source, target, sems, rows=None):
     me = lax.axis_index("dp")
+
+    def block(place):
+        return source.at[place] if rows is None else source.at[place, rows]
+
     copies = [
-        send_to(
-            source.at[partner(k)], target.at[me], sems[0].at[k], sems[1].at[k], partner(k)
-        )
+        send_to(block(partner(k)), target.at[me], sems[0].at[k], sems[1].at[k], partner(k))
         for k in range(1, source.shape[0])
     ]
-    copies.append(pltpu.make_async_copy(source.at[me], target.at[me], sems[0].at[0]))
+    copies.append(pltpu.make_async_copy(block(me), target.at[me], sems[0].at[0]))
     for copy in copies:
         copy.start()
     return copies
@@ -630,10 +632,11 @@
 
 
 def back_kernel(
-    back, pick, hit_0, hit_1, hidden, cot_here, gain, router, hots, gates, rows_hbm, gate_hbm, up_hbm,
-    grad_out, pair_out, gain_out, hot_out, mixed_out, gate_maps, up_maps,
+    back, pick, hit_0, hit_1, hidden, cot_here, gain, router, hots, gates, att_pick, gated,
+    rows_hbm, gate_hbm, up_hbm,
+    grad_out, pair_out, gain_out, hot_out, mixed_out, att_rows, gate_maps, up_maps, grad_output,
     parts, sent, got, z_send, z_recv, g_send, g_recv, e_send, e_recv, w_send, w_recv, u_send, u_recv,
-    rows_in, columns_here, mlp_got, m_send, m_recv, own,
+    rows_in, columns_here, mlp_got, m_send, m_recv, own, stage, stage_sem,
 ):
     count = z_send.shape[0] + 1
     width = back.shape[1] - HD
@@ -709,13 +712,39 @@
     mixed_out[...] = (hidden[...] + mlp_got[...].astype(F32)).astype(BF16)
     for copy in copies:
         copy.wait_send()
-    for copy in (*more, *dealt):
+    for copy in more:
+        copy.wait()
+
+    @pl.loop(0, width // 512)
+    def _(i):
+        at = rows_of(i, 512)
+        att_rows[:, at] = dot(att_pick[...], pair_out[:, at]).astype(BF16)
+
+    experts, cap = grad_output.shape[0], gated.shape[0] // grad_output.shape[0]
+
+    def store(e):
+        slot = lax.rem(e, 2)
+        return pltpu.make_async_copy(stage.at[slot], grad_output.at[e], stage_sem.at[slot])
+
+    @pl.loop(0, experts)
+    def _(e):
+        @pl.when(e > 1)
+        def _():
+            store(e - 2).wait()
+
+        at = rows_of(e, cap)
+        stage[lax.rem(e, 2)] = dot_tn(gated[at, :], att_rows[at, :]).astype(BF16)
+        store(e).start()
+
+    for e in (experts - 2, experts - 1):
+        store(e).wait()
+    for copy in dealt:
         copy.wait()
 
 
 def back_step(
     tensor_size, peers, back, pick, hits, hidden, cot_here, gain, router, hots, gates,
-    rows_send, gate_maps, up_maps,
+    att_pick, gated, experts, rows_send, gate_maps, up_maps,
 ):
     tokens, width = pick.shape[1], back.shape[1] - HD
     size = tokens // tensor_size
@@ -723,16 +752,18 @@
     wide = width + 2 * HD
     return pl.pallas_call(
         back_kernel,
-        in_specs=[VMEM] * 10 + [HBM] * 3,
-        out_specs=[VMEM] * 5 + [HBM] * 2,
+        in_specs=[VMEM] * 12 + [HBM] * 3,
+        out_specs=[VMEM] * 6 + [HBM] * 3,
         out_shape=[
             jax.ShapeDtypeStruct((size, width), F32),
             jax.ShapeDtypeStruct((tokens, width), BF16),
             jax.ShapeDtypeStruct((1, width), F32),
             jax.ShapeDtypeStruct((size, HD), BF16),
             jax.ShapeDtypeStruct((size, width), BF16),
+            jax.ShapeDtypeStruct((att_pick.shape[0], width), BF16),
             jax.ShapeDtypeStruct(gate_maps.shape, BF16),
             jax.ShapeDtypeStruct(up_maps.shape, BF16),
+            jax.ShapeDtypeStruct((experts, gated.shape[1], width), BF16),
         ],
         scratch_shapes=[
             pltpu.VMEM((tokens, wide), F32),
@@ -744,14 +775,16 @@
             pltpu.VMEM((tokens, width // tensor_size), BF16),
             pltpu.VMEM((size, width), BF16),
             sems(around), sems(around), sems(1),
+            pltpu.VMEM((2, gated.shape[1], width), BF16),
+            sems(2),
         ],
         compiler_params=pltpu.CompilerParams(
-            collective_id=4, has_side_effects=True, vmem_limit_bytes=40 << 20
+            collective_id=4, has_side_effects=True, vmem_limit_bytes=56 << 20
         ),
         cost_estimate=pl.CostEstimate(
             flops=2 * pick.shape[0] * tokens * width, bytes_accessed=300 << 20, transcendentals=0
         ),
-    )(back, pick, hits[0], hits[1], hidden, cot_here, gain, router, hots, gates, rows_send, gate_maps, up_maps)
+    )(back, pick, hits[0], hits[1], hidden, cot_here, gain, router, hots, gates, att_pick, gated, rows_send, gate_maps, up_maps)
 
 
 GIVE = 4
@@ -760,13 +793,13 @@
 
 def final_kernel(
     routed_hbm, grad_q, normed, grad_kv, part_hbm,
-    grad_hidden, x_here, gain, router, hots, small, mixed_here,
-    out, tokens_out, small_out, mixed_out,
+    grad_hidden, x_here, gain, router, hots, small, maps_hbm,
+    out, tokens_out, small_out, maps_out,
     give, keep, twin_in, far_in, near_in, routed, got_part, tokens_here,
     twin_send, twin_recv, far_send, far_recv, near_send, near_recv, load, own,
     p_send, p_recv, t_send, t_recv,
     hot_here, small_all, small_in, small_sum, small_got,
-    s_send, s_recv, w_send, w_recv, a_send, a_recv,
+    s_send, s_recv, w_send, w_recv, d_send, d_recv,
 ):
     at = Square()
     experts = grad_q.shape[0]
@@ -791,13 +824,10 @@
         send_across(part_hbm.at[rows_of(p, share)], got_part.at[k], p_send.at[k], p_recv.at[k], p)
         for k, p in enumerate(peers)
     ]
-    mixed_copies = [
-        send_across(mixed_here, mixed_out.at[here], a_send.at[k], a_recv.at[k], p)
-        for k, p in enumerate(peers)
-    ]
-    mixed_copies.append(pltpu.make_async_copy(mixed_here, mixed_out.at[here], own.at[2]))
-    for copy in (*part_copies, *mixed_copies):
+    for copy in part_copies:
         copy.start()
+    late = maps_out.shape[1]
+    dealt = deal(maps_hbm, maps_out, (d_send, d_recv), pl.ds(maps_hbm.shape[1] - late, late))
 
     def to_twin(u):
         slot = lax.rem(u, GIVE)
@@ -963,13 +993,13 @@
     small_out[...] = block
     for copy in (*part_copies, *small_copies, *last_copies):
         copy.wait_send()
-    for copy in (*token_copies, *mixed_copies, kept):
+    for copy in (*token_copies, *dealt, kept):
         copy.wait()
 
 
 def final_step(
     tensor_size, routed, grad_q, normed, grad_kv, part, grad_hidden, x_here, gain,
-    router, hots, small, mixed_here,
+    router, hots, small, maps, late,
 ):
     experts, rows, width = routed.shape
     columns = grad_q.shape[2]
@@ -980,13 +1010,13 @@
     around = tensor_size - 1
     return pl.pallas_call(
         final_kernel,
-        in_specs=[HBM, VMEM, VMEM, VMEM, HBM] + [VMEM] * 7,
+        in_specs=[HBM, VMEM, VMEM, VMEM, HBM] + [VMEM] * 6 + [HBM],
         out_specs=[VMEM, HBM, VMEM, HBM],
         out_shape=[
             jax.ShapeDtypeStruct((units, size, columns), BF16),
             jax.ShapeDtypeStruct((tokens, width), BF16),
             jax.ShapeDtypeStruct((3 * HALF_SMALL, size), F32),
-            jax.ShapeDtypeStruct((tokens, width), BF16),
+            jax.ShapeDtypeStruct((maps.shape[0], late) + maps.shape[2:], BF16),
         ],
         scratch_shapes=[
             pltpu.VMEM((GIVE, 4, size, columns), BF16),
@@ -1005,7 +1035,7 @@
             pltpu.VMEM((8, 3 * HALF_SMALL, size), F32),
             pltpu.VMEM((3 * HALF_SMALL, size), F32),
             pltpu.VMEM((around, 3 * HALF_SMALL, size), F32),
-            sems(8), sems(8), sems(around), sems(around), sems(around), sems(around),
+            sems(8), sems(8), sems(around), sems(around), sems(8), sems(8),
         ],
         compiler_params=pltpu.CompilerParams(
             collective_id=1, has_side_effects=True, vmem_limit_bytes=60 << 20
@@ -1013,34 +1043,230 @@
         cost_estimate=pl.CostEstimate(flops=0, bytes_accessed=1 << 20, transcendentals=0),
     )(
         routed, grad_q, normed, grad_kv, part, grad_hidden, x_here, gain, router, hots, small,
-        mixed_here,
-    )
-
-
-def widen_kernel(first, second, third, both_out, third_out):
+        maps,
+    )
+
+
+def widen_kernel(first, second, third, fourth, both_out, third_out):
     both_out[:, 0] = first[...].astype(F32)
     both_out[:, 1] = second[...].astype(F32)
-    third_out[...] = third[...].astype(F32)
-
-
-def widen(first, second, third):
+    early = third.shape[1]
+    third_out[:, 0:early] = third[...].astype(F32)
+    third_out[:, early:] = fourth[...].astype(F32)
+
+
+def widen(first, second, third, fourth):
     experts, rows, columns = first.shape
     narrow = pl.BlockSpec((1, rows, columns), lambda e: (e, 0, 0))
-    turned = pl.BlockSpec((1,) + third.shape[1:], lambda e: (e, 0, 0))
+    whole = (experts, third.shape[1] + fourth.shape[1], third.shape[2])
+
+    def block(shape):
+        return pl.BlockSpec((1,) + shape[1:], lambda e: (e, 0, 0))
+
     return pl.pallas_call(
         widen_kernel,
         grid=(experts,),
-        in_specs=[narrow, narrow, turned],
-        out_specs=[pl.BlockSpec((1, 2, rows, columns), lambda e: (e, 0, 0, 0)), turned],
+        in_specs=[narrow, narrow, block(third.shape), block(fourth.shape)],
+        out_specs=[pl.BlockSpec((1, 2, rows, columns), lambda e: (e, 0, 0, 0)), block(whole)],
         out_shape=[
             jax.ShapeDtypeStruct((experts, 2, rows, columns), F32),
-            jax.ShapeDtypeStruct(third.shape, F32),
+            jax.ShapeDtypeStruct(whole, F32),
         ],
         compiler_params=pltpu.CompilerParams(vmem_limit_bytes=32 << 20),
         cost_estimate=pl.CostEstimate(
-            flops=0, bytes_accessed=6 * (2 * first.size + third.size), transcendentals=0
+            flops=0, bytes_accessed=6 * (2 * first.size + third.size + fourth.size), transcendentals=0
         ),
-    )(first, second, third)
+    )(first, second, third, fourth)
+
+
+def turn_kernel(
+    rows, q_ref, k_ref, v_ref, bias, gate, slot_cos, slot_sin, tok_cos, tok_sin, attended,
+    hit_0, hit_1, mixed_here, output_hbm, query_hbm, keyval_hbm, maps_hbm,
+    gq_out, gkv_out, part_out, maps_out, mixed_out,
+    grad_gated, grad_routed, weight, product, gk_sum, gv_sum,
+    load, d_send, d_recv, a_send, a_recv, own,
+):
+    count = a_send.shape[0] + 1
+    peers = tensor_peers(count)
+    experts, cap, width = rows.shape
+    slots, here_width = q_ref.shape
+    heads = here_width // HD
+    step = 256
+    greet(
+        [{"dp": partner(k)} for k in range(1, d_send.shape[0])] + [{"tensor": p} for p in peers]
+    )
+    dealt = deal(maps_hbm, maps_out, (d_send, d_recv), pl.ds(0, maps_out.shape[1]))
+    here = share_rows(mixed_here.shape[0])
+    mixed_copies = [
+        send_across(mixed_here, mixed_out.at[here], a_send.at[k], a_recv.at[k], p)
+        for k, p in enumerate(peers)
+    ]
+    mixed_copies.append(pltpu.make_async_copy(mixed_here, mixed_out.at[here], own.at[0]))
+    for copy in mixed_copies:
+        copy.start()
+
+    def fetch_output(e):
+        slot = lax.rem(e, 2)
+        return pltpu.make_async_copy(output_hbm.at[e], weight.at[slot], load.at[slot])
+
+    def fetch_query(e, half):
+        size = width // 2
+        return pltpu.make_async_copy(
+            query_hbm.at[e, pl.ds(half * size, size)], weight_rows(half), load.at[2 + half]
+        )
+
+    def weight_rows(half):
+        return turned.at[half]
+
+    turned = grad_routed[1]
+    routed_out = grad_routed[0]
+
+    fetch_output(0).start()
+
+    @pl.loop(0, experts)
+    def _(e):
+        fetch_output(e).wait()
+
+        @pl.when(e < experts - 1)
+        def _():
+            fetch_output(e + 1).start()
+
+        at = pl.ds(pl.multiple_of(e * cap, cap), cap)
+        grad_gated[at, :] = dot_nt(rows[e], weight[lax.rem(e, 2)])
+
+    fetch_query(0, 0).start()
+    fetch_query(0, 1).start()
+
+    @pl.loop(0, heads)
+    def _(h):
+        lanes = rows_of(h, HD)
+        gk_sum[...] = jnp.zeros_like(gk_sum)
+        gv_sum[...] = jnp.zeros_like(gv_sum)
+
+        @pl.loop(0, slots // step)
+        def _(i):
+            at = pl.ds(pl.multiple_of(i * step, step), step)
+            q = q_ref[at, lanes]
+            keys, values = k_ref[:, lanes], v_ref[:, lanes]
+            probs = softmax_block(q, keys, bias[at, :].astype(F32))
+            scaled = grad_gated[at, lanes] * gate[at, :]
+            joined = scaled * attended[at, lanes]
+
+            @pl.when(h == 0)
+            def _():
+                product[at, :] = joined
+
+            @pl.when(h > 0)
+            def _():
+                product[at, :] += joined
+
+            grad_att = scaled.astype(BF16)
+            grad_probs = dot_nt(grad_att, values)
+            centre = jnp.sum(probs * grad_probs, axis=-1, keepdims=True)
+            grad_scores = (probs * (grad_probs - centre)).astype(BF16)
+            grad_q = dot(grad_scores, keys) * HD ** (-0.5)
+            gq_out[at, lanes] = rope_back(grad_q, slot_cos[at, :], slot_sin[at, :]).astype(BF16)
+            gk_sum[...] += dot_tn(grad_scores, q)
+            gv_sum[...] += dot_tn(probs.astype(BF16), grad_att)
+
+        grad_k = gk_sum[...] * HD ** (-0.5)
+        gkv_out[0, :, lanes] = rope_back(grad_k, tok_cos[...], tok_sin[...]).astype(BF16)
+        gkv_out[1, :, lanes] = gv_sum[...].astype(BF16)
+
+    @pl.loop(0, experts)
+    def _(e):
+        at = pl.ds(pl.multiple_of(e * cap, cap), cap)
+        for half in range(2):
+            fetch_query(e, half).wait()
+            routed_out[at, pl.ds(half * (width // 2), width // 2)] = dot_nt(
+                gq_out[at, :], turned[half]
+            ).astype(BF16)
+
+            @pl.when(e < experts - 1)
+            def _():
+                fetch_query(e + 1, half).start()
+
+    def fetch_keyval(i):
+        slot = lax.rem(i, 2)
+        block = pl.ds(pl.multiple_of(i * 512, 512), 512)
+        return [
+            pltpu.make_async_copy(
+                keyval_hbm.at[c, block], turned.at[slot, pl.ds(c * 512, 512)],
+                load.at[4 + 2 * slot + c],
+            )
+            for c in range(2)
+        ]
+
+    for copy in fetch_keyval(0):
+        copy.start()
+
+    @pl.loop(0, width // 512)
+    def _(i):
+        for copy in fetch_keyval(i):
+            copy.wait()
+
+        @pl.when(i < width // 512 - 1)
+        def _():
+            for copy in fetch_keyval(i + 1):
+                copy.start()
+
+        at = rows_of(i, 512)
+        maps = turned.at[lax.rem(i, 2)]
+        part_out[:, at] = (
+            dot_tn(hit_0[...] + hit_1[...], routed_out[:, at])
+            + dot_nt(gkv_out[0], maps[0:512, :])
+            + dot_nt(gkv_out[1], maps[512:1024, :])
+        ).astype(BF16)
+
+    columns = in_columns(
+        jnp.sum(product[...], axis=1, keepdims=True),
+        lax.broadcasted_iota(jnp.int32, (slots, HD), 1),
+    )
+    part_out[:, width : width + HD] = dot_tn(hit_0[...], columns).astype(BF16)
+    part_out[:, width + HD :] = dot_tn(hit_1[...], columns).astype(BF16)
+    for copy in (*mixed_copies, *dealt):
+        copy.wait()
+
+
+def turn_step(
+    tensor_size, rows, q, k, v, bias, gate, slot_tables, tok_tables, attended, hits, mixed_here,
+    output_full, query_full, keyval_full, maps, early,
+):
+    experts, cap, width = rows.shape
+    slots, here_width = q.shape
+    tok = k.shape[0]
+    around = tensor_size - 1
+    return pl.pallas_call(
+        lambda *refs: turn_kernel(*refs[:24], (refs[24], refs[25]), *refs[26:]),
+        in_specs=[VMEM] * 14 + [HBM] * 4,
+        out_specs=[VMEM, VMEM, VMEM, HBM, HBM],
+        out_shape=[
+            jax.ShapeDtypeStruct((slots, here_width), BF16),
+            jax.ShapeDtypeStruct((2, tok, here_width), BF16),
+            jax.ShapeDtypeStruct((tok, width + 2 * HD), BF16),
+            jax.ShapeDtypeStruct((maps.shape[0], early) + maps.shape[2:], BF16),
+            jax.ShapeDtypeStruct((tok, width), BF16),
+        ],
+        scratch_shapes=[
+            pltpu.VMEM((slots, here_width), F32),
+            pltpu.VMEM((slots, width), BF16),
+            pltpu.VMEM((2, width // 2, here_width), BF16),
+            pltpu.VMEM((2, here_width, width), BF16),
+            pltpu.VMEM((slots, HD), F32),
+            pltpu.VMEM((tok, HD), F32),
+            pltpu.VMEM((tok, HD), F32),
+            sems(8), sems(8), sems(8), sems(around), sems(around), sems(1),
+        ],
+        compiler_params=pltpu.CompilerParams(
+            collective_id=6, has_side_effects=True, vmem_limit_bytes=58 << 20
+        ),
+        cost_estimate=pl.CostEstimate(
+            flops=10 * slots * tok * here_width, bytes_accessed=300 << 20, transcendentals=0
+        ),
+    )(
+        rows, q, k, v, bias, gate, *slot_tables, *tok_tables, attended, *hits, mixed_here,
+        output_full, query_full, keyval_full, maps,
+    )
 
 
 def partner(k):
@@ -1568,13 +1794,14 @@
 
     if fast:
         (
-            grad_hidden, grad_att_pair, grad_gain_mlp, grad_mlp_logits, mixed, grad_gate_w,
-            grad_up_w,
+            grad_hidden, _, grad_gain_mlp, grad_mlp_logits, mixed, grad_att_rows, grad_gate_w,
+            grad_up_w, grad_output_w,
         ) = back_step(
             tensor_size, mlp_experts, grad_in_slots, mlp_pick,
             mlp_bits, hidden, share(cotangent),
             gain_mlp_full[None], padded(router_mlp),
-            hots(mlp_gates, expert_routes, mlp_experts), mlp_gates.T, expert_out, grad_gate_w, grad_up_w,
+            hots(mlp_gates, expert_routes, mlp_experts), mlp_gates.T, att_pick, gated, att_experts,
+            expert_out, grad_gate_w, grad_up_w,
         )
         grad_gain_mlp = grad_gain_mlp[0]
         grad_mlp_logits = grad_mlp_logits[:, :mlp_experts]
@@ -1595,6 +1822,13 @@
         )
         grad_hidden = share(cotangent).astype(F32) + grad_hidden_norm
         grad_att_pair = movers.gather_rows(grad_hidden)
+        grad_att_rows = dot(att_pick, grad_att_pair, BF16)
+        grad_output_w = jnp.einsum(
+            "ecf,ecd->efd",
+            gated_slots,
+            grad_att_rows.reshape(att_experts, att_cap, model_width),
+            preferred_element_type=BF16,
+        )
         gate_matrix = sum(
             jnp.where(mlp_hits[k], mlp_gates[:, k][None, :], 0.0) for k in range(TOPK)
         )
@@ -1604,36 +1838,39 @@
         mixed = movers.gather_rows(hidden + movers.reduce_rows(mlp_part))
     grad_router_mlp = dot_tn(share(mlp_in), grad_mlp_logits)
 
-    grad_att_pair, grad_down_w = tie((grad_att_pair, grad_down_w))
-    grad_down_w = movers.give_back(grad_down_w)
-
-    grad_att_rows = dot(att_pick, grad_att_pair, BF16).reshape(att_experts, att_cap, model_width)
-    grad_output_w = jnp.einsum(
-        "ecf,ecd->efd", gated_slots, grad_att_rows, preferred_element_type=BF16
-    )
-    grad_att_rows, grad_output_w = tie((grad_att_rows, grad_output_w))
-    grad_gated = jnp.einsum(
-        "ecd,efd->ecf", grad_att_rows, output_full, preferred_element_type=F32
-    ).reshape(att_slots, width_here)
+    grad_att_rows = grad_att_rows.reshape(att_experts, att_cap, model_width)
     grad_output_out = lax.psum_scatter(grad_output_w, "dp", scatter_dimension=2, tiled=True)
-    att_products = to_pairs(
-        att_hits, jnp.sum(grad_gated * attended, axis=1) * att_gate_slots[:, 0]
-    )
-    grad_q, grad_k, grad_v = attend_back(
-        queries, key_rows, values, bias, att_gate_slots, slot_tables, tok_tables, grad_gated
-    )
+    if fast:
+        half = grad_down_w.shape[1] // 2
+        grad_q, grad_kv, normed_part, grad_down_early, mixed = turn_step(
+            tensor_size, grad_att_rows, queries, key_rows, values, bias, att_gate_slots,
+            slot_tables, tok_tables, attended, [hit.astype(BF16) for hit in att_hits], mixed,
+            output_full, query_full, keyval_full, grad_down_w, half,
+        )
+    else:
+        grad_down_early, grad_down_late = jnp.split(movers.give_back(grad_down_w), 2, axis=1)
+        grad_gated = jnp.einsum(
+            "ecd,efd->ecf", grad_att_rows, output_full, preferred_element_type=F32
+        ).reshape(att_slots, width_here)
+        att_products = to_pairs(
+            att_hits, jnp.sum(grad_gated * attended, axis=1) * att_gate_slots[:, 0]
+        )
+        grad_q, grad_k, grad_v = attend_back(
+            queries, key_rows, values, bias, att_gate_slots, slot_tables, tok_tables, grad_gated
+        )
+        grad_routed = jnp.einsum(
+            "ecf,edf->ecd",
+            grad_q.reshape(att_experts, att_cap, width_here),
+            query_full,
+            preferred_element_type=F32,
+        ).reshape(att_slots, model_width)
+        normed_part = (
+            dot_tn(att_pick, grad_routed.astype(BF16))
+            + dot_nt(grad_k, keyval_full[0])
+            + dot_nt(grad_v, keyval_full[1])
+        )
+        grad_kv = jnp.stack([grad_k, grad_v])
     grad_query_slots = grad_q.reshape(att_experts, att_cap, width_here)
-    grad_routed = jnp.einsum(
-        "ecf,edf->ecd", grad_query_slots, query_full, preferred_element_type=F32
-    ).reshape(att_slots, model_width)
-    normed_part = (
-        dot_tn(att_pick, grad_routed.astype(BF16))
-        + dot_nt(grad_k, keyval_full[0])
-        + dot_nt(grad_v, keyval_full[1])
-    )
-    normed_part = with_column(normed_part.astype(BF16), att_products[:, :1])
-    normed_part = with_column(normed_part, att_products[:, 1:])
-    grad_kv = jnp.stack([grad_k, grad_v])
     if fast:
         small = jnp.concatenate(
             [
@@ -1644,10 +1881,11 @@
             ],
             axis=0,
         )
-        map_sums, grad_tokens, small_grads, mixed = final_step(
+        map_sums, grad_tokens, small_grads, grad_down_late = final_step(
             tensor_size, routed, grad_query_slots, normed, grad_kv, normed_part,
             grad_hidden, share(tokens), gain_attn_full[None], padded(router_att),
-            hots(att_gates, attention_routes, att_experts), small, mixed,
+            hots(att_gates, attention_routes, att_experts), small, grad_down_w,
+            grad_down_w.shape[1] - half,
         )
         small_grads = jnp.concatenate([small_grads[:2], small_grads[HALF_SMALL:]], axis=0).T
         grad_query_out, grad_keyval_out = map_sums[:att_experts], map_sums[att_experts:]
@@ -1655,10 +1893,10 @@
         grad_query_w = jnp.einsum(
             "ecd,ecf->edf", routed, grad_query_slots, preferred_element_type=BF16
         )
-        grad_keyval_w = jnp.stack([dot_tn(normed, grad, BF16) for grad in (grad_k, grad_v)])
+        grad_keyval_w = jnp.stack([dot_tn(normed, grad, BF16) for grad in grad_kv])
         grad_query_out = lax.psum_scatter(grad_query_w, "dp", scatter_dimension=1, tiled=True)
         grad_keyval_out = lax.psum_scatter(grad_keyval_w, "dp", scatter_dimension=1, tiled=True)
-        grad_normed = movers.reduce_rows(normed_part[:, :model_width])
+        grad_normed = movers.reduce_rows(normed_part)
         grad_att_logits = router_backward(
             share(att_gates), movers.reduce_rows(att_products, F32), share(attention_routes),
             att_experts,
@@ -1676,9 +1914,11 @@
         small_grads = lax.psum(
             lax.psum_scatter(small_grads, "dp", scatter_dimension=0, tiled=True), "tensor"
         )
-    grad_tokens, grad_output_out, grad_down_w = tie((grad_tokens, grad_output_out, grad_down_w))
+    grad_tokens, grad_output_out = tie((grad_tokens, grad_output_out))
     grad_tokens = grad_tokens.astype(F32)
-    grad_up_w, grad_down_w = widen(grad_gate_w, grad_up_w, grad_down_w)
+    grad_up_w, grad_down_w = widen(
+        grad_gate_w, grad_up_w, grad_down_early, grad_down_late
+    )
     return (
         mixed,
         grad_tokens,

time: 995 us -> 968 us (0.973)
  Pallas kernels: 758 us -> 816 us
  matrix products: 89.2 us -> 41 us
  local copies, waits for them, and re-layouts: 61.7 us -> 36.9 us
    pallas_call x3, Pallas kernels: 179 us -> 239 us  [the longest x1 156 us: back_step(): pl.pallas_call(back_kernel, in_specs=[VMEM] * 12 + [HBM] * 3, out_specs=[...]
    dot_general x5 -> x0, matrix products: 39 us -> none  [the longest x1 14.5 us: on_device(): jnp.einsum('ecd,efd->ecf', grad_att_rows, output_full, preferred_element_...]
    unnamed x162 -> x104, local copies, waits for them, and re-layouts: 27.4 us -> 15.2 us
    dot_general x7 -> x6, matrix products: 21.2 us -> 16.7 us  [dot(): return jnp.dot(a, b, preferred_element_type=out)]
  transfers between devices with their start and end apart: 4 -> 3, of which waited for: 0 -> 0; matrix products, arithmetic and copies ran while one was open for 13% -> 8% of each run, Pallas kernels for 49% -> 57%
where the time goes in v5:
time: 968 us; the launch traced here: 959 us
  Pallas kernels  816 us (84%)
  matrix products  41 us (4%)
  local copies, waits for them, and re-layouts  36.9 us (4%)
  other arithmetic  28.6 us (3%)
  between operations  15.3 us (2%)
  blocking collectives  11.3 us (1%)
  starting transfers between devices  9.87 us (1%)
    pallas_call x1, Pallas kernels, gather_maps(): pl.pallas_call(functools.partial(gather_kernel, axes, chunks), in_specs=[...  173 us
    pallas_call x1, Pallas kernels, final_step(): pl.pallas_call(final_kernel, in_specs=[HBM, VMEM, VMEM, VMEM, HBM] + [VME...  163 us
    pallas_call x1, Pallas kernels, back_step(): pl.pallas_call(back_kernel, in_specs=[VMEM] * 12 + [HBM] * 3, out_specs=[...  156 us
    pallas_call x1, Pallas kernels, expert_step(): pl.pallas_call(expert_kernel, in_specs=[hbm] * 5, out_specs=[vmem, vmem,...  116 us
    pallas_call x1, Pallas kernels, hidden_step(): pl.pallas_call(hidden_kernel, in_specs=[VMEM] * 9 + [HBM], out_specs=[VME...  99.9 us
    pallas_call x1, Pallas kernels, turn_step(): pl.pallas_call(lambda *refs: turn_kernel(*refs[:24], (refs[24], refs[25])...  72.3 us
    pallas_call x1, Pallas kernels, attend(): pl.pallas_call(functools.partial(attend_kernel, rows), grid=(heads,), in_...  24.2 us
  transfers between devices with their start and end apart: 3, of which 0 were waited for; matrix products, arithmetic and copies ran while one was open for 8% of the time, Pallas kernels for 57%

profile of v5, /device:TPU:0, one launch (start us, length us, event | category | flops | bytes accessed | tf_op | source)
XLA Modules:
  0.0 958.7 jit_solution(204121782133399837)
XLA Ops:
  9.4 11.3 %all_gather.3 = bf16[2048,18]{1,0:T(8,128)(2,1)S(1)} all-gather(bf16[256,18]{1,0:T(8,128)(2,1)S(1)} %copy.78), channel_id=1, replica_groups=mesh['dp'=8,'tensor'=4] {'dp'}, dimensions={0}, use_global_device_ids=true | all-gather | bytes 82944 | tf_op jit(solution)/shard_map/all_gather | solution.py:1658
  20.7 5.9 fusion.69
  26.6 4.6 all-to-all-start
  33.4 2.5 fusion.21
  40.8 1.3 copy-done.25
  42.1 0.8 fusion.66
  43.6 1.0 convert_reduce_fusion
  45.0 1.0 fusion.34
  46.6 1.0 fusion.31
  48.0 1.0 pad_maximum_fusion.3
  49.0 2.5 select_convert_fusion.bias.refs_4_
  51.5 2.4 fusion.33
  53.9 1.3 pad_maximum_fusion.1
  55.1 2.1 fusion.18
  57.2 4.4 fusion.19.refs_3_
  61.6 4.6 fusion.22
  66.2 173.1 %shard_map.230 = (bf16[2,2048,512]{2,1,0:T(8,128)(2,1)}, bf16[8,2048,512]{2,1,0:T(8,128)(2,1)}, bf16[8,512,2048]{2,1,0:T(8,128)(2,1)}, bf16[1024,2048]{1,0:T(8,128)(2,1)}) custom-call(bf16[2,256,512]{2,1,0:T(8,128)(2,1)} %refs_0_, bf16[8,256,512]{2,1,0:T(8,128)(2,1)} %refs_1_, bf16[8,512,256]{2,1,0:T(8,128)(2,1)} %refs_2_, bf16[1024,2048]{1,0:T(8,128)(2,1)} %fusion.19.refs_3_), custom_call_target="tpu_custom_call" | custom-call | bytes 629145600 | tf_op jit(solution)/shard_map/pallas_call | solution.py:473
  239.3 5.3 all-to-all-start.1
  244.9 2.6 fusion.70
  248.8 2.3 constant_dynamic-slice_fusion.4
  251.1 3.1 fusion.11
  254.2 1.2 fusion.9
  255.7 10.4 %fusion.75 = f32[8,160,512]{2,1,0:T(8,128)} fusion(bf16[8,160,2048]{2,1,0:T(8,128)(2,1)S(1)} %bitcast.80, bf16[8,2048,512]{2,1,0:T(8,128)(2,1)} %get-tuple-element.83.refs_15_), kind=kOutput, calls=%fused_computation.176 | convolution fusion | flops 2684354560 | bytes 24641536 | tf_op jit(solution)/shard_map/ecd,edf->ecf/dot_general | solution.py:1746
  266.2 24.2 %shard_map.231 = (bf16[1280,512]{1,0:T(8,128)(2,1)S(1)}, bf16[512,512]{1,0:T(8,128)(2,1)S(1)}, bf16[512,512]{1,0:T(8,128)(2,1)S(1)}, f32[1280,512]{1,0:T(8,128)S(1)}, bf16[1280,512]{1,0:T(8,128)(2,1)S(1)}) custom-call(f32[1280,512]{1,0:T(8,128)} %bitcast.81, f32[512,1024]{1,0:T(8,128)S(1)} %pad_maximum_fusion.k_raw.v_raw, ...), custom_call_target="tpu_custom_call" | custom-call | flops 1342177280 | bytes 9175040 | tf_op jit(solution)/shard_map/pallas_call | solution.py:154
  290.4 1.0 copy-done.18
  291.4 0.8 copy-done.22
  292.2 0.8 copy-done.23
  293.1 12.6 %convolution_convert_fusion = bf16[8,160,2048]{2,1,0:T(8,128)(2,1)} fusion(bf16[8,160,512]{2,1,0:T(8,128)(2,1)S(1)} %bitcast.73, bf16[8,512,2048]{2,1,0:T(8,128)(2,1)} %get-tuple-element.92.refs_14_), kind=kOutput, calls=%fused_computation.13 | convolution fusion | flops 2686976000 | bytes 23330816 | tf_op jit(solution)/shard_map/ecf,efd->ecd/dot_general | solution.py:1753
  305.8 99.9 %shard_map.232 = (f32[128,2048]{1,0:T(8,128)S(1)}, bf16[512,2048]{1,0:T(8,128)(2,1)}, f32[512,128]{1,0:T(8,128)S(1)}, bf16[1024,2176]{1,0:T(8,128)(2,1)}, bf16[8,704,256]{2,1,0:T(8,128)(2,1)}) custom-call(bf16[1280,512]{1,0:T(8,128)(2,1)} %get-tuple-element.163.pick.att_pick, bf16[1280,2048]{1,0:T(8,128)(2,1)} %bitcast.76, ...), custom_call_target="tpu_custom_call" | custom-call | flops 2684354560 | bytes 314572800 | tf_op jit(solution)/shard_map/pallas_call | solution.py:607
  405.7 1.0 copy-done.19
  408.3 116.3 %shard_map.233 = (bf16[1024,2176]{1,0:T(8,128)(2,1)}, bf16[1024,512]{1,0:T(8,128)(2,1)}, bf16[8,256,1408]{2,1,0:T(8,128)(2,1)}, bf16[8,256,1408]{2,1,0:T(8,128)(2,1)}, bf16[8,1408,256]{2,1,0:T(8,128)(2,1)}) custom-call(bf16[1024,2176]{1,0:T(8,128)(2,1)} %get-tuple-element.99.x_hbm, bf16[1024,2048]{1,0:T(8,128)(2,1)} %get-tuple-element.100.cot_hbm, ...), custom_call_target="tpu_custom_call" | custom-call | flops 53150220288 | bytes 314572800 | tf_op jit(solution)/shard_map/pallas_call | solution.py:1496
  524.5 155.6 %shard_map.234 = (f32[128,2048]{1,0:T(8,128)}, bf16[512,2048]{1,0:T(8,128)(2,1)}, f32[1,2048]{1,0:T(1,128)}, bf16[128,128]{1,0:T(8,128)(2,1)}, bf16[128,2048]{1,...) custom-call(bf16[1024,2176]{1,0:T(8,128)(2,1)} %get-tuple-element.10, ...), custom_call_target="tpu_custom_call" | custom-call | flops 2147483648 | bytes 314572800 | tf_op jit(solution)/shard_map/pallas_call | solution.py:753
  680.3 0.9 copy-done.35
  681.2 0.9 pad.9.router
  683.1 1.3 fusion.29
  684.4 72.3 %shard_map.235 = (bf16[1280,512]{1,0:T(8,128)(2,1)}, bf16[2,512,512]{2,1,0:T(8,128)(2,1)}, bf16[512,2304]{1,0:T(8,128)(2,1)}, bf16[8,704,256]{2,1,0:T(8,128)(2,1)}, bf16[512,2048]{1,0:T(8,128)(2,1)}) custom-call(bf16[8,160,2048]{2,1,0:T(8,128)(2,1)} %bitcast.82, bf16[1280,512]{1,0:T(8,128)(2,1)} %copy-done.18, bf16[512,512]{1,0:T(8,128)(2,1)} %copy-done.22, ...), custom_call_target="tpu_custom_call" | custom-call | flops 3355443200 | bytes 314572800 | tf_op jit(solution)/shard_map/pallas_call | solution.py:1239
  756.7 0.7 pad_maximum_fusion.7.small
  757.4 162.9 %shard_map.236 = (bf16[10,256,512]{2,1,0:T(8,128)(2,1)}, bf16[512,2048]{1,0:T(8,128)(2,1)}, f32[24,256]{1,0:T(8,128)}, bf16[8,704,256]{2,1,0:T(8,128)(2,1)}) custom-call(bf16[8,160,2048]{2,1,0:T(8,128)(2,1)} %bitcast.77, bf16[8,160,512]{2,1,0:T(8,128)(2,1)} %bitcast.83, bf16[512,2048]{1,0:T(8,128)(2,1)} %copy-done.25, ...), custom_call_target="tpu_custom_call" | custom-call | bytes 1048576 | tf_op jit(solution)/shard_map/pallas_call | solution.py:1011
  920.3 0.7 slice.131
  921.7 2.6 copy-done.7
  924.3 2.6 copy-done.8
  927.0 1.8 copy-done.14
  928.8 11.4 %shard_map.237 = (f32[8,2,256,1408]{3,2,1,0:T(8,128)}, f32[8,1408,256]{2,1,0:T(8,128)}) custom-call(bf16[8,256,1408]{2,1,0:T(8,128)(2,1)S(1)} %copy-done.7, bf16[8,256,1408]{2,1,0:T(8,128)(2,1)S(1)} %copy-done.8, bf16[8,704,256]{2,1,0:T(8,128)(2,1)S(1)} %copy-done.13, bf16[8,704,256]{2,1,0:T(8,128)(2,1)S(1)} %copy-done.14), custom_call_target="tpu_custom_call" | custom-call | bytes 51904512 | tf_op jit(solution)/shard_map/pallas_call | solution.py:1066
  941.4 1.1 slice_convert_fusion.1
  942.5 2.6 slice_convert_fusion
  945.1 2.5 convert_element_type.185
  947.7 2.4 convert_element_type.188
  950.1 1.3 copy.93
  (181 shorter events, 17.4 us)
Async XLA Ops:
  7.2 28.9 %copy-start = (s32[1,4]{1,0:T(1,128)S(1)}, s32[1,4]{1,0:T(1,128)}, u32[]{:S(2)}) copy-start(s32[1,4]{1,0:T(1,128)} %param.17) | copy-start | bytes 52
  20.7 20.1 %copy-start.28 = (bf16[2048,18]{1,0:T(8,128)(2,1)}, bf16[2048,18]{1,0:T(8,128)(2,1)S(1)}, u32[]{:S(2)}) copy-start(bf16[2048,18]{1,0:T(8,128)(2,1)S(1)} %all_gather.3) | copy-start | bytes 221188
  26.6 4.6 copy-start.38
  26.6 212.7 %all-to-all-start = ((bf16[8,704,256]{2,1,0:T(8,128)(2,1)}), bf16[8,704,256]{2,1,0:T(8,128)(2,1)}, u32[]{:S(2)}, u32[]{:S(2)}) async-start(bf16[8,704,256]{2,1,0:T(8,128)(2,1)} %get-tuple-element.146), calls=%async_computation | async-start | bytes 5767168 | tf_op jit(solution)/shard_map/all_to_all | solution.py:1547
  32.4 3.5 copy-start.40
  35.9 3.8 copy-start.29
  39.7 1.1 copy-start.37
  39.7 266.0 %copy-start.24 = (f32[2048]{0:T(1024)}, f32[2048]{0:T(1024)S(1)}, u32[]{:S(2)}) copy-start(f32[2048]{0:T(1024)S(1)} %get-tuple-element.137) | copy-start | bytes 24580
  40.8 1.3 copy-start.25
  42.1 1.2 copy-start.47
  53.9 3.3 copy-start.36
  55.1 211.0 %copy-start.5 = (f32[1280,128]{1,0:T(8,128)}, f32[1280,128]{1,0:T(8,128)S(1)}, u32[]{:S(2)}) copy-start(f32[1280,128]{1,0:T(8,128)S(1)} %get-tuple-element.87.slot_cos.refs_6_) | copy-start | bytes 1966084
  57.2 248.5 %copy-start.2 = (bf16[1024,512]{1,0:T(8,128)(2,1)}, bf16[1024,512]{1,0:T(8,128)(2,1)S(1)}, u32[]{:S(2)}) copy-start(bf16[1024,512]{1,0:T(8,128)(2,1)S(1)} %get-tuple-element.95.hit_0) | copy-start | bytes 3145732
  57.2 248.5 %copy-start.3 = (bf16[1024,512]{1,0:T(8,128)(2,1)}, bf16[1024,512]{1,0:T(8,128)(2,1)S(1)}, u32[]{:S(2)}) copy-start(bf16[1024,512]{1,0:T(8,128)(2,1)S(1)} %get-tuple-element.96.hit_1) | copy-start | bytes 3145732
  57.2 4.4 copy-start.26
  239.3 169.0 %all-to-all-start.1 = ((bf16[8,2,256,1408]{3,2,1,0:T(8,128)(2,1)}), bf16[8,2,256,1408]{3,2,1,0:T(8,128)(2,1)}, u32[]{:S(2)}, u32[]{:S(2)}) async-start(bf16[8,2,256,1408]{3,2,1,0:T(8,128)(2,1)} %param.28), calls=%async_computation.1 | async-start | bytes 23068672 | tf_op jit(solution)/shard_map/all_to_all | solution.py:1547
  244.5 700.6 %reduce-scatter.2.cloned.1.call-start = ((), (), s32[]{:S(2)}) async-start(), calls=%async_computation.3 | async-start | bytes 18874368 | tf_op jit(solution)/shard_map/reduce_scatter | solution.py:1842
  244.8 21.3 %copy-start.4 = (f32[1280,1]{1,0:T(8,128)}, f32[1280,1]{1,0:T(8,128)S(1)}, u32[]{:S(2)}) copy-start(f32[1280,1]{1,0:T(8,128)S(1)} %copy.82.gate.refs_5_) | copy-start | bytes 15364
  244.9 6.2 copy-start.27
  247.6 58.1 %copy-start.12 = (bf16[2048,128]{1,0:T(8,128)(2,1)}, bf16[2048,128]{1,0:T(8,128)(2,1)S(1)}, u32[]{:S(2)}) copy-start(bf16[2048,128]{1,0:T(8,128)(2,1)S(1)} %pad.8.router) | copy-start | bytes 1572868
  248.2 6.0 copy-start.42
  248.8 5.4 copy-start.30
  251.1 54.6 %copy-start.11 = (bf16[128,2048]{1,0:T(8,128)(2,1)}, bf16[128,2048]{1,0:T(8,128)(2,1)S(1)}, u32[]{:S(2)}) copy-start(bf16[128,2048]{1,0:T(8,128)(2,1)S(1)} %get-tuple-element.189.x_here) | copy-start | bytes 1572868
  251.1 4.6 slice-start
  254.2 1.5 slice-start.1
  255.7 10.5 %copy-start.6 = (f32[1280,128]{1,0:T(8,128)S(1)}, f32[1280,128]{1,0:T(8,128)}, u32[]{:S(2)}) copy-start(f32[1280,128]{1,0:T(8,128)} %get-tuple-element.88.slot_sin.refs_7_) | copy-start | bytes 1966084
  255.7 10.5 %copy-start.10 = (bf16[1280,512]{1,0:T(8,128)(2,1)S(1)}, bf16[1280,512]{1,0:T(8,128)(2,1)}, u32[]{:S(2)}) copy-start(bf16[1280,512]{1,0:T(8,128)(2,1)} %select_convert_fusion.bias.refs_4_) | copy-start | bytes 3932164
  255.7 10.5 %copy-start.16 = (f32[512,128]{1,0:T(8,128)S(1)}, f32[512,128]{1,0:T(8,128)}, u32[]{:S(2)}) copy-start(f32[512,128]{1,0:T(8,128)} %get-tuple-element.89.tok_cos.refs_8_) | copy-start | bytes 786436
  255.7 10.5 %copy-start.17 = (f32[512,128]{1,0:T(8,128)S(1)}, f32[512,128]{1,0:T(8,128)}, u32[]{:S(2)}) copy-start(f32[512,128]{1,0:T(8,128)} %get-tuple-element.90.tok_sin.refs_9_) | copy-start | bytes 786436
  293.0 12.6 %copy-start.9 = (bf16[1280,512]{1,0:T(8,128)(2,1)}, bf16[1280,512]{1,0:T(8,128)(2,1)S(1)}, u32[]{:S(2)}) copy-start(bf16[1280,512]{1,0:T(8,128)(2,1)S(1)} %get-tuple-element.91.gated) | copy-start | bytes 3932164
  293.0 12.6 %copy-start.15 = (f32[1280,512]{1,0:T(8,128)}, f32[1280,512]{1,0:T(8,128)S(1)}, u32[]{:S(2)}) copy-start(f32[1280,512]{1,0:T(8,128)S(1)} %get-tuple-element.114.refs_10_) | copy-start | bytes 7864324
  293.0 12.7 %copy-start.20 = (f32[512,128]{1,0:T(8,128)S(1)}, f32[512,128]{1,0:T(8,128)}, u32[]{:S(2)}) copy-start(f32[512,128]{1,0:T(8,128)} %get-tuple-element.93.hot_0) | copy-start | bytes 786436
  293.0 12.7 %copy-start.21 = (f32[512,128]{1,0:T(8,128)S(1)}, f32[512,128]{1,0:T(8,128)}, u32[]{:S(2)}) copy-start(f32[512,128]{1,0:T(8,128)} %get-tuple-element.94.hot_1) | copy-start | bytes 786436
  305.7 101.7 %copy-start.43 = (s32[128]{0:T(128)S(1)}, s32[128]{0:T(128)}, u32[]{:S(2)}) copy-start(s32[128]{0:T(128)} %copy-done.42) | copy-start | bytes 1540
  305.7 101.7 %copy-start.45 = (s32[128]{0:T(128)S(1)}, s32[128]{0:T(128)}, u32[]{:S(2)}) copy-start(s32[128]{0:T(128)} %copy-done.44) | copy-start | bytes 1540
  680.1 1.0 copy-start.35
  680.2 1.9 copy-start.46
  680.2 3.0 copy-start.39
  684.4 72.3 %copy-start.41 = (f32[1,2048]{1,0:T(1,128)S(1)}, f32[1,2048]{1,0:T(1,128)}, u32[]{:S(2)}) copy-start(f32[1,2048]{1,0:T(1,128)} %get-tuple-element.122) | copy-start | bytes 24580
  757.4 164.3 %copy-start.13 = (bf16[8,704,256]{2,1,0:T(8,128)(2,1)S(1)}, bf16[8,704,256]{2,1,0:T(8,128)(2,1)}, u32[]{:S(2)}) copy-start(bf16[8,704,256]{2,1,0:T(8,128)(2,1)} %get-tuple-element.133.third) | copy-start | bytes 8650756
  921.7 2.6 copy-start.7
  924.3 2.6 copy-start.8
  927.0 1.8 copy-start.14
  928.8 12.6 %copy-start.31 = (bf16[10,256,512]{2,1,0:T(8,128)(2,1)S(1)}, bf16[10,256,512]{2,1,0:T(8,128)(2,1)}, u32[]{:S(2)}) copy-start(bf16[10,256,512]{2,1,0:T(8,128)(2,1)} %get-tuple-element.129) | copy-start | bytes 7864324
  942.5 2.6 copy-start.33
  945.1 2.5 copy-start.32
  947.7 2.4 copy-start.34
  947.7 3.7 copy-start.1
  (5 other events, 4.1 us)
Sparse Core Ops, SparseCore 0:
  680.3 170.3 reduce-scatter.1

commit v6 on v5

--- a/solution.py
+++ b/solution.py
@@ -826,8 +826,6 @@
     ]
     for copy in part_copies:
         copy.start()
-    late = maps_out.shape[1]
-    dealt = deal(maps_hbm, maps_out, (d_send, d_recv), pl.ds(maps_hbm.shape[1] - late, late))
 
     def to_twin(u):
         slot = lax.rem(u, GIVE)
@@ -957,6 +955,9 @@
         ).astype(BF16)
         for copy in to_near(u):
             copy.start()
+
+    late = maps_out.shape[1]
+    dealt = deal(maps_hbm, maps_out, (d_send, d_recv), pl.ds(maps_hbm.shape[1] - late, late))
 
     @pl.loop(0, units)
     def _(u):
@@ -1841,7 +1842,7 @@
     grad_att_rows = grad_att_rows.reshape(att_experts, att_cap, model_width)
     grad_output_out = lax.psum_scatter(grad_output_w, "dp", scatter_dimension=2, tiled=True)
     if fast:
-        half = grad_down_w.shape[1] // 2
+        half = grad_down_w.shape[1] * 5 // 128 * 16
         grad_q, grad_kv, normed_part, grad_down_early, mixed = turn_step(
             tensor_size, grad_att_rows, queries, key_rows, values, bias, att_gate_slots,
             slot_tables, tok_tables, attended, [hit.astype(BF16) for hit in att_hits], mixed,

time: 968 us -> 963 us (level)
  no operation moved by 1% of the time
where the time goes in v6:
time: 963 us; the launch traced here: 954 us
  Pallas kernels  811 us (84%)
  matrix products  41 us (4%)
  local copies, waits for them, and re-layouts  36.7 us (4%)
  other arithmetic  28.6 us (3%)
  between operations  15.3 us (2%)
  blocking collectives  11.3 us (1%)
  starting transfers between devices  9.87 us (1%)
    pallas_call x1, Pallas kernels, gather_maps(): pl.pallas_call(functools.partial(gather_kernel, axes, chunks), in_specs=[...  173 us
    pallas_call x1, Pallas kernels, final_step(): pl.pallas_call(final_kernel, in_specs=[HBM, VMEM, VMEM, VMEM, HBM] + [VME...  159 us
    pallas_call x1, Pallas kernels, back_step(): pl.pallas_call(back_kernel, in_specs=[VMEM] * 12 + [HBM] * 3, out_specs=[...  156 us
    pallas_call x1, Pallas kernels, expert_step(): pl.pallas_call(expert_kernel, in_specs=[hbm] * 5, out_specs=[vmem, vmem,...  116 us
    pallas_call x1, Pallas kernels, hidden_step(): pl.pallas_call(hidden_kernel, in_specs=[VMEM] * 9 + [HBM], out_specs=[VME...  99.9 us
    pallas_call x1, Pallas kernels, turn_step(): pl.pallas_call(lambda *refs: turn_kernel(*refs[:24], (refs[24], refs[25])...  71.9 us
    pallas_call x1, Pallas kernels, attend(): pl.pallas_call(functools.partial(attend_kernel, rows), grid=(heads,), in_...  24.2 us
  transfers between devices with their start and end apart: 3, of which 0 were waited for; matrix products, arithmetic and copies ran while one was open for 8% of the time, Pallas kernels for 57%

profile of v6, /device:TPU:0, one launch (start us, length us, event | category | flops | bytes accessed | tf_op | source)
XLA Modules:
  0.0 953.9 jit_solution(9591068715086337558)
XLA Ops:
  9.4 11.3 %all_gather.3 = bf16[2048,18]{1,0:T(8,128)(2,1)S(1)} all-gather(bf16[256,18]{1,0:T(8,128)(2,1)S(1)} %copy.78), channel_id=1, replica_groups=mesh['dp'=8,'tensor'=4] {'dp'}, dimensions={0}, use_global_device_ids=true | all-gather | bytes 82944 | tf_op jit(solution)/shard_map/all_gather | solution.py:1659
  20.7 5.9 fusion.69
  26.6 4.6 all-to-all-start
  33.4 2.5 fusion.21
  40.8 1.3 copy-done.25
  42.1 0.8 fusion.66
  43.6 1.0 convert_reduce_fusion
  45.0 1.0 fusion.34
  46.6 1.0 fusion.31
  48.0 1.0 pad_maximum_fusion.3
  49.0 2.5 select_convert_fusion.bias.refs_4_
  51.5 2.4 fusion.33
  53.9 1.3 pad_maximum_fusion.1
  55.2 2.1 fusion.18
  57.2 4.4 fusion.19.refs_3_
  61.6 4.6 fusion.22
  66.2 173.1 %shard_map.230 = (bf16[2,2048,512]{2,1,0:T(8,128)(2,1)}, bf16[8,2048,512]{2,1,0:T(8,128)(2,1)}, bf16[8,512,2048]{2,1,0:T(8,128)(2,1)}, bf16[1024,2048]{1,0:T(8,128)(2,1)}) custom-call(bf16[2,256,512]{2,1,0:T(8,128)(2,1)} %refs_0_, bf16[8,256,512]{2,1,0:T(8,128)(2,1)} %refs_1_, bf16[8,512,256]{2,1,0:T(8,128)(2,1)} %refs_2_, bf16[1024,2048]{1,0:T(8,128)(2,1)} %fusion.19.refs_3_), custom_call_target="tpu_custom_call" | custom-call | bytes 629145600 | tf_op jit(solution)/shard_map/pallas_call | solution.py:473
  239.3 5.3 all-to-all-start.1
  244.9 2.6 fusion.70
  248.8 2.3 constant_dynamic-slice_fusion.4
  251.1 3.1 fusion.11
  254.2 1.2 fusion.9
  255.8 10.4 %fusion.75 = f32[8,160,512]{2,1,0:T(8,128)} fusion(bf16[8,160,2048]{2,1,0:T(8,128)(2,1)S(1)} %bitcast.80, bf16[8,2048,512]{2,1,0:T(8,128)(2,1)} %get-tuple-element.83.refs_15_), kind=kOutput, calls=%fused_computation.176 | convolution fusion | flops 2684354560 | bytes 24641536 | tf_op jit(solution)/shard_map/ecd,edf->ecf/dot_general | solution.py:1747
  266.2 24.2 %shard_map.231 = (bf16[1280,512]{1,0:T(8,128)(2,1)S(1)}, bf16[512,512]{1,0:T(8,128)(2,1)S(1)}, bf16[512,512]{1,0:T(8,128)(2,1)S(1)}, f32[1280,512]{1,0:T(8,128)S(1)}, bf16[1280,512]{1,0:T(8,128)(2,1)S(1)}) custom-call(f32[1280,512]{1,0:T(8,128)} %bitcast.81, f32[512,1024]{1,0:T(8,128)S(1)} %pad_maximum_fusion.k_raw.v_raw, ...), custom_call_target="tpu_custom_call" | custom-call | flops 1342177280 | bytes 9175040 | tf_op jit(solution)/shard_map/pallas_call | solution.py:154
  290.4 1.0 copy-done.18
  291.5 0.8 copy-done.22
  292.3 0.8 copy-done.23
  293.1 12.6 %convolution_convert_fusion = bf16[8,160,2048]{2,1,0:T(8,128)(2,1)} fusion(bf16[8,160,512]{2,1,0:T(8,128)(2,1)S(1)} %bitcast.73, bf16[8,512,2048]{2,1,0:T(8,128)(2,1)} %get-tuple-element.92.refs_14_), kind=kOutput, calls=%fused_computation.13 | convolution fusion | flops 2686976000 | bytes 23330816 | tf_op jit(solution)/shard_map/ecf,efd->ecd/dot_general | solution.py:1754
  305.8 99.9 %shard_map.232 = (f32[128,2048]{1,0:T(8,128)S(1)}, bf16[512,2048]{1,0:T(8,128)(2,1)}, f32[512,128]{1,0:T(8,128)S(1)}, bf16[1024,2176]{1,0:T(8,128)(2,1)}, bf16[8,704,256]{2,1,0:T(8,128)(2,1)}) custom-call(bf16[1280,512]{1,0:T(8,128)(2,1)} %get-tuple-element.163.pick.att_pick, bf16[1280,2048]{1,0:T(8,128)(2,1)} %bitcast.76, ...), custom_call_target="tpu_custom_call" | custom-call | flops 2684354560 | bytes 314572800 | tf_op jit(solution)/shard_map/pallas_call | solution.py:607
  405.7 1.0 copy-done.19
  408.3 116.3 %shard_map.233 = (bf16[1024,2176]{1,0:T(8,128)(2,1)}, bf16[1024,512]{1,0:T(8,128)(2,1)}, bf16[8,256,1408]{2,1,0:T(8,128)(2,1)}, bf16[8,256,1408]{2,1,0:T(8,128)(2,1)}, bf16[8,1408,256]{2,1,0:T(8,128)(2,1)}) custom-call(bf16[1024,2176]{1,0:T(8,128)(2,1)} %get-tuple-element.99.x_hbm, bf16[1024,2048]{1,0:T(8,128)(2,1)} %get-tuple-element.100.cot_hbm, ...), custom_call_target="tpu_custom_call" | custom-call | flops 53150220288 | bytes 314572800 | tf_op jit(solution)/shard_map/pallas_call | solution.py:1497
  524.5 155.6 %shard_map.234 = (f32[128,2048]{1,0:T(8,128)}, bf16[512,2048]{1,0:T(8,128)(2,1)}, f32[1,2048]{1,0:T(1,128)}, bf16[128,128]{1,0:T(8,128)(2,1)}, bf16[128,2048]{1,...) custom-call(bf16[1024,2176]{1,0:T(8,128)(2,1)} %get-tuple-element.10, ...), custom_call_target="tpu_custom_call" | custom-call | flops 2147483648 | bytes 314572800 | tf_op jit(solution)/shard_map/pallas_call | solution.py:753
  680.3 0.9 copy-done.35
  681.2 0.9 pad.9.router
  683.1 1.3 fusion.29
  684.4 71.9 %shard_map.235 = (bf16[1280,512]{1,0:T(8,128)(2,1)}, bf16[2,512,512]{2,1,0:T(8,128)(2,1)}, bf16[512,2304]{1,0:T(8,128)(2,1)}, bf16[8,880,256]{2,1,0:T(8,128)(2,1)}, bf16[512,2048]{1,0:T(8,128)(2,1)}) custom-call(bf16[8,160,2048]{2,1,0:T(8,128)(2,1)} %bitcast.82, bf16[1280,512]{1,0:T(8,128)(2,1)} %copy-done.18, bf16[512,512]{1,0:T(8,128)(2,1)} %copy-done.22, ...), custom_call_target="tpu_custom_call" | custom-call | flops 3355443200 | bytes 314572800 | tf_op jit(solution)/shard_map/pallas_call | solution.py:1240
  756.4 0.7 pad_maximum_fusion.7.small
  757.1 158.6 %shard_map.236 = (bf16[10,256,512]{2,1,0:T(8,128)(2,1)}, bf16[512,2048]{1,0:T(8,128)(2,1)}, f32[24,256]{1,0:T(8,128)}, bf16[8,528,256]{2,1,0:T(8,128)(2,1)}) custom-call(bf16[8,160,2048]{2,1,0:T(8,128)(2,1)} %bitcast.77, bf16[8,160,512]{2,1,0:T(8,128)(2,1)} %bitcast.83, bf16[512,2048]{1,0:T(8,128)(2,1)} %copy-done.25, ...), custom_call_target="tpu_custom_call" | custom-call | bytes 1048576 | tf_op jit(solution)/shard_map/pallas_call | solution.py:1012
  915.7 0.7 slice.131
  917.2 2.6 copy-done.7
  919.8 2.6 copy-done.8
  922.4 1.6 copy-done.17
  924.0 11.4 %shard_map.237 = (f32[8,2,256,1408]{3,2,1,0:T(8,128)}, f32[8,1408,256]{2,1,0:T(8,128)}) custom-call(bf16[8,256,1408]{2,1,0:T(8,128)(2,1)S(1)} %copy-done.7, bf16[8,256,1408]{2,1,0:T(8,128)(2,1)S(1)} %copy-done.8, bf16[8,880,256]{2,1,0:T(8,128)(2,1)S(1)} %copy-done.13, bf16[8,528,256]{2,1,0:T(8,128)(2,1)S(1)} %copy-done.17), custom_call_target="tpu_custom_call" | custom-call | bytes 51904512 | tf_op jit(solution)/shard_map/pallas_call | solution.py:1067
  936.7 1.1 slice_convert_fusion.1
  937.8 2.6 slice_convert_fusion
  940.4 2.5 convert_element_type.185
  942.9 2.4 convert_element_type.188
  945.3 1.3 copy.93
  (181 shorter events, 17.4 us)
Async XLA Ops:
  7.2 28.9 %copy-start = (s32[1,4]{1,0:T(1,128)S(1)}, s32[1,4]{1,0:T(1,128)}, u32[]{:S(2)}) copy-start(s32[1,4]{1,0:T(1,128)} %param.17) | copy-start | bytes 52
  20.7 20.1 %copy-start.28 = (bf16[2048,18]{1,0:T(8,128)(2,1)}, bf16[2048,18]{1,0:T(8,128)(2,1)S(1)}, u32[]{:S(2)}) copy-start(bf16[2048,18]{1,0:T(8,128)(2,1)S(1)} %all_gather.3) | copy-start | bytes 221188
  26.6 4.6 copy-start.38
  26.6 212.7 %all-to-all-start = ((bf16[8,704,256]{2,1,0:T(8,128)(2,1)}), bf16[8,704,256]{2,1,0:T(8,128)(2,1)}, u32[]{:S(2)}, u32[]{:S(2)}) async-start(bf16[8,704,256]{2,1,0:T(8,128)(2,1)} %get-tuple-element.146), calls=%async_computation | async-start | bytes 5767168 | tf_op jit(solution)/shard_map/all_to_all | solution.py:1548
  32.4 3.5 copy-start.40
  35.9 3.8 copy-start.29
  39.7 1.1 copy-start.37
  39.7 266.0 %copy-start.24 = (f32[2048]{0:T(1024)}, f32[2048]{0:T(1024)S(1)}, u32[]{:S(2)}) copy-start(f32[2048]{0:T(1024)S(1)} %get-tuple-element.137) | copy-start | bytes 24580
  40.8 1.3 copy-start.25
  42.1 1.2 copy-start.47
  53.9 3.3 copy-start.36
  55.1 211.0 %copy-start.5 = (f32[1280,128]{1,0:T(8,128)}, f32[1280,128]{1,0:T(8,128)S(1)}, u32[]{:S(2)}) copy-start(f32[1280,128]{1,0:T(8,128)S(1)} %get-tuple-element.87.slot_cos.refs_6_) | copy-start | bytes 1966084
  57.2 248.5 %copy-start.2 = (bf16[1024,512]{1,0:T(8,128)(2,1)}, bf16[1024,512]{1,0:T(8,128)(2,1)S(1)}, u32[]{:S(2)}) copy-start(bf16[1024,512]{1,0:T(8,128)(2,1)S(1)} %get-tuple-element.95.hit_0) | copy-start | bytes 3145732
  57.2 248.5 %copy-start.3 = (bf16[1024,512]{1,0:T(8,128)(2,1)}, bf16[1024,512]{1,0:T(8,128)(2,1)S(1)}, u32[]{:S(2)}) copy-start(bf16[1024,512]{1,0:T(8,128)(2,1)S(1)} %get-tuple-element.96.hit_1) | copy-start | bytes 3145732
  57.2 4.4 copy-start.26
  239.3 169.0 %all-to-all-start.1 = ((bf16[8,2,256,1408]{3,2,1,0:T(8,128)(2,1)}), bf16[8,2,256,1408]{3,2,1,0:T(8,128)(2,1)}, u32[]{:S(2)}, u32[]{:S(2)}) async-start(bf16[8,2,256,1408]{3,2,1,0:T(8,128)(2,1)} %param.28), calls=%async_computation.1 | async-start | bytes 23068672 | tf_op jit(solution)/shard_map/all_to_all | solution.py:1548
  244.5 695.8 %reduce-scatter.2.cloned.1.call-start = ((), (), s32[]{:S(2)}) async-start(), calls=%async_computation.3 | async-start | bytes 18874368 | tf_op jit(solution)/shard_map/reduce_scatter | solution.py:1843
  244.8 21.3 %copy-start.4 = (f32[1280,1]{1,0:T(8,128)}, f32[1280,1]{1,0:T(8,128)S(1)}, u32[]{:S(2)}) copy-start(f32[1280,1]{1,0:T(8,128)S(1)} %copy.82.gate.refs_5_) | copy-start | bytes 15364
  244.9 6.2 copy-start.27
  247.6 58.1 %copy-start.12 = (bf16[2048,128]{1,0:T(8,128)(2,1)}, bf16[2048,128]{1,0:T(8,128)(2,1)S(1)}, u32[]{:S(2)}) copy-start(bf16[2048,128]{1,0:T(8,128)(2,1)S(1)} %pad.8.router) | copy-start | bytes 1572868
  248.2 6.0 copy-start.42
  248.8 5.4 copy-start.30
  251.1 54.6 %copy-start.11 = (bf16[128,2048]{1,0:T(8,128)(2,1)}, bf16[128,2048]{1,0:T(8,128)(2,1)S(1)}, u32[]{:S(2)}) copy-start(bf16[128,2048]{1,0:T(8,128)(2,1)S(1)} %get-tuple-element.189.x_here) | copy-start | bytes 1572868
  251.1 4.6 slice-start
  254.2 1.5 slice-start.1
  255.7 10.5 %copy-start.6 = (f32[1280,128]{1,0:T(8,128)S(1)}, f32[1280,128]{1,0:T(8,128)}, u32[]{:S(2)}) copy-start(f32[1280,128]{1,0:T(8,128)} %get-tuple-element.88.slot_sin.refs_7_) | copy-start | bytes 1966084
  255.7 10.5 %copy-start.10 = (bf16[1280,512]{1,0:T(8,128)(2,1)S(1)}, bf16[1280,512]{1,0:T(8,128)(2,1)}, u32[]{:S(2)}) copy-start(bf16[1280,512]{1,0:T(8,128)(2,1)} %select_convert_fusion.bias.refs_4_) | copy-start | bytes 3932164
  255.7 10.5 %copy-start.15 = (f32[512,128]{1,0:T(8,128)S(1)}, f32[512,128]{1,0:T(8,128)}, u32[]{:S(2)}) copy-start(f32[512,128]{1,0:T(8,128)} %get-tuple-element.89.tok_cos.refs_8_) | copy-start | bytes 786436
  255.7 10.5 %copy-start.16 = (f32[512,128]{1,0:T(8,128)S(1)}, f32[512,128]{1,0:T(8,128)}, u32[]{:S(2)}) copy-start(f32[512,128]{1,0:T(8,128)} %get-tuple-element.90.tok_sin.refs_9_) | copy-start | bytes 786436
  293.1 12.6 %copy-start.9 = (bf16[1280,512]{1,0:T(8,128)(2,1)}, bf16[1280,512]{1,0:T(8,128)(2,1)S(1)}, u32[]{:S(2)}) copy-start(bf16[1280,512]{1,0:T(8,128)(2,1)S(1)} %get-tuple-element.91.gated) | copy-start | bytes 3932164
  293.1 12.6 %copy-start.14 = (f32[1280,512]{1,0:T(8,128)}, f32[1280,512]{1,0:T(8,128)S(1)}, u32[]{:S(2)}) copy-start(f32[1280,512]{1,0:T(8,128)S(1)} %get-tuple-element.114.refs_10_) | copy-start | bytes 7864324
  293.1 12.7 %copy-start.20 = (f32[512,128]{1,0:T(8,128)S(1)}, f32[512,128]{1,0:T(8,128)}, u32[]{:S(2)}) copy-start(f32[512,128]{1,0:T(8,128)} %get-tuple-element.93.hot_0) | copy-start | bytes 786436
  293.1 12.7 %copy-start.21 = (f32[512,128]{1,0:T(8,128)S(1)}, f32[512,128]{1,0:T(8,128)}, u32[]{:S(2)}) copy-start(f32[512,128]{1,0:T(8,128)} %get-tuple-element.94.hot_1) | copy-start | bytes 786436
  305.8 101.7 %copy-start.43 = (s32[128]{0:T(128)S(1)}, s32[128]{0:T(128)}, u32[]{:S(2)}) copy-start(s32[128]{0:T(128)} %copy-done.42) | copy-start | bytes 1540
  305.8 101.7 %copy-start.45 = (s32[128]{0:T(128)S(1)}, s32[128]{0:T(128)}, u32[]{:S(2)}) copy-start(s32[128]{0:T(128)} %copy-done.44) | copy-start | bytes 1540
  680.2 1.0 copy-start.35
  680.2 1.9 copy-start.46
  680.2 3.0 copy-start.39
  684.4 71.9 %copy-start.41 = (f32[1,2048]{1,0:T(1,128)S(1)}, f32[1,2048]{1,0:T(1,128)}, u32[]{:S(2)}) copy-start(f32[1,2048]{1,0:T(1,128)} %get-tuple-element.122) | copy-start | bytes 24580
  757.1 160.0 %copy-start.13 = (bf16[8,880,256]{2,1,0:T(8,128)(2,1)S(1)}, bf16[8,880,256]{2,1,0:T(8,128)(2,1)}, u32[]{:S(2)}) copy-start(bf16[8,880,256]{2,1,0:T(8,128)(2,1)} %get-tuple-element.133.third) | copy-start | bytes 10813444
  917.2 2.6 copy-start.7
  919.8 2.6 copy-start.8
  922.4 1.6 copy-start.17
  924.0 12.6 %copy-start.31 = (bf16[10,256,512]{2,1,0:T(8,128)(2,1)S(1)}, bf16[10,256,512]{2,1,0:T(8,128)(2,1)}, u32[]{:S(2)}) copy-start(bf16[10,256,512]{2,1,0:T(8,128)(2,1)} %get-tuple-element.129) | copy-start | bytes 7864324
  937.8 2.6 copy-start.33
  940.4 2.5 copy-start.32
  942.9 2.4 copy-start.34
  942.9 3.7 copy-start.1
  (5 other events, 4.1 us)
Sparse Core Ops, SparseCore 0:
  680.3 169.5 reduce-scatter.1

commit v7 on v6

--- a/solution.py
+++ b/solution.py
@@ -1842,7 +1842,7 @@
     grad_att_rows = grad_att_rows.reshape(att_experts, att_cap, model_width)
     grad_output_out = lax.psum_scatter(grad_output_w, "dp", scatter_dimension=2, tiled=True)
     if fast:
-        half = grad_down_w.shape[1] * 5 // 128 * 16
+        half = grad_down_w.shape[1] * 6 // 128 * 16
         grad_q, grad_kv, normed_part, grad_down_early, mixed = turn_step(
             tensor_size, grad_att_rows, queries, key_rows, values, bias, att_gate_slots,
             slot_tables, tok_tables, attended, [hit.astype(BF16) for hit in att_hits], mixed,

time: 963 us -> 965 us (level)
    pallas_call x1, Pallas kernels: 159 us -> 143 us  [final_step(): pl.pallas_call(final_kernel, in_specs=[HBM, VMEM, VMEM, VMEM, HBM] + [VME...]
    pallas_call x1, Pallas kernels: 71.9 us -> 87 us  [turn_step(): pl.pallas_call(lambda *refs: turn_kernel(*refs[:24], (refs[24], refs[25])...]
  transfers between devices with their start and end apart: 3 -> 3, of which waited for: 0 -> 0; matrix products, arithmetic and copies ran while one was open for 8% -> 8% of each run, Pallas kernels for 57% -> 56%
where the time goes in v7:
time: 965 us; the launch traced here: 956 us
  Pallas kernels  811 us (84%)
  matrix products  41 us (4%)
  local copies, waits for them, and re-layouts  38.7 us (4%)
  other arithmetic  28.6 us (3%)
  between operations  15.3 us (2%)
  blocking collectives  11.3 us (1%)
  starting transfers between devices  9.87 us (1%)
    pallas_call x1, Pallas kernels, gather_maps(): pl.pallas_call(functools.partial(gather_kernel, axes, chunks), in_specs=[...  173 us
    pallas_call x1, Pallas kernels, back_step(): pl.pallas_call(back_kernel, in_specs=[VMEM] * 12 + [HBM] * 3, out_specs=[...  156 us
    pallas_call x1, Pallas kernels, final_step(): pl.pallas_call(final_kernel, in_specs=[HBM, VMEM, VMEM, VMEM, HBM] + [VME...  143 us
    pallas_call x1, Pallas kernels, expert_step(): pl.pallas_call(expert_kernel, in_specs=[hbm] * 5, out_specs=[vmem, vmem,...  116 us
    pallas_call x1, Pallas kernels, hidden_step(): pl.pallas_call(hidden_kernel, in_specs=[VMEM] * 9 + [HBM], out_specs=[VME...  99.9 us
    pallas_call x1, Pallas kernels, turn_step(): pl.pallas_call(lambda *refs: turn_kernel(*refs[:24], (refs[24], refs[25])...  87 us
    pallas_call x1, Pallas kernels, attend(): pl.pallas_call(functools.partial(attend_kernel, rows), grid=(heads,), in_...  24.2 us
  transfers between devices with their start and end apart: 3, of which 0 were waited for; matrix products, arithmetic and copies ran while one was open for 8% of the time, Pallas kernels for 56%

profile of v7, /device:TPU:0, one launch (start us, length us, event | category | flops | bytes accessed | tf_op | source)
XLA Modules:
  0.0 955.8 jit_solution(6700047317723706276)
XLA Ops:
  9.4 11.3 %all_gather.3 = bf16[2048,18]{1,0:T(8,128)(2,1)S(1)} all-gather(bf16[256,18]{1,0:T(8,128)(2,1)S(1)} %copy.78), channel_id=1, replica_groups=mesh['dp'=8,'tensor'=4] {'dp'}, dimensions={0}, use_global_device_ids=true | all-gather | bytes 82944 | tf_op jit(solution)/shard_map/all_gather | solution.py:1659
  20.7 5.9 fusion.69
  26.6 4.6 all-to-all-start
  33.4 2.5 fusion.21
  40.8 1.3 copy-done.25
  42.1 0.8 fusion.66
  43.6 1.0 convert_reduce_fusion
  45.0 1.0 fusion.34
  46.6 1.0 fusion.31
  48.0 1.0 pad_maximum_fusion.3
  49.0 2.5 select_convert_fusion.bias.refs_4_
  51.5 2.4 fusion.33
  53.9 1.3 pad_maximum_fusion.1
  55.1 2.1 fusion.18
  57.2 4.4 fusion.19.refs_3_
  61.6 4.6 fusion.22
  66.2 173.1 %shard_map.230 = (bf16[2,2048,512]{2,1,0:T(8,128)(2,1)}, bf16[8,2048,512]{2,1,0:T(8,128)(2,1)}, bf16[8,512,2048]{2,1,0:T(8,128)(2,1)}, bf16[1024,2048]{1,0:T(8,128)(2,1)}) custom-call(bf16[2,256,512]{2,1,0:T(8,128)(2,1)} %refs_0_, bf16[8,256,512]{2,1,0:T(8,128)(2,1)} %refs_1_, bf16[8,512,256]{2,1,0:T(8,128)(2,1)} %refs_2_, bf16[1024,2048]{1,0:T(8,128)(2,1)} %fusion.19.refs_3_), custom_call_target="tpu_custom_call" | custom-call | bytes 629145600 | tf_op jit(solution)/shard_map/pallas_call | solution.py:473
  239.3 5.3 all-to-all-start.1
  244.9 2.6 fusion.70
  248.8 2.3 constant_dynamic-slice_fusion.4
  251.1 3.1 fusion.11
  254.2 1.2 fusion.9
  255.7 10.4 %fusion.75 = f32[8,160,512]{2,1,0:T(8,128)} fusion(bf16[8,160,2048]{2,1,0:T(8,128)(2,1)S(1)} %bitcast.80, bf16[8,2048,512]{2,1,0:T(8,128)(2,1)} %get-tuple-element.83.refs_15_), kind=kOutput, calls=%fused_computation.176 | convolution fusion | flops 2684354560 | bytes 24641536 | tf_op jit(solution)/shard_map/ecd,edf->ecf/dot_general | solution.py:1747
  266.2 24.2 %shard_map.231 = (bf16[1280,512]{1,0:T(8,128)(2,1)S(1)}, bf16[512,512]{1,0:T(8,128)(2,1)S(1)}, bf16[512,512]{1,0:T(8,128)(2,1)S(1)}, f32[1280,512]{1,0:T(8,128)S(1)}, bf16[1280,512]{1,0:T(8,128)(2,1)S(1)}) custom-call(f32[1280,512]{1,0:T(8,128)} %bitcast.81, f32[512,1024]{1,0:T(8,128)S(1)} %pad_maximum_fusion.k_raw.v_raw, ...), custom_call_target="tpu_custom_call" | custom-call | flops 1342177280 | bytes 9175040 | tf_op jit(solution)/shard_map/pallas_call | solution.py:154
  290.4 1.0 copy-done.18
  291.4 0.8 copy-done.22
  292.2 0.8 copy-done.23
  293.1 12.6 %convolution_convert_fusion = bf16[8,160,2048]{2,1,0:T(8,128)(2,1)} fusion(bf16[8,160,512]{2,1,0:T(8,128)(2,1)S(1)} %bitcast.73, bf16[8,512,2048]{2,1,0:T(8,128)(2,1)} %get-tuple-element.92.refs_14_), kind=kOutput, calls=%fused_computation.13 | convolution fusion | flops 2686976000 | bytes 23330816 | tf_op jit(solution)/shard_map/ecf,efd->ecd/dot_general | solution.py:1754
  305.8 99.9 %shard_map.232 = (f32[128,2048]{1,0:T(8,128)S(1)}, bf16[512,2048]{1,0:T(8,128)(2,1)}, f32[512,128]{1,0:T(8,128)S(1)}, bf16[1024,2176]{1,0:T(8,128)(2,1)}, bf16[8,704,256]{2,1,0:T(8,128)(2,1)}) custom-call(bf16[1280,512]{1,0:T(8,128)(2,1)} %get-tuple-element.163.pick.att_pick, bf16[1280,2048]{1,0:T(8,128)(2,1)} %bitcast.76, ...), custom_call_target="tpu_custom_call" | custom-call | flops 2684354560 | bytes 314572800 | tf_op jit(solution)/shard_map/pallas_call | solution.py:607
  405.7 1.0 copy-done.19
  408.3 116.3 %shard_map.233 = (bf16[1024,2176]{1,0:T(8,128)(2,1)}, bf16[1024,512]{1,0:T(8,128)(2,1)}, bf16[8,256,1408]{2,1,0:T(8,128)(2,1)}, bf16[8,256,1408]{2,1,0:T(8,128)(2,1)}, bf16[8,1408,256]{2,1,0:T(8,128)(2,1)}) custom-call(bf16[1024,2176]{1,0:T(8,128)(2,1)} %get-tuple-element.99.x_hbm, bf16[1024,2048]{1,0:T(8,128)(2,1)} %get-tuple-element.100.cot_hbm, ...), custom_call_target="tpu_custom_call" | custom-call | flops 53150220288 | bytes 314572800 | tf_op jit(solution)/shard_map/pallas_call | solution.py:1497
  524.5 155.6 %shard_map.234 = (f32[128,2048]{1,0:T(8,128)}, bf16[512,2048]{1,0:T(8,128)(2,1)}, f32[1,2048]{1,0:T(1,128)}, bf16[128,128]{1,0:T(8,128)(2,1)}, bf16[128,2048]{1,...) custom-call(bf16[1024,2176]{1,0:T(8,128)(2,1)} %get-tuple-element.10, ...), custom_call_target="tpu_custom_call" | custom-call | flops 2147483648 | bytes 314572800 | tf_op jit(solution)/shard_map/pallas_call | solution.py:753
  680.3 0.9 copy-done.35
  681.2 0.9 pad.9.router
  683.1 1.3 fusion.29
  684.4 87.0 %shard_map.235 = (bf16[1280,512]{1,0:T(8,128)(2,1)}, bf16[2,512,512]{2,1,0:T(8,128)(2,1)}, bf16[512,2304]{1,0:T(8,128)(2,1)}, bf16[8,1056,256]{2,1,0:T(8,128)(2,1)}, bf16[512,2048]{1,0:T(8,128)(2,1)}) custom-call(bf16[8,160,2048]{2,1,0:T(8,128)(2,1)} %bitcast.82, bf16[1280,512]{1,0:T(8,128)(2,1)} %copy-done.18, bf16[512,512]{1,0:T(8,128)(2,1)} %copy-done.22, ...), custom_call_target="tpu_custom_call" | custom-call | flops 3355443200 | bytes 314572800 | tf_op jit(solution)/shard_map/pallas_call | solution.py:1240
  771.4 0.7 pad_maximum_fusion.7.small
  772.1 143.5 %shard_map.236 = (bf16[10,256,512]{2,1,0:T(8,128)(2,1)}, bf16[512,2048]{1,0:T(8,128)(2,1)}, f32[24,256]{1,0:T(8,128)}, bf16[8,352,256]{2,1,0:T(8,128)(2,1)}) custom-call(bf16[8,160,2048]{2,1,0:T(8,128)(2,1)} %bitcast.77, bf16[8,160,512]{2,1,0:T(8,128)(2,1)} %bitcast.83, bf16[512,2048]{1,0:T(8,128)(2,1)} %copy-done.25, ...), custom_call_target="tpu_custom_call" | custom-call | bytes 1048576 | tf_op jit(solution)/shard_map/pallas_call | solution.py:1012
  917.0 2.6 copy-done.7
  919.7 2.6 copy-done.8
  922.3 2.2 copy-done.13
  924.5 1.4 copy-done.17
  925.9 11.4 %shard_map.237 = (f32[8,2,256,1408]{3,2,1,0:T(8,128)}, f32[8,1408,256]{2,1,0:T(8,128)}) custom-call(bf16[8,256,1408]{2,1,0:T(8,128)(2,1)S(1)} %copy-done.7, bf16[8,256,1408]{2,1,0:T(8,128)(2,1)S(1)} %copy-done.8, bf16[8,1056,256]{2,1,0:T(8,128)(2,1)S(1)} %copy-done.13, bf16[8,352,256]{2,1,0:T(8,128)(2,1)S(1)} %copy-done.17), custom_call_target="tpu_custom_call" | custom-call | bytes 51904512 | tf_op jit(solution)/shard_map/pallas_call | solution.py:1067
  938.5 1.1 slice_convert_fusion.1
  939.6 2.6 slice_convert_fusion
  942.2 2.5 convert_element_type.185
  944.8 2.4 convert_element_type.188
  947.2 1.3 copy.93
  (181 shorter events, 18.1 us)
Async XLA Ops:
  7.2 28.9 %copy-start = (s32[1,4]{1,0:T(1,128)S(1)}, s32[1,4]{1,0:T(1,128)}, u32[]{:S(2)}) copy-start(s32[1,4]{1,0:T(1,128)} %param.17) | copy-start | bytes 52
  20.7 20.1 %copy-start.28 = (bf16[2048,18]{1,0:T(8,128)(2,1)}, bf16[2048,18]{1,0:T(8,128)(2,1)S(1)}, u32[]{:S(2)}) copy-start(bf16[2048,18]{1,0:T(8,128)(2,1)S(1)} %all_gather.3) | copy-start | bytes 221188
  26.6 4.6 copy-start.38
  26.6 212.7 %all-to-all-start = ((bf16[8,704,256]{2,1,0:T(8,128)(2,1)}), bf16[8,704,256]{2,1,0:T(8,128)(2,1)}, u32[]{:S(2)}, u32[]{:S(2)}) async-start(bf16[8,704,256]{2,1,0:T(8,128)(2,1)} %get-tuple-element.146), calls=%async_computation | async-start | bytes 5767168 | tf_op jit(solution)/shard_map/all_to_all | solution.py:1548
  32.4 3.5 copy-start.40
  35.9 3.8 copy-start.29
  39.7 1.1 copy-start.37
  39.7 266.0 %copy-start.24 = (f32[2048]{0:T(1024)}, f32[2048]{0:T(1024)S(1)}, u32[]{:S(2)}) copy-start(f32[2048]{0:T(1024)S(1)} %get-tuple-element.137) | copy-start | bytes 24580
  40.8 1.3 copy-start.25
  42.1 1.2 copy-start.47
  53.9 3.3 copy-start.36
  55.1 211.0 %copy-start.5 = (f32[1280,128]{1,0:T(8,128)}, f32[1280,128]{1,0:T(8,128)S(1)}, u32[]{:S(2)}) copy-start(f32[1280,128]{1,0:T(8,128)S(1)} %get-tuple-element.87.slot_cos.refs_6_) | copy-start | bytes 1966084
  57.2 248.5 %copy-start.2 = (bf16[1024,512]{1,0:T(8,128)(2,1)}, bf16[1024,512]{1,0:T(8,128)(2,1)S(1)}, u32[]{:S(2)}) copy-start(bf16[1024,512]{1,0:T(8,128)(2,1)S(1)} %get-tuple-element.95.hit_0) | copy-start | bytes 3145732
  57.2 248.5 %copy-start.3 = (bf16[1024,512]{1,0:T(8,128)(2,1)}, bf16[1024,512]{1,0:T(8,128)(2,1)S(1)}, u32[]{:S(2)}) copy-start(bf16[1024,512]{1,0:T(8,128)(2,1)S(1)} %get-tuple-element.96.hit_1) | copy-start | bytes 3145732
  57.2 4.4 copy-start.26
  239.3 169.0 %all-to-all-start.1 = ((bf16[8,2,256,1408]{3,2,1,0:T(8,128)(2,1)}), bf16[8,2,256,1408]{3,2,1,0:T(8,128)(2,1)}, u32[]{:S(2)}, u32[]{:S(2)}) async-start(bf16[8,2,256,1408]{3,2,1,0:T(8,128)(2,1)} %param.28), calls=%async_computation.1 | async-start | bytes 23068672 | tf_op jit(solution)/shard_map/all_to_all | solution.py:1548
  244.5 697.7 %reduce-scatter.2.cloned.1.call-start = ((), (), s32[]{:S(2)}) async-start(), calls=%async_computation.3 | async-start | bytes 18874368 | tf_op jit(solution)/shard_map/reduce_scatter | solution.py:1843
  244.8 21.3 %copy-start.4 = (f32[1280,1]{1,0:T(8,128)}, f32[1280,1]{1,0:T(8,128)S(1)}, u32[]{:S(2)}) copy-start(f32[1280,1]{1,0:T(8,128)S(1)} %copy.82.gate.refs_5_) | copy-start | bytes 15364
  244.9 6.2 copy-start.27
  247.6 58.1 %copy-start.12 = (bf16[2048,128]{1,0:T(8,128)(2,1)}, bf16[2048,128]{1,0:T(8,128)(2,1)S(1)}, u32[]{:S(2)}) copy-start(bf16[2048,128]{1,0:T(8,128)(2,1)S(1)} %pad.8.router) | copy-start | bytes 1572868
  248.2 6.0 copy-start.42
  248.8 5.4 copy-start.30
  251.1 54.6 %copy-start.11 = (bf16[128,2048]{1,0:T(8,128)(2,1)}, bf16[128,2048]{1,0:T(8,128)(2,1)S(1)}, u32[]{:S(2)}) copy-start(bf16[128,2048]{1,0:T(8,128)(2,1)S(1)} %get-tuple-element.189.x_here) | copy-start | bytes 1572868
  251.1 4.6 slice-start
  254.2 1.5 slice-start.1
  255.7 10.5 %copy-start.6 = (f32[1280,128]{1,0:T(8,128)S(1)}, f32[1280,128]{1,0:T(8,128)}, u32[]{:S(2)}) copy-start(f32[1280,128]{1,0:T(8,128)} %get-tuple-element.88.slot_sin.refs_7_) | copy-start | bytes 1966084
  255.7 10.5 %copy-start.10 = (bf16[1280,512]{1,0:T(8,128)(2,1)S(1)}, bf16[1280,512]{1,0:T(8,128)(2,1)}, u32[]{:S(2)}) copy-start(bf16[1280,512]{1,0:T(8,128)(2,1)} %select_convert_fusion.bias.refs_4_) | copy-start | bytes 3932164
  255.7 10.5 %copy-start.15 = (f32[512,128]{1,0:T(8,128)S(1)}, f32[512,128]{1,0:T(8,128)}, u32[]{:S(2)}) copy-start(f32[512,128]{1,0:T(8,128)} %get-tuple-element.89.tok_cos.refs_8_) | copy-start | bytes 786436
  255.7 10.5 %copy-start.16 = (f32[512,128]{1,0:T(8,128)S(1)}, f32[512,128]{1,0:T(8,128)}, u32[]{:S(2)}) copy-start(f32[512,128]{1,0:T(8,128)} %get-tuple-element.90.tok_sin.refs_9_) | copy-start | bytes 786436
  293.0 12.6 %copy-start.9 = (bf16[1280,512]{1,0:T(8,128)(2,1)}, bf16[1280,512]{1,0:T(8,128)(2,1)S(1)}, u32[]{:S(2)}) copy-start(bf16[1280,512]{1,0:T(8,128)(2,1)S(1)} %get-tuple-element.91.gated) | copy-start | bytes 3932164
  293.0 12.6 %copy-start.14 = (f32[1280,512]{1,0:T(8,128)}, f32[1280,512]{1,0:T(8,128)S(1)}, u32[]{:S(2)}) copy-start(f32[1280,512]{1,0:T(8,128)S(1)} %get-tuple-element.114.refs_10_) | copy-start | bytes 7864324
  293.0 12.7 %copy-start.20 = (f32[512,128]{1,0:T(8,128)S(1)}, f32[512,128]{1,0:T(8,128)}, u32[]{:S(2)}) copy-start(f32[512,128]{1,0:T(8,128)} %get-tuple-element.93.hot_0) | copy-start | bytes 786436
  293.0 12.7 %copy-start.21 = (f32[512,128]{1,0:T(8,128)S(1)}, f32[512,128]{1,0:T(8,128)}, u32[]{:S(2)}) copy-start(f32[512,128]{1,0:T(8,128)} %get-tuple-element.94.hot_1) | copy-start | bytes 786436
  305.7 101.7 %copy-start.43 = (s32[128]{0:T(128)S(1)}, s32[128]{0:T(128)}, u32[]{:S(2)}) copy-start(s32[128]{0:T(128)} %copy-done.42) | copy-start | bytes 1540
  305.7 101.7 %copy-start.45 = (s32[128]{0:T(128)S(1)}, s32[128]{0:T(128)}, u32[]{:S(2)}) copy-start(s32[128]{0:T(128)} %copy-done.44) | copy-start | bytes 1540
  680.1 1.0 copy-start.35
  680.2 1.9 copy-start.46
  680.2 3.0 copy-start.39
  684.4 87.0 %copy-start.41 = (f32[1,2048]{1,0:T(1,128)S(1)}, f32[1,2048]{1,0:T(1,128)}, u32[]{:S(2)}) copy-start(f32[1,2048]{1,0:T(1,128)} %get-tuple-element.122) | copy-start | bytes 24580
  917.0 2.6 copy-start.7
  919.7 2.6 copy-start.8
  922.3 2.2 copy-start.13
  924.5 1.4 copy-start.17
  925.9 12.6 %copy-start.31 = (bf16[10,256,512]{2,1,0:T(8,128)(2,1)S(1)}, bf16[10,256,512]{2,1,0:T(8,128)(2,1)}, u32[]{:S(2)}) copy-start(bf16[10,256,512]{2,1,0:T(8,128)(2,1)} %get-tuple-element.129) | copy-start | bytes 7864324
  939.6 2.6 copy-start.33
  942.2 2.5 copy-start.32
  944.8 2.4 copy-start.34
  944.8 3.7 copy-start.1
  (5 other events, 4.1 us)
Sparse Core Ops, SparseCore 0:
  680.3 169.0 reduce-scatter.1
